TPU v7x, 32 devices: a whole 2x2x4 slice. The times are simulated.
32 devices in a mesh: dp: 32 (over z, y, x, core).
Axes of the slice: x: 2, y: 2, z: 4, core: 2. Of those that a mesh axis runs over, the one named last changes fastest.
Arguments:
- tokens: bfloat16 [65536, 512], P('dp'), may hold values from -11 to 11
- cotangent: bfloat16 [65536, 512], P('dp'), may hold values from -6 to 6
- segment_ids: int32 [65536], P('dp'), may hold values from 0 to 1023, never falling along the last dimension, each value on 1 to 128 neighbouring positions
- row_lengths: int32 [64], P('dp'), may hold values from 0 to 2048, as said below
- row_widths: int32 [32], P('dp'), may hold values from 0 to 1, as said below
- params: float32 [3151872], P('dp'), may hold values from -3 to 3, as said below
- momenta: float32 [3151872], P('dp'), may hold values from -0.0034179688 to 0.0034179688
- averages: float32 [3151872], P('dp'), may hold values from -3 to 3
Outputs:
- layer_output: bfloat16 [65536, 512], P('dp')
- input_grad: float32 [65536, 512], P('dp')
- grad_norm: float32 [], replicated
- vector_grads: float32 [512, 12], replicated
- new_params: float32 [3151872], P('dp')
- new_momenta: float32 [3151872], P('dp')
- new_averages: float32 [3151872], P('dp')
Inputs may be any that keep to these rules, and one draw needn't show every extreme that they name: `segment_ids`: never falling along the slots; each sentence covers 1 to 128 consecutive slots, some exactly 128. `row_lengths`: entries 2g and 2g + 1 belong to group g. In a group of two rows they are the live slots of each row, 512 to 1024; in a group of one row the first is its live slots, 1024 to 2048, and the second is 0. In every draw some group is one row with all 2048 slots live. `row_widths`: in every draw some groups are one row and some are two. `params`: gains are positive.
All inputs are finite; a program needn't handle non-finite values.
Results may differ from a plain program's by a relative error of at most 0.012.
Values may be sent and summed in bfloat16 or wider, within the bound.
No kernel may reach another device: no remote copies, remote signals or barrier semaphores. Data moves between devices by JAX's collectives and lax.ppermute only.
A program may use at most 192 MiB of HBM per device.

v0:
```python
import jax
import jax.numpy as jnp
from jax import lax
from jax.sharding import PartitionSpec as P

HD = 64
ROW = 1024
SENT = 64


EPSILON = 1e-05
CLIP_NORM = 1.0
LEARN_RATE = 20.0
MOMENTUM = 0.5
AVERAGE_DECAY = 0.5
MASKED = -1e30


def mixed_dot(left_side, right_side):
    return jnp.dot(left_side, right_side, preferred_element_type=jnp.float32)


def cross_rows(left_side, right_side):
    return jnp.einsum("ta,tb->ab", left_side, right_side, preferred_element_type=jnp.float32)


def column_sum(values):
    return jnp.sum(values.astype(jnp.float32), axis=0)


def unpack(buffer, model_width):
    table = buffer.reshape(model_width, 12 * (model_width + 1))
    hidden_width = 4 * model_width
    matrices = (
        table[:, :model_width],
        table[:, model_width : 2 * model_width],
        table[:, 2 * model_width : 3 * model_width],
        table[:, 3 * model_width : 4 * model_width],
        table[:, 4 * model_width : 4 * model_width + hidden_width],
        table[:, 4 * model_width + hidden_width : 12 * model_width],
    )
    vectors = table[:, 12 * model_width :].astype(jnp.float32)
    return (matrices, vectors)


def norm_forward(values, gain_vec, shift_vec):
    centre = jnp.mean(values, axis=-1, keepdims=True)
    centred = values - centre
    inverse = lax.rsqrt(jnp.mean(centred * centred, axis=-1, keepdims=True) + EPSILON)
    normed = centred * inverse
    return (normed * gain_vec + shift_vec, normed, inverse)


def norm_backward(grad_out, normed, inverse, gain_vec):
    scaled = grad_out * gain_vec
    grad_in = inverse * (
        scaled
        - jnp.mean(scaled, axis=-1, keepdims=True)
        - normed * jnp.mean(scaled * normed, axis=-1, keepdims=True)
    )
    return (grad_in, jnp.sum(grad_out * normed, axis=0), jnp.sum(grad_out, axis=0))


def block_allowed(layout, begin_at, block_rows, window):
    row_number, segments, positions, key_rows, key_groups, key_live, key_places = layout
    query_row = lax.dynamic_slice_in_dim(row_number, begin_at, block_rows)
    query_group = lax.dynamic_slice_in_dim(segments, begin_at, block_rows)
    query_place = lax.dynamic_slice_in_dim(positions, begin_at, block_rows)
    key_row = lax.dynamic_slice_in_dim(key_rows, begin_at, window)
    key_group = lax.dynamic_slice_in_dim(key_groups, begin_at, window)
    key_alive = lax.dynamic_slice_in_dim(key_live, begin_at, window)
    key_place = lax.dynamic_slice_in_dim(key_places, begin_at, window)
    joined = (
        (query_row[:, None] == key_row[None, :])
        & (query_group[:, None] == key_group[None, :])
        & key_alive[None, :]
    )
    return joined | (query_place[:, None] == key_place[None, :])


def pad_keys(values, margin):
    return jnp.pad(values, ((margin, margin), (0, 0), (0, 0)))


def attend_forward(query_low, key_low, value_low, layout, block_rows, margin):
    slot_count, head_count, head_dim = query_low.shape
    window = block_rows + 2 * margin
    score_scale = head_dim ** (-0.5)
    key_wide = pad_keys(key_low, margin)
    value_wide = pad_keys(value_low, margin)

    def forward_block(block_index):
        begin_at = block_index * block_rows
        query_block = lax.dynamic_slice_in_dim(query_low, begin_at, block_rows, 0)
        key_block = lax.dynamic_slice_in_dim(key_wide, begin_at, window, 0)
        value_block = lax.dynamic_slice_in_dim(value_wide, begin_at, window, 0)
        allowed = block_allowed(layout, begin_at, block_rows, window)
        scores = (
            jnp.einsum("qhd,khd->hqk", query_block, key_block, preferred_element_type=jnp.float32)
            * score_scale
        )
        scores = jnp.where(allowed[None], scores, MASKED)
        highest = jnp.max(scores, axis=-1, keepdims=True)
        exponent = jnp.exp(scores - highest)
        row_total = jnp.sum(exponent, axis=-1, keepdims=True)
        chances_low = (exponent / row_total).astype(jnp.bfloat16)
        outputs = jnp.einsum(
            "hqk,khd->qhd", chances_low, value_block, preferred_element_type=jnp.float32
        )
        return (outputs.astype(jnp.bfloat16), highest + jnp.log(row_total))

    outputs, logsum = lax.map(forward_block, jnp.arange(slot_count // block_rows))
    return (outputs.reshape(slot_count, head_count * head_dim), logsum)


def attend_backward(grad_out, query_low, key_low, value_low, logsum, layout, block_rows, margin):
    slot_count, head_count, head_dim = query_low.shape
    window = block_rows + 2 * margin
    score_scale = head_dim ** (-0.5)
    key_wide = pad_keys(key_low, margin)
    value_wide = pad_keys(value_low, margin)
    zeros_wide = jnp.zeros(key_wide.shape, jnp.float32)

    def backward_block(carried, block_index):
        key_grads, value_grads = carried
        begin_at = block_index * block_rows
        query_block = lax.dynamic_slice_in_dim(query_low, begin_at, block_rows, 0)
        key_block = lax.dynamic_slice_in_dim(key_wide, begin_at, window, 0)
        value_block = lax.dynamic_slice_in_dim(value_wide, begin_at, window, 0)
        grad_block = lax.dynamic_slice_in_dim(grad_out, begin_at, block_rows, 0)
        allowed = block_allowed(layout, begin_at, block_rows, window)
        scores = (
            jnp.einsum("qhd,khd->hqk", query_block, key_block, preferred_element_type=jnp.float32)
            * score_scale
        )
        scores = jnp.where(allowed[None], scores, MASKED)
        chances = jnp.exp(scores - logsum[block_index])
        chances_low = chances.astype(jnp.bfloat16)
        value_part = jnp.einsum(
            "hqk,qhd->khd", chances_low, grad_block, preferred_element_type=jnp.float32
        )
        grad_chance = jnp.einsum(
            "qhd,khd->hqk", grad_block, value_block, preferred_element_type=jnp.float32
        )
        centre = jnp.sum(chances * grad_chance, axis=-1, keepdims=True)
        grad_score = (chances * (grad_chance - centre)).astype(jnp.bfloat16)
        query_part = (
            jnp.einsum("hqk,khd->qhd", grad_score, key_block, preferred_element_type=jnp.float32)
            * score_scale
        )
        key_part = (
            jnp.einsum("hqk,qhd->khd", grad_score, query_block, preferred_element_type=jnp.float32)
            * score_scale
        )
        key_grads = lax.dynamic_update_slice_in_dim(
            key_grads,
            lax.dynamic_slice_in_dim(key_grads, begin_at, window, 0) + key_part,
            begin_at,
            0,
        )
        value_grads = lax.dynamic_update_slice_in_dim(
            value_grads,
            lax.dynamic_slice_in_dim(value_grads, begin_at, window, 0) + value_part,
            begin_at,
            0,
        )
        return ((key_grads, value_grads), query_part)

    (key_grads, value_grads), query_parts = lax.scan(
        backward_block, (zeros_wide, zeros_wide), jnp.arange(slot_count // block_rows)
    )
    flat_width = head_count * head_dim
    grad_query = query_parts.reshape(slot_count, flat_width)
    grad_key = key_grads[margin : margin + slot_count].reshape(slot_count, flat_width)
    grad_value = value_grads[margin : margin + slot_count].reshape(slot_count, flat_width)
    return (grad_query, grad_key, grad_value)


def body(tokens, cotangent, segment_ids, row_lengths, row_widths, params, momenta, averages):
    slot_count, model_width = tokens.shape
    head_dim = HD
    head_count = model_width // head_dim
    split_shape = (slot_count, head_count, head_dim)
    block_rows = min(512, slot_count)
    margin = 2 * SENT
    positions = jnp.arange(slot_count, dtype=jnp.int32)
    row_number = jnp.where(row_widths[0] == 1, 0, positions // ROW)
    row_limit = jnp.where(row_number == 0, row_lengths[0], row_lengths[1])
    live_slot = positions - row_number * ROW < row_limit
    layout = (
        row_number,
        segment_ids,
        positions,
        jnp.pad(row_number, margin, constant_values=-1),
        jnp.pad(segment_ids, margin, constant_values=-1),
        jnp.pad(live_slot, margin),
        jnp.arange(slot_count + 2 * margin, dtype=jnp.int32) - margin,
    )
    gathered = lax.all_gather(params.astype(jnp.bfloat16), "dp", axis=0, tiled=True)
    matrices, vectors = unpack(gathered, model_width)
    w_query, w_key, w_value, w_out, w_up, w_down = matrices
    bias_up = vectors[:, 8:].reshape(-1)
    inputs = tokens.astype(jnp.float32)
    query_low = (mixed_dot(tokens, w_query) + vectors[:, 0]).astype(jnp.bfloat16)
    key_low = mixed_dot(tokens, w_key).astype(jnp.bfloat16)
    value_low = (mixed_dot(tokens, w_value) + vectors[:, 1]).astype(jnp.bfloat16)
    attended, logsum = attend_forward(
        query_low.reshape(split_shape),
        key_low.reshape(split_shape),
        value_low.reshape(split_shape),
        layout,
        block_rows,
        margin,
    )
    branch_one = mixed_dot(attended, w_out.T) + vectors[:, 2]
    first_norm, normed_one, inverse_one = norm_forward(
        inputs + branch_one, vectors[:, 4], vectors[:, 5]
    )
    first_low = first_norm.astype(jnp.bfloat16)
    hidden_pre = mixed_dot(first_low, w_up) + bias_up
    hidden_low = jax.nn.gelu(hidden_pre).astype(jnp.bfloat16)
    branch_two = mixed_dot(hidden_low, w_down.T) + vectors[:, 3]
    second_norm, normed_two, inverse_two = norm_forward(
        first_norm + branch_two + inputs, vectors[:, 6], vectors[:, 7]
    )
    live_column = live_slot[:, None]
    layer_output = jnp.where(live_column, second_norm, 0.0).astype(jnp.bfloat16)
    regathered = lax.all_gather(params.astype(jnp.bfloat16), "dp", axis=0, tiled=True)
    matrices, _ = unpack(regathered, model_width)
    w_query, w_key, w_value, w_out, w_up, w_down = matrices
    grad_output = jnp.where(live_column, cotangent.astype(jnp.float32), 0.0)
    grad_two, grad_gain_two, grad_shift_two = norm_backward(
        grad_output, normed_two, inverse_two, vectors[:, 6]
    )
    grad_feed = grad_two.astype(jnp.bfloat16)
    grad_w_down = cross_rows(grad_feed, hidden_low)
    grad_hidden = mixed_dot(grad_feed, w_down)
    _, gelu_back = jax.vjp(jax.nn.gelu, hidden_pre)
    grad_up = gelu_back(grad_hidden)[0].astype(jnp.bfloat16)
    grad_w_up = cross_rows(first_low, grad_up)
    grad_first = grad_two + mixed_dot(grad_up, w_up.T)
    grad_one, grad_gain_one, grad_shift_one = norm_backward(
        grad_first, normed_one, inverse_one, vectors[:, 4]
    )
    grad_branch = grad_one.astype(jnp.bfloat16)
    grad_w_out = cross_rows(grad_branch, attended)
    grad_attended = mixed_dot(grad_branch, w_out).astype(jnp.bfloat16)
    grad_query, grad_key, grad_value = attend_backward(
        grad_attended.reshape(split_shape),
        query_low.reshape(split_shape),
        key_low.reshape(split_shape),
        value_low.reshape(split_shape),
        logsum,
        layout,
        block_rows,
        margin,
    )
    query_back = grad_query.astype(jnp.bfloat16)
    key_back = grad_key.astype(jnp.bfloat16)
    value_back = grad_value.astype(jnp.bfloat16)
    grad_w_query = cross_rows(tokens, query_back)
    grad_w_key = cross_rows(tokens, key_back)
    grad_w_value = cross_rows(tokens, value_back)
    input_grad = (
        grad_two
        + grad_one
        + mixed_dot(query_back, w_query.T)
        + mixed_dot(key_back, w_key.T)
        + mixed_dot(value_back, w_value.T)
    )
    vector_local = jnp.concatenate(
        [
            jnp.stack(
                [
                    column_sum(query_back),
                    column_sum(value_back),
                    column_sum(grad_branch),
                    column_sum(grad_feed),
                    grad_gain_one,
                    grad_shift_one,
                    grad_gain_two,
                    grad_shift_two,
                ],
                axis=1,
            ),
            column_sum(grad_up).reshape(model_width, 4),
        ],
        axis=1,
    )
    flat_grad = jnp.concatenate(
        [grad_w_query, grad_w_key, grad_w_value, grad_w_out, grad_w_up, grad_w_down, vector_local],
        axis=1,
    ).reshape(-1)
    own_rows = lax.psum_scatter(flat_grad, "dp", scatter_dimension=0, tiled=True)
    squares, vector_grads = lax.psum((jnp.sum(own_rows * own_rows), vector_local), "dp")
    grad_norm = jnp.sqrt(squares)
    factor = jnp.minimum(1.0, CLIP_NORM / (grad_norm + 1e-06))
    clipped = own_rows * factor
    new_momenta = MOMENTUM * momenta + clipped
    new_params = params - LEARN_RATE * (clipped + MOMENTUM * new_momenta)
    new_averages = AVERAGE_DECAY * averages + (1.0 - AVERAGE_DECAY) * new_params
    return (
        layer_output,
        input_grad,
        grad_norm,
        vector_grads,
        new_params,
        new_momenta,
        new_averages,
    )


def solution(mesh):
    placed = (P("dp", None), P("dp", None), P("dp"), P("dp"), P("dp"), P("dp"), P("dp"), P("dp"))
    return jax.shard_map(
        body,
        mesh=mesh,
        in_specs=placed,
        out_specs=(P("dp", None), P("dp", None), P(), P(), P("dp"), P("dp"), P("dp")),
        check_vma=False,
    )
```

profile of v0, /device:TPU:0, one launch (start us, length us, event | category | flops | bytes accessed | tf_op | source)
XLA Modules:
  0.0 866.7 jit_solution(4028912190826128299)
XLA Ops:
  11.3 4.5 dynamic-update-slice
  19.1 3.9 copy.61
  25.5 150.3 %all-reduce.11.cloned.1.call-done = bf16[3151872]{0:T(1024)(128)(2,1)} async-done(((bf16[3151872]{0:T(1024)(128)(2,1)}), bf16[3151872]{0:T(1024)(128)(2,1)}) %all-reduce.11.cloned.1.call-update) | async-done | bytes 6303760
  175.7 13.4 %reshape.347 = bf16[512,6156]{1,0:T(8,128)(2,1)} reshape(bf16[3151872]{0:T(1024)(128)(2,1)} %all-reduce.11.cloned.1.call-done) | data formatting | bytes 12607488 | tf_op jit(solution)/shard_map/reshape | solution.py:32
  195.6 3.8 add_convert_fusion
  204.6 61.0 %while.26 = (s32[]{:T(128)}, bf16[4,512,8,64]{1,3,2,0:T(8,128)(2,1)}, f32[4,8,512,1]{2,1,3,0:T(8,128)S(1)}, s32[4]{0:T(128)S(1)}, bf16[2304,8,64]{0,2,1:T(8,128)...) while((s32[]{:T(128)}, ...), condition=%wide.region_3.4_spmd, body=%wide.region_0.3_spmd.sunk | while | flops 845672448 | bytes 42122808 | solution.py:112
  214.1 5.8 fusion.119
  229.4 5.8 fusion.119
  244.5 5.8 fusion.119
  252.8 3.7 fusion.117
  259.8 5.8 fusion.119
  272.6 10.5 %fusion.54 = f32[2048,2048]{1,0:T(8,128)} fusion(bf16[512,6156]{1,0:T(8,128)(2,1)} %reshape.347, f32[2048,512]{0,1:T(8,128)S(1)} %get-tuple-element.292, f32[512]{0:T(512)S(1)} %get-tuple-element.206, f32[512]{0:T(512)S(1)} %get-tuple-element.207, f32[2048]{0:T(1024)S(1)} %add_rsqrt_fusion.1, f32[2048]{0:T(1024)S(1)} %broadcast_multiply_fusion.5), kind=kOutput, calls=%fused_computation.96 | convolution fusion | flops 4300210176 | bytes 23089152 | tf_op jit(solution)/shard_map/dot_general | solution.py:20
  283.1 12.2 %fusion.81 = (f32[2048]{0:T(1024)S(1)}, f32[2048,512]{0,1:T(8,128)S(1)}) fusion(bf16[2048,512]{0,1:T(8,128)(2,1)S(1)} %copy-done.12, f32[512]{0:T(512)S(1)} %get-tuple-element.205, bf16[512,6156]{1,0:T(8,128)(2,1)} %reshape.347, f32[2048,2048]{1,0:T(8,128)} %fusion.54, f32[2048]{0:T(1024)S(1)} %add.229, f32[512]{0:T(512)S(1)} %get-tuple-element.206, ...), kind=kOutput, calls=%fused_computation.151 | convolution fusion | flops 4346345472 | bytes 29399040 | tf_op jit(solution)/shard_map/dot_general | solution.py:20
  299.9 4.4 convert_reduce_fusion.1
  306.3 12.0 %fusion.73 = f32[512,2048]{1,0:T(8,128)} fusion(f32[2048,512]{0,1:T(8,128)S(1)} %get-tuple-element.279, f32[2048,2048]{1,0:T(8,128)} %fusion.54, f32[2048]{0:T(1024)S(1)} %add.229), kind=kOutput, calls=%fused_computation.145 | convolution fusion | flops 4337958912 | bytes 25174016 | tf_op jit(solution)/shard_map/ta,tb->ab/dot_general | solution.py:24
  318.4 23.2 %convert_reduce_fusion = (f32[2048]{0:T(1024)}, bf16[2048,2048]{1,0:T(8,128)(2,1)}) fusion(f32[2048,2048]{1,0:T(8,128)} %fusion.54, f32[2048]{0:T(1024)S(1)} %add.229, bf16[512,6156]{1,0:T(8,128)(2,1)} %reshape.347, f32[2048,512]{0,1:T(8,128)} %copy-done.5), kind=kOutput, calls=%fused_computation.59 | convolution fusion | flops 4392482816 | bytes 31473664 | tf_op jit(solution)/shard_map/dot_general | solution.py:20
  341.6 10.1 %fusion.76 = f32[512,2048]{1,0:T(8,128)} fusion(bf16[2048,2048]{1,0:T(8,128)(2,1)} %get-tuple-element.297, f32[2048,512]{0,1:T(8,128)S(1)} %get-tuple-element.292, f32[512]{0:T(512)S(1)} %get-tuple-element.206, f32[512]{0:T(512)S(1)} %get-tuple-element.207, f32[2048]{0:T(1024)S(1)} %add_rsqrt_fusion.1, f32[2048]{0:T(1024)S(1)} %broadcast_multiply_fusion.5), kind=kOutput, calls=%fused_computation.148 | convolution fusion | flops 4300210176 | bytes 16797696 | tf_op jit(solution)/shard_map/ta,tb->ab/dot_general | solution.py:24
  351.7 9.4 %multiply_reduce_fusion.2 = (f32[512]{0:T(512)}, f32[2048]{0:T(1024)S(1)}, f32[2048]{0:T(1024)S(1)}, f32[512]{0:T(512)}, f32[2048,512]{0,1:T(8,128)S(1)}) fusion(f32[2048,512]{0,1:T(8,128)S(1)} %get-tuple-element.292, f32[2048]{0:T(1024)S(1)} %add_rsqrt_fusion.1, f32[2048]{0:T(1024)S(1)} %broadcast_multiply_fusion.5, f32[512]{0:T(512)S(1)} %get-tuple-element.207, ...), kind=kOutput, calls=%fused_computation.67 | convolution fusion | flops 4305447936 | bytes 23107584 | tf_op jit(solution)/shard_map/dot_general | solution.py:20
  374.4 122.3 %while.27 = (s32[]{:T(128)}, f32[2304,8,64]{0,2,1:T(8,128)}, f32[2304,8,64]{0,2,1:T(8,128)}, bf16[4,512,8,64]{1,3,2,0:T(8,128)(2,1)}, s32[4]{0:T(128)S(1)}, /*in...) while((s32[]{:T(128)}, f32[2304,8,64]{0,2,1:T(8,128)}, ...), condition=%wide.region_14.15_spmd, body=%wide.region_12.14_spmd.sunk | while | flops 2064248832 | bytes 126779080 | solution.py:169
  381.9 5.7 fusion.130
  387.7 5.8 multiply_reduce_fusion.10
  397.0 4.0 fusion.131
  400.9 4.1 fusion.129
  412.4 5.7 fusion.130
  418.1 5.8 multiply_reduce_fusion.10
  427.4 4.0 fusion.131
  431.3 4.1 fusion.129
  442.8 5.7 fusion.130
  448.5 5.8 multiply_reduce_fusion.10
  457.8 3.9 fusion.131
  461.7 4.2 fusion.129
  473.2 5.7 fusion.130
  478.9 5.8 multiply_reduce_fusion.10
  488.1 4.0 fusion.131
  492.1 4.1 fusion.129
  498.7 4.5 copy.66
  511.3 4.3 copy.92
  516.4 4.4 convolution_bitcast_fusion.2
  522.4 3.8 convolution_bitcast_fusion.1
  531.4 3.8 convolution_bitcast_fusion
  538.6 15.7 %concatenate.7 = f32[512,6156]{1,0:T(8,128)} concatenate(f32[512,512]{1,0:T(8,128)S(1)} %copy.70, f32[512,512]{1,0:T(8,128)} %copy.71, f32[512,512]{1,0:T(8,128)} %copy.72, f32[512,512]{1,0:T(8,128)} %fusion.70, f32[512,2048]{1,0:T(8,128)} %fusion.76, f32[512,2048]{1,0:T(8,128)} %fusion.73, f32[512,1]{1,0:T(8,128)} %copy.74, f32[512,1]{1,0:T(8,128)} %copy.75, f32[512,1]{1,0:T(8,128)} %copy.76, ...), dimensions={1} | concatenate | bytes 25214976 | tf_op jit(solution)/shard_map/concatenate | solution.py:290
  554.3 21.7 %reshape.354 = f32[3151872]{0:T(1024)} reshape(f32[512,6156]{1,0:T(8,128)} %concatenate.7) | data formatting | bytes 25214976 | tf_op jit(solution)/shard_map/reshape | solution.py:293
  576.1 3.9 copy.83
  580.1 3.8 fusion.56
  586.5 4.5 add_add_fusion
  591.0 217.0 %all-reduce.13.cloned.1.call-done = f32[3151872]{0:T(1024)} async-done(((f32[3151872]{0:T(1024)}), f32[3151872]{0:T(1024)}) %all-reduce.13.cloned.1.call-update) | async-done | bytes 12607504
  809.8 5.4 copy.84
  815.2 40.3 %all-reduce.7 = (f32[]{:T(128)}, f32[512,12]{0,1:T(8,128)}) all-reduce(f32[]{:T(128)} %multiply_reduce_fusion.8, f32[512,12]{0,1:T(8,128)S(1)} %concatenate.8), channel_id=1, replica_groups=mesh['dp'=32] {'dp'}, use_global_device_ids=true, to_apply=%region_26.27 | all-reduce | flops 6145 | bytes 49160 | tf_op jit(solution)/shard_map/psum | solution.py:295
  (236 shorter events, 138.5 us)
Async XLA Ops:
  7.2 168.6 %all-reduce.11.cloned.1.call-start = ((), (), s32[]{:S(2)}) async-start(), calls=%async_computation | async-start | bytes 12607488
  11.3 5.3 copy-start.17
  11.3 5.4 copy-start.10
  15.9 792.1 %all-reduce.13.cloned.1.call-start = ((), (), s32[]{:S(2)}) async-start(), calls=%async_computation.1 | async-start | bytes 25214976
  16.7 6.3 copy-start.29
  24.9 0.6 copy-start.18
  25.5 166.3 %copy-start.11 = (bf16[2048,512]{1,0:T(8,128)(2,1)S(1)}, bf16[2048,512]{1,0:T(8,128)(2,1)}, u32[]{:S(2)}) copy-start(bf16[2048,512]{1,0:T(8,128)(2,1)} %param.12) | copy-start | bytes 6291460
  201.9 2.4 copy-start.13
  265.6 4.0 copy-start.12
  295.3 1.6 copy-start.4
  295.3 1.6 copy-start.19
  295.3 1.6 copy-start.24
  295.8 4.0 copy-start.28
  304.3 2.0 copy-start.5
  341.6 10.1 %copy-start.6 = (f32[2048,512]{0,1:T(8,128)S(1)}, f32[2048,512]{0,1:T(8,128)}, u32[]{:S(2)}) copy-start(f32[2048,512]{0,1:T(8,128)} %copy-done.5) | copy-start | bytes 12582916
  363.2 2.4 copy-start.2
  374.6 7.3 copy-start
  400.9 4.1 copy-start.1
  405.1 7.3 copy-start
  431.3 4.1 copy-start.1
  435.5 7.3 copy-start
  461.7 4.2 copy-start.1
  465.9 7.3 copy-start
  492.1 4.2 copy-start.1
  496.7 6.6 copy-start.23
  496.7 7.4 copy-start.20
  496.7 8.3 copy-start.21
  496.7 9.1 %copy-start.27 = (f32[2048]{0:T(1024)S(1)}, f32[2048]{0:T(1024)}, u32[]{:S(2)}) copy-start(f32[2048]{0:T(1024)} %get-tuple-element.296) | copy-start | bytes 24580
  496.8 9.4 %copy-start.22 = (f32[512]{0:T(512)S(1)}, f32[512]{0:T(512)}, u32[]{:S(2)}) copy-start(f32[512]{0:T(512)} %get-tuple-element.280) | copy-start | bytes 6148
  496.8 10.2 %copy-start.25 = (f32[512]{0:T(512)S(1)}, f32[512]{0:T(512)}, u32[]{:S(2)}) copy-start(f32[512]{0:T(512)} %get-tuple-element.195) | copy-start | bytes 6148
  496.8 11.1 %copy-start.26 = (f32[512]{0:T(512)S(1)}, f32[512]{0:T(512)}, u32[]{:S(2)}) copy-start(f32[512]{0:T(512)} %get-tuple-element.200) | copy-start | bytes 6148
  511.2 11.2 %copy-start.8 = (bf16[2048,8,64]{0,2,1:T(8,128)(2,1)}, bf16[2048,8,64]{0,2,1:T(8,128)(2,1)S(1)}, u32[]{:S(2)}) copy-start(bf16[2048,8,64]{0,2,1:T(8,128)(2,1)S(1)} %slice.141) | copy-start | bytes 6291460
  580.1 3.9 copy-start.9
  580.1 6.3 copy-start.7
  584.0 2.5 copy-start.3
  809.8 46.5 %copy-start.14 = (f32[98496]{0:T(1024)S(1)}, f32[98496]{0:T(1024)}, u32[]{:S(2)}) copy-start(f32[98496]{0:T(1024)} %param.17) | copy-start | bytes 1181956
  809.8 46.5 %copy-start.15 = (f32[98496]{0:T(1024)S(1)}, f32[98496]{0:T(1024)}, u32[]{:S(2)}) copy-start(f32[98496]{0:T(1024)} %param.19) | copy-start | bytes 1181956
  809.8 46.5 %copy-start.16 = (f32[98496]{0:T(1024)S(1)}, f32[98496]{0:T(1024)}, u32[]{:S(2)}) copy-start(f32[98496]{0:T(1024)} %param.18) | copy-start | bytes 1181956
Sparse Core Ops, SparseCore 0:
  16.0 159.6 all-reduce.10
  576.1 231.7 all-reduce.12
where the time goes:
time: 878 us; the launch traced here: 867 us
  waiting for transfers between devices  367 us (42%)
  matrix products  247 us (28%)
  local copies, waits for them, and re-layouts  127 us (14%)
  other arithmetic  53.8 us (6%)
  blocking collectives  40.3 us (5%)
  between operations  17.2 us (2%)
  loops' own time  14.4 us (2%)
    unnamed x4, waiting for transfers between devices  367 us
    dot_general x12, matrix products, mixed_dot(): return jnp.dot(left_side, right_side, preferred_element_type=jnp.float32)  82.2 us
    psum x1, blocking collectives, body(): lax.psum((jnp.sum(own_rows * own_rows), vector_local), 'dp')  40.3 us
    dot_general x6, matrix products, cross_rows(): jnp.einsum('ta,tb->ab', left_side, right_side, preferred_element_type=jnp...  36.6 us
    unnamed x64, local copies, waits for them, and re-layouts  32.6 us
    dot_general x4, matrix products, forward_block(): jnp.einsum('hqk,khd->qhd', chances_low, value_block, preferred_element_ty...  23.3 us
    dot_general x4, matrix products, backward_block(): jnp.einsum('qhd,khd->hqk', grad_block, value_block, preferred_element_typ...  23.2 us
    dot_general x4, matrix products, backward_block(): jnp.einsum('hqk,qhd->khd', chances_low, grad_block, preferred_element_typ...  22.8 us
  transfers between devices with their start and end apart: 2, of which 2 were waited for; matrix products, arithmetic and copies ran while one was open for 3% of the time, Pallas kernels for 0%

commit v1 on v0

--- a/solution.py
+++ b/solution.py
@@ -41,6 +41,54 @@
     )
     vectors = table[:, 12 * model_width :].astype(jnp.float32)
     return (matrices, vectors)
+
+
+def exchange(values, bit, count):
+    return lax.ppermute(values, "dp", [(at, at ^ bit) for at in range(count)])
+
+
+def gather_blocks(block, count):
+    bit = count // 2
+    while bit:
+        block = jnp.concatenate([block, exchange(block, bit, count)], axis=0)
+        bit //= 2
+    return block
+
+
+def scatter_blocks(blocks, count):
+    bit = 1
+    while bit < count:
+        half = blocks.shape[0] // 2
+        arrived = exchange(blocks[half:], bit, count)
+        total = blocks[:half].astype(jnp.float32) + arrived.astype(jnp.float32)
+        blocks = total.astype(blocks.dtype) if bit * 2 < count else total
+        bit *= 2
+    return blocks
+
+
+def sum_everywhere(values, count):
+    bit = 1
+    while bit < count:
+        values = values + exchange(values, bit, count)
+        bit *= 2
+    return values
+
+
+def reversed_bits(count):
+    width = count.bit_length() - 1
+    return [sum(((at >> k) & 1) << (width - 1 - k) for k in range(width)) for at in range(count)]
+
+
+def to_natural(blocks, count, mine):
+    rows = blocks.shape[0] // count
+    places = jnp.array(reversed_bits(count), jnp.int32)[jnp.arange(count) ^ mine]
+    return jnp.take(blocks.reshape(count, rows, -1), places, axis=0).reshape(blocks.shape)
+
+
+def from_natural(table, count, mine):
+    rows = table.shape[0] // count
+    owners = jnp.array(reversed_bits(count), jnp.int32) ^ mine
+    return jnp.take(table.reshape(count, rows, -1), owners, axis=0).reshape(table.shape)
 
 
 def norm_forward(values, gain_vec, shift_vec):
@@ -196,7 +244,11 @@
         jnp.pad(live_slot, margin),
         jnp.arange(slot_count + 2 * margin, dtype=jnp.int32) - margin,
     )
-    gathered = lax.all_gather(params.astype(jnp.bfloat16), "dp", axis=0, tiled=True)
+    count = lax.axis_size("dp")
+    mine = lax.axis_index("dp")
+    table_width = 12 * (model_width + 1)
+    own_weights = params.astype(jnp.bfloat16).reshape(-1, table_width)
+    gathered = to_natural(gather_blocks(own_weights, count), count, mine)
     matrices, vectors = unpack(gathered, model_width)
     w_query, w_key, w_value, w_out, w_up, w_down = matrices
     bias_up = vectors[:, 8:].reshape(-1)
@@ -225,9 +277,6 @@
     )
     live_column = live_slot[:, None]
     layer_output = jnp.where(live_column, second_norm, 0.0).astype(jnp.bfloat16)
-    regathered = lax.all_gather(params.astype(jnp.bfloat16), "dp", axis=0, tiled=True)
-    matrices, _ = unpack(regathered, model_width)
-    w_query, w_key, w_value, w_out, w_up, w_down = matrices
     grad_output = jnp.where(live_column, cotangent.astype(jnp.float32), 0.0)
     grad_two, grad_gain_two, grad_shift_two = norm_backward(
         grad_output, normed_two, inverse_two, vectors[:, 6]
@@ -287,13 +336,16 @@
         ],
         axis=1,
     )
-    flat_grad = jnp.concatenate(
-        [grad_w_query, grad_w_key, grad_w_value, grad_w_out, grad_w_up, grad_w_down, vector_local],
-        axis=1,
-    ).reshape(-1)
-    own_rows = lax.psum_scatter(flat_grad, "dp", scatter_dimension=0, tiled=True)
-    squares, vector_grads = lax.psum((jnp.sum(own_rows * own_rows), vector_local), "dp")
-    grad_norm = jnp.sqrt(squares)
+    matrix_grads = jnp.concatenate(
+        [grad_w_query, grad_w_key, grad_w_value, grad_w_out, grad_w_up, grad_w_down], axis=1
+    ).astype(jnp.bfloat16)
+    own_matrix = scatter_blocks(from_natural(matrix_grads, count, mine), count)
+    vector_grads = sum_everywhere(vector_local.T, count).T
+    squares = sum_everywhere(jnp.sum(own_matrix * own_matrix).reshape(1, 1), count)[0, 0]
+    grad_norm = jnp.sqrt(squares + jnp.sum(vector_grads * vector_grads))
+    own_count = own_matrix.shape[0]
+    own_vector = lax.dynamic_slice_in_dim(vector_grads, mine * own_count, own_count)
+    own_rows = jnp.concatenate([own_matrix, own_vector], axis=1).reshape(-1)
     factor = jnp.minimum(1.0, CLIP_NORM / (grad_norm + 1e-06))
     clipped = own_rows * factor
     new_momenta = MOMENTUM * momenta + clipped

time: 878 us -> 601 us (0.68)
  waiting for transfers between devices: 367 us -> 119 us
  blocking collectives: 40.3 us -> 0 us
  starting transfers between devices: 0.08 us -> 35.6 us
  local copies, waits for them, and re-layouts: 127 us -> 113 us
  matrix products: 247 us -> 236 us
  other arithmetic: 53.8 us -> 64.5 us
  between operations: 17.2 us -> 8.32 us
    unnamed x4 -> x0, waiting for transfers between devices: 367 us -> none
    ppermute x0 -> x20, waiting for transfers between devices: none -> 119 us  [exchange(): return lax.ppermute(values, 'dp', [(at, at ^ bit) for at in range(count)])]
    psum x1 -> x0, blocking collectives: 40.3 us -> none  [body(): lax.psum((jnp.sum(own_rows * own_rows), vector_local), 'dp')]
    ppermute x0 -> x20, starting transfers between devices: none -> 35.6 us  [exchange(): return lax.ppermute(values, 'dp', [(at, at ^ bit) for at in range(count)])]
    concatenate x0 -> x4, local copies, waits for them, and re-layouts: none -> 34.1 us  [gather_blocks(): block = jnp.concatenate([block, exchange(block, bit, count)], axis=0)]
    reshape x2, local copies, waits for them, and re-layouts: 35.1 us -> 1.72 us  [body(): own_weights = params.astype(jnp.bfloat16).reshape(-1, table_width)]
    concatenate x1, local copies, waits for them, and re-layouts: 15.7 us -> 1.45 us  [body(): jnp.concatenate([grad_w_query, grad_w_key, grad_w_value, grad_w_out, grad...]
    gather x0 -> x3, local copies, waits for them, and re-layouts: none -> 13.9 us  [the longest x1 6.65 us: to_natural(): jnp.take(blocks.reshape(count, rows, -1), places, axis=0)]
  transfers between devices with their start and end apart: 2 -> 20, of which waited for: 2 -> 14; matrix products, arithmetic and copies ran while one was open for 3% -> 7% of each run, Pallas kernels for 0% -> 0%
where the time goes in v1:
time: 601 us; the launch traced here: 590 us
  matrix products  236 us (39%)
  waiting for transfers between devices  119 us (20%)
  local copies, waits for them, and re-layouts  113 us (19%)
  other arithmetic  64.5 us (11%)
  starting transfers between devices  35.6 us (6%)
  loops' own time  13.6 us (2%)
  between operations  8.32 us (1%)
    ppermute x20, waiting for transfers between devices, exchange(): return lax.ppermute(values, 'dp', [(at, at ^ bit) for at in range(count)])  119 us
    dot_general x12, matrix products, mixed_dot(): return jnp.dot(left_side, right_side, preferred_element_type=jnp.float32)  80 us
    ppermute x20, starting transfers between devices, exchange(): return lax.ppermute(values, 'dp', [(at, at ^ bit) for at in range(count)])  35.6 us
    concatenate x4, local copies, waits for them, and re-layouts, gather_blocks(): block = jnp.concatenate([block, exchange(block, bit, count)], axis=0)  34.1 us
    dot_general x6, matrix products, cross_rows(): jnp.einsum('ta,tb->ab', left_side, right_side, preferred_element_type=jnp...  27.9 us
    unnamed x126, local copies, waits for them, and re-layouts  25.8 us
    dot_general x4, matrix products, forward_block(): jnp.einsum('hqk,khd->qhd', chances_low, value_block, preferred_element_ty...  23.3 us
    dot_general x4, matrix products, backward_block(): jnp.einsum('qhd,khd->hqk', grad_block, value_block, preferred_element_typ...  23.3 us
  transfers between devices with their start and end apart: 20, of which 14 were waited for; matrix products, arithmetic and copies ran while one was open for 7% of the time, Pallas kernels for 0%

profile of v1, /device:TPU:0, one launch (start us, length us, event | category | flops | bytes accessed | tf_op | source)
XLA Modules:
  0.0 589.9 jit_solution(18151743386643977328)
XLA Ops:
  1.9 4.1 collective-permute-start
  6.0 9.3 %collective-permute-done = bf16[16,6156]{1,0:T(8,128)(2,1)S(1)} collective-permute-done((bf16[16,6156]{1,0:T(8,128)(2,1)S(1)}, bf16[16,6156]{1,0:T(8,128)(2,1)S(1)}, u32[]{:S(2)}, u32[]{:S(2)}) %collective-permute-start) | collective-permute-done | bytes 197024 | tf_op jit(solution)/shard_map/ppermute | solution.py:47
  16.1 9.8 %collective-permute-done.1 = bf16[32,6156]{1,0:T(8,128)(2,1)S(1)} collective-permute-done((bf16[32,6156]{1,0:T(8,128)(2,1)S(1)}, bf16[32,6156]{1,0:T(8,128)(2,1)S(1)}, u32[]{:S(2)}, u32[]{:S(2)}) %collective-permute-start.1) | collective-permute-done | bytes 394016 | tf_op jit(solution)/shard_map/ppermute | solution.py:47
  27.3 16.9 %collective-permute-done.2 = bf16[64,6156]{1,0:T(8,128)(2,1)S(1)} collective-permute-done((bf16[64,6156]{1,0:T(8,128)(2,1)S(1)}, bf16[64,6156]{1,0:T(8,128)(2,1)S(1)}, u32[]{:S(2)}, u32[]{:S(2)}) %collective-permute-start.2) | collective-permute-done | bytes 788000 | tf_op jit(solution)/shard_map/ppermute | solution.py:47
  55.8 24.9 %collective-permute-done.3 = bf16[128,6156]{0,1:T(8,128)(2,1)} collective-permute-done((bf16[128,6156]{0,1:T(8,128)(2,1)}, bf16[128,6156]{0,1:T(8,128)(2,1)}, u32[]{:S(2)}, u32[]{:S(2)}) %collective-permute-start.3) | collective-permute-done | bytes 1575968 | tf_op jit(solution)/shard_map/ppermute | solution.py:47
  80.7 9.0 %concatenate.43 = bf16[256,6156]{0,1:T(8,128)(2,1)} concatenate(bf16[16,6156]{0,1:T(8,128)(2,1)S(1)} %copy.75, bf16[16,6156]{0,1:T(8,128)(2,1)S(1)} %copy.76, bf16[32,6156]{0,1:T(8,128)(2,1)} %copy.77, bf16[64,6156]{0,1:T(8,128)(2,1)} %copy.78, bf16[128,6156]{0,1:T(8,128)(2,1)} %collective-permute-done.3), dimensions={0} | concatenate | bytes 6303744 | tf_op jit(solution)/shard_map/concatenate | solution.py:53
  95.3 4.0 copy.69
  102.3 13.7 %concatenate.44 = bf16[512,6156]{0,1:T(8,128)(2,1)} concatenate(bf16[16,6156]{0,1:T(8,128)(2,1)S(1)} %copy.75, bf16[16,6156]{0,1:T(8,128)(2,1)S(1)} %copy.76, bf16[32,6156]{0,1:T(8,128)(2,1)} %copy.77, bf16[64,6156]{0,1:T(8,128)(2,1)} %copy.78, bf16[128,6156]{0,1:T(8,128)(2,1)} %collective-permute-done.3, bf16[256,6156]{0,1:T(8,128)(2,1)} %collective-permute-done.4), dimensions={0} | concatenate | bytes 12607488 | tf_op jit(solution)/shard_map/concatenate | solution.py:53
  116.1 9.1 %copy.79 = bf16[512,6156]{1,0:T(8,128)(2,1)} copy(bf16[512,6156]{0,1:T(8,128)(2,1)} %concatenate.44) | data formatting | bytes 12607488 | tf_op jit(solution)/shard_map/concatenate | solution.py:53
  125.2 6.6 %gather_fusion.1 = bf16[32,16,6156]{2,1,0:T(8,128)(2,1)} fusion(bf16[32,16,6156]{2,1,0:T(8,128)(2,1)} %bitcast.139, s32[1024]{0:T(1024)S(1)} %get-tuple-element.317), kind=kCustom, calls=%fused_computation.1 | custom fusion | bytes 12607616 | tf_op jit(solution)/shard_map/jit(_take)/gather | solution.py:85
  150.1 61.3 %while.26 = (s32[]{:T(128)}, bf16[4,512,8,64]{1,3,2,0:T(8,128)(2,1)}, f32[4,8,512,1]{2,1,3,0:T(8,128)S(1)}, s32[4]{0:T(128)S(1)}, bf16[2304,8,64]{0,2,1:T(8,128)...) while((s32[]{:T(128)}, ...), condition=%wide.region_3.4_spmd, body=%wide.region_0.3_spmd.sunk | while | flops 845672448 | bytes 42122808 | solution.py:160
  159.9 5.9 fusion.129
  175.2 5.8 fusion.129
  190.4 5.8 fusion.129
  205.6 5.8 fusion.129
  218.9 10.8 %fusion.57 = f32[2048,2048]{1,0:T(8,128)} fusion(bf16[512,6156]{1,0:T(8,128)(2,1)} %copy-done.11, f32[2048,512]{0,1:T(8,128)S(1)} %get-tuple-element.310, f32[512]{0:T(512)S(1)} %get-tuple-element.220, f32[512]{0:T(512)S(1)} %get-tuple-element.221, f32[2048]{0:T(1024)S(1)} %add_rsqrt_fusion.1, f32[2048]{0:T(1024)S(1)} %broadcast_multiply_fusion.5), kind=kOutput, calls=%fused_computation.108 | convolution fusion | flops 4300210176 | bytes 23089152 | tf_op jit(solution)/shard_map/dot_general | solution.py:20
  229.7 12.1 %fusion.90 = (f32[2048]{0:T(1024)S(1)}, f32[2048,512]{0,1:T(8,128)S(1)}) fusion(bf16[2048,512]{0,1:T(8,128)(2,1)S(1)} %copy-done.28, f32[512]{0:T(512)S(1)} %get-tuple-element.219, bf16[512,6156]{1,0:T(8,128)(2,1)} %copy-done.11, f32[2048,2048]{1,0:T(8,128)} %fusion.57, f32[2048]{0:T(1024)S(1)} %add.319, f32[512]{0:T(512)S(1)} %get-tuple-element.220, ...), kind=kOutput, calls=%fused_computation.188 | convolution fusion | flops 4346345472 | bytes 29399040 | tf_op jit(solution)/shard_map/dot_general | solution.py:20
  246.4 4.4 convert_reduce_fusion.1
  252.9 11.8 %convolution_convert_fusion = bf16[512,2048]{1,0:T(8,128)(2,1)} fusion(f32[2048,512]{0,1:T(8,128)S(1)} %get-tuple-element.291, f32[2048,2048]{1,0:T(8,128)} %fusion.57, f32[2048]{0:T(1024)S(1)} %add.319), kind=kOutput, calls=%fused_computation.99 | convolution fusion | flops 4339007488 | bytes 23076864 | tf_op jit(solution)/shard_map/ta,tb->ab/dot_general | solution.py:24
  264.7 23.2 %convert_reduce_fusion = (f32[2048]{0:T(1024)}, bf16[2048,2048]{1,0:T(8,128)(2,1)}) fusion(f32[2048,2048]{1,0:T(8,128)} %fusion.57, f32[2048]{0:T(1024)S(1)} %add.319, bf16[512,6156]{1,0:T(8,128)(2,1)} %copy-done.11, f32[2048,512]{0,1:T(8,128)} %copy-done.8), kind=kOutput, calls=%fused_computation.62 | convolution fusion | flops 4392482816 | bytes 31473664 | tf_op jit(solution)/shard_map/dot_general | solution.py:20
  287.9 9.9 %convolution_convert_fusion.1 = bf16[512,2048]{1,0:T(8,128)(2,1)} fusion(bf16[2048,2048]{1,0:T(8,128)(2,1)} %get-tuple-element.315, f32[2048,512]{0,1:T(8,128)S(1)} %get-tuple-element.310, f32[512]{0:T(512)S(1)} %get-tuple-element.220, f32[512]{0:T(512)S(1)} %get-tuple-element.221, f32[2048]{0:T(1024)S(1)} %add_rsqrt_fusion.1, ...), kind=kOutput, calls=%fused_computation.100 | convolution fusion | flops 4301258752 | bytes 14700544 | tf_op jit(solution)/shard_map/ta,tb->ab/dot_general | solution.py:24
  297.8 7.4 %multiply_reduce_fusion.2 = (f32[512]{0:T(512)}, f32[2048]{0:T(1024)S(1)}, f32[2048]{0:T(1024)S(1)}, f32[512]{0:T(512)}, f32[2048,512]{0,1:T(8,128)S(1)}) fusion(f32[2048,512]{0,1:T(8,128)S(1)} %get-tuple-element.310, f32[2048]{0:T(1024)S(1)} %add_rsqrt_fusion.1, f32[2048]{0:T(1024)S(1)} %broadcast_multiply_fusion.5, f32[512]{0:T(512)S(1)} %get-tuple-element.221, ...), kind=kOutput, calls=%fused_computation.72 | convolution fusion | flops 4305447936 | bytes 23107584 | tf_op jit(solution)/shard_map/dot_general | solution.py:20
  307.3 4.1 convolution_convert_fusion.2
  316.5 121.3 %while.27 = (s32[]{:T(128)}, f32[2304,8,64]{0,2,1:T(8,128)}, f32[2304,8,64]{0,2,1:T(8,128)}, bf16[4,512,8,64]{1,3,2,0:T(8,128)(2,1)}, s32[4]{0:T(128)S(1)}, /*in...) while((s32[]{:T(128)}, f32[2304,8,64]{0,2,1:T(8,128)}, ...), condition=%wide.region_14.15_spmd, body=%wide.region_12.14_spmd.sunk | while | flops 2064248832 | bytes 126779080 | solution.py:217
  323.8 5.7 fusion.140
  329.5 5.8 multiply_reduce_fusion.11
  338.8 3.9 fusion.141
  342.8 4.1 fusion.139
  354.1 5.7 fusion.140
  359.8 5.8 multiply_reduce_fusion.11
  369.1 4.0 fusion.141
  373.0 4.2 fusion.139
  384.4 5.7 fusion.140
  390.0 5.8 multiply_reduce_fusion.11
  399.3 4.0 fusion.141
  403.2 4.1 fusion.139
  414.6 5.7 fusion.140
  420.3 5.8 multiply_reduce_fusion.11
  429.5 4.0 fusion.141
  433.5 4.1 fusion.139
  457.2 6.5 %gather_fusion.2 = bf16[32,16,6144]{2,1,0:T(8,128)(2,1)} fusion(bf16[32,16,6144]{2,1,0:T(8,128)(2,1)} %constant_dynamic-update-slice_fusion, s32[1024]{0:T(1024)} %get-tuple-element.316), kind=kCustom, calls=%fused_computation.2 | custom fusion | bytes 12583040 | tf_op jit(solution)/shard_map/jit(_take)/gather | solution.py:91
  468.2 5.3 collective-permute-done.5
  482.3 31.5 %collective-permute-done.16 = f32[12,512]{1,0:T(8,128)S(1)} collective-permute-done((f32[12,512]{1,0:T(8,128)S(1)}, f32[12,512]{1,0:T(8,128)S(1)}, u32[]{:S(2)}, u32[]{:S(2)}) %collective-permute-start.16) | collective-permute-done | bytes 24608 | tf_op jit(solution)/shard_map/ppermute | solution.py:47
  525.8 3.9 collective-permute-start.19
  529.8 6.1 %collective-permute-done.7 = bf16[64,6144]{1,0:T(8,128)(2,1)S(1)} collective-permute-done((bf16[64,6144]{1,0:T(8,128)(2,1)S(1)}, bf16[64,6144]{1,0:T(8,128)(2,1)S(1)}, u32[]{:S(2)}, u32[]{:S(2)}) %collective-permute-start.7) | collective-permute-done | bytes 786464 | tf_op jit(solution)/shard_map/ppermute | solution.py:47
  539.5 5.8 add_add_fusion
  547.8 5.4 copy.90
  558.6 6.7 %collective-permute-done.9 = bf16[16,6144]{1,0:T(8,128)(2,1)S(1)} collective-permute-done((bf16[16,6144]{1,0:T(8,128)(2,1)S(1)}, bf16[16,6144]{1,0:T(8,128)(2,1)S(1)}, u32[]{:S(2)}, u32[]{:S(2)}) %collective-permute-start.9) | collective-permute-done | bytes 196640 | tf_op jit(solution)/shard_map/ppermute | solution.py:47
  (363 shorter events, 203.9 us)
Async XLA Ops:
  1.9 13.4 %collective-permute-start = (bf16[16,6156]{1,0:T(8,128)(2,1)S(1)}, bf16[16,6156]{1,0:T(8,128)(2,1)S(1)}, u32[]{:S(2)}, u32[]{:S(2)}) collective-permute-start(bf16[16,6156]{1,0:T(8,128)(2,1)S(1)} %reshape.412), channel_id=1, source_target_pairs={{0,16},{1,17},{2,18},{3,19},{4,20},{5,21},{6,22},{7,23},{8,24},{9,... | collective-permute-start | bytes 590984 | tf_op jit(solution)/shard_map/ppermute | solution.py:47
  15.4 10.5 %collective-permute-start.1 = (bf16[32,6156]{1,0:T(8,128)(2,1)S(1)}, bf16[32,6156]{1,0:T(8,128)(2,1)S(1)}, u32[]{:S(2)}, u32[]{:S(2)}) collective-permute-start(bf16[32,6156]{1,0:T(8,128)(2,1)S(1)} %pad_maximum_fusion.2), channel_id=1, source_target_pairs={{0,8},{1,9},{2,10},{3,11},{4,12},{5,13},{6,14},{7,15},{8,0},{9,1},... | collective-permute-start | bytes 1181960 | tf_op jit(solution)/shard_map/ppermute | solution.py:47
  25.9 18.3 %copy-start.19 = (bf16[32,6156]{1,0:T(8,128)(2,1)}, bf16[32,6156]{1,0:T(8,128)(2,1)S(1)}, u32[]{:S(2)}) copy-start(bf16[32,6156]{1,0:T(8,128)(2,1)S(1)} %collective-permute-done.1) | copy-start | bytes 1181956
  26.0 18.2 %collective-permute-start.2 = (bf16[64,6156]{1,0:T(8,128)(2,1)S(1)}, bf16[64,6156]{1,0:T(8,128)(2,1)S(1)}, u32[]{:S(2)}, u32[]{:S(2)}) collective-permute-start(bf16[64,6156]{1,0:T(8,128)(2,1)S(1)} %pad_maximum_fusion.1), channel_id=1, source_target_pairs={{0,4},{1,5},{2,6},{3,7},{4,0},{5,1},{6,2},{7,3},{8,12},{9,13},{10,... | collective-permute-start | bytes 2363912 | tf_op jit(solution)/shard_map/ppermute | solution.py:47
  46.6 34.1 %collective-permute-start.3 = (bf16[128,6156]{0,1:T(8,128)(2,1)}, bf16[128,6156]{0,1:T(8,128)(2,1)}, u32[]{:S(2)}, u32[]{:S(2)}) collective-permute-start(bf16[128,6156]{0,1:T(8,128)(2,1)} %copy.70), channel_id=1, source_target_pairs={{0,2},{1,3},{2,0},{3,1},{4,6},{5,7},{6,4},{7,5},{8,10},{9,11},{10,... | collective-permute-start | bytes 4727816 | tf_op jit(solution)/shard_map/ppermute | solution.py:47
  55.8 34.6 %copy-start = (s32[32]{0:T(128)S(1)}, s32[32]{0:T(128)}, u32[]{:S(2)}) copy-start(s32[32]{0:T(128)} %constant.161.clone) | copy-start | bytes 388
  55.8 35.5 %copy-start.37 = (s32[2048]{0:T(1024)S(1)}, s32[2048]{0:T(1024)}, u32[]{:S(2)}) copy-start(s32[2048]{0:T(1024)} %param.16) | copy-start | bytes 24580
  89.8 12.6 %collective-permute-start.4 = (bf16[256,6156]{0,1:T(8,128)(2,1)}, bf16[256,6156]{0,1:T(8,128)(2,1)}, u32[]{:S(2)}, u32[]{:S(2)}) collective-permute-start(bf16[256,6156]{0,1:T(8,128)(2,1)} %concatenate.43), channel_id=1, source_target_pairs={{0,1},{1,0},{2,3},{3,2},{4,5},{5,4},{6,7},{7,6},{8,9},{9,8},{10,11... | collective-permute-start | bytes 9455624 | tf_op jit(solution)/shard_map/ppermute | solution.py:47
  91.4 7.9 %copy-start.58 = (s32[2]{0:T(128)S(1)}, s32[2]{0:T(128)}, u32[]{:S(2)}) copy-start(s32[2]{0:T(128)} %param.17) | copy-start | bytes 28
  101.2 14.9 %copy-start.44 = (pred[2048]{0:T(1024)(128)(4,1)}, pred[2048]{0:T(1024)(128)(4,1)S(1)}, u32[]{:S(2)}) copy-start(pred[2048]{0:T(1024)(128)(4,1)S(1)} %select_compare_fusion) | copy-start | bytes 6148
  137.6 167.6 %copy-start.46 = (f32[512]{0:T(512)}, f32[512]{0:T(512)S(1)}, u32[]{:S(2)}) copy-start(f32[512]{0:T(512)S(1)} %get-tuple-element.221) | copy-start | bytes 6148
  218.3 87.0 %copy-start.3 = (f32[2048,512]{0,1:T(8,128)}, f32[2048,512]{0,1:T(8,128)S(1)}, u32[]{:S(2)}) copy-start(f32[2048,512]{0,1:T(8,128)S(1)} %get-tuple-element.310) | copy-start | bytes 12582916
  218.3 87.0 %copy-start.35 = (f32[2048]{0:T(1024)}, f32[2048]{0:T(1024)S(1)}, u32[]{:S(2)}) copy-start(f32[2048]{0:T(1024)S(1)} %broadcast_multiply_fusion.5) | copy-start | bytes 24580
  218.8 86.4 %copy-start.38 = (f32[2048]{0:T(1024)}, f32[2048]{0:T(1024)S(1)}, u32[]{:S(2)}) copy-start(f32[2048]{0:T(1024)S(1)} %add_rsqrt_fusion.1) | copy-start | bytes 24580
  287.9 9.9 %copy-start.9 = (f32[2048,512]{0,1:T(8,128)S(1)}, f32[2048,512]{0,1:T(8,128)}, u32[]{:S(2)}) copy-start(f32[2048,512]{0,1:T(8,128)} %copy-done.8) | copy-start | bytes 12582916
  287.9 9.9 %copy-start.59 = (bf16[2048,2048]{1,0:T(8,128)(2,1)S(1)}, bf16[2048,2048]{1,0:T(8,128)(2,1)}, u32[]{:S(2)}) copy-start(bf16[2048,2048]{1,0:T(8,128)(2,1)} %get-tuple-element.315) | copy-start | bytes 25165828
  316.7 7.2 %copy-start.1 = (bf16[2304,8,64]{0,2,1:T(8,128)(2,1)}, bf16[2304,8,64]{0,2,1:T(8,128)(2,1)S(1)}, u32[]{:S(2)}) copy-start(bf16[2304,8,64]{0,2,1:T(8,128)(2,1)S(1)} %get-tuple-element.630) | copy-start | bytes 7077892 | tf_op jit(solution)/shard_map/while
  346.9 7.2 %copy-start.1 = (bf16[2304,8,64]{0,2,1:T(8,128)(2,1)}, bf16[2304,8,64]{0,2,1:T(8,128)(2,1)S(1)}, u32[]{:S(2)}) copy-start(bf16[2304,8,64]{0,2,1:T(8,128)(2,1)S(1)} %get-tuple-element.630) | copy-start | bytes 7077892 | tf_op jit(solution)/shard_map/while
  407.4 7.2 %copy-start.1 = (bf16[2304,8,64]{0,2,1:T(8,128)(2,1)}, bf16[2304,8,64]{0,2,1:T(8,128)(2,1)S(1)}, u32[]{:S(2)}) copy-start(bf16[2304,8,64]{0,2,1:T(8,128)(2,1)S(1)} %get-tuple-element.630) | copy-start | bytes 7077892 | tf_op jit(solution)/shard_map/while
  467.7 5.9 collective-permute-start.5
  476.2 38.9 %collective-permute-start.6 = (bf16[128,6144]{1,0:T(8,128)(2,1)}, bf16[128,6144]{1,0:T(8,128)(2,1)}, u32[]{:S(2)}, u32[]{:S(2)}) collective-permute-start(bf16[128,6144]{1,0:T(8,128)(2,1)} %slice.154), channel_id=1, source_target_pairs={{0,2},{1,3},{2,0},{3,1},{4,6},{5,7},{6,4},{7,5},{8,10},{9,11},{10,... | collective-permute-start | bytes 4718600 | tf_op jit(solution)/shard_map/ppermute | solution.py:47
  480.1 1.5 collective-permute-start.15
  481.6 32.2 %collective-permute-start.16 = (f32[12,512]{1,0:T(8,128)S(1)}, f32[12,512]{1,0:T(8,128)S(1)}, u32[]{:S(2)}, u32[]{:S(2)}) collective-permute-start(f32[12,512]{1,0:T(8,128)S(1)} %bitcast_add_fusion.2), channel_id=1, source_target_pairs={{0,2},{1,3},{2,0},{3,1},{4,6},{5,7},{6,4},{7,5},{8,10},{9,11},{10,... | collective-permute-start | bytes 73736 | tf_op jit(solution)/shard_map/ppermute | solution.py:47
  482.3 35.4 %copy-start.16 = (bf16[2048,8,64]{0,2,1:T(8,128)(2,1)S(1)}, bf16[2048,8,64]{0,2,1:T(8,128)(2,1)}, u32[]{:S(2)}) copy-start(bf16[2048,8,64]{0,2,1:T(8,128)(2,1)} %copy-done.15) | copy-start | bytes 6291460
  513.8 6.4 %collective-permute-start.17 = (f32[12,512]{1,0:T(8,128)S(1)}, f32[12,512]{1,0:T(8,128)S(1)}, u32[]{:S(2)}, u32[]{:S(2)}) collective-permute-start(f32[12,512]{1,0:T(8,128)S(1)} %add.350), channel_id=1, source_target_pairs={{0,4},{1,5},{2,6},{3,7},{4,0},{5,1},{6,2},{7,3},{8,12},{9,13},{10,... | collective-permute-start | bytes 73736 | tf_op jit(solution)/shard_map/ppermute | solution.py:47
  517.0 18.9 %collective-permute-start.7 = (bf16[64,6144]{1,0:T(8,128)(2,1)S(1)}, bf16[64,6144]{1,0:T(8,128)(2,1)S(1)}, u32[]{:S(2)}, u32[]{:S(2)}) collective-permute-start(bf16[64,6144]{1,0:T(8,128)(2,1)S(1)} %slice.156), channel_id=1, source_target_pairs={{0,4},{1,5},{2,6},{3,7},{4,0},{5,1},{6,2},{7,3},{8,12},{9,13},{10,... | collective-permute-start | bytes 2359304 | tf_op jit(solution)/shard_map/ppermute | solution.py:47
  517.7 21.7 %copy-start.10 = (f32[2048,512]{0,1:T(8,128)S(1)}, f32[2048,512]{0,1:T(8,128)}, u32[]{:S(2)}) copy-start(f32[2048,512]{0,1:T(8,128)} %copy-done.8) | copy-start | bytes 12582916
  520.2 19.2 %copy-start.4 = (f32[2048,512]{0,1:T(8,128)S(1)}, f32[2048,512]{0,1:T(8,128)}, u32[]{:S(2)}) copy-start(f32[2048,512]{0,1:T(8,128)} %copy-done.3) | copy-start | bytes 12582916
  520.2 19.2 %copy-start.7 = (f32[2048,512]{0,1:T(8,128)S(1)}, f32[2048,512]{0,1:T(8,128)}, u32[]{:S(2)}) copy-start(f32[2048,512]{0,1:T(8,128)} %copy-done.6) | copy-start | bytes 12582916
  520.2 19.2 %copy-start.36 = (f32[2048]{0:T(1024)S(1)}, f32[2048]{0:T(1024)}, u32[]{:S(2)}) copy-start(f32[2048]{0:T(1024)} %copy-done.35) | copy-start | bytes 24580
  520.3 19.2 %copy-start.39 = (f32[2048]{0:T(1024)S(1)}, f32[2048]{0:T(1024)}, u32[]{:S(2)}) copy-start(f32[2048]{0:T(1024)} %copy-done.38) | copy-start | bytes 24580
  520.3 19.2 %copy-start.41 = (f32[2048]{0:T(1024)S(1)}, f32[2048]{0:T(1024)}, u32[]{:S(2)}) copy-start(f32[2048]{0:T(1024)} %copy-done.40) | copy-start | bytes 24580
  520.3 19.2 %copy-start.43 = (f32[2048]{0:T(1024)S(1)}, f32[2048]{0:T(1024)}, u32[]{:S(2)}) copy-start(f32[2048]{0:T(1024)} %copy-done.42) | copy-start | bytes 24580
  520.3 19.2 %copy-start.47 = (f32[512]{0:T(512)S(1)}, f32[512]{0:T(512)}, u32[]{:S(2)}) copy-start(f32[512]{0:T(512)} %copy-done.46) | copy-start | bytes 6148
  520.3 5.5 collective-permute-start.18
  525.8 27.5 %collective-permute-start.19 = (f32[12,512]{1,0:T(8,128)S(1)}, f32[12,512]{1,0:T(8,128)S(1)}, u32[]{:S(2)}, u32[]{:S(2)}) collective-permute-start(f32[12,512]{1,0:T(8,128)S(1)} %add.352), channel_id=1, source_target_pairs={{0,16},{1,17},{2,18},{3,19},{4,20},{5,21},{6,22},{7,23},{8,24},{9,... | collective-permute-start | bytes 73736 | tf_op jit(solution)/shard_map/ppermute | solution.py:47
  536.1 9.2 %copy-start.17 = (bf16[2048,512]{0,1:T(8,128)(2,1)S(1)}, bf16[2048,512]{0,1:T(8,128)(2,1)}, u32[]{:S(2)}) copy-start(bf16[2048,512]{0,1:T(8,128)(2,1)} %get-tuple-element.304) | copy-start | bytes 6291460
  536.1 17.2 %collective-permute-start.8 = (bf16[32,6144]{1,0:T(8,128)(2,1)S(1)}, bf16[32,6144]{1,0:T(8,128)(2,1)}, u32[]{:S(2)}, u32[]{:S(2)}) collective-permute-start(bf16[32,6144]{1,0:T(8,128)(2,1)S(1)} %slice.158), channel_id=1, source_target_pairs={{0,8},{1,9},{2,10},{3,11},{4,12},{5,13},{6,14},{7,15},{8,0},{9,1},... | collective-permute-start | bytes 1179656 | tf_op jit(solution)/shard_map/ppermute | solution.py:47
  547.8 39.3 %copy-start.31 = (f32[98496]{0:T(1024)S(1)}, f32[98496]{0:T(1024)}, u32[]{:S(2)}) copy-start(f32[98496]{0:T(1024)} %param.19) | copy-start | bytes 1181956
  547.8 39.4 %copy-start.32 = (f32[98496]{0:T(1024)S(1)}, f32[98496]{0:T(1024)}, u32[]{:S(2)}) copy-start(f32[98496]{0:T(1024)} %param.21) | copy-start | bytes 1181956
  547.8 39.4 %copy-start.33 = (f32[98496]{0:T(1024)S(1)}, f32[98496]{0:T(1024)}, u32[]{:S(2)}) copy-start(f32[98496]{0:T(1024)} %param.20) | copy-start | bytes 1181956
  553.3 35.0 %copy-start.34 = (f32[12,512]{1,0:T(8,128)}, f32[12,512]{1,0:T(8,128)S(1)}, u32[]{:S(2)}) copy-start(f32[12,512]{1,0:T(8,128)S(1)} %add.353) | copy-start | bytes 73732
  554.4 10.9 %collective-permute-start.9 = (bf16[16,6144]{1,0:T(8,128)(2,1)S(1)}, bf16[16,6144]{1,0:T(8,128)(2,1)S(1)}, u32[]{:S(2)}, u32[]{:S(2)}) collective-permute-start(bf16[16,6144]{1,0:T(8,128)(2,1)S(1)} %slice.160), channel_id=1, source_target_pairs={{0,16},{1,17},{2,18},{3,19},{4,20},{5,21},{6,22},{7,23},{8,24},{9,... | collective-permute-start | bytes 589832 | tf_op jit(solution)/shard_map/ppermute | solution.py:47
  566.0 1.2 collective-permute-start.10
  568.5 3.6 collective-permute-start.11
  572.7 3.6 collective-permute-start.12
  576.9 3.6 collective-permute-start.13
  581.1 4.5 collective-permute-start.14
  (38 other events, 141.3 us)

commit v2 on v0

v2 whole, which is shorter than its diff:
```python
import functools

import jax
import jax.numpy as jnp
from jax import lax
from jax.experimental import pallas as pl
from jax.experimental.pallas import tpu as pltpu
from jax.sharding import PartitionSpec as P

HD = 64
ROW = 1024
EPSILON = 1e-05
CLIP_NORM = 1.0
LEARN_RATE = 20.0
MOMENTUM = 0.5
AVERAGE_DECAY = 0.5
MASKED = -1e30
GELU_IN = 0.7978845608028654
GELU_CUBE = 0.044715

D = 512
FF = 2048
PAIR = 2 * HD
PAIRS = D // PAIR
LANES = 128
WINDOW = 3 * LANES
BLOCK = 16
BLOCKS = D // BLOCK
VECTORS = 12
FIRST_WIDTH = 3 * D + LANES
REST_WIDTH = D + 2 * FF
VMEM_BYTES = 60 * 1024 * 1024

f32 = jnp.float32
bf16 = jnp.bfloat16


def nn(left, right):
    return lax.dot_general(left, right, (((1,), (0,)), ((), ())), preferred_element_type=f32)


def nt(left, right):
    return lax.dot_general(left, right, (((1,), (1,)), ((), ())), preferred_element_type=f32)


def identity(size):
    down = lax.broadcasted_iota(jnp.int32, (size, size), 0)
    across = lax.broadcasted_iota(jnp.int32, (size, size), 1)
    return jnp.where(down == across, 1.0, 0.0).astype(bf16)


def turned(values, unit):
    return nt(unit, values).astype(bf16)


def place_blocks(target, halves, codes, mine, width):
    for half_at, half in enumerate(halves):
        for block_at in range(BLOCKS // 2):
            natural = mine ^ codes[half_at * (BLOCKS // 2) + block_at]
            to_rows = pl.ds(pl.multiple_of(natural * BLOCK, BLOCK), BLOCK)
            target[to_rows, :width] = half[block_at * BLOCK : (block_at + 1) * BLOCK, :width]


def spread_blocks(halves, source, codes, mine, begin, width):
    for half_at, half in enumerate(halves):
        for block_at in range(BLOCKS // 2):
            natural = mine ^ codes[half_at * (BLOCKS // 2) + block_at]
            from_rows = pl.ds(pl.multiple_of(natural * BLOCK, BLOCK), BLOCK)
            half[block_at * BLOCK : (block_at + 1) * BLOCK, begin : begin + width] = source[
                from_rows, :
            ].astype(bf16)


def project_kernel(
    codes, mine_ref, x_ref, near_ref, far_ref,
    xt_ref, qt_ref, kt_ref, vt_ref, k_ref, v_ref, vec_ref, pairs_ref,
    table, turned_weights, columns, rows,
):
    @pl.when(pl.program_id(0) == 0)
    def _():
        place_blocks(table, (near_ref, far_ref), codes, mine_ref[0], FIRST_WIDTH)
        unit = identity(256)
        for kind in range(3):
            for half in range(2):
                turned_weights[kind * D + half * 256 : kind * D + half * 256 + 256, :] = turned(
                    table[:, kind * D + half * 256 : kind * D + half * 256 + 256], unit
                )
        for pair in range(PAIRS):
            for kind in range(3):
                at = pair * 3 * PAIR + kind * PAIR
                pairs_ref[:, at : at + PAIR] = table[
                    :, kind * D + pair * PAIR : kind * D + (pair + 1) * PAIR
                ]
        vectors = table[:, 3 * D :].astype(f32)
        vec_ref[...] = vectors
        columns[0] = jnp.broadcast_to(vectors[:, 0:1], (D, LANES))
        columns[1] = jnp.broadcast_to(vectors[:, 1:2], (D, LANES))
        rows[...] = vectors.T[:8, :]

    x = x_ref[...]
    width = x.shape[0]
    reps = width // LANES
    unit = identity(256)
    for half in range(2):
        xt_ref[half * 256 : half * 256 + 256, :] = turned(x[:, half * 256 : half * 256 + 256], unit)
    bias_q = jnp.concatenate([columns[0]] * reps, axis=1)
    bias_v = jnp.concatenate([columns[1]] * reps, axis=1)
    query = nt(turned_weights[:D, :], x) + bias_q
    qt_ref[...] = (query.astype(bf16).astype(f32) * HD ** (-0.5)).astype(bf16)
    kt_ref[...] = nt(turned_weights[D : 2 * D, :], x).astype(bf16)
    vt_ref[...] = (nt(turned_weights[2 * D :, :], x) + bias_v).astype(bf16)
    k_ref[...] = nn(x, table[:, D : 2 * D]).astype(bf16)
    v_ref[...] = (nn(x, table[:, 2 * D : 3 * D]) + rows[1:2, :]).astype(bf16)


def fill_bias(bias, seg_ref, limits_ref):
    blocks = bias.shape[0]
    lane = lax.broadcasted_iota(jnp.int32, (1, LANES), 1)
    across = lax.broadcasted_iota(jnp.int32, (LANES, LANES), 1)
    down = lax.broadcasted_iota(jnp.int32, (LANES, LANES), 0)

    def codes_of(block):
        row = jnp.where(limits_ref[2] == 1, 0, block // (ROW // LANES))
        limit = jnp.where(row == 0, limits_ref[0], limits_ref[1])
        code = seg_ref[pl.ds(block, 1), :] * 2 + row
        live = lane + block * LANES - row * ROW < limit
        return code.astype(f32), jnp.where(live, code, -1).astype(f32)

    def one_block(block, carry):
        query_code, _ = codes_of(block)
        first = jnp.clip(block - 1, 0, blocks - 3)
        for part in range(3):
            _, key_code = codes_of(first + part)
            key_column = jnp.broadcast_to(key_code, (LANES, LANES)).T
            same = (first + part - block) * LANES
            allowed = (key_column == query_code) | (down + same == across)
            bias[block, part * LANES : (part + 1) * LANES, :] = jnp.where(allowed, 0.0, MASKED)
        return carry

    lax.fori_loop(0, blocks, one_block, 0)


def two_heads(values):
    zeros = jnp.zeros((HD, values.shape[1]), values.dtype)
    left = jnp.concatenate([values[:HD], zeros], axis=0)
    right = jnp.concatenate([zeros, values[HD:]], axis=0)
    return jnp.concatenate([left, right], axis=1)


def own_heads(values):
    return jnp.concatenate([values[:HD, :LANES], values[HD:, LANES:]], axis=0)


def attend_kernel(limits_ref, seg_ref, qt_ref, k_ref, vt_ref, att_ref, logsum_ref, bias):
    @pl.when(pl.program_id(0) == 0)
    def _():
        fill_bias(bias, seg_ref, limits_ref)

    blocks = bias.shape[0]

    def one_block(block, carry):
        here = pl.ds(pl.multiple_of(block * LANES, LANES), LANES)
        begin = pl.multiple_of(jnp.clip(block - 1, 0, blocks - 3) * LANES, LANES)
        window = pl.ds(begin, WINDOW)
        mask = bias[block]
        scores = nn(k_ref[window, :], two_heads(qt_ref[:, here]))
        scores = scores + jnp.concatenate([mask, mask], axis=1)
        highest = jnp.max(scores, axis=0, keepdims=True)
        exponent = jnp.exp(scores - highest)
        total = jnp.sum(exponent, axis=0, keepdims=True)
        outputs = nn(vt_ref[:, window], exponent.astype(bf16)) * (1.0 / total)
        att_ref[:, here] = own_heads(outputs).astype(bf16)
        logsum_ref[0, pl.ds(block, 1), :] = highest + jnp.log(total)
        return carry

    lax.fori_loop(0, blocks, one_block, 0, unroll=2)


def mean_down(values):
    return jnp.sum(values, axis=0, keepdims=True) * (1.0 / D)


def lane_parts(values):
    total = values[:, :LANES]
    for at in range(LANES, values.shape[1], LANES):
        total = total + values[:, at : at + LANES]
    return total


def feed_kernel(
    codes, mine_ref, limits_ref, xt_ref, att_ref, cot_ref, vec_ref, up_bias_ref, near_ref, far_ref,
    layer_ref, ga_ref, both_ref, keep_ref, send_ref, sums_ref,
    table, out_turned, up_turned, down_turned, columns, slopes, hidden, grad_up,
    acc_down, acc_up, acc_out, acc_vec,
):
    step = pl.program_id(0)
    width = xt_ref.shape[1]
    reps = width // LANES
    unit = identity(256)
    chunk = 512

    @pl.when(step == 0)
    def _():
        place_blocks(table, (near_ref, far_ref), codes, mine_ref[0], REST_WIDTH)
        for at in range(0, D, 256):
            out_turned[at : at + 256, :] = turned(table[:, at : at + 256], unit)
        for at in range(0, FF, 256):
            up_turned[at : at + 256, :] = turned(table[:, D + at : D + at + 256], unit)
            down_turned[at : at + 256, :] = turned(table[:, D + FF + at : D + FF + at + 256], unit)
        for kind in range(6):
            columns[kind] = jnp.broadcast_to(vec_ref[:, kind + 2 : kind + 3], (D, LANES))
        acc_down[...] = jnp.zeros_like(acc_down)
        acc_up[...] = jnp.zeros_like(acc_up)
        acc_out[...] = jnp.zeros_like(acc_out)
        acc_vec[...] = jnp.zeros_like(acc_vec)

    def column(kind):
        return jnp.concatenate([columns[kind]] * reps, axis=1)

    place = lax.broadcasted_iota(jnp.int32, (1, width), 1) + step * width
    row = jnp.where(limits_ref[2] == 1, 0, place // ROW)
    limit = jnp.where(row == 0, limits_ref[0], limits_ref[1])
    live = place - row * ROW < limit

    x = xt_ref[...].astype(f32)
    att = att_ref[...]
    z_one = x + nn(table[:, :D], att) + column(0)
    centred = z_one - mean_down(z_one)
    inverse_one = lax.rsqrt(mean_down(centred * centred) + EPSILON)
    normed_one = centred * inverse_one
    first = normed_one * column(2) + column(3)
    first_low = first.astype(bf16)
    z_two = first + x + column(1)
    for at in range(0, FF, chunk):
        bias = jnp.concatenate([up_bias_ref[at : at + chunk, :]] * reps, axis=1)
        pre = nn(up_turned[at : at + chunk, :], first_low) + bias
        square = pre * pre
        tanh = jnp.tanh(pre * (GELU_IN + (GELU_IN * GELU_CUBE) * square))
        half = 0.5 + 0.5 * tanh
        value = pre * half
        slopes[at : at + chunk, :] = half + value * (1.0 - tanh) * (
            GELU_IN + (3.0 * GELU_IN * GELU_CUBE) * square
        )
        hidden[at : at + chunk, :] = value.astype(bf16)
    z_two = z_two + nn(table[:, D + FF :], hidden[...])
    centred = z_two - mean_down(z_two)
    inverse_two = lax.rsqrt(mean_down(centred * centred) + EPSILON)
    normed_two = centred * inverse_two
    gain_two = column(4)
    layer = jnp.where(live, normed_two * gain_two + column(5), 0.0).astype(bf16)
    for at in range(0, width, 256):
        layer_ref[at : at + 256, :] = nt(unit, layer[:, at : at + 256]).astype(bf16)
    cot = jnp.concatenate([nt(unit, cot_ref[:, at : at + 256]) for at in range(0, D, 256)], axis=0)
    cot = jnp.where(live, cot, 0.0)
    scaled = cot * gain_two
    grad_two = inverse_two * (scaled - mean_down(scaled) - normed_two * mean_down(scaled * normed_two))
    grad_feed = grad_two.astype(bf16)
    acc_vec[1] += lane_parts(grad_feed.astype(f32))
    acc_vec[4] += lane_parts(cot * normed_two)
    acc_vec[5] += lane_parts(cot)
    for at in range(0, FF, chunk):
        grad_hidden = nn(down_turned[at : at + chunk, :], grad_feed)
        grad_up[at : at + chunk, :] = (grad_hidden * slopes[at : at + chunk, :]).astype(bf16)
    grad_first = grad_two + nn(table[:, D : D + FF], grad_up[...])
    acc_vec[2] += lane_parts(grad_first * normed_one)
    acc_vec[3] += lane_parts(grad_first)
    scaled = grad_first * column(2)
    grad_one = inverse_one * (scaled - mean_down(scaled) - normed_one * mean_down(scaled * normed_one))
    both_ref[...] = grad_two + grad_one
    grad_branch = grad_one.astype(bf16)
    acc_vec[0] += lane_parts(grad_branch.astype(f32))
    ga_ref[...] = nn(out_turned[...], grad_branch).astype(bf16)
    acc_down[...] += nt(grad_feed, hidden[...])
    ones = jnp.ones((BLOCK, width), bf16)
    acc_up[...] += nt(jnp.concatenate([first_low, ones], axis=0), grad_up[...])
    acc_out[...] += nt(grad_branch, att)

    @pl.when(step == pl.num_programs(0) - 1)
    def _():
        halves = (keep_ref, send_ref)
        spread_blocks(halves, acc_out, codes, mine_ref[0], 0, D)
        spread_blocks(halves, acc_up, codes, mine_ref[0], D, FF)
        spread_blocks(halves, acc_down, codes, mine_ref[0], D + FF, FF)
        for kind in range(6):
            sums_ref[kind : kind + 1, :] = jnp.sum(acc_vec[kind].T, axis=0, keepdims=True)
        sums_ref[6:8, :] = jnp.zeros((2, D), f32)
        for at in range(4):
            sums_ref[8 + at : 9 + at, :] = acc_up[D : D + 1, at * D : (at + 1) * D]
        sums_ref[12:16, :] = jnp.zeros((4, D), f32)


def attend_back_kernel(
    codes, mine_ref, limits_ref, seg_ref, xt_ref, qt_ref, kt_ref, k_ref, v_ref, att_ref, ga_ref,
    logsum_ref, grads_ref, keep_ref, send_ref, sums_ref, bias, acc_key, acc_value, weight_grad,
):
    @pl.when(pl.program_id(0) == 0)
    def _():
        fill_bias(bias, seg_ref, limits_ref)

    blocks = bias.shape[0]
    acc_key[...] = jnp.zeros_like(acc_key)
    acc_value[...] = jnp.zeros_like(acc_value)

    def one_block(block, carry):
        here = pl.ds(pl.multiple_of(block * LANES, LANES), LANES)
        begin = pl.multiple_of(jnp.clip(block - 1, 0, blocks - 3) * LANES, LANES)
        window = pl.ds(begin, WINDOW)
        mask = bias[block]
        query = two_heads(qt_ref[:, here])
        grad_low = ga_ref[:, here]
        grad = two_heads(grad_low)
        product = grad_low.astype(f32) * att_ref[:, here].astype(f32)
        centre = jnp.concatenate(
            [
                jnp.sum(product[:HD], axis=0, keepdims=True),
                jnp.sum(product[HD:], axis=0, keepdims=True),
            ],
            axis=1,
        )
        scores = nn(k_ref[window, :], query) + jnp.concatenate([mask, mask], axis=1)
        chances = jnp.exp(scores - logsum_ref[0, pl.ds(block, 1), :])
        grad_chances = nn(v_ref[window, :], grad)
        grad_scores = (chances * (grad_chances - centre)).astype(bf16)
        grad_query = own_heads(nn(kt_ref[:, window], grad_scores)) * HD ** (-0.5)
        grads_ref[0, :PAIR, here] = grad_query.astype(bf16)
        acc_key[:, window] += nt(query, grad_scores)
        acc_value[:, window] += nt(grad, chances.astype(bf16))
        return carry

    lax.fori_loop(0, blocks, one_block, 0, unroll=2)
    grads_ref[0, PAIR : 2 * PAIR, :] = acc_key[...].astype(bf16)
    grads_ref[0, 2 * PAIR :, :] = acc_value[...].astype(bf16)
    grads = grads_ref[0]
    weight_grad[...] = nt(xt_ref[...], grads)
    spread_blocks((keep_ref, send_ref), weight_grad, codes, mine_ref[0], 0, 3 * PAIR)
    sums_ref[0] = nt(jnp.ones((BLOCK, grads.shape[1]), bf16), grads)[:8]


def input_kernel(grads_ref, weights_ref, both_ref, out_ref):
    total = both_ref[...]
    for pair in range(PAIRS):
        total = total + nn(weights_ref[:, pair * 3 * PAIR : (pair + 1) * 3 * PAIR], grads_ref[pair])
    unit = identity(256)
    high = total.astype(bf16)
    rest = (total - high.astype(f32)).astype(bf16)
    for at in range(0, total.shape[1], 256):
        out_ref[at : at + 256, :] = nt(unit, high[:, at : at + 256]) + nt(unit, rest[:, at : at + 256])


def exchange(values, bit, count):
    return lax.ppermute(values, "dp", [(at, at ^ bit) for at in range(count)])


def gather_halves(block, count):
    bit = count // 2
    while bit > 1:
        block = jnp.concatenate([block, exchange(block, bit, count)], axis=0)
        bit //= 2
    return block, exchange(block, 1, count)


def scatter_sum(keep, send, count):
    bit = 1
    while True:
        arrived = exchange(send, bit, count)
        total = keep.astype(f32) + arrived.astype(f32)
        bit *= 2
        if bit == count:
            return total
        half = total.shape[0] // 2
        total = total.astype(bf16)
        keep, send = total[:half], total[half:]


def sum_everywhere(values, count):
    bit = 1
    while bit < count:
        values = values + exchange(values, bit, count)
        bit *= 2
    return values


def reversed_bits(count):
    width = count.bit_length() - 1
    return [sum(((at >> k) & 1) << (width - 1 - k) for k in range(width)) for at in range(count)]


def whole(shape):
    return pl.BlockSpec(shape, lambda *at: (0,) * len(shape))


def smem():
    return pl.BlockSpec(memory_space=pltpu.SMEM)


def shaped(shape, dtype):
    return jax.ShapeDtypeStruct(shape, dtype)


def params_of(**more):
    return pltpu.CompilerParams(vmem_limit_bytes=VMEM_BYTES, **more)


def body(tokens, cotangent, segment_ids, row_lengths, row_widths, params, momenta, averages):
    slots = tokens.shape[0]
    count = lax.axis_size("dp")
    mine = lax.axis_index("dp").astype(jnp.int32)
    own_count = D // count
    table_width = params.shape[0] // own_count
    blocks = slots // LANES
    direct = own_count == BLOCK
    if direct:
        codes = reversed_bits(count)
        origin = mine.reshape(1)
    else:
        codes = list(range(BLOCKS))
        origin = jnp.zeros((1,), jnp.int32)
        reverse = jnp.array(reversed_bits(count), jnp.int32)

    def to_kernel(near, far):
        if direct:
            return near, far
        table = jnp.concatenate([near, far], axis=0).reshape(count, own_count, -1)
        table = jnp.take(table, reverse[jnp.arange(count) ^ mine], axis=0).reshape(D, -1)
        return table[: D // 2], table[D // 2 :]

    def from_kernel(keep, send):
        if direct:
            return keep, send
        table = jnp.concatenate([keep, send], axis=0).reshape(count, own_count, -1)
        table = jnp.take(table, reverse ^ mine, axis=0).reshape(D, -1)
        return table[: D // 2], table[D // 2 :]

    own_table = params.astype(bf16).reshape(own_count, table_width)
    own_first = jnp.concatenate(
        [
            own_table[:, : 3 * D],
            jnp.pad(own_table[:, 12 * D :], ((0, 0), (0, LANES - VECTORS))),
        ],
        axis=1,
    )
    first_near, first_far = to_kernel(*gather_halves(own_first, count))
    rest_near, rest_far = to_kernel(*gather_halves(own_table[:, 3 * D : 12 * D], count))
    limits = jnp.concatenate([row_lengths, row_widths])
    segments = segment_ids.reshape(blocks, LANES)

    tile = 256
    steps = slots // tile
    across = pl.BlockSpec((D, tile), lambda at: (0, at))
    down = pl.BlockSpec((tile, D), lambda at: (at, 0))
    half_first = whole((D // 2, FIRST_WIDTH))
    xt, qt, kt, vt, key, value, vectors, pair_weights = pl.pallas_call(
        functools.partial(project_kernel, codes),
        grid=(steps,),
        in_specs=[smem(), down, half_first, half_first],
        out_specs=[across] * 4 + [down] * 2 + [whole((D, LANES)), whole((D, 3 * D))],
        out_shape=[shaped((D, slots), bf16)] * 4
        + [shaped((slots, D), bf16)] * 2
        + [shaped((D, LANES), f32), shaped((D, 3 * D), bf16)],
        scratch_shapes=[
            pltpu.VMEM((D, FIRST_WIDTH), bf16),
            pltpu.VMEM((3 * D, D), bf16),
            pltpu.VMEM((2, D, LANES), f32),
            pltpu.VMEM((8, D), f32),
        ],
        compiler_params=params_of(),
        name="project",
    )(origin, tokens, first_near, first_far)

    pair_rows = pl.BlockSpec((PAIR, slots), lambda at: (at, 0))
    pair_columns = pl.BlockSpec((slots, PAIR), lambda at: (0, at))
    sums_block = pl.BlockSpec((1, blocks, 2 * LANES), lambda at: (at, 0, 0))
    attended, logsum = pl.pallas_call(
        attend_kernel,
        grid=(PAIRS,),
        in_specs=[smem(), whole((blocks, LANES)), pair_rows, pair_columns, pair_rows],
        out_specs=[pair_rows, sums_block],
        out_shape=[shaped((D, slots), bf16), shaped((PAIRS, blocks, 2 * LANES), f32)],
        scratch_shapes=[pltpu.VMEM((blocks, WINDOW, LANES), f32)],
        compiler_params=params_of(),
        name="attend",
    )(limits, segments, qt, key, vt)

    up_bias = jnp.broadcast_to(vectors[:, 8:VECTORS].reshape(FF, 1), (FF, LANES))
    half_rest = whole((D // 2, REST_WIDTH))
    layer_output, grad_attended, grad_both, keep_rest, send_rest, feed_sums = pl.pallas_call(
        functools.partial(feed_kernel, codes),
        grid=(steps,),
        in_specs=[
            smem(), smem(), across, across, down,
            whole((D, LANES)), whole((FF, LANES)), half_rest, half_rest,
        ],
        out_specs=[down, across, across, half_rest, half_rest, whole((16, D))],
        out_shape=[
            shaped((slots, D), bf16),
            shaped((D, slots), bf16),
            shaped((D, slots), f32),
            shaped((D // 2, REST_WIDTH), bf16),
            shaped((D // 2, REST_WIDTH), bf16),
            shaped((16, D), f32),
        ],
        scratch_shapes=[
            pltpu.VMEM((D, REST_WIDTH), bf16),
            pltpu.VMEM((D, D), bf16),
            pltpu.VMEM((FF, D), bf16),
            pltpu.VMEM((FF, D), bf16),
            pltpu.VMEM((6, D, LANES), f32),
            pltpu.VMEM((FF, tile), f32),
            pltpu.VMEM((FF, tile), bf16),
            pltpu.VMEM((FF, tile), bf16),
            pltpu.VMEM((D, FF), f32),
            pltpu.VMEM((D + BLOCK, FF), f32),
            pltpu.VMEM((D, D), f32),
            pltpu.VMEM((6, D, LANES), f32),
        ],
        compiler_params=params_of(),
        name="feed",
    )(origin, limits, xt, attended, cotangent, vectors, up_bias, rest_near, rest_far)

    own_rest = scatter_sum(*from_kernel(keep_rest, send_rest), count)
    feed_sums = sum_everywhere(feed_sums, count)

    half_pairs = pl.BlockSpec((D // 2, 3 * PAIR), lambda at: (0, at))
    grads, keep_first, send_first, pair_sums = pl.pallas_call(
        functools.partial(attend_back_kernel, codes),
        grid=(PAIRS,),
        in_specs=[
            smem(), smem(), whole((blocks, LANES)), whole((D, slots)),
            pair_rows, pair_rows, pair_columns, pair_columns, pair_rows, pair_rows, sums_block,
        ],
        out_specs=[
            pl.BlockSpec((1, 3 * PAIR, slots), lambda at: (at, 0, 0)),
            half_pairs,
            half_pairs,
            pl.BlockSpec((1, 8, 3 * PAIR), lambda at: (at, 0, 0)),
        ],
        out_shape=[
            shaped((PAIRS, 3 * PAIR, slots), bf16),
            shaped((D // 2, 3 * D), bf16),
            shaped((D // 2, 3 * D), bf16),
            shaped((PAIRS, 8, 3 * PAIR), f32),
        ],
        scratch_shapes=[
            pltpu.VMEM((blocks, WINDOW, LANES), f32),
            pltpu.VMEM((PAIR, slots), f32),
            pltpu.VMEM((PAIR, slots), f32),
            pltpu.VMEM((D, 3 * PAIR), f32),
        ],
        compiler_params=params_of(),
        name="attend_back",
    )(origin, limits, segments, xt, qt, kt, key, value, attended, grad_attended, logsum)

    own_first_grad = scatter_sum(*from_kernel(keep_first, send_first), count)
    pair_sums = sum_everywhere(pair_sums[:, 0, :], count)

    input_grad = pl.pallas_call(
        input_kernel,
        grid=(steps,),
        in_specs=[
            pl.BlockSpec((PAIRS, 3 * PAIR, tile), lambda at: (0, 0, at)),
            whole((D, 3 * D)),
            across,
        ],
        out_specs=down,
        out_shape=shaped((slots, D), f32),
        compiler_params=params_of(),
        name="input_grad",
    )(grads, pair_weights, grad_both)

    pair_sums = pair_sums.reshape(PAIRS, 3, PAIR)
    vector_grads = jnp.concatenate(
        [
            jnp.stack([pair_sums[:, 0].reshape(D), pair_sums[:, 2].reshape(D)], axis=1),
            feed_sums[:6].T,
            feed_sums[8:12].reshape(D, 4),
        ],
        axis=1,
    )
    own_first_grad = own_first_grad.reshape(own_count, PAIRS, 3, PAIR)
    own_first_grad = own_first_grad.transpose(0, 2, 1, 3).reshape(own_count, 3 * D)
    squares = jnp.sum(own_first_grad * own_first_grad) + jnp.sum(own_rest * own_rest)
    squares = sum_everywhere(squares.reshape(1, 1), count)[0, 0]
    grad_norm = jnp.sqrt(squares + jnp.sum(vector_grads * vector_grads))
    own_vectors = lax.dynamic_slice_in_dim(vector_grads, mine * own_count, own_count)
    own_grad = jnp.concatenate([own_first_grad, own_rest, own_vectors], axis=1).reshape(-1)
    clipped = own_grad * jnp.minimum(1.0, CLIP_NORM / (grad_norm + 1e-06))
    new_momenta = MOMENTUM * momenta + clipped
    new_params = params - LEARN_RATE * (clipped + MOMENTUM * new_momenta)
    new_averages = AVERAGE_DECAY * averages + (1.0 - AVERAGE_DECAY) * new_params
    return (
        layer_output, input_grad, grad_norm, vector_grads, new_params, new_momenta, new_averages,
    )


def solution(mesh):
    placed = (P("dp", None), P("dp", None), P("dp"), P("dp"), P("dp"), P("dp"), P("dp"), P("dp"))
    return jax.shard_map(
        body,
        mesh=mesh,
        in_specs=placed,
        out_specs=(P("dp", None), P("dp", None), P(), P(), P("dp"), P("dp"), P("dp")),
        check_vma=False,
    )
```

time: 878 us -> 392 us (0.45); the launches traced: 867 us -> 391 us
  matrix products: 247 us -> 0 us
  waiting for transfers between devices: 367 us -> 140 us
  Pallas kernels: 0 us -> 171 us
  local copies, waits for them, and re-layouts: 127 us -> 9.91 us
  starting transfers between devices: 0.08 us -> 49 us
  blocking collectives: 40.3 us -> 0 us
  other arithmetic: 53.8 us -> 13.9 us
  loops' own time: 14.4 us -> 0 us
  between operations: 17.2 us -> 8.09 us
    unnamed x4 -> x0, waiting for transfers between devices: 367 us -> none
    dot_general x46 -> x0, matrix products: 247 us -> none  [the longest x12 82.2 us: mixed_dot(): return jnp.dot(left_side, right_side, preferred_element_type=jnp.float32)]
    pallas_call x0 -> x5, Pallas kernels: none -> 171 us  [the longest x1 70.6 us: body(): pl.pallas_call(functools.partial(feed_kernel, codes), grid=(steps,), in_s...]
    ppermute x0 -> x35, waiting for transfers between devices: none -> 140 us  [exchange(): return lax.ppermute(values, 'dp', [(at, at ^ bit) for at in range(count)])]
    ppermute x0 -> x35, starting transfers between devices: none -> 49 us  [exchange(): return lax.ppermute(values, 'dp', [(at, at ^ bit) for at in range(count)])]
    psum x1 -> x0, blocking collectives: 40.3 us -> none  [body(): lax.psum((jnp.sum(own_rows * own_rows), vector_local), 'dp')]
    reshape x4 -> x5, local copies, waits for them, and re-layouts: 35.5 us -> 0.76 us  [the longest x2 0.37 us: body(): feed_sums[8:12].reshape(D, 4)]
    unnamed x64 -> x29, local copies, waits for them, and re-layouts: 32.6 us -> 2.49 us
  transfers between devices with their start and end apart: 2 -> 35, of which waited for: 2 -> 23; matrix products, arithmetic and copies ran while one was open for 3% -> 4% of each run, Pallas kernels for 0% -> 26%
where the time goes in v2:
time: 392 us; the launch traced here: 391 us
  Pallas kernels  171 us (44%)
  waiting for transfers between devices  140 us (36%)
  starting transfers between devices  49 us (12%)
  other arithmetic  13.9 us (4%)
  local copies, waits for them, and re-layouts  9.91 us (3%)
  between operations  8.09 us (2%)
    ppermute x35, waiting for transfers between devices, exchange(): return lax.ppermute(values, 'dp', [(at, at ^ bit) for at in range(count)])  140 us
    pallas_call x1, Pallas kernels, body(): pl.pallas_call(functools.partial(feed_kernel, codes), grid=(steps,), in_s...  70.6 us
    ppermute x35, starting transfers between devices, exchange(): return lax.ppermute(values, 'dp', [(at, at ^ bit) for at in range(count)])  49 us
    pallas_call x1, Pallas kernels, body(): pl.pallas_call(functools.partial(attend_back_kernel, codes), grid=(PAIRS,...  41.7 us
    pallas_call x1, Pallas kernels, body(): pl.pallas_call(attend_kernel, grid=(PAIRS,), in_specs=[smem(), whole((blo...  32.2 us
    pallas_call x1, Pallas kernels, body(): pl.pallas_call(input_kernel, grid=(steps,), in_specs=[pl.BlockSpec((PAIRS...  13.7 us
    pallas_call x1, Pallas kernels, body(): pl.pallas_call(functools.partial(project_kernel, codes), grid=(steps,), i...  12.4 us
    convert_element_type x8, other arithmetic, scatter_sum(): total = total.astype(bf16)  8.18 us
  transfers between devices with their start and end apart: 35, of which 23 were waited for; matrix products, arithmetic and copies ran while one was open for 4% of the time, Pallas kernels for 26%

profile of v2, /device:TPU:0, one launch (start us, length us, event | category | flops | bytes accessed | tf_op | source)
XLA Modules:
  0.0 391.3 jit_solution(16973159196316645968)
XLA Ops:
  2.0 4.1 %collective-permute-start.5 = (bf16[16,4608]{1,0:T(8,128)(2,1)S(1)}, bf16[16,4608]{1,0:T(8,128)(2,1)S(1)}, u32[]{:S(2)}, u32[]{:S(2)}) collective-permute-start(bf16[16,4608]{1,0:T(8,128)(2,1)S(1)} %get-tuple-element.54), channel_id=1, source_target_pairs={{0,16},{1,17},{2,18},{3,19},{4,20},{5,21},{6,22},{7,23},{8,24},{9,... | collective-permute-start | bytes 442376 | tf_op jit(solution)/shard_map/ppermute | solution.py:351
  6.1 7.0 %collective-permute-done.5 = bf16[16,4608]{1,0:T(8,128)(2,1)S(1)} collective-permute-done((bf16[16,4608]{1,0:T(8,128)(2,1)S(1)}, bf16[16,4608]{1,0:T(8,128)(2,1)S(1)}, u32[]{:S(2)}, u32[]{:S(2)}) %collective-permute-start.5) | collective-permute-done | bytes 147488 | tf_op jit(solution)/shard_map/ppermute | solution.py:351
  13.9 7.5 %collective-permute-done.6 = bf16[32,4608]{1,0:T(8,128)(2,1)S(1)} collective-permute-done((bf16[32,4608]{1,0:T(8,128)(2,1)S(1)}, bf16[32,4608]{1,0:T(8,128)(2,1)S(1)}, u32[]{:S(2)}, u32[]{:S(2)}) %collective-permute-start.6) | collective-permute-done | bytes 294944 | tf_op jit(solution)/shard_map/ppermute | solution.py:351
  21.4 1.3 collective-permute-start.7
  22.8 3.4 collective-permute-start
  26.2 8.9 %collective-permute-done.7 = bf16[64,4608]{1,0:T(8,128)(2,1)S(1)} collective-permute-done((bf16[64,4608]{1,0:T(8,128)(2,1)S(1)}, bf16[64,4608]{1,0:T(8,128)(2,1)S(1)}, u32[]{:S(2)}, u32[]{:S(2)}) %collective-permute-start.7) | collective-permute-done | bytes 589856 | tf_op jit(solution)/shard_map/ppermute | solution.py:351
  35.1 1.3 collective-permute-start.8
  36.6 23.9 %collective-permute-done.8 = bf16[128,4608]{1,0:T(8,128)(2,1)S(1)} collective-permute-done((bf16[128,4608]{1,0:T(8,128)(2,1)S(1)}, bf16[128,4608]{1,0:T(8,128)(2,1)S(1)}, u32[]{:S(2)}, u32[]{:S(2)}) %collective-permute-start.8) | collective-permute-done | bytes 1179680 | tf_op jit(solution)/shard_map/ppermute | solution.py:351
  60.7 3.1 collective-permute-start.1
  63.9 3.6 collective-permute-done.1
  67.5 1.6 collective-permute-start.2
  69.1 5.5 %collective-permute-done.2 = bf16[64,1664]{1,0:T(8,128)(2,1)S(1)} collective-permute-done((bf16[64,1664]{1,0:T(8,128)(2,1)S(1)}, bf16[64,1664]{1,0:T(8,128)(2,1)S(1)}, u32[]{:S(2)}, u32[]{:S(2)}) %collective-permute-start.2) | collective-permute-done | bytes 213024 | tf_op jit(solution)/shard_map/ppermute | solution.py:351
  74.7 1.6 collective-permute-start.3
  76.3 9.2 %collective-permute-done.3 = bf16[128,1664]{1,0:T(8,128)(2,1)S(1)} collective-permute-done((bf16[128,1664]{1,0:T(8,128)(2,1)S(1)}, bf16[128,1664]{1,0:T(8,128)(2,1)S(1)}, u32[]{:S(2)}, u32[]{:S(2)}) %collective-permute-start.3) | collective-permute-done | bytes 426016 | tf_op jit(solution)/shard_map/ppermute | solution.py:351
  88.1 12.4 %project.1 = (bf16[512,2048]{1,0:T(8,128)(2,1)}, bf16[512,2048]{1,0:T(8,128)(2,1)}, bf16[512,2048]{1,0:T(8,128)(2,1)}, bf16[512,2048]{1,0:T(8,128)(2,1)}, bf16[2...) custom-call(s32[1]{0:T(128)} %bitcast.mine_ref, ...), custom_call_target="tpu_custom_call" | custom-call | tf_op jit(solution)/shard_map/project/pallas_call | solution.py:452
  101.8 32.2 %attend.1 = (bf16[512,2048]{1,0:T(8,128)(2,1)}, f32[4,16,256]{2,1,0:T(8,128)}) custom-call(s32[3]{0:T(128)} %pad_add_fusion.limits_ref, s32[16,128]{1,0:T(8,128)} %bitcast.18, bf16[512,2048]{1,0:T(8,128)(2,1)} %get-tuple-element.28.qt_ref, bf16[2048,512]{1,0:T(8,128)(2,1)} %get-tuple-element.29.k_ref, bf16[512,2048]{1,0:T(8,128)(2,1)} %get-tuple-element.30.vt_ref), custom_call_target="tpu_custom_call" | custom-call | tf_op jit(solution)/shard_map/attend/pallas_call | solution.py:473
  134.0 1.3 broadcast_in_dim.8.up_bias_ref
  135.3 70.6 %feed.1 = (bf16[2048,512]{1,0:T(8,128)(2,1)}, bf16[512,2048]{1,0:T(8,128)(2,1)}, f32[512,2048]{1,0:T(8,128)}, bf16[256,4608]{1,0:T(8,128)(2,1)}, bf16[256,4608]{1,0:T(8,128)(2,1)}, /*index=5*/f32[16,512]{1,0:T(8,128)}) custom-call(s32[1]{0:T(128)} %bitcast.mine_ref, s32[3]{0:T(128)} %pad_add_fusion.limits_ref, bf16[512,2048]{1,0:T(8,128)(2,1)} %get-tuple-element.27.xt_ref, ...), custom_call_target="tpu_custom_call" | custom-call | tf_op jit(solution)/shard_map/feed/pallas_call | solution.py:486
  206.4 4.3 %collective-permute-done.30 = f32[16,512]{1,0:T(8,128)S(1)} collective-permute-done((f32[16,512]{1,0:T(8,128)}, f32[16,512]{1,0:T(8,128)S(1)}, u32[]{:S(2)}, u32[]{:S(2)}) %collective-permute-start.30) | collective-permute-done | bytes 32800 | tf_op jit(solution)/shard_map/ppermute | solution.py:351
  211.5 1.5 collective-permute-start.31
  212.9 41.7 %attend_back.1 = (bf16[4,384,2048]{2,1,0:T(8,128)(2,1)}, bf16[256,1536]{1,0:T(8,128)(2,1)}, bf16[256,1536]{1,0:T(8,128)(2,1)}, f32[4,8,384]{2,1,0:T(8,128)}) custom-call(s32[1]{0:T(128)} %bitcast.mine_ref, s32[3]{0:T(128)} %pad_add_fusion.limits_ref, s32[16,128]{1,0:T(8,128)} %bitcast.19, bf16[512,2048]{1,0:T(8,128)(2,1)} %get-tuple-element.27.xt_ref, ...), custom_call_target="tpu_custom_call" | custom-call | tf_op jit(solution)/shard_map/attend_back/pallas_call | solution.py:524
  255.5 1.6 collective-permute-start.32
  257.7 3.1 collective-permute-done.26
  261.9 2.6 collective-permute-done.27
  264.4 1.3 collective-permute-start.28
  265.7 2.3 collective-permute-done.28
  268.0 3.6 collective-permute-start.29
  271.6 13.7 %input_grad.1 = f32[2048,512]{1,0:T(8,128)} custom-call(bf16[4,384,2048]{2,1,0:T(8,128)(2,1)} %get-tuple-element.38.grads_ref, bf16[512,1536]{1,0:T(8,128)(2,1)} %get-tuple-element.39.weights_ref, f32[512,2048]{1,0:T(8,128)} %get-tuple-element.40.both_ref), custom_call_target="tpu_custom_call" | custom-call | tf_op jit(solution)/shard_map/input_grad/pallas_call | solution.py:556
  286.5 2.8 collective-permute-done.33
  289.3 1.4 copy-done.1
  290.7 2.9 add_convert_fusion
  296.2 1.3 add_convert_fusion.2
  298.3 1.5 collective-permute-start.11
  300.2 30.5 %collective-permute-done.11 = bf16[128,1536]{1,0:T(8,128)(2,1)} collective-permute-done((bf16[128,1536]{1,0:T(8,128)(2,1)}, bf16[128,1536]{1,0:T(8,128)(2,1)}, u32[]{:S(2)}, u32[]{:S(2)}) %collective-permute-start.11) | collective-permute-done | bytes 393248 | tf_op jit(solution)/shard_map/ppermute | solution.py:351
  333.7 1.5 add_convert_fusion.1
  337.1 3.6 collective-permute-done.12
  343.0 7.9 %collective-permute-done.17 = bf16[64,4608]{1,0:T(8,128)(2,1)S(1)} collective-permute-done((bf16[64,4608]{1,0:T(8,128)(2,1)S(1)}, bf16[64,4608]{1,0:T(8,128)(2,1)S(1)}, u32[]{:S(2)}, u32[]{:S(2)}) %collective-permute-start.17) | collective-permute-done | bytes 589856 | tf_op jit(solution)/shard_map/ppermute | solution.py:351
  352.3 2.4 collective-permute-start.14
  354.7 4.1 %collective-permute-done.18 = bf16[32,4608]{1,0:T(8,128)(2,1)S(1)} collective-permute-done((bf16[32,4608]{1,0:T(8,128)(2,1)S(1)}, bf16[32,4608]{1,0:T(8,128)(2,1)S(1)}, u32[]{:S(2)}, u32[]{:S(2)}) %collective-permute-start.18) | collective-permute-done | bytes 294944 | tf_op jit(solution)/shard_map/ppermute | solution.py:351
  358.9 2.4 collective-permute-start.19
  362.2 4.4 %collective-permute-done.19 = bf16[16,4608]{1,0:T(8,128)(2,1)S(1)} collective-permute-done((bf16[16,4608]{1,0:T(8,128)(2,1)S(1)}, bf16[16,4608]{1,0:T(8,128)(2,1)S(1)}, u32[]{:S(2)}, u32[]{:S(2)}) %collective-permute-start.19) | collective-permute-done | bytes 147488 | tf_op jit(solution)/shard_map/ppermute | solution.py:351
  370.4 1.9 collective-permute-start.21
  372.3 1.7 collective-permute-done.21
  374.6 2.3 collective-permute-start.22
  378.8 1.4 collective-permute-start.23
  380.1 2.2 collective-permute-done.23
  383.0 2.6 collective-permute-start.24
  385.6 1.9 collective-permute-done.24
  (119 shorter events, 28.2 us)
Async XLA Ops:
  2.0 11.1 %collective-permute-start.5 = (bf16[16,4608]{1,0:T(8,128)(2,1)S(1)}, bf16[16,4608]{1,0:T(8,128)(2,1)S(1)}, u32[]{:S(2)}, u32[]{:S(2)}) collective-permute-start(bf16[16,4608]{1,0:T(8,128)(2,1)S(1)} %get-tuple-element.54), channel_id=1, source_target_pairs={{0,16},{1,17},{2,18},{3,19},{4,20},{5,21},{6,22},{7,23},{8,24},{9,... | collective-permute-start | bytes 442376 | tf_op jit(solution)/shard_map/ppermute | solution.py:351
  13.1 8.3 %collective-permute-start.6 = (bf16[32,4608]{1,0:T(8,128)(2,1)S(1)}, bf16[32,4608]{1,0:T(8,128)(2,1)S(1)}, u32[]{:S(2)}, u32[]{:S(2)}) collective-permute-start(bf16[32,4608]{1,0:T(8,128)(2,1)S(1)} %pad_maximum_fusion.3), channel_id=1, source_target_pairs={{0,8},{1,9},{2,10},{3,11},{4,12},{5,13},{6,14},{7,15},{8,0},{9,1},... | collective-permute-start | bytes 884744 | tf_op jit(solution)/shard_map/ppermute | solution.py:351
  21.4 13.7 %collective-permute-start.7 = (bf16[64,4608]{1,0:T(8,128)(2,1)S(1)}, bf16[64,4608]{1,0:T(8,128)(2,1)S(1)}, u32[]{:S(2)}, u32[]{:S(2)}) collective-permute-start(bf16[64,4608]{1,0:T(8,128)(2,1)S(1)} %pad_maximum_fusion.1), channel_id=1, source_target_pairs={{0,4},{1,5},{2,6},{3,7},{4,0},{5,1},{6,2},{7,3},{8,12},{9,13},{10,... | collective-permute-start | bytes 1769480 | tf_op jit(solution)/shard_map/ppermute | solution.py:351
  22.8 37.9 %collective-permute-start = (bf16[16,1664]{1,0:T(8,128)(2,1)S(1)}, bf16[16,1664]{1,0:T(8,128)(2,1)S(1)}, u32[]{:S(2)}, u32[]{:S(2)}) collective-permute-start(bf16[16,1664]{1,0:T(8,128)(2,1)S(1)} %get-tuple-element.56), channel_id=1, source_target_pairs={{0,16},{1,17},{2,18},{3,19},{4,20},{5,21},{6,22},{7,23},{8,24},{9,... | collective-permute-start | bytes 159752 | tf_op jit(solution)/shard_map/ppermute | solution.py:351
  35.1 25.4 %collective-permute-start.8 = (bf16[128,4608]{1,0:T(8,128)(2,1)S(1)}, bf16[128,4608]{1,0:T(8,128)(2,1)S(1)}, u32[]{:S(2)}, u32[]{:S(2)}) collective-permute-start(bf16[128,4608]{1,0:T(8,128)(2,1)S(1)} %pad_maximum_fusion), channel_id=1, source_target_pairs={{0,2},{1,3},{2,0},{3,1},{4,6},{5,7},{6,4},{7,5},{8,10},{9,11},{10,... | collective-permute-start | bytes 3538952 | tf_op jit(solution)/shard_map/ppermute | solution.py:351
  36.6 49.8 %copy-start.10 = (s32[2]{0:T(128)S(1)}, s32[2]{0:T(128)}, u32[]{:S(2)}) copy-start(s32[2]{0:T(128)} %param.11) | copy-start | bytes 28
  60.6 39.9 %copy-start = (bf16[256,4608]{1,0:T(8,128)(2,1)}, bf16[256,4608]{1,0:T(8,128)(2,1)S(1)}, u32[]{:S(2)}) copy-start(bf16[256,4608]{1,0:T(8,128)(2,1)S(1)} %constant_dynamic-update-slice_fusion.5.near_ref) | copy-start | bytes 7077892
  60.6 73.4 %collective-permute-start.9 = (bf16[256,4608]{1,0:T(8,128)(2,1)S(1)}, bf16[256,4608]{1,0:T(8,128)(2,1)}, u32[]{:S(2)}, u32[]{:S(2)}) collective-permute-start(bf16[256,4608]{1,0:T(8,128)(2,1)S(1)} %constant_dynamic-update-slice_fusion.5.near_ref), channel_id=1, source_target_pairs={{0,1},{1,0},{2,3},{3,2},{4,5},{5,4},{6,7},{7,6},{8,9},{9,8},{10,11... | collective-permute-start | bytes 7077896 | tf_op jit(solution)/shard_map/ppermute | solution.py:351
  60.7 6.8 %collective-permute-start.1 = (bf16[32,1664]{1,0:T(8,128)(2,1)S(1)}, bf16[32,1664]{1,0:T(8,128)(2,1)S(1)}, u32[]{:S(2)}, u32[]{:S(2)}) collective-permute-start(bf16[32,1664]{1,0:T(8,128)(2,1)S(1)} %pad_maximum_fusion.5), channel_id=1, source_target_pairs={{0,8},{1,9},{2,10},{3,11},{4,12},{5,13},{6,14},{7,15},{8,0},{9,1},... | collective-permute-start | bytes 319496 | tf_op jit(solution)/shard_map/ppermute | solution.py:351
  67.5 7.1 %collective-permute-start.2 = (bf16[64,1664]{1,0:T(8,128)(2,1)S(1)}, bf16[64,1664]{1,0:T(8,128)(2,1)S(1)}, u32[]{:S(2)}, u32[]{:S(2)}) collective-permute-start(bf16[64,1664]{1,0:T(8,128)(2,1)S(1)} %pad_maximum_fusion.4), channel_id=1, source_target_pairs={{0,4},{1,5},{2,6},{3,7},{4,0},{5,1},{6,2},{7,3},{8,12},{9,13},{10,... | collective-permute-start | bytes 638984 | tf_op jit(solution)/shard_map/ppermute | solution.py:351
  74.7 10.8 %collective-permute-start.3 = (bf16[128,1664]{1,0:T(8,128)(2,1)S(1)}, bf16[128,1664]{1,0:T(8,128)(2,1)S(1)}, u32[]{:S(2)}, u32[]{:S(2)}) collective-permute-start(bf16[128,1664]{1,0:T(8,128)(2,1)S(1)} %pad_maximum_fusion.2), channel_id=1, source_target_pairs={{0,2},{1,3},{2,0},{3,1},{4,6},{5,7},{6,4},{7,5},{8,10},{9,11},{10,... | collective-permute-start | bytes 1277960 | tf_op jit(solution)/shard_map/ppermute | solution.py:351
  85.5 2.6 copy-start.4
  85.6 2.6 collective-permute-start.4
  205.8 83.5 %collective-permute-start.15 = (bf16[256,4608]{1,0:T(8,128)(2,1)}, bf16[256,4608]{1,0:T(8,128)(2,1)S(1)}, u32[]{:S(2)}, u32[]{:S(2)}) collective-permute-start(bf16[256,4608]{1,0:T(8,128)(2,1)} %get-tuple-element.44), channel_id=1, source_target_pairs={{0,1},{1,0},{2,3},{3,2},{4,5},{5,4},{6,7},{7,6},{8,9},{9,8},{10,11... | collective-permute-start | bytes 7077896 | tf_op jit(solution)/shard_map/ppermute | solution.py:351
  206.1 4.6 %collective-permute-start.30 = (f32[16,512]{1,0:T(8,128)}, f32[16,512]{1,0:T(8,128)S(1)}, u32[]{:S(2)}, u32[]{:S(2)}) collective-permute-start(f32[16,512]{1,0:T(8,128)} %get-tuple-element.46), channel_id=1, source_target_pairs={{0,1},{1,0},{2,3},{3,2},{4,5},{5,4},{6,7},{7,6},{8,9},{9,8},{10,11... | collective-permute-start | bytes 98312 | tf_op jit(solution)/shard_map/ppermute | solution.py:351
  211.5 44.1 %collective-permute-start.31 = (f32[16,512]{1,0:T(8,128)S(1)}, f32[16,512]{1,0:T(8,128)S(1)}, u32[]{:S(2)}, u32[]{:S(2)}) collective-permute-start(f32[16,512]{1,0:T(8,128)S(1)} %add.120), channel_id=1, source_target_pairs={{0,2},{1,3},{2,0},{3,1},{4,6},{5,7},{6,4},{7,5},{8,10},{9,11},{10,... | collective-permute-start | bytes 98312 | tf_op jit(solution)/shard_map/ppermute | solution.py:351
  255.5 1.6 collective-permute-start.25
  255.5 29.8 %collective-permute-start.32 = (f32[16,512]{1,0:T(8,128)S(1)}, f32[16,512]{1,0:T(8,128)S(1)}, u32[]{:S(2)}, u32[]{:S(2)}) collective-permute-start(f32[16,512]{1,0:T(8,128)S(1)} %add.121), channel_id=1, source_target_pairs={{0,4},{1,5},{2,6},{3,7},{4,0},{5,1},{6,2},{7,3},{8,12},{9,13},{10,... | collective-permute-start | bytes 98312 | tf_op jit(solution)/shard_map/ppermute | solution.py:351
  257.1 3.6 collective-permute-start.26
  260.8 3.6 collective-permute-start.27
  264.4 3.6 collective-permute-start.28
  268.0 18.4 %collective-permute-start.29 = (f32[4,384]{1,0:T(4,128)S(1)}, f32[4,384]{1,0:T(4,128)S(1)}, u32[]{:S(2)}, u32[]{:S(2)}) collective-permute-start(f32[4,384]{1,0:T(4,128)S(1)} %add.118), channel_id=1, source_target_pairs={{0,16},{1,17},{2,18},{3,19},{4,20},{5,21},{6,22},{7,23},{8,24},{9,... | collective-permute-start | bytes 18440 | tf_op jit(solution)/shard_map/ppermute | solution.py:351
  271.6 23.7 %collective-permute-start.10 = (bf16[256,1536]{1,0:T(8,128)(2,1)}, bf16[256,1536]{1,0:T(8,128)(2,1)S(1)}, u32[]{:S(2)}, u32[]{:S(2)}) collective-permute-start(bf16[256,1536]{1,0:T(8,128)(2,1)} %get-tuple-element.42), channel_id=1, source_target_pairs={{0,1},{1,0},{2,3},{3,2},{4,5},{5,4},{6,7},{7,6},{8,9},{9,8},{10,11... | collective-permute-start | bytes 2359304 | tf_op jit(solution)/shard_map/ppermute | solution.py:351
  285.3 4.0 %collective-permute-start.33 = (f32[16,512]{1,0:T(8,128)S(1)}, f32[16,512]{1,0:T(8,128)S(1)}, u32[]{:S(2)}, u32[]{:S(2)}) collective-permute-start(f32[16,512]{1,0:T(8,128)S(1)} %add.122), channel_id=1, source_target_pairs={{0,8},{1,9},{2,10},{3,11},{4,12},{5,13},{6,14},{7,15},{8,0},{9,1},... | collective-permute-start | bytes 98312 | tf_op jit(solution)/shard_map/ppermute | solution.py:351
  289.3 10.5 %collective-permute-start.34 = (f32[16,512]{1,0:T(8,128)S(1)}, f32[16,512]{1,0:T(8,128)S(1)}, u32[]{:S(2)}, u32[]{:S(2)}) collective-permute-start(f32[16,512]{1,0:T(8,128)S(1)} %add.123), channel_id=1, source_target_pairs={{0,16},{1,17},{2,18},{3,19},{4,20},{5,21},{6,22},{7,23},{8,24},{9,... | collective-permute-start | bytes 98312 | tf_op jit(solution)/shard_map/ppermute | solution.py:351
  289.3 1.4 copy-start.1
  293.7 2.5 copy-start.5
  294.8 38.9 %collective-permute-start.16 = (bf16[128,4608]{1,0:T(8,128)(2,1)}, bf16[128,4608]{1,0:T(8,128)(2,1)}, u32[]{:S(2)}, u32[]{:S(2)}) collective-permute-start(bf16[128,4608]{1,0:T(8,128)(2,1)} %slice.112), channel_id=1, source_target_pairs={{0,2},{1,3},{2,0},{3,1},{4,6},{5,7},{6,4},{7,5},{8,10},{9,11},{10,... | collective-permute-start | bytes 3538952 | tf_op jit(solution)/shard_map/ppermute | solution.py:351
  295.3 0.9 copy-start.6
  298.3 32.4 %collective-permute-start.11 = (bf16[128,1536]{1,0:T(8,128)(2,1)}, bf16[128,1536]{1,0:T(8,128)(2,1)}, u32[]{:S(2)}, u32[]{:S(2)}) collective-permute-start(bf16[128,1536]{1,0:T(8,128)(2,1)} %slice.104), channel_id=1, source_target_pairs={{0,2},{1,3},{2,0},{3,1},{4,6},{5,7},{6,4},{7,5},{8,10},{9,11},{10,... | collective-permute-start | bytes 1179656 | tf_op jit(solution)/shard_map/ppermute | solution.py:351
  331.9 1.9 copy-start.3
  332.6 8.1 %collective-permute-start.12 = (bf16[64,1536]{1,0:T(8,128)(2,1)}, bf16[64,1536]{1,0:T(8,128)(2,1)}, u32[]{:S(2)}, u32[]{:S(2)}) collective-permute-start(bf16[64,1536]{1,0:T(8,128)(2,1)} %slice.106), channel_id=1, source_target_pairs={{0,4},{1,5},{2,6},{3,7},{4,0},{5,1},{6,2},{7,3},{8,12},{9,13},{10,... | collective-permute-start | bytes 589832 | tf_op jit(solution)/shard_map/ppermute | solution.py:351
  335.3 15.6 %collective-permute-start.17 = (bf16[64,4608]{1,0:T(8,128)(2,1)S(1)}, bf16[64,4608]{1,0:T(8,128)(2,1)S(1)}, u32[]{:S(2)}, u32[]{:S(2)}) collective-permute-start(bf16[64,4608]{1,0:T(8,128)(2,1)S(1)} %slice.114), channel_id=1, source_target_pairs={{0,4},{1,5},{2,6},{3,7},{4,0},{5,1},{6,2},{7,3},{8,12},{9,13},{10,... | collective-permute-start | bytes 1769480 | tf_op jit(solution)/shard_map/ppermute | solution.py:351
  337.0 14.1 %copy-start.9 = (f32[512,12]{0,1:T(8,128)}, f32[512,12]{0,1:T(8,128)S(1)}, u32[]{:S(2)}) copy-start(f32[512,12]{0,1:T(8,128)S(1)} %get-tuple-element.51) | copy-start | bytes 73732
  341.8 10.4 %collective-permute-start.13 = (bf16[32,1536]{1,0:T(8,128)(2,1)S(1)}, bf16[32,1536]{1,0:T(8,128)(2,1)S(1)}, u32[]{:S(2)}, u32[]{:S(2)}) collective-permute-start(bf16[32,1536]{1,0:T(8,128)(2,1)S(1)} %slice.108), channel_id=1, source_target_pairs={{0,8},{1,9},{2,10},{3,11},{4,12},{5,13},{6,14},{7,15},{8,0},{9,1},... | collective-permute-start | bytes 294920 | tf_op jit(solution)/shard_map/ppermute | solution.py:351
  351.0 38.0 %copy-start.2 = (f32[98496]{0:T(1024)S(1)}, f32[98496]{0:T(1024)}, u32[]{:S(2)}) copy-start(f32[98496]{0:T(1024)} %param.13) | copy-start | bytes 1181956
  351.1 38.0 %copy-start.7 = (f32[98496]{0:T(1024)S(1)}, f32[98496]{0:T(1024)}, u32[]{:S(2)}) copy-start(f32[98496]{0:T(1024)} %param.15) | copy-start | bytes 1181956
  351.1 38.0 %copy-start.8 = (f32[98496]{0:T(1024)S(1)}, f32[98496]{0:T(1024)}, u32[]{:S(2)}) copy-start(f32[98496]{0:T(1024)} %param.14) | copy-start | bytes 1181956
  351.1 7.7 %collective-permute-start.18 = (bf16[32,4608]{1,0:T(8,128)(2,1)S(1)}, bf16[32,4608]{1,0:T(8,128)(2,1)S(1)}, u32[]{:S(2)}, u32[]{:S(2)}) collective-permute-start(bf16[32,4608]{1,0:T(8,128)(2,1)S(1)} %slice.116), channel_id=1, source_target_pairs={{0,8},{1,9},{2,10},{3,11},{4,12},{5,13},{6,14},{7,15},{8,0},{9,1},... | collective-permute-start | bytes 884744 | tf_op jit(solution)/shard_map/ppermute | solution.py:351
  352.3 9.0 %collective-permute-start.14 = (bf16[16,1536]{1,0:T(8,128)(2,1)S(1)}, bf16[16,1536]{1,0:T(8,128)(2,1)S(1)}, u32[]{:S(2)}, u32[]{:S(2)}) collective-permute-start(bf16[16,1536]{1,0:T(8,128)(2,1)S(1)} %slice.110), channel_id=1, source_target_pairs={{0,16},{1,17},{2,18},{3,19},{4,20},{5,21},{6,22},{7,23},{8,24},{9,... | collective-permute-start | bytes 147464 | tf_op jit(solution)/shard_map/ppermute | solution.py:351
  358.9 7.7 %collective-permute-start.19 = (bf16[16,4608]{1,0:T(8,128)(2,1)S(1)}, bf16[16,4608]{1,0:T(8,128)(2,1)S(1)}, u32[]{:S(2)}, u32[]{:S(2)}) collective-permute-start(bf16[16,4608]{1,0:T(8,128)(2,1)S(1)} %slice.118), channel_id=1, source_target_pairs={{0,16},{1,17},{2,18},{3,19},{4,20},{5,21},{6,22},{7,23},{8,24},{9,... | collective-permute-start | bytes 442376 | tf_op jit(solution)/shard_map/ppermute | solution.py:351
  368.6 1.2 collective-permute-start.20
  370.4 3.6 collective-permute-start.21
  374.6 3.6 collective-permute-start.22
  378.8 3.6 collective-permute-start.23
  383.0 4.5 %collective-permute-start.24 = (f32[1,1]{1,0:T(1,128)}, f32[1,1]{1,0:T(1,128)}, u32[]{:S(2)}, u32[]{:S(2)}) collective-permute-start(f32[1,1]{1,0:T(1,128)} %add.113), channel_id=1, source_target_pairs={{0,16},{1,17},{2,18},{3,19},{4,20},{5,21},{6,22},{7,23},{8,24},{9,... | collective-permute-start | bytes 20 | tf_op jit(solution)/shard_map/ppermute | solution.py:351

commit v3 on v2

v3 whole, which is shorter than its diff:
```python
import functools

import jax
import jax.numpy as jnp
from jax import lax
from jax.experimental import pallas as pl
from jax.experimental.pallas import tpu as pltpu
from jax.sharding import PartitionSpec as P

HD = 64
ROW = 1024
EPSILON = 1e-05
CLIP_NORM = 1.0
LEARN_RATE = 20.0
MOMENTUM = 0.5
AVERAGE_DECAY = 0.5
MASKED = -1e30
GELU_IN = 0.7978845608028654
GELU_CUBE = 0.044715

D = 512
FF = 2048
PAIR = 2 * HD
PAIRS = D // PAIR
LANES = 128
WINDOW = 3 * LANES
BLOCK = 16
BLOCKS = D // BLOCK
VECTORS = 12
TILE = 256
FIRST_WIDTH = 3 * D + LANES
REST_WIDTH = D + 2 * FF
VMEM_BYTES = 60 * 1024 * 1024

f32 = jnp.float32
bf16 = jnp.bfloat16


def nn(left, right):
    return lax.dot_general(left, right, (((1,), (0,)), ((), ())), preferred_element_type=f32)


def nt(left, right):
    return lax.dot_general(left, right, (((1,), (1,)), ((), ())), preferred_element_type=f32)


def identity(size):
    down = lax.broadcasted_iota(jnp.int32, (size, size), 0)
    across = lax.broadcasted_iota(jnp.int32, (size, size), 1)
    return jnp.where(down == across, 1.0, 0.0).astype(bf16)


def turned(values, unit):
    return nt(unit, values).astype(bf16)


def place_blocks(target, halves, codes, mine, width):
    for half_at, half in enumerate(halves):
        for block_at in range(BLOCKS // 2):
            natural = mine ^ codes[half_at * (BLOCKS // 2) + block_at]
            to_rows = pl.ds(pl.multiple_of(natural * BLOCK, BLOCK), BLOCK)
            target[to_rows, :width] = half[block_at * BLOCK : (block_at + 1) * BLOCK, :width]


def spread_blocks(halves, source, codes, mine, begin, width):
    for half_at, half in enumerate(halves):
        for block_at in range(BLOCKS // 2):
            natural = mine ^ codes[half_at * (BLOCKS // 2) + block_at]
            from_rows = pl.ds(pl.multiple_of(natural * BLOCK, BLOCK), BLOCK)
            rows = slice(block_at * BLOCK, (block_at + 1) * BLOCK)
            half[rows, pl.ds(begin, width)] = source[from_rows, :].astype(bf16)


def project_kernel(
    codes, mine_ref, x_ref, near_ref, far_ref,
    xt_ref, qt_ref, kt_ref, vt_ref, k_ref, v_ref, vec_ref, pairs_ref,
    table, turned_weights, columns, rows,
):
    @pl.when(pl.program_id(0) == 0)
    def _():
        place_blocks(table, (near_ref, far_ref), codes, mine_ref[0], FIRST_WIDTH)
        unit = identity(256)
        for kind in range(3):
            for half in range(2):
                turned_weights[kind * D + half * 256 : kind * D + half * 256 + 256, :] = turned(
                    table[:, kind * D + half * 256 : kind * D + half * 256 + 256], unit
                )
        for pair in range(PAIRS):
            for kind in range(3):
                at = pair * 3 * PAIR + kind * PAIR
                pairs_ref[:, at : at + PAIR] = table[
                    :, kind * D + pair * PAIR : kind * D + (pair + 1) * PAIR
                ]
        vectors = table[:, 3 * D :].astype(f32)
        vec_ref[...] = vectors
        columns[0] = jnp.broadcast_to(vectors[:, 0:1], (D, LANES))
        columns[1] = jnp.broadcast_to(vectors[:, 1:2], (D, LANES))
        rows[...] = vectors.T[:8, :]

    x = x_ref[...]
    width = x.shape[0]
    reps = width // LANES
    unit = identity(256)
    for half in range(2):
        xt_ref[half * 256 : half * 256 + 256, :] = turned(x[:, half * 256 : half * 256 + 256], unit)
    bias_q = jnp.concatenate([columns[0]] * reps, axis=1)
    bias_v = jnp.concatenate([columns[1]] * reps, axis=1)
    query = nt(turned_weights[:D, :], x) + bias_q
    qt_ref[...] = (query.astype(bf16).astype(f32) * HD ** (-0.5)).astype(bf16)
    kt_ref[...] = nt(turned_weights[D : 2 * D, :], x).astype(bf16)
    vt_ref[...] = (nt(turned_weights[2 * D :, :], x) + bias_v).astype(bf16)
    k_ref[...] = nn(x, table[:, D : 2 * D]).astype(bf16)
    v_ref[...] = (nn(x, table[:, 2 * D : 3 * D]) + rows[1:2, :]).astype(bf16)


def fill_bias(bias, seg_ref, limits_ref):
    blocks = bias.shape[0]
    lane = lax.broadcasted_iota(jnp.int32, (1, LANES), 1)
    across = lax.broadcasted_iota(jnp.int32, (LANES, LANES), 1)
    down = lax.broadcasted_iota(jnp.int32, (LANES, LANES), 0)

    def codes_of(block):
        row = jnp.where(limits_ref[2] == 1, 0, block // (ROW // LANES))
        limit = jnp.where(row == 0, limits_ref[0], limits_ref[1])
        code = seg_ref[pl.ds(block, 1), :] * 2 + row
        live = lane + block * LANES - row * ROW < limit
        return code.astype(f32), jnp.where(live, code, -1).astype(f32)

    def one_block(block, carry):
        query_code, _ = codes_of(block)
        first = jnp.clip(block - 1, 0, blocks - 3)
        for part in range(3):
            _, key_code = codes_of(first + part)
            key_column = jnp.broadcast_to(key_code, (LANES, LANES)).T
            same = (first + part - block) * LANES
            allowed = (key_column == query_code) | (down + same == across)
            bias[block, part * LANES : (part + 1) * LANES, :] = jnp.where(allowed, 0.0, MASKED)
        return carry

    lax.fori_loop(0, blocks, one_block, 0)


def two_heads(values):
    zeros = jnp.zeros((HD, values.shape[1]), values.dtype)
    left = jnp.concatenate([values[:HD], zeros], axis=0)
    right = jnp.concatenate([zeros, values[HD:]], axis=0)
    return jnp.concatenate([left, right], axis=1)


def own_heads(values):
    return jnp.concatenate([values[:HD, :LANES], values[HD:, LANES:]], axis=0)


def down_tree(values, combine):
    rows = values.shape[0]
    if rows == WINDOW:
        values = combine(
            combine(values[:LANES], values[LANES : 2 * LANES]), values[2 * LANES : 3 * LANES]
        )
        rows = LANES
    while rows > 8:
        rows //= 2
        values = combine(values[:rows], values[rows : 2 * rows])
    return values


def top_down(values):
    return jnp.max(down_tree(values, jnp.maximum), axis=0, keepdims=True)


def sum_down(values):
    return jnp.sum(down_tree(values, jnp.add), axis=0, keepdims=True)


def places(block, blocks):
    begin = min(max(block - 1, 0), blocks - 3) * LANES
    return slice(block * LANES, (block + 1) * LANES), slice(begin, begin + WINDOW)


def pipelined(amount, *stages):
    depth = len(stages)
    held = {}
    for step in range(amount + depth - 1):
        for at, stage in enumerate(stages):
            item = step - at
            if 0 <= item < amount:
                held[item] = stage(item, held.get(item))
                if at == depth - 1:
                    del held[item]


def attend_kernel(limits_ref, seg_ref, qt_ref, k_ref, vt_ref, att_ref, logsum_ref, bias):
    @pl.when(pl.program_id(0) == 0)
    def _():
        fill_bias(bias, seg_ref, limits_ref)

    blocks = bias.shape[0]

    def score(block, _):
        here, window = places(block, blocks)
        mask = bias[block]
        scores = nn(k_ref[window, :], two_heads(qt_ref[:, here]))
        return scores + jnp.concatenate([mask, mask], axis=1)

    def finish(block, scores):
        here, window = places(block, blocks)
        highest = top_down(scores)
        exponent = jnp.exp(scores - highest)
        total = sum_down(exponent)
        outputs = nn(vt_ref[:, window], exponent.astype(bf16)) * (1.0 / total)
        att_ref[:, here] = own_heads(outputs).astype(bf16)
        logsum_ref[0, block : block + 1, :] = highest + jnp.log(total)

    pipelined(blocks, score, finish)


def mean_down(values):
    return sum_down(values) * (1.0 / D)


def lane_parts(values):
    return values[:, :LANES] + values[:, LANES:]


def weight_parts(kept, acc_down, acc_up, acc_out):
    hidden, grad_up, first_low, grad_feed, grad_branch, att = kept

    def part(target, left, right, at):
        def run():
            target[:, at : at + TILE] += nt(left[...], right[at : at + TILE, :])

        return run

    parts = [part(acc_down, grad_feed, hidden, at) for at in range(0, FF, TILE)]
    parts += [part(acc_up, first_low, grad_up, at) for at in range(0, FF, TILE)]
    parts += [part(acc_out, grad_branch, att, at) for at in range(0, D, TILE)]
    return parts


def feed_kernel(
    codes, mine_ref, limits_ref, xt_ref, att_ref, cot_ref, vec_ref, near_ref, far_ref,
    layer_ref, ga_ref, both_ref, keep_ref, send_ref, sums_ref,
    table, out_turned, up_turned, down_turned, columns, up_bias, slopes,
    acc_down, acc_up, acc_out, acc_vec, *kept,
):
    step = pl.program_id(0)
    unit = identity(TILE)
    chunk = 512
    chunks = FF // chunk
    each = len(kept) // 2

    @pl.when(step == 0)
    def _():
        place_blocks(table, (near_ref, far_ref), codes, mine_ref[0], REST_WIDTH)
        for at in range(0, D, TILE):
            out_turned[at : at + TILE, :] = turned(table[:, at : at + TILE], unit)
        for at in range(0, FF, TILE):
            up_turned[at : at + TILE, :] = turned(table[:, D + at : D + at + TILE], unit)
            down_turned[at : at + TILE, :] = turned(
                table[:, D + FF + at : D + FF + at + TILE], unit
            )
        for kind in range(6):
            columns[kind] = jnp.broadcast_to(vec_ref[:, kind + 2 : kind + 3], (D, LANES))
        for at in range(4):
            up_bias[pl.ds(at, D, stride=4), :] = jnp.broadcast_to(
                vec_ref[:, 8 + at : 9 + at], (D, LANES)
            )
        for buffer in (acc_down, acc_up, acc_out, acc_vec) + kept[each:]:
            buffer[...] = jnp.zeros_like(buffer)
        for buffer in (kept[2], kept[each + 2]):
            buffer[D:, :] = jnp.ones((BLOCK, TILE), bf16)

    def column(kind):
        return jnp.concatenate([columns[kind]] * 2, axis=1)

    def one_tile(tile, now, before):
        hidden, grad_up, first_keep, feed_keep, branch_keep, att_keep = now
        fill = weight_parts(before, acc_down, acc_up, acc_out)
        here = slice(tile * TILE, (tile + 1) * TILE)
        place = lax.broadcasted_iota(jnp.int32, (1, TILE), 1) + (step * 2 + tile) * TILE
        row = jnp.where(limits_ref[2] == 1, 0, place // ROW)
        limit = jnp.where(row == 0, limits_ref[0], limits_ref[1])
        live = place - row * ROW < limit

        x = xt_ref[:, here].astype(f32)
        att = att_ref[:, here]
        att_keep[...] = att
        z_one = x + nn(table[:, :D], att) + column(0)
        for part in fill[:5]:
            part()
        centred = z_one - mean_down(z_one)
        inverse_one = lax.rsqrt(mean_down(centred * centred) + EPSILON)
        normed_one = centred * inverse_one
        first = normed_one * column(2) + column(3)
        first_low = first.astype(bf16)
        first_keep[:D, :] = first_low
        partial = [first + x + column(1)]

        def widen(at, _):
            rows = slice(at * chunk, (at + 1) * chunk)
            bias = jnp.concatenate([up_bias[rows, :]] * 2, axis=1)
            return nn(up_turned[rows, :], first_low) + bias

        def bend(at, pre):
            rows = slice(at * chunk, (at + 1) * chunk)
            square = pre * pre
            tanh = jnp.tanh(pre * (GELU_IN + (GELU_IN * GELU_CUBE) * square))
            half = 0.5 + 0.5 * tanh
            value = pre * half
            slopes[rows, :] = half + value * (1.0 - tanh) * (
                GELU_IN + (3.0 * GELU_IN * GELU_CUBE) * square
            )
            low = value.astype(bf16)
            hidden[rows, :] = low
            return low

        def narrow(at, low):
            columns_at = slice(D + FF + at * chunk, D + FF + (at + 1) * chunk)
            partial[0] = partial[0] + nn(table[:, columns_at], low)

        pipelined(chunks, widen, bend, narrow)
        z_two = partial[0]
        cot = jnp.concatenate(
            [nt(unit, cot_ref[here, at : at + TILE]) for at in range(0, D, TILE)], axis=0
        )
        for part in fill[5:13]:
            part()
        centred = z_two - mean_down(z_two)
        inverse_two = lax.rsqrt(mean_down(centred * centred) + EPSILON)
        normed_two = centred * inverse_two
        gain_two = column(4)
        layer = jnp.where(live, normed_two * gain_two + column(5), 0.0).astype(bf16)
        cot = jnp.where(live, cot, 0.0)
        scaled = cot * gain_two
        grad_two = inverse_two * (
            scaled - mean_down(scaled) - normed_two * mean_down(scaled * normed_two)
        )
        grad_feed = grad_two.astype(bf16)
        feed_keep[...] = grad_feed
        acc_vec[1] += lane_parts(grad_feed.astype(f32))
        acc_vec[4] += lane_parts(cot * normed_two)
        acc_vec[5] += lane_parts(cot)
        partial[0] = grad_two

        def widen_back(at, _):
            return nn(down_turned[at * chunk : (at + 1) * chunk, :], grad_feed)

        def bend_back(at, grad_hidden):
            rows = slice(at * chunk, (at + 1) * chunk)
            low = (grad_hidden * slopes[rows, :]).astype(bf16)
            grad_up[rows, :] = low
            return low

        def narrow_back(at, low):
            partial[0] = partial[0] + nn(table[:, D + at * chunk : D + (at + 1) * chunk], low)

        pipelined(chunks, widen_back, bend_back, narrow_back)
        grad_first = partial[0]
        layer_ref[here, :] = nt(unit, layer).astype(bf16)
        for part in fill[13:]:
            part()
        acc_vec[2] += lane_parts(grad_first * normed_one)
        acc_vec[3] += lane_parts(grad_first)
        scaled = grad_first * column(2)
        grad_one = inverse_one * (
            scaled - mean_down(scaled) - normed_one * mean_down(scaled * normed_one)
        )
        both_ref[:, here] = grad_two + grad_one
        grad_branch = grad_one.astype(bf16)
        branch_keep[...] = grad_branch
        acc_vec[0] += lane_parts(grad_branch.astype(f32))
        ga_ref[:, here] = nn(out_turned[...], grad_branch).astype(bf16)

    one_tile(0, kept[:each], kept[each:])
    one_tile(1, kept[each:], kept[:each])

    @pl.when(step == pl.num_programs(0) - 1)
    def _():
        for part in weight_parts(kept[each:], acc_down, acc_up, acc_out):
            part()
        halves = (keep_ref, send_ref)
        spread_blocks(halves, acc_out, codes, mine_ref[0], 0, D)
        spread_blocks(halves, acc_up, codes, mine_ref[0], D, FF)
        spread_blocks(halves, acc_down, codes, mine_ref[0], D + FF, FF)
        up_sums = jnp.broadcast_to(acc_up[D : D + 1, :], (LANES, FF))
        for at in range(0, FF, LANES):
            up_bias[at : at + LANES, :] = up_sums[:, at : at + LANES].T
        lane = lax.broadcasted_iota(jnp.int32, (D, LANES), 1)
        vectors = jnp.zeros((D, LANES), f32)
        for kind in range(6):
            total = jnp.sum(acc_vec[kind], axis=1, keepdims=True)
            vectors = jnp.where(lane == kind + 2, total, vectors)
        for at in range(4):
            vectors = jnp.where(lane == 8 + at, up_bias[pl.ds(at, D, stride=4), :], vectors)
        sums_ref[...] = vectors


def attend_back_kernel(
    codes, mine_ref, limits_ref, seg_ref, xt_ref, qt_ref, kt_ref, k_ref, v_ref, att_ref, ga_ref,
    logsum_ref, sums_ref, grads_ref, keep_ref, send_ref, bias, acc_key, acc_value, weight_grad,
    vectors,
):
    pair = pl.program_id(0)

    @pl.when(pair == 0)
    def _():
        fill_bias(bias, seg_ref, limits_ref)

    blocks = bias.shape[0]
    acc_key[...] = jnp.zeros_like(acc_key)
    acc_value[...] = jnp.zeros_like(acc_value)

    def score(block, _):
        here, window = places(block, blocks)
        mask = bias[block]
        query = two_heads(qt_ref[:, here])
        grad = two_heads(ga_ref[:, here])
        scores = nn(k_ref[window, :], query) + jnp.concatenate([mask, mask], axis=1)
        return query, grad, scores, nn(v_ref[window, :], grad)

    def finish(block, held):
        query, grad, scores, grad_chances = held
        here, window = places(block, blocks)
        product = ga_ref[:, here].astype(f32) * att_ref[:, here].astype(f32)
        centre = jnp.concatenate([sum_down(product[:HD]), sum_down(product[HD:])], axis=1)
        chances = jnp.exp(scores - logsum_ref[0, block : block + 1, :])
        grad_scores = (chances * (grad_chances - centre)).astype(bf16)
        acc_value[:, window] += nt(grad, chances.astype(bf16))
        grad_query = own_heads(nn(kt_ref[:, window], grad_scores)) * HD ** (-0.5)
        grads_ref[0, :PAIR, here] = grad_query.astype(bf16)
        acc_key[:, window] += nt(query, grad_scores)

    pipelined(blocks, score, finish)
    grads_ref[0, PAIR : 2 * PAIR, :] = acc_key[...].astype(bf16)
    grads_ref[0, 2 * PAIR :, :] = acc_value[...].astype(bf16)
    grads = grads_ref[0]
    weight_grad[...] = nt(xt_ref[...], grads)
    halves = (keep_ref, send_ref)
    begin = pl.multiple_of(pair * (3 * PAIR), 3 * PAIR)
    spread_blocks(halves, weight_grad, codes, mine_ref[0], begin, 3 * PAIR)
    rows = pl.ds(pl.multiple_of(pair * PAIR, PAIR), PAIR)
    lane = lax.broadcasted_iota(jnp.int32, (PAIR, LANES), 1)
    query_sum = jnp.sum(grads[:PAIR].astype(f32), axis=1, keepdims=True)
    value_sum = jnp.sum(grads[2 * PAIR :].astype(f32), axis=1, keepdims=True)
    total = jnp.where(lane == 0, query_sum, jnp.where(lane == 1, value_sum, sums_ref[rows, :]))
    high = total.astype(bf16).astype(f32)
    vectors[rows, :LANES] = high
    vectors[rows, LANES:] = total - high

    @pl.when(pair == PAIRS - 1)
    def _():
        spread_blocks(halves, vectors, codes, mine_ref[0], 3 * D, 2 * LANES)


def input_kernel(grads_ref, weights_ref, both_ref, out_ref):
    unit = identity(TILE)
    width = both_ref.shape[1]

    def multiply(at, _):
        here = slice(at * TILE, (at + 1) * TILE)
        grads = jnp.concatenate([grads_ref[pair, :, here] for pair in range(PAIRS)], axis=0)
        return both_ref[:, here] + nn(weights_ref[...], grads)

    def turn(at, total):
        high = total.astype(bf16)
        rest = (total - high.astype(f32)).astype(bf16)
        out_ref[at * TILE : (at + 1) * TILE, :] = nt(unit, high) + nt(unit, rest)

    pipelined(width // TILE, multiply, turn)


def own_kernel(*refs):
    own_ref, share_ref = refs[-2:]
    rest_ref = refs[-3]
    total = sum(part[...].astype(f32) for part in refs[:-3])
    squares = jnp.sum(rest_ref[...] * rest_ref[...], axis=1, keepdims=True)
    for pair in range(PAIRS):
        for kind in range(3):
            at = pair * 3 * PAIR + kind * PAIR
            piece = total[:, at : at + PAIR]
            own_ref[:, kind * D + pair * PAIR : kind * D + (pair + 1) * PAIR] = piece
            squares = squares + jnp.sum(piece * piece, axis=1, keepdims=True)
    vectors = total[:, -2 * LANES : -LANES] + total[:, -LANES:]
    lane = lax.broadcasted_iota(jnp.int32, vectors.shape, 1)
    vectors = jnp.where(lane < VECTORS, vectors, 0.0)
    squares = squares + jnp.sum(vectors * vectors, axis=1, keepdims=True)
    share_ref[...] = jnp.where(lane == VECTORS, squares, vectors)


def settle_kernel(codes, mine_ref, near_ref, far_ref, vectors_ref, norm_ref, table):
    place_blocks(table, (near_ref, far_ref), codes, mine_ref[0], LANES)
    vectors_ref[...] = table[...].T[:VECTORS, :]
    squares = jnp.sum(table[...], axis=0, keepdims=True)[:, VECTORS : VECTORS + 1]
    norm_ref[...] = jnp.broadcast_to(jnp.sqrt(squares), (8, LANES))


def exchange(values, bit, count):
    return lax.ppermute(values, "dp", [(at, at ^ bit) for at in range(count)])


def mask_phases(count):
    bits = [1 << at for at in range(1, count.bit_length() - 1)]
    phases = [bits[at : at + 2] for at in range(0, len(bits), 2)]
    return [[0, 1]] + [
        [sum(bit for at, bit in enumerate(phase) if choice >> at & 1) for choice in range(1 << len(phase))]
        for phase in phases
    ]


def block_codes(count):
    codes = [0]
    for masks in reversed(mask_phases(count)):
        codes = [mask ^ code for mask in masks for code in codes]
    return codes


def gather_phase(block, masks, count):
    return [block] + [exchange(block, mask, count) for mask in masks[1:]]


def scatter_phase(pieces, masks, count):
    return [pieces[0]] + [
        exchange(piece, mask, count) for piece, mask in zip(pieces[1:], masks[1:], strict=True)
    ]


def with_vectors(total):
    vectors = total[:, -2 * LANES : -LANES] + total[:, -LANES:]
    high = vectors.astype(bf16).astype(f32)
    before = [total[:, : -2 * LANES]] if total.shape[1] > 2 * LANES else []
    return jnp.concatenate(before + [high, vectors - high], axis=1)


def cut_kernel(*refs):
    width = refs[0].shape[1]
    rows = refs[-1].shape[0]
    amount = refs[0].shape[0] // rows
    pieces = refs[len(refs) - amount :]
    parts = refs[: len(refs) - amount]
    for at, piece in enumerate(pieces):
        for begin in range(0, width, 2 * LANES):
            here = slice(begin, begin + 2 * LANES)
            total = sum(part[at * rows : (at + 1) * rows, here].astype(f32) for part in parts)
            if begin + 2 * LANES == width:
                total = with_vectors(total)
            piece[:, here] = total.astype(piece.dtype)


def cut_sum(parts, amount, dtype, holds_vectors):
    rows, width = parts[0].shape
    few = rows // amount
    if few % BLOCK or not holds_vectors:
        total = sum(part.astype(f32) for part in parts)
        total = (with_vectors(total) if holds_vectors else total).astype(dtype)
        return [total[at * few : (at + 1) * few] for at in range(amount)]
    return pl.pallas_call(
        cut_kernel,
        out_shape=[shaped((few, width), dtype)] * amount,
        compiler_params=params_of(),
        name="cut",
    )(*parts)


def together(*values):
    return lax.optimization_barrier(values)


def whole(shape):
    return pl.BlockSpec(shape, lambda *at: (0,) * len(shape))


def smem():
    return pl.BlockSpec(memory_space=pltpu.SMEM)


def shaped(shape, dtype):
    return jax.ShapeDtypeStruct(shape, dtype)


def params_of(**more):
    return pltpu.CompilerParams(vmem_limit_bytes=VMEM_BYTES, **more)


def body(tokens, cotangent, segment_ids, row_lengths, row_widths, params, momenta, averages):
    slots = tokens.shape[0]
    count = lax.axis_size("dp")
    mine = lax.axis_index("dp").astype(jnp.int32)
    own_count = D // count
    table_width = params.shape[0] // own_count
    blocks = slots // LANES
    direct = own_count == BLOCK
    if direct:
        codes = block_codes(count)
        origin = mine.reshape(1)
    else:
        codes = list(range(BLOCKS))
        origin = jnp.zeros((1,), jnp.int32)
        spread = jnp.array(block_codes(count), jnp.int32)
        places_of = jnp.argsort(spread)

    def to_kernel(near, far):
        if direct:
            return near, far
        table = jnp.concatenate([near, far], axis=0).reshape(count, own_count, -1)
        table = jnp.take(table, places_of[jnp.arange(count) ^ mine], axis=0).reshape(D, -1)
        return table[: D // 2], table[D // 2 :]

    def from_kernel(keep, send):
        if direct:
            return keep, send
        table = jnp.concatenate([keep, send], axis=0).reshape(count, own_count, -1)
        table = jnp.take(table, spread ^ mine, axis=0).reshape(D, -1)
        return table[: D // 2], table[D // 2 :]

    own_table = params.astype(bf16).reshape(own_count, table_width)
    own_first = jnp.concatenate(
        [
            own_table[:, : 3 * D],
            jnp.pad(own_table[:, 12 * D :], ((0, 0), (0, LANES - VECTORS))),
        ],
        axis=1,
    )
    own_rest = own_table[:, 3 * D : 12 * D]
    phases = mask_phases(count)
    outer = phases[:0:-1]
    first, rest = own_first, own_rest
    for masks in outer:
        first = jnp.concatenate(gather_phase(first, masks, count), axis=0)
        first, rest = together(first, rest)
        rest_pieces = gather_phase(rest, masks, count)
        if masks is not outer[-1]:
            rest = jnp.concatenate(rest_pieces, axis=0)
    first_near, first_far = to_kernel(*gather_phase(first, phases[0], count))
    limits = jnp.concatenate([row_lengths, row_widths])
    segments = segment_ids.reshape(blocks, LANES)

    tile = 2 * TILE
    steps = slots // tile
    across = pl.BlockSpec((D, tile), lambda at: (0, at))
    down = pl.BlockSpec((tile, D), lambda at: (at, 0))
    half_first = whole((D // 2, FIRST_WIDTH))
    xt, qt, kt, vt, key, value, vectors, pair_weights = pl.pallas_call(
        functools.partial(project_kernel, codes),
        grid=(steps,),
        in_specs=[smem(), down, half_first, half_first],
        out_specs=[across] * 4 + [down] * 2 + [whole((D, LANES)), whole((D, 3 * D))],
        out_shape=[shaped((D, slots), bf16)] * 4
        + [shaped((slots, D), bf16)] * 2
        + [shaped((D, LANES), f32), shaped((D, 3 * D), bf16)],
        scratch_shapes=[
            pltpu.VMEM((D, FIRST_WIDTH), bf16),
            pltpu.VMEM((3 * D, D), bf16),
            pltpu.VMEM((2, D, LANES), f32),
            pltpu.VMEM((8, D), f32),
        ],
        compiler_params=params_of(),
        name="project",
    )(origin, tokens, first_near, first_far)

    pair_rows = pl.BlockSpec((PAIR, slots), lambda at: (at, 0))
    pair_columns = pl.BlockSpec((slots, PAIR), lambda at: (0, at))
    sums_block = pl.BlockSpec((1, blocks, 2 * LANES), lambda at: (at, 0, 0))
    attended, logsum = pl.pallas_call(
        attend_kernel,
        grid=(PAIRS,),
        in_specs=[smem(), whole((blocks, LANES)), pair_rows, pair_columns, pair_rows],
        out_specs=[pair_rows, sums_block],
        out_shape=[shaped((D, slots), bf16), shaped((PAIRS, blocks, 2 * LANES), f32)],
        scratch_shapes=[pltpu.VMEM((blocks, WINDOW, LANES), f32)],
        compiler_params=params_of(),
        name="attend",
    )(limits, segments, qt, key, vt)

    attended, *rest_pieces = together(attended, *rest_pieces)
    rest = jnp.concatenate(rest_pieces, axis=0)
    rest_near, rest_far = to_kernel(*gather_phase(rest, phases[0], count))
    half_rest = whole((D // 2, REST_WIDTH))
    layer_output, grad_attended, grad_both, keep_rest, send_rest, feed_sums = pl.pallas_call(
        functools.partial(feed_kernel, codes),
        grid=(steps,),
        in_specs=[
            smem(), smem(), across, across, down,
            whole((D, LANES)), half_rest, half_rest,
        ],
        out_specs=[down, across, across, half_rest, half_rest, whole((D, LANES))],
        out_shape=[
            shaped((slots, D), bf16),
            shaped((D, slots), bf16),
            shaped((D, slots), f32),
            shaped((D // 2, REST_WIDTH), bf16),
            shaped((D // 2, REST_WIDTH), bf16),
            shaped((D, LANES), f32),
        ],
        scratch_shapes=[
            pltpu.VMEM((D, REST_WIDTH), bf16),
            pltpu.VMEM((D, D), bf16),
            pltpu.VMEM((FF, D), bf16),
            pltpu.VMEM((FF, D), bf16),
            pltpu.VMEM((6, D, LANES), f32),
            pltpu.VMEM((FF, LANES), f32),
            pltpu.VMEM((FF, TILE), f32),
            pltpu.VMEM((D, FF), f32),
            pltpu.VMEM((D + BLOCK, FF), f32),
            pltpu.VMEM((D, D), f32),
            pltpu.VMEM((6, D, LANES), f32),
        ]
        + [pltpu.VMEM((rows, TILE), bf16) for rows in (FF, FF, D + BLOCK, D, D, D)] * 2,
        compiler_params=params_of(),
        name="feed",
    )(origin, limits, xt, attended, cotangent, vectors, rest_near, rest_far)

    def scatter(parts, at, holds_vectors):
        if at == len(phases) - 1:
            return cut_sum(parts, 1, f32, holds_vectors)
        return cut_sum(parts, len(phases[at + 1]), bf16, holds_vectors)

    parts = scatter_phase(from_kernel(keep_rest, send_rest), phases[0], count)
    grad_attended, *pieces = together(grad_attended, *scatter(parts, 0, False))
    rest_parts = scatter_phase(pieces, phases[1], count)

    half_all = whole((D // 2, 3 * D + 2 * LANES))
    grads, keep_first, send_first = pl.pallas_call(
        functools.partial(attend_back_kernel, codes),
        grid=(PAIRS,),
        in_specs=[
            smem(), smem(), whole((blocks, LANES)), whole((D, slots)),
            pair_rows, pair_rows, pair_columns, pair_columns, pair_rows, pair_rows, sums_block,
            whole((D, LANES)),
        ],
        out_specs=[
            pl.BlockSpec((1, 3 * PAIR, slots), lambda at: (at, 0, 0)),
            half_all,
            half_all,
        ],
        out_shape=[
            shaped((PAIRS, 3 * PAIR, slots), bf16),
            shaped((D // 2, 3 * D + 2 * LANES), bf16),
            shaped((D // 2, 3 * D + 2 * LANES), bf16),
        ],
        scratch_shapes=[
            pltpu.VMEM((blocks, WINDOW, LANES), f32),
            pltpu.VMEM((PAIR, slots), f32),
            pltpu.VMEM((PAIR, slots), f32),
            pltpu.VMEM((D, 3 * PAIR), f32),
            pltpu.VMEM((D, 2 * LANES), f32),
        ],
        compiler_params=params_of(),
        name="attend_back",
    )(origin, limits, segments, xt, qt, kt, key, value, attended, grad_attended, logsum, feed_sums)

    keep_first, send_first, *rest_parts = together(keep_first, send_first, *rest_parts)
    parts = scatter_phase(from_kernel(keep_first, send_first), phases[0], count)
    pieces = scatter(parts, 0, True)
    grads, *held = together(grads, *pieces, *rest_parts)
    pieces, rest_parts = held[: len(pieces)], held[len(pieces) :]
    parts = scatter_phase(pieces, phases[1], count)
    rest_pieces = scatter(rest_parts, 1, False)
    grads, *rest_pieces = together(grads, *rest_pieces)
    input_grad = pl.pallas_call(
        input_kernel,
        grid=(steps,),
        in_specs=[
            pl.BlockSpec((PAIRS, 3 * PAIR, tile), lambda at: (0, 0, at)),
            whole((D, 3 * D)),
            across,
        ],
        out_specs=down,
        out_shape=shaped((slots, D), f32),
        compiler_params=params_of(),
        name="input_grad",
    )(grads, pair_weights, grad_both)

    input_grad, *parts = together(input_grad, *parts)
    for at in range(2, len(phases)):
        pieces = scatter(parts, at - 1, True)
        parts = scatter_phase(pieces, phases[at], count)
        rest_parts = scatter_phase(rest_pieces, phases[at], count)
        rest_pieces = scatter(rest_parts, at, False)
    (own_rest,) = rest_pieces
    own_first, share = pl.pallas_call(
        own_kernel,
        out_shape=[shaped((own_count, 3 * D), f32), shaped((own_count, LANES), f32)],
        compiler_params=params_of(),
        name="own",
    )(*parts, own_rest)
    shares = share
    for masks in outer:
        shares = jnp.concatenate(gather_phase(shares, masks, count), axis=0)
    vector_grads, norms = pl.pallas_call(
        functools.partial(settle_kernel, codes),
        in_specs=[smem()] + [whole((D // 2, LANES))] * 2,
        out_specs=[whole((VECTORS, D)), whole((8, LANES))],
        out_shape=[shaped((VECTORS, D), f32), shaped((8, LANES), f32)],
        scratch_shapes=[pltpu.VMEM((D, LANES), f32)],
        compiler_params=params_of(),
        name="settle",
    )(origin, *to_kernel(*gather_phase(shares, phases[0], count)))
    grad_norm = norms[0, 0]
    vector_grads = vector_grads.T

    own_grad = jnp.concatenate([own_first, own_rest, share[:, :VECTORS]], axis=1).reshape(-1)
    clipped = own_grad * jnp.minimum(1.0, CLIP_NORM / (grad_norm + 1e-06))
    new_momenta = MOMENTUM * momenta + clipped
    new_params = params - LEARN_RATE * (clipped + MOMENTUM * new_momenta)
    new_averages = AVERAGE_DECAY * averages + (1.0 - AVERAGE_DECAY) * new_params
    return (
        layer_output, input_grad, grad_norm, vector_grads, new_params, new_momenta, new_averages,
    )


def solution(mesh):
    placed = (P("dp", None), P("dp", None), P("dp"), P("dp"), P("dp"), P("dp"), P("dp"), P("dp"))
    return jax.shard_map(
        body,
        mesh=mesh,
        in_specs=placed,
        out_specs=(P("dp", None), P("dp", None), P(), P(), P("dp"), P("dp"), P("dp")),
        check_vma=False,
    )
```

time: 392 us -> 230 us (0.59)
  waiting for transfers between devices: 140 us -> 32.6 us
  Pallas kernels: 171 us -> 132 us
  other arithmetic: 13.9 us -> 7.19 us
  between operations: 8.09 us -> 2.33 us
    ppermute x35, waiting for transfers between devices: 140 us -> 32.6 us  [exchange(): return lax.ppermute(values, 'dp', [(at, at ^ bit) for at in range(count)])]
    pallas_call x1, Pallas kernels: 32.2 us -> 17.2 us  [body(): pl.pallas_call(attend_kernel, grid=(PAIRS,), in_specs=[smem(), whole((blo...]
    pallas_call x1, Pallas kernels: 41.7 us -> 27.9 us  [body(): pl.pallas_call(functools.partial(attend_back_kernel, codes), grid=(PAIRS,...]
    pallas_call x1, Pallas kernels: 70.6 us -> 58 us  [body(): pl.pallas_call(functools.partial(feed_kernel, codes), grid=(steps,), in_s...]
    pallas_call x0 -> x4, Pallas kernels: none -> 8.08 us  [the longest x2 4.47 us: cut_sum(): pl.pallas_call(cut_kernel, out_shape=[shaped((few, width), dtype)] * amou...]
    convert_element_type x8 -> x2, other arithmetic: 8.18 us -> 2.51 us  [cut_sum(): total = (with_vectors(total) if holds_vectors else total).astype(dtype)]
    unnamed x29 -> x40, local copies, waits for them, and re-layouts: 2.49 us -> 7.2 us
    pallas_call x1, Pallas kernels: 13.7 us -> 9.62 us  [body(): pl.pallas_call(input_kernel, grid=(steps,), in_specs=[pl.BlockSpec((PAIRS...]
  transfers between devices with their start and end apart: 35 -> 35, of which waited for: 23 -> 17; matrix products, arithmetic and copies ran while one was open for 4% -> 1% of each run, Pallas kernels for 26% -> 30%
where the time goes in v3:
time: 230 us; the launch traced here: 229 us
  Pallas kernels  132 us (57%)
  starting transfers between devices  45.9 us (20%)
  waiting for transfers between devices  32.6 us (14%)
  local copies, waits for them, and re-layouts  9.16 us (4%)
  other arithmetic  7.19 us (3%)
  between operations  2.33 us (1%)
    pallas_call x1, Pallas kernels, body(): pl.pallas_call(functools.partial(feed_kernel, codes), grid=(steps,), in_s...  58 us
    ppermute x35, starting transfers between devices, exchange(): return lax.ppermute(values, 'dp', [(at, at ^ bit) for at in range(count)])  45.9 us
    ppermute x35, waiting for transfers between devices, exchange(): return lax.ppermute(values, 'dp', [(at, at ^ bit) for at in range(count)])  32.6 us
    pallas_call x1, Pallas kernels, body(): pl.pallas_call(functools.partial(attend_back_kernel, codes), grid=(PAIRS,...  27.9 us
    pallas_call x1, Pallas kernels, body(): pl.pallas_call(attend_kernel, grid=(PAIRS,), in_specs=[smem(), whole((blo...  17.2 us
    pallas_call x1, Pallas kernels, body(): pl.pallas_call(functools.partial(project_kernel, codes), grid=(steps,), i...  11.6 us
    pallas_call x1, Pallas kernels, body(): pl.pallas_call(input_kernel, grid=(steps,), in_specs=[pl.BlockSpec((PAIRS...  9.62 us
    unnamed x40, local copies, waits for them, and re-layouts  7.2 us
  transfers between devices with their start and end apart: 35, of which 17 were waited for; matrix products, arithmetic and copies ran while one was open for 1% of the time, Pallas kernels for 30%

profile of v3, /device:TPU:0, one launch (start us, length us, event | category | flops | bytes accessed | tf_op | source)
XLA Modules:
  0.0 229.5 jit_solution(2002604583089311199)
XLA Ops:
  0.6 1.0 convert_element_type.41
  2.0 5.1 %collective-permute-start.2 = (bf16[16,1664]{1,0:T(8,128)(2,1)S(1)}, bf16[16,1664]{1,0:T(8,128)(2,1)S(1)}, u32[]{:S(2)}, u32[]{:S(2)}) collective-permute-start(bf16[16,1664]{1,0:T(8,128)(2,1)S(1)} %pad_maximum_fusion.3), channel_id=1, source_target_pairs={{0,24},{1,25},{2,26},{3,27},{4,28},{5,29},{6,30},{7,31},{8,16},{9,... | collective-permute-start | bytes 159752 | tf_op jit(solution)/shard_map/ppermute | solution.py:498
  7.8 1.7 collective-permute-done.2
  9.4 2.7 %collective-permute-done.1 = bf16[16,1664]{1,0:T(8,128)(2,1)S(1)} collective-permute-done((bf16[16,1664]{1,0:T(8,128)(2,1)S(1)}, bf16[16,1664]{1,0:T(8,128)(2,1)S(1)}, u32[]{:S(2)}, u32[]{:S(2)}) %collective-permute-start.1) | collective-permute-done | bytes 53280 | tf_op jit(solution)/shard_map/ppermute | solution.py:498
  12.2 2.4 %collective-permute-start.8 = (bf16[16,4608]{1,0:T(8,128)(2,1)S(1)}, bf16[16,4608]{1,0:T(8,128)(2,1)S(1)}, u32[]{:S(2)}, u32[]{:S(2)}) collective-permute-start(bf16[16,4608]{1,0:T(8,128)(2,1)S(1)} %slice.54), channel_id=1, source_target_pairs={{0,24},{1,25},{2,26},{3,27},{4,28},{5,29},{6,30},{7,31},{8,16},{9,... | collective-permute-start | bytes 442376 | tf_op jit(solution)/shard_map/ppermute | solution.py:498
  14.6 2.0 collective-permute-start.6
  16.6 2.4 %collective-permute-start.5 = (bf16[64,1664]{1,0:T(8,128)(2,1)S(1)}, bf16[64,1664]{1,0:T(8,128)(2,1)S(1)}, u32[]{:S(2)}, u32[]{:S(2)}) collective-permute-start(bf16[64,1664]{1,0:T(8,128)(2,1)S(1)} %pad_maximum_fusion.2), channel_id=1, source_target_pairs={{0,6},{1,7},{2,4},{3,5},{4,2},{5,3},{6,0},{7,1},{8,14},{9,15},{10,... | collective-permute-start | bytes 638984 | tf_op jit(solution)/shard_map/ppermute | solution.py:498
  19.6 1.3 collective-permute-done.8
  20.9 1.5 collective-permute-start.3
  22.4 4.3 %collective-permute-done.7 = bf16[16,4608]{1,0:T(8,128)(2,1)S(1)} collective-permute-done((bf16[16,4608]{1,0:T(8,128)(2,1)S(1)}, bf16[16,4608]{1,0:T(8,128)(2,1)S(1)}, u32[]{:S(2)}, u32[]{:S(2)}) %collective-permute-start.7) | collective-permute-done | bytes 147488 | tf_op jit(solution)/shard_map/ppermute | solution.py:498
  27.7 1.8 collective-permute-start.12
  29.4 1.2 collective-permute-start.11
  32.5 0.9 copy-done.5
  33.4 11.6 %project.1 = (bf16[512,2048]{1,0:T(8,128)(2,1)}, bf16[512,2048]{1,0:T(8,128)(2,1)}, bf16[512,2048]{1,0:T(8,128)(2,1)}, bf16[512,2048]{1,0:T(8,128)(2,1)}, bf16[2...) custom-call(s32[1]{0:T(128)} %bitcast.mine_ref, ...), custom_call_target="tpu_custom_call" | custom-call | tf_op jit(solution)/shard_map/project/pallas_call | solution.py:642
  45.0 17.2 %attend.1 = (bf16[512,2048]{1,0:T(8,128)(2,1)}, f32[4,16,256]{2,1,0:T(8,128)}) custom-call(s32[3]{0:T(128)} %pad_add_fusion.limits_ref, s32[16,128]{1,0:T(8,128)} %bitcast.5, bf16[512,2048]{1,0:T(8,128)(2,1)} %get-tuple-element.81.qt_ref, bf16[2048,512]{1,0:T(8,128)(2,1)} %get-tuple-element.82.k_ref, bf16[512,2048]{1,0:T(8,128)(2,1)} %get-tuple-element.83.vt_ref), custom_call_target="tpu_custom_call" | custom-call | tf_op jit(solution)/shard_map/attend/pallas_call | solution.py:663
  62.2 1.1 constant_dynamic-update-slice_fusion.2
  63.5 4.5 %collective-permute-done.13.far_ref = bf16[256,4608]{1,0:T(8,128)(2,1)S(1)} collective-permute-done((bf16[256,4608]{1,0:T(8,128)(2,1)S(1)}, bf16[256,4608]{1,0:T(8,128)(2,1)S(1)}, u32[]{:S(2)}, u32[]{:S(2)}) %collective-permute-start.13) | collective-permute-done | bytes 2359328 | tf_op jit(solution)/shard_map/ppermute | solution.py:498
  68.0 1.4 copy-done.2
  69.4 58.0 %feed.1 = (bf16[2048,512]{1,0:T(8,128)(2,1)}, bf16[512,2048]{1,0:T(8,128)(2,1)}, f32[512,2048]{1,0:T(8,128)}, bf16[256,4608]{1,0:T(8,128)(2,1)}, bf16[256,4608]{1,0:T(8,128)(2,1)}, /*index=5*/f32[512,128]{1,0:T(8,128)}) custom-call(s32[1]{0:T(128)} %bitcast.mine_ref, s32[3]{0:T(128)} %pad_add_fusion.limits_ref, bf16[512,2048]{1,0:T(8,128)(2,1)} %get-tuple-element.80.xt_ref, ...), custom_call_target="tpu_custom_call" | custom-call | tf_op jit(solution)/shard_map/feed/pallas_call | solution.py:678
  127.7 4.6 %collective-permute-done.14 = bf16[256,4608]{1,0:T(8,128)(2,1)S(1)} collective-permute-done((bf16[256,4608]{1,0:T(8,128)(2,1)}, bf16[256,4608]{1,0:T(8,128)(2,1)S(1)}, u32[]{:S(2)}, u32[]{:S(2)}) %collective-permute-start.14) | collective-permute-done | bytes 2359328 | tf_op jit(solution)/shard_map/ppermute | solution.py:498
  132.3 2.2 add_convert_fusion
  134.7 1.6 collective-permute-start.15
  137.0 1.2 collective-permute-start.17
  138.2 27.9 %attend_back.1 = (bf16[4,384,2048]{2,1,0:T(8,128)(2,1)}, bf16[256,1792]{1,0:T(8,128)(2,1)}, bf16[256,1792]{1,0:T(8,128)(2,1)}) custom-call(s32[1]{0:T(128)} %bitcast.mine_ref, s32[3]{0:T(128)} %pad_add_fusion.limits_ref, s32[16,128]{1,0:T(8,128)} %bitcast.6, bf16[512,2048]{1,0:T(8,128)(2,1)} %get-tuple-element.80.xt_ref, ...), custom_call_target="tpu_custom_call" | custom-call | tf_op jit(solution)/shard_map/attend_back/pallas_call | solution.py:722
  166.2 2.7 %collective-permute-done.18.refs_1_ = bf16[256,1792]{1,0:T(8,128)(2,1)S(1)} collective-permute-done((bf16[256,1792]{1,0:T(8,128)(2,1)}, bf16[256,1792]{1,0:T(8,128)(2,1)S(1)}, u32[]{:S(2)}, u32[]{:S(2)}) %collective-permute-start.18) | collective-permute-done | bytes 917536 | tf_op jit(solution)/shard_map/ppermute | solution.py:498
  169.8 2.4 %cut.2 = (bf16[64,1792]{1,0:T(8,128)(2,1)}, bf16[64,1792]{1,0:T(8,128)(2,1)}, bf16[64,1792]{1,0:T(8,128)(2,1)}, bf16[64,1792]{1,0:T(8,128)(2,1)}) custom-call(bf16[256,1792]{1,0:T(8,128)(2,1)} %get-tuple-element.108.refs_0_, bf16[256,1792]{1,0:T(8,128)(2,1)} %copy-done.4), custom_call_target="tpu_custom_call" | custom-call | tf_op jit(solution)/shard_map/cut/pallas_call | solution.py:556
  172.3 1.5 collective-permute-start.19
  174.6 1.2 collective-permute-start.21
  176.1 4.0 %collective-permute-start.25 = (bf16[16,4608]{1,0:T(8,128)(2,1)S(1)}, bf16[16,4608]{1,0:T(8,128)(2,1)S(1)}, u32[]{:S(2)}, u32[]{:S(2)}) collective-permute-start(bf16[16,4608]{1,0:T(8,128)(2,1)S(1)} %get-tuple-element.140), channel_id=1, source_target_pairs={{0,8},{1,9},{2,10},{3,11},{4,12},{5,13},{6,14},{7,15},{8,0},{9,1},... | collective-permute-start | bytes 442376 | tf_op jit(solution)/shard_map/ppermute | solution.py:498
  180.9 2.0 collective-permute-start.27
  183.0 9.6 %input_grad.1 = f32[2048,512]{1,0:T(8,128)} custom-call(bf16[4,384,2048]{2,1,0:T(8,128)(2,1)} %get-tuple-element.123.grads_ref, bf16[512,1536]{1,0:T(8,128)(2,1)} %get-tuple-element.124.weights_ref, f32[512,2048]{1,0:T(8,128)} %get-tuple-element.125.both_ref), custom_call_target="tpu_custom_call" | custom-call | tf_op jit(solution)/shard_map/input_grad/pallas_call | solution.py:759
  193.3 2.0 cut.3
  195.3 3.1 %collective-permute-start.22 = (bf16[16,1792]{1,0:T(8,128)(2,1)}, bf16[16,1792]{1,0:T(8,128)(2,1)S(1)}, u32[]{:S(2)}, u32[]{:S(2)}) collective-permute-start(bf16[16,1792]{1,0:T(8,128)(2,1)} %get-tuple-element.136), channel_id=1, source_target_pairs={{0,8},{1,9},{2,10},{3,11},{4,12},{5,13},{6,14},{7,15},{8,0},{9,1},... | collective-permute-start | bytes 172040 | tf_op jit(solution)/shard_map/ppermute | solution.py:498
  198.8 2.1 collective-permute-start.24
  201.6 2.2 collective-permute-done.23.refs_2_
  203.8 1.3 collective-permute-done.24.refs_3_
  205.7 1.8 own.1
  207.5 2.1 collective-permute-start.30
  209.7 2.2 collective-permute-start.28
  212.7 1.1 collective-permute-done.28
  214.4 1.6 collective-permute-start.31
  215.9 1.5 collective-permute-start.33
  218.3 3.0 %collective-permute-done.32 = f32[64,128]{1,0:T(8,128)S(1)} collective-permute-done((f32[64,128]{1,0:T(8,128)S(1)}, f32[64,128]{1,0:T(8,128)S(1)}, u32[]{:S(2)}, u32[]{:S(2)}) %collective-permute-start.32) | collective-permute-done | bytes 32800 | tf_op jit(solution)/shard_map/ppermute | solution.py:498
  221.4 1.3 collective-permute-done.34.far_ref
  223.4 1.8 settle.1
  225.2 1.2 slice.50
  227.1 1.0 maximum_multiply_fusion
  228.3 1.1 add_multiply_fusion
  (94 shorter events, 13.6 us)
Async XLA Ops:
  1.7 30.2 %copy-start.15 = (s32[2]{0:T(128)S(1)}, s32[2]{0:T(128)}, u32[]{:S(2)}) copy-start(s32[2]{0:T(128)} %param.11) | copy-start | bytes 28
  2.0 7.4 %collective-permute-start.2 = (bf16[16,1664]{1,0:T(8,128)(2,1)S(1)}, bf16[16,1664]{1,0:T(8,128)(2,1)S(1)}, u32[]{:S(2)}, u32[]{:S(2)}) collective-permute-start(bf16[16,1664]{1,0:T(8,128)(2,1)S(1)} %pad_maximum_fusion.3), channel_id=1, source_target_pairs={{0,24},{1,25},{2,26},{3,27},{4,28},{5,29},{6,30},{7,31},{8,16},{9,... | collective-permute-start | bytes 159752 | tf_op jit(solution)/shard_map/ppermute | solution.py:498
  7.1 5.0 %collective-permute-start.1 = (bf16[16,1664]{1,0:T(8,128)(2,1)S(1)}, bf16[16,1664]{1,0:T(8,128)(2,1)S(1)}, u32[]{:S(2)}, u32[]{:S(2)}) collective-permute-start(bf16[16,1664]{1,0:T(8,128)(2,1)S(1)} %pad_maximum_fusion.3), channel_id=1, source_target_pairs={{0,16},{1,17},{2,18},{3,19},{4,20},{5,21},{6,22},{7,23},{8,24},{9,... | collective-permute-start | bytes 159752 | tf_op jit(solution)/shard_map/ppermute | solution.py:498
  7.1 5.0 %collective-permute-start = (bf16[16,1664]{1,0:T(8,128)(2,1)S(1)}, bf16[16,1664]{1,0:T(8,128)(2,1)S(1)}, u32[]{:S(2)}, u32[]{:S(2)}) collective-permute-start(bf16[16,1664]{1,0:T(8,128)(2,1)S(1)} %pad_maximum_fusion.3), channel_id=1, source_target_pairs={{0,8},{1,9},{2,10},{3,11},{4,12},{5,13},{6,14},{7,15},{8,0},{9,1},... | collective-permute-start | bytes 159752 | tf_op jit(solution)/shard_map/ppermute | solution.py:498
  12.2 8.7 %collective-permute-start.8 = (bf16[16,4608]{1,0:T(8,128)(2,1)S(1)}, bf16[16,4608]{1,0:T(8,128)(2,1)S(1)}, u32[]{:S(2)}, u32[]{:S(2)}) collective-permute-start(bf16[16,4608]{1,0:T(8,128)(2,1)S(1)} %slice.54), channel_id=1, source_target_pairs={{0,24},{1,25},{2,26},{3,27},{4,28},{5,29},{6,30},{7,31},{8,16},{9,... | collective-permute-start | bytes 442376 | tf_op jit(solution)/shard_map/ppermute | solution.py:498
  14.6 12.1 %collective-permute-start.7 = (bf16[16,4608]{1,0:T(8,128)(2,1)S(1)}, bf16[16,4608]{1,0:T(8,128)(2,1)S(1)}, u32[]{:S(2)}, u32[]{:S(2)}) collective-permute-start(bf16[16,4608]{1,0:T(8,128)(2,1)S(1)} %slice.54), channel_id=1, source_target_pairs={{0,16},{1,17},{2,18},{3,19},{4,20},{5,21},{6,22},{7,23},{8,24},{9,... | collective-permute-start | bytes 442376 | tf_op jit(solution)/shard_map/ppermute | solution.py:498
  14.6 12.1 %collective-permute-start.6 = (bf16[16,4608]{1,0:T(8,128)(2,1)S(1)}, bf16[16,4608]{1,0:T(8,128)(2,1)S(1)}, u32[]{:S(2)}, u32[]{:S(2)}) collective-permute-start(bf16[16,4608]{1,0:T(8,128)(2,1)S(1)} %slice.54), channel_id=1, source_target_pairs={{0,8},{1,9},{2,10},{3,11},{4,12},{5,13},{6,14},{7,15},{8,0},{9,1},... | collective-permute-start | bytes 442376 | tf_op jit(solution)/shard_map/ppermute | solution.py:498
  16.6 10.1 %collective-permute-start.5 = (bf16[64,1664]{1,0:T(8,128)(2,1)S(1)}, bf16[64,1664]{1,0:T(8,128)(2,1)S(1)}, u32[]{:S(2)}, u32[]{:S(2)}) collective-permute-start(bf16[64,1664]{1,0:T(8,128)(2,1)S(1)} %pad_maximum_fusion.2), channel_id=1, source_target_pairs={{0,6},{1,7},{2,4},{3,5},{4,2},{5,3},{6,0},{7,1},{8,14},{9,15},{10,... | collective-permute-start | bytes 638984 | tf_op jit(solution)/shard_map/ppermute | solution.py:498
  19.1 8.3 %collective-permute-start.4 = (bf16[64,1664]{1,0:T(8,128)(2,1)S(1)}, bf16[64,1664]{1,0:T(8,128)(2,1)S(1)}, u32[]{:S(2)}, u32[]{:S(2)}) collective-permute-start(bf16[64,1664]{1,0:T(8,128)(2,1)S(1)} %pad_maximum_fusion.2), channel_id=1, source_target_pairs={{0,4},{1,5},{2,6},{3,7},{4,0},{5,1},{6,2},{7,3},{8,12},{9,13},{10,... | collective-permute-start | bytes 638984 | tf_op jit(solution)/shard_map/ppermute | solution.py:498
  20.9 6.6 %collective-permute-start.3 = (bf16[64,1664]{1,0:T(8,128)(2,1)S(1)}, bf16[64,1664]{1,0:T(8,128)(2,1)S(1)}, u32[]{:S(2)}, u32[]{:S(2)}) collective-permute-start(bf16[64,1664]{1,0:T(8,128)(2,1)S(1)} %pad_maximum_fusion.2), channel_id=1, source_target_pairs={{0,2},{1,3},{2,0},{3,1},{4,6},{5,7},{6,4},{7,5},{8,10},{9,11},{10,... | collective-permute-start | bytes 638984 | tf_op jit(solution)/shard_map/ppermute | solution.py:498
  27.6 4.9 %copy-start.1 = (bf16[256,1664]{1,0:T(8,128)(2,1)}, bf16[256,1664]{1,0:T(8,128)(2,1)S(1)}, u32[]{:S(2)}) copy-start(bf16[256,1664]{1,0:T(8,128)(2,1)S(1)} %pad_maximum_fusion.near_ref) | copy-start | bytes 2555908
  27.6 4.9 %collective-permute-start.9 = (bf16[256,1664]{1,0:T(8,128)(2,1)S(1)}, bf16[256,1664]{1,0:T(8,128)(2,1)S(1)}, u32[]{:S(2)}, u32[]{:S(2)}) collective-permute-start(bf16[256,1664]{1,0:T(8,128)(2,1)S(1)} %pad_maximum_fusion.near_ref), channel_id=1, source_target_pairs={{0,1},{1,0},{2,3},{3,2},{4,5},{5,4},{6,7},{7,6},{8,9},{9,8},{10,11... | collective-permute-start | bytes 2555912 | tf_op jit(solution)/shard_map/ppermute | solution.py:498
  27.7 34.5 %collective-permute-start.12 = (bf16[64,4608]{1,0:T(8,128)(2,1)S(1)}, bf16[64,4608]{1,0:T(8,128)(2,1)S(1)}, u32[]{:S(2)}, u32[]{:S(2)}) collective-permute-start(bf16[64,4608]{1,0:T(8,128)(2,1)S(1)} %pad_maximum_fusion.1), channel_id=1, source_target_pairs={{0,6},{1,7},{2,4},{3,5},{4,2},{5,3},{6,0},{7,1},{8,14},{9,15},{10,... | collective-permute-start | bytes 1769480 | tf_op jit(solution)/shard_map/ppermute | solution.py:498
  29.4 32.7 %collective-permute-start.11 = (bf16[64,4608]{1,0:T(8,128)(2,1)S(1)}, bf16[64,4608]{1,0:T(8,128)(2,1)S(1)}, u32[]{:S(2)}, u32[]{:S(2)}) collective-permute-start(bf16[64,4608]{1,0:T(8,128)(2,1)S(1)} %pad_maximum_fusion.1), channel_id=1, source_target_pairs={{0,4},{1,5},{2,6},{3,7},{4,0},{5,1},{6,2},{7,3},{8,12},{9,13},{10,... | collective-permute-start | bytes 1769480 | tf_op jit(solution)/shard_map/ppermute | solution.py:498
  30.7 31.5 %collective-permute-start.10 = (bf16[64,4608]{1,0:T(8,128)(2,1)S(1)}, bf16[64,4608]{1,0:T(8,128)(2,1)}, u32[]{:S(2)}, u32[]{:S(2)}) collective-permute-start(bf16[64,4608]{1,0:T(8,128)(2,1)S(1)} %pad_maximum_fusion.1), channel_id=1, source_target_pairs={{0,2},{1,3},{2,0},{3,1},{4,6},{5,7},{6,4},{7,5},{8,10},{9,11},{10,... | collective-permute-start | bytes 1769480 | tf_op jit(solution)/shard_map/ppermute | solution.py:498
  32.5 0.9 copy-start.5
  63.4 6.0 %copy-start = (bf16[256,4608]{1,0:T(8,128)(2,1)}, bf16[256,4608]{1,0:T(8,128)(2,1)S(1)}, u32[]{:S(2)}) copy-start(bf16[256,4608]{1,0:T(8,128)(2,1)S(1)} %constant_dynamic-update-slice_fusion.near_ref) | copy-start | bytes 7077892
  63.4 4.6 %collective-permute-start.13 = (bf16[256,4608]{1,0:T(8,128)(2,1)S(1)}, bf16[256,4608]{1,0:T(8,128)(2,1)S(1)}, u32[]{:S(2)}, u32[]{:S(2)}) collective-permute-start(bf16[256,4608]{1,0:T(8,128)(2,1)S(1)} %constant_dynamic-update-slice_fusion.near_ref), channel_id=1, source_target_pairs={{0,1},{1,0},{2,3},{3,2},{4,5},{5,4},{6,7},{7,6},{8,9},{9,8},{10,11... | collective-permute-start | bytes 7077896 | tf_op jit(solution)/shard_map/ppermute | solution.py:498
  68.0 1.4 copy-start.2
  127.5 4.8 %collective-permute-start.14 = (bf16[256,4608]{1,0:T(8,128)(2,1)}, bf16[256,4608]{1,0:T(8,128)(2,1)S(1)}, u32[]{:S(2)}, u32[]{:S(2)}) collective-permute-start(bf16[256,4608]{1,0:T(8,128)(2,1)} %get-tuple-element.97), channel_id=1, source_target_pairs={{0,1},{1,0},{2,3},{3,2},{4,5},{5,4},{6,7},{7,6},{8,9},{9,8},{10,11... | collective-permute-start | bytes 7077896 | tf_op jit(solution)/shard_map/ppermute | solution.py:498
  134.7 31.4 %collective-permute-start.15 = (bf16[64,4608]{1,0:T(8,128)(2,1)S(1)}, bf16[64,4608]{1,0:T(8,128)(2,1)S(1)}, u32[]{:S(2)}, u32[]{:S(2)}) collective-permute-start(bf16[64,4608]{1,0:T(8,128)(2,1)S(1)} %get-tuple-element.105), channel_id=1, source_target_pairs={{0,2},{1,3},{2,0},{3,1},{4,6},{5,7},{6,4},{7,5},{8,10},{9,11},{10,... | collective-permute-start | bytes 1769480 | tf_op jit(solution)/shard_map/ppermute | solution.py:498
  136.3 29.9 %collective-permute-start.16 = (bf16[64,4608]{1,0:T(8,128)(2,1)S(1)}, bf16[64,4608]{1,0:T(8,128)(2,1)S(1)}, u32[]{:S(2)}, u32[]{:S(2)}) collective-permute-start(bf16[64,4608]{1,0:T(8,128)(2,1)S(1)} %get-tuple-element.106), channel_id=1, source_target_pairs={{0,4},{1,5},{2,6},{3,7},{4,0},{5,1},{6,2},{7,3},{8,12},{9,13},{10,... | collective-permute-start | bytes 1769480 | tf_op jit(solution)/shard_map/ppermute | solution.py:498
  137.0 29.1 %collective-permute-start.17 = (bf16[64,4608]{1,0:T(8,128)(2,1)S(1)}, bf16[64,4608]{1,0:T(8,128)(2,1)S(1)}, u32[]{:S(2)}, u32[]{:S(2)}) collective-permute-start(bf16[64,4608]{1,0:T(8,128)(2,1)S(1)} %get-tuple-element.107), channel_id=1, source_target_pairs={{0,6},{1,7},{2,4},{3,5},{4,2},{5,3},{6,0},{7,1},{8,14},{9,15},{10,... | collective-permute-start | bytes 1769480 | tf_op jit(solution)/shard_map/ppermute | solution.py:498
  166.2 2.7 %collective-permute-start.18 = (bf16[256,1792]{1,0:T(8,128)(2,1)}, bf16[256,1792]{1,0:T(8,128)(2,1)S(1)}, u32[]{:S(2)}, u32[]{:S(2)}) collective-permute-start(bf16[256,1792]{1,0:T(8,128)(2,1)} %get-tuple-element.109), channel_id=1, source_target_pairs={{0,1},{1,0},{2,3},{3,2},{4,5},{5,4},{6,7},{7,6},{8,9},{9,8},{10,11... | collective-permute-start | bytes 2752520 | tf_op jit(solution)/shard_map/ppermute | solution.py:498
  168.9 0.9 copy-start.4
  172.3 8.7 %collective-permute-start.19 = (bf16[64,1792]{1,0:T(8,128)(2,1)}, bf16[64,1792]{1,0:T(8,128)(2,1)S(1)}, u32[]{:S(2)}, u32[]{:S(2)}) collective-permute-start(bf16[64,1792]{1,0:T(8,128)(2,1)} %get-tuple-element.127), channel_id=1, source_target_pairs={{0,2},{1,3},{2,0},{3,1},{4,6},{5,7},{6,4},{7,5},{8,10},{9,11},{10,... | collective-permute-start | bytes 688136 | tf_op jit(solution)/shard_map/ppermute | solution.py:498
  173.8 18.8 %collective-permute-start.20 = (bf16[64,1792]{1,0:T(8,128)(2,1)}, bf16[64,1792]{1,0:T(8,128)(2,1)S(1)}, u32[]{:S(2)}, u32[]{:S(2)}) collective-permute-start(bf16[64,1792]{1,0:T(8,128)(2,1)} %get-tuple-element.128), channel_id=1, source_target_pairs={{0,4},{1,5},{2,6},{3,7},{4,0},{5,1},{6,2},{7,3},{8,12},{9,13},{10,... | collective-permute-start | bytes 688136 | tf_op jit(solution)/shard_map/ppermute | solution.py:498
  174.6 18.1 %collective-permute-start.21 = (bf16[64,1792]{1,0:T(8,128)(2,1)}, bf16[64,1792]{1,0:T(8,128)(2,1)}, u32[]{:S(2)}, u32[]{:S(2)}) collective-permute-start(bf16[64,1792]{1,0:T(8,128)(2,1)} %get-tuple-element.129), channel_id=1, source_target_pairs={{0,6},{1,7},{2,4},{3,5},{4,2},{5,3},{6,0},{7,1},{8,14},{9,15},{10,... | collective-permute-start | bytes 688136 | tf_op jit(solution)/shard_map/ppermute | solution.py:498
  176.1 22.7 %collective-permute-start.25 = (bf16[16,4608]{1,0:T(8,128)(2,1)S(1)}, bf16[16,4608]{1,0:T(8,128)(2,1)S(1)}, u32[]{:S(2)}, u32[]{:S(2)}) collective-permute-start(bf16[16,4608]{1,0:T(8,128)(2,1)S(1)} %get-tuple-element.140), channel_id=1, source_target_pairs={{0,8},{1,9},{2,10},{3,11},{4,12},{5,13},{6,14},{7,15},{8,0},{9,1},... | collective-permute-start | bytes 442376 | tf_op jit(solution)/shard_map/ppermute | solution.py:498
  180.1 20.7 %collective-permute-start.26 = (bf16[16,4608]{1,0:T(8,128)(2,1)S(1)}, bf16[16,4608]{1,0:T(8,128)(2,1)S(1)}, u32[]{:S(2)}, u32[]{:S(2)}) collective-permute-start(bf16[16,4608]{1,0:T(8,128)(2,1)S(1)} %get-tuple-element.141), channel_id=1, source_target_pairs={{0,16},{1,17},{2,18},{3,19},{4,20},{5,21},{6,22},{7,23},{8,24},{9,... | collective-permute-start | bytes 442376 | tf_op jit(solution)/shard_map/ppermute | solution.py:498
  180.9 11.6 %copy-start.8 = (bf16[64,1792]{1,0:T(8,128)(2,1)}, bf16[64,1792]{1,0:T(8,128)(2,1)S(1)}, u32[]{:S(2)}) copy-start(bf16[64,1792]{1,0:T(8,128)(2,1)S(1)} %collective-permute-done.19.refs_1_) | copy-start | bytes 688132
  180.9 19.9 %collective-permute-start.27 = (bf16[16,4608]{1,0:T(8,128)(2,1)S(1)}, bf16[16,4608]{1,0:T(8,128)(2,1)S(1)}, u32[]{:S(2)}, u32[]{:S(2)}) collective-permute-start(bf16[16,4608]{1,0:T(8,128)(2,1)S(1)} %get-tuple-element.142), channel_id=1, source_target_pairs={{0,24},{1,25},{2,26},{3,27},{4,28},{5,29},{6,30},{7,31},{8,16},{9,... | collective-permute-start | bytes 442376 | tf_op jit(solution)/shard_map/ppermute | solution.py:498
  192.6 35.7 %copy-start.3 = (f32[98496]{0:T(1024)S(1)}, f32[98496]{0:T(1024)}, u32[]{:S(2)}) copy-start(f32[98496]{0:T(1024)} %param.13) | copy-start | bytes 1181956
  192.6 35.7 %copy-start.6 = (f32[98496]{0:T(1024)S(1)}, f32[98496]{0:T(1024)}, u32[]{:S(2)}) copy-start(f32[98496]{0:T(1024)} %param.15) | copy-start | bytes 1181956
  192.6 35.8 %copy-start.7 = (f32[98496]{0:T(1024)S(1)}, f32[98496]{0:T(1024)}, u32[]{:S(2)}) copy-start(f32[98496]{0:T(1024)} %param.14) | copy-start | bytes 1181956
  195.3 6.3 %collective-permute-start.22 = (bf16[16,1792]{1,0:T(8,128)(2,1)}, bf16[16,1792]{1,0:T(8,128)(2,1)S(1)}, u32[]{:S(2)}, u32[]{:S(2)}) collective-permute-start(bf16[16,1792]{1,0:T(8,128)(2,1)} %get-tuple-element.136), channel_id=1, source_target_pairs={{0,8},{1,9},{2,10},{3,11},{4,12},{5,13},{6,14},{7,15},{8,0},{9,1},... | collective-permute-start | bytes 172040 | tf_op jit(solution)/shard_map/ppermute | solution.py:498
  198.4 5.4 %collective-permute-start.23 = (bf16[16,1792]{1,0:T(8,128)(2,1)}, bf16[16,1792]{1,0:T(8,128)(2,1)S(1)}, u32[]{:S(2)}, u32[]{:S(2)}) collective-permute-start(bf16[16,1792]{1,0:T(8,128)(2,1)} %get-tuple-element.137), channel_id=1, source_target_pairs={{0,16},{1,17},{2,18},{3,19},{4,20},{5,21},{6,22},{7,23},{8,24},{9,... | collective-permute-start | bytes 172040 | tf_op jit(solution)/shard_map/ppermute | solution.py:498
  198.8 6.3 %collective-permute-start.24 = (bf16[16,1792]{1,0:T(8,128)(2,1)}, bf16[16,1792]{1,0:T(8,128)(2,1)S(1)}, u32[]{:S(2)}, u32[]{:S(2)}) collective-permute-start(bf16[16,1792]{1,0:T(8,128)(2,1)} %get-tuple-element.138), channel_id=1, source_target_pairs={{0,24},{1,25},{2,26},{3,27},{4,28},{5,29},{6,30},{7,31},{8,16},{9,... | collective-permute-start | bytes 172040 | tf_op jit(solution)/shard_map/ppermute | solution.py:498
  201.6 3.4 %copy-start.12 = (bf16[16,1792]{1,0:T(8,128)(2,1)}, bf16[16,1792]{1,0:T(8,128)(2,1)S(1)}, u32[]{:S(2)}) copy-start(bf16[16,1792]{1,0:T(8,128)(2,1)S(1)} %collective-permute-done.22.refs_1_) | copy-start | bytes 172036
  203.8 1.3 copy-start.13
  207.5 6.8 %collective-permute-start.30 = (f32[16,128]{1,0:T(8,128)}, f32[16,128]{1,0:T(8,128)S(1)}, u32[]{:S(2)}, u32[]{:S(2)}) collective-permute-start(f32[16,128]{1,0:T(8,128)} %get-tuple-element.143), channel_id=1, source_target_pairs={{0,24},{1,25},{2,26},{3,27},{4,28},{5,29},{6,30},{7,31},{8,16},{9,... | collective-permute-start | bytes 24584 | tf_op jit(solution)/shard_map/ppermute | solution.py:498
  209.6 4.8 %collective-permute-start.29 = (f32[16,128]{1,0:T(8,128)}, f32[16,128]{1,0:T(8,128)S(1)}, u32[]{:S(2)}, u32[]{:S(2)}) collective-permute-start(f32[16,128]{1,0:T(8,128)} %get-tuple-element.143), channel_id=1, source_target_pairs={{0,16},{1,17},{2,18},{3,19},{4,20},{5,21},{6,22},{7,23},{8,24},{9,... | collective-permute-start | bytes 24584 | tf_op jit(solution)/shard_map/ppermute | solution.py:498
  209.7 4.1 %collective-permute-start.28 = (f32[16,128]{1,0:T(8,128)}, f32[16,128]{1,0:T(8,128)S(1)}, u32[]{:S(2)}, u32[]{:S(2)}) collective-permute-start(f32[16,128]{1,0:T(8,128)} %get-tuple-element.143), channel_id=1, source_target_pairs={{0,8},{1,9},{2,10},{3,11},{4,12},{5,13},{6,14},{7,15},{8,0},{9,1},... | collective-permute-start | bytes 24584 | tf_op jit(solution)/shard_map/ppermute | solution.py:498
  214.4 4.0 %collective-permute-start.31 = (f32[64,128]{1,0:T(8,128)S(1)}, f32[64,128]{1,0:T(8,128)S(1)}, u32[]{:S(2)}, u32[]{:S(2)}) collective-permute-start(f32[64,128]{1,0:T(8,128)S(1)} %get-tuple-element.158), channel_id=1, source_target_pairs={{0,2},{1,3},{2,0},{3,1},{4,6},{5,7},{6,4},{7,5},{8,10},{9,11},{10,... | collective-permute-start | bytes 98312 | tf_op jit(solution)/shard_map/ppermute | solution.py:498
  215.9 5.4 %collective-permute-start.33 = (f32[64,128]{1,0:T(8,128)S(1)}, f32[64,128]{1,0:T(8,128)S(1)}, u32[]{:S(2)}, u32[]{:S(2)}) collective-permute-start(f32[64,128]{1,0:T(8,128)S(1)} %get-tuple-element.158), channel_id=1, source_target_pairs={{0,6},{1,7},{2,4},{3,5},{4,2},{5,3},{6,0},{7,1},{8,14},{9,15},{10,... | collective-permute-start | bytes 98312 | tf_op jit(solution)/shard_map/ppermute | solution.py:498
  217.4 3.9 %collective-permute-start.32 = (f32[64,128]{1,0:T(8,128)S(1)}, f32[64,128]{1,0:T(8,128)S(1)}, u32[]{:S(2)}, u32[]{:S(2)}) collective-permute-start(f32[64,128]{1,0:T(8,128)S(1)} %get-tuple-element.158), channel_id=1, source_target_pairs={{0,4},{1,5},{2,6},{3,7},{4,0},{5,1},{6,2},{7,3},{8,12},{9,13},{10,... | collective-permute-start | bytes 98312 | tf_op jit(solution)/shard_map/ppermute | solution.py:498
  221.3 1.4 copy-start.10
  221.3 1.4 collective-permute-start.34
  (3 other events, 2.0 us)

commit v4 on v3

--- a/solution.py
+++ b/solution.py
@@ -30,7 +30,7 @@
 TILE = 256
 FIRST_WIDTH = 3 * D + LANES
 REST_WIDTH = D + 2 * FF
-VMEM_BYTES = 60 * 1024 * 1024
+MIB = 1024 * 1024
 
 f32 = jnp.float32
 bf16 = jnp.bfloat16
@@ -44,22 +44,18 @@
     return lax.dot_general(left, right, (((1,), (1,)), ((), ())), preferred_element_type=f32)
 
 
-def identity(size):
-    down = lax.broadcasted_iota(jnp.int32, (size, size), 0)
-    across = lax.broadcasted_iota(jnp.int32, (size, size), 1)
-    return jnp.where(down == across, 1.0, 0.0).astype(bf16)
-
-
-def turned(values, unit):
-    return nt(unit, values).astype(bf16)
-
-
-def place_blocks(target, halves, codes, mine, width):
-    for half_at, half in enumerate(halves):
-        for block_at in range(BLOCKS // 2):
-            natural = mine ^ codes[half_at * (BLOCKS // 2) + block_at]
-            to_rows = pl.ds(pl.multiple_of(natural * BLOCK, BLOCK), BLOCK)
-            target[to_rows, :width] = half[block_at * BLOCK : (block_at + 1) * BLOCK, :width]
+def turned(values):
+    return values.T
+
+
+def place_blocks(target, pieces, codes, mine):
+    place = 0
+    for piece in pieces:
+        width = piece.shape[1]
+        for begin in range(0, piece.shape[0], BLOCK):
+            to_rows = pl.ds(pl.multiple_of((mine ^ codes[place]) * BLOCK, BLOCK), BLOCK)
+            target[to_rows, :width] = piece[begin : begin + BLOCK, :]
+            place += 1
 
 
 def spread_blocks(halves, source, codes, mine, begin, width):
@@ -78,13 +74,11 @@
 ):
     @pl.when(pl.program_id(0) == 0)
     def _():
-        place_blocks(table, (near_ref, far_ref), codes, mine_ref[0], FIRST_WIDTH)
-        unit = identity(256)
+        place_blocks(table, (near_ref, far_ref), codes, mine_ref[0])
         for kind in range(3):
             for half in range(2):
-                turned_weights[kind * D + half * 256 : kind * D + half * 256 + 256, :] = turned(
-                    table[:, kind * D + half * 256 : kind * D + half * 256 + 256], unit
-                )
+                at = kind * D + half * TILE
+                turned_weights[at : at + TILE, :] = turned(table[:, at : at + TILE])
         for pair in range(PAIRS):
             for kind in range(3):
                 at = pair * 3 * PAIR + kind * PAIR
@@ -100,9 +94,8 @@
     x = x_ref[...]
     width = x.shape[0]
     reps = width // LANES
-    unit = identity(256)
     for half in range(2):
-        xt_ref[half * 256 : half * 256 + 256, :] = turned(x[:, half * 256 : half * 256 + 256], unit)
+        xt_ref[half * 256 : half * 256 + 256, :] = turned(x[:, half * 256 : half * 256 + 256])
     bias_q = jnp.concatenate([columns[0]] * reps, axis=1)
     bias_v = jnp.concatenate([columns[1]] * reps, axis=1)
     query = nt(turned_weights[:D, :], x) + bias_q
@@ -122,22 +115,21 @@
     def codes_of(block):
         row = jnp.where(limits_ref[2] == 1, 0, block // (ROW // LANES))
         limit = jnp.where(row == 0, limits_ref[0], limits_ref[1])
-        code = seg_ref[pl.ds(block, 1), :] * 2 + row
+        code = seg_ref[block : block + 1, :] * 2 + row
         live = lane + block * LANES - row * ROW < limit
         return code.astype(f32), jnp.where(live, code, -1).astype(f32)
 
-    def one_block(block, carry):
-        query_code, _ = codes_of(block)
-        first = jnp.clip(block - 1, 0, blocks - 3)
-        for part in range(3):
-            _, key_code = codes_of(first + part)
-            key_column = jnp.broadcast_to(key_code, (LANES, LANES)).T
-            same = (first + part - block) * LANES
-            allowed = (key_column == query_code) | (down + same == across)
-            bias[block, part * LANES : (part + 1) * LANES, :] = jnp.where(allowed, 0.0, MASKED)
-        return carry
-
-    lax.fori_loop(0, blocks, one_block, 0)
+    codes = [codes_of(block) for block in range(blocks)]
+    for block in range(blocks):
+        key_column = jnp.broadcast_to(codes[block][1], (LANES, LANES)).T
+        for query in range(max(block - 2, 0), min(block + 3, blocks)):
+            first = min(max(query - 1, 0), blocks - 3)
+            if 0 <= block - first < 3:
+                allowed = key_column == codes[query][0]
+                if query == block:
+                    allowed = allowed | (down == across)
+                at = (block - first) * LANES
+                bias[query, at : at + LANES, :] = jnp.where(allowed, 0.0, MASKED)
 
 
 def two_heads(values):
@@ -237,35 +229,34 @@
     return parts
 
 
-def feed_kernel(
-    codes, mine_ref, limits_ref, xt_ref, att_ref, cot_ref, vec_ref, near_ref, far_ref,
-    layer_ref, ga_ref, both_ref, keep_ref, send_ref, sums_ref,
-    table, out_turned, up_turned, down_turned, columns, up_bias, slopes,
-    acc_down, acc_up, acc_out, acc_vec, *kept,
-):
+def feed_kernel(codes, amount, *refs):
+    mine_ref, limits_ref, xt_ref, att_ref, cot_ref, vec_ref = refs[:6]
+    piece_refs = refs[6 : 6 + amount]
+    layer_ref, ga_ref, both_ref, keep_ref, send_ref, sums_ref = refs[6 + amount : 12 + amount]
+    table, out_turned, up_turned, down_turned, columns, up_bias, slopes = refs[
+        12 + amount : 19 + amount
+    ]
+    acc_down, acc_up, acc_out, acc_vec, *kept = refs[19 + amount :]
     step = pl.program_id(0)
-    unit = identity(TILE)
-    chunk = 512
+    chunk = TILE
     chunks = FF // chunk
     each = len(kept) // 2
 
     @pl.when(step == 0)
     def _():
-        place_blocks(table, (near_ref, far_ref), codes, mine_ref[0], REST_WIDTH)
+        place_blocks(table, piece_refs, codes, mine_ref[0])
         for at in range(0, D, TILE):
-            out_turned[at : at + TILE, :] = turned(table[:, at : at + TILE], unit)
+            out_turned[at : at + TILE, :] = turned(table[:, at : at + TILE])
         for at in range(0, FF, TILE):
-            up_turned[at : at + TILE, :] = turned(table[:, D + at : D + at + TILE], unit)
-            down_turned[at : at + TILE, :] = turned(
-                table[:, D + FF + at : D + FF + at + TILE], unit
-            )
+            up_turned[at : at + TILE, :] = turned(table[:, D + at : D + at + TILE])
+            down_turned[at : at + TILE, :] = turned(table[:, D + FF + at : D + FF + at + TILE])
         for kind in range(6):
             columns[kind] = jnp.broadcast_to(vec_ref[:, kind + 2 : kind + 3], (D, LANES))
         for at in range(4):
             up_bias[pl.ds(at, D, stride=4), :] = jnp.broadcast_to(
                 vec_ref[:, 8 + at : 9 + at], (D, LANES)
             )
-        for buffer in (acc_down, acc_up, acc_out, acc_vec) + kept[each:]:
+        for buffer in (acc_down, acc_up, acc_out, acc_vec, *kept[each:]):
             buffer[...] = jnp.zeros_like(buffer)
         for buffer in (kept[2], kept[each + 2]):
             buffer[D:, :] = jnp.ones((BLOCK, TILE), bf16)
@@ -275,7 +266,12 @@
 
     def one_tile(tile, now, before):
         hidden, grad_up, first_keep, feed_keep, branch_keep, att_keep = now
-        fill = weight_parts(before, acc_down, acc_up, acc_out)
+        fill = iter(weight_parts(before, acc_down, acc_up, acc_out))
+
+        def tick(amount=1):
+            for _ in range(amount):
+                next(fill)()
+
         here = slice(tile * TILE, (tile + 1) * TILE)
         place = lax.broadcasted_iota(jnp.int32, (1, TILE), 1) + (step * 2 + tile) * TILE
         row = jnp.where(limits_ref[2] == 1, 0, place // ROW)
@@ -286,8 +282,7 @@
         att = att_ref[:, here]
         att_keep[...] = att
         z_one = x + nn(table[:, :D], att) + column(0)
-        for part in fill[:5]:
-            part()
+        tick(5)
         centred = z_one - mean_down(z_one)
         inverse_one = lax.rsqrt(mean_down(centred * centred) + EPSILON)
         normed_one = centred * inverse_one
@@ -320,11 +315,8 @@
 
         pipelined(chunks, widen, bend, narrow)
         z_two = partial[0]
-        cot = jnp.concatenate(
-            [nt(unit, cot_ref[here, at : at + TILE]) for at in range(0, D, TILE)], axis=0
-        )
-        for part in fill[5:13]:
-            part()
+        cot = cot_ref[here, :].T.astype(f32)
+        tick(8)
         centred = z_two - mean_down(z_two)
         inverse_two = lax.rsqrt(mean_down(centred * centred) + EPSILON)
         normed_two = centred * inverse_two
@@ -332,9 +324,9 @@
         layer = jnp.where(live, normed_two * gain_two + column(5), 0.0).astype(bf16)
         cot = jnp.where(live, cot, 0.0)
         scaled = cot * gain_two
-        grad_two = inverse_two * (
-            scaled - mean_down(scaled) - normed_two * mean_down(scaled * normed_two)
-        )
+        scaled_mean = mean_down(scaled)
+        product_mean = mean_down(scaled * normed_two)
+        grad_two = inverse_two * (scaled - scaled_mean - normed_two * product_mean)
         grad_feed = grad_two.astype(bf16)
         feed_keep[...] = grad_feed
         acc_vec[1] += lane_parts(grad_feed.astype(f32))
@@ -356,16 +348,15 @@
 
         pipelined(chunks, widen_back, bend_back, narrow_back)
         grad_first = partial[0]
-        layer_ref[here, :] = nt(unit, layer).astype(bf16)
-        for part in fill[13:]:
-            part()
+        layer_ref[here, :] = layer.T
+        tick(5)
         acc_vec[2] += lane_parts(grad_first * normed_one)
         acc_vec[3] += lane_parts(grad_first)
         scaled = grad_first * column(2)
-        grad_one = inverse_one * (
-            scaled - mean_down(scaled) - normed_one * mean_down(scaled * normed_one)
-        )
-        both_ref[:, here] = grad_two + grad_one
+        scaled_mean = mean_down(scaled)
+        product_mean = mean_down(scaled * normed_one)
+        grad_one = inverse_one * (scaled - scaled_mean - normed_one * product_mean)
+        both_ref[:, here] = (grad_two + grad_one).astype(bf16)
         grad_branch = grad_one.astype(bf16)
         branch_keep[...] = grad_branch
         acc_vec[0] += lane_parts(grad_branch.astype(f32))
@@ -443,28 +434,23 @@
     query_sum = jnp.sum(grads[:PAIR].astype(f32), axis=1, keepdims=True)
     value_sum = jnp.sum(grads[2 * PAIR :].astype(f32), axis=1, keepdims=True)
     total = jnp.where(lane == 0, query_sum, jnp.where(lane == 1, value_sum, sums_ref[rows, :]))
-    high = total.astype(bf16).astype(f32)
-    vectors[rows, :LANES] = high
-    vectors[rows, LANES:] = total - high
+    vectors[rows, :] = total
 
     @pl.when(pair == PAIRS - 1)
     def _():
-        spread_blocks(halves, vectors, codes, mine_ref[0], 3 * D, 2 * LANES)
+        spread_blocks(halves, vectors, codes, mine_ref[0], 3 * D, LANES)
 
 
 def input_kernel(grads_ref, weights_ref, both_ref, out_ref):
-    unit = identity(TILE)
     width = both_ref.shape[1]
 
     def multiply(at, _):
         here = slice(at * TILE, (at + 1) * TILE)
         grads = jnp.concatenate([grads_ref[pair, :, here] for pair in range(PAIRS)], axis=0)
-        return both_ref[:, here] + nn(weights_ref[...], grads)
+        return both_ref[:, here].astype(f32) + nn(weights_ref[...], grads)
 
     def turn(at, total):
-        high = total.astype(bf16)
-        rest = (total - high.astype(f32)).astype(bf16)
-        out_ref[at * TILE : (at + 1) * TILE, :] = nt(unit, high) + nt(unit, rest)
+        out_ref[at * TILE : (at + 1) * TILE, :] = total.T
 
     pipelined(width // TILE, multiply, turn)
 
@@ -480,7 +466,7 @@
             piece = total[:, at : at + PAIR]
             own_ref[:, kind * D + pair * PAIR : kind * D + (pair + 1) * PAIR] = piece
             squares = squares + jnp.sum(piece * piece, axis=1, keepdims=True)
-    vectors = total[:, -2 * LANES : -LANES] + total[:, -LANES:]
+    vectors = total[:, -LANES:]
     lane = lax.broadcasted_iota(jnp.int32, vectors.shape, 1)
     vectors = jnp.where(lane < VECTORS, vectors, 0.0)
     squares = squares + jnp.sum(vectors * vectors, axis=1, keepdims=True)
@@ -488,7 +474,7 @@
 
 
 def settle_kernel(codes, mine_ref, near_ref, far_ref, vectors_ref, norm_ref, table):
-    place_blocks(table, (near_ref, far_ref), codes, mine_ref[0], LANES)
+    place_blocks(table, (near_ref, far_ref), codes, mine_ref[0])
     vectors_ref[...] = table[...].T[:VECTORS, :]
     squares = jnp.sum(table[...], axis=0, keepdims=True)[:, VECTORS : VECTORS + 1]
     norm_ref[...] = jnp.broadcast_to(jnp.sqrt(squares), (8, LANES))
@@ -524,41 +510,12 @@
     ]
 
 
-def with_vectors(total):
-    vectors = total[:, -2 * LANES : -LANES] + total[:, -LANES:]
-    high = vectors.astype(bf16).astype(f32)
-    before = [total[:, : -2 * LANES]] if total.shape[1] > 2 * LANES else []
-    return jnp.concatenate(before + [high, vectors - high], axis=1)
-
-
-def cut_kernel(*refs):
-    width = refs[0].shape[1]
-    rows = refs[-1].shape[0]
-    amount = refs[0].shape[0] // rows
-    pieces = refs[len(refs) - amount :]
-    parts = refs[: len(refs) - amount]
-    for at, piece in enumerate(pieces):
-        for begin in range(0, width, 2 * LANES):
-            here = slice(begin, begin + 2 * LANES)
-            total = sum(part[at * rows : (at + 1) * rows, here].astype(f32) for part in parts)
-            if begin + 2 * LANES == width:
-                total = with_vectors(total)
-            piece[:, here] = total.astype(piece.dtype)
-
-
-def cut_sum(parts, amount, dtype, holds_vectors):
-    rows, width = parts[0].shape
-    few = rows // amount
-    if few % BLOCK or not holds_vectors:
-        total = sum(part.astype(f32) for part in parts)
-        total = (with_vectors(total) if holds_vectors else total).astype(dtype)
-        return [total[at * few : (at + 1) * few] for at in range(amount)]
-    return pl.pallas_call(
-        cut_kernel,
-        out_shape=[shaped((few, width), dtype)] * amount,
-        compiler_params=params_of(),
-        name="cut",
-    )(*parts)
+def cut_sum(parts, amount, dtype):
+    rows = parts[0].shape[0] // amount
+    return [
+        sum(part[at * rows : (at + 1) * rows].astype(f32) for part in parts).astype(dtype)
+        for at in range(amount)
+    ]
 
 
 def together(*values):
@@ -577,8 +534,12 @@
     return jax.ShapeDtypeStruct(shape, dtype)
 
 
-def params_of(**more):
-    return pltpu.CompilerParams(vmem_limit_bytes=VMEM_BYTES, **more)
+def resident():
+    return pl.BlockSpec(memory_space=pltpu.VMEM)
+
+
+def params_of(mib):
+    return pltpu.CompilerParams(vmem_limit_bytes=mib * MIB)
 
 
 def body(tokens, cotangent, segment_ids, row_lengths, row_widths, params, momenta, averages):
@@ -598,12 +559,12 @@
         spread = jnp.array(block_codes(count), jnp.int32)
         places_of = jnp.argsort(spread)
 
-    def to_kernel(near, far):
+    def to_kernel(pieces, amount):
         if direct:
-            return near, far
-        table = jnp.concatenate([near, far], axis=0).reshape(count, own_count, -1)
-        table = jnp.take(table, places_of[jnp.arange(count) ^ mine], axis=0).reshape(D, -1)
-        return table[: D // 2], table[D // 2 :]
+            return pieces
+        table = jnp.concatenate(pieces, axis=0).reshape(count, own_count, -1)
+        table = jnp.take(table, places_of[jnp.arange(count) ^ mine], axis=0)
+        return list(table.reshape(amount, D // amount, -1))
 
     def from_kernel(keep, send):
         if direct:
@@ -630,7 +591,8 @@
         rest_pieces = gather_phase(rest, masks, count)
         if masks is not outer[-1]:
             rest = jnp.concatenate(rest_pieces, axis=0)
-    first_near, first_far = to_kernel(*gather_phase(first, phases[0], count))
+    rest_far = [exchange(rest, 1, count)]
+    first_near, first_far = to_kernel(gather_phase(first, phases[0], count), 2)
     limits = jnp.concatenate([row_lengths, row_widths])
     segments = segment_ids.reshape(blocks, LANES)
 
@@ -638,11 +600,10 @@
     steps = slots // tile
     across = pl.BlockSpec((D, tile), lambda at: (0, at))
     down = pl.BlockSpec((tile, D), lambda at: (at, 0))
-    half_first = whole((D // 2, FIRST_WIDTH))
     xt, qt, kt, vt, key, value, vectors, pair_weights = pl.pallas_call(
         functools.partial(project_kernel, codes),
         grid=(steps,),
-        in_specs=[smem(), down, half_first, half_first],
+        in_specs=[smem(), down, resident(), resident()],
         out_specs=[across] * 4 + [down] * 2 + [whole((D, LANES)), whole((D, 3 * D))],
         out_shape=[shaped((D, slots), bf16)] * 4
         + [shaped((slots, D), bf16)] * 2
@@ -653,7 +614,7 @@
             pltpu.VMEM((2, D, LANES), f32),
             pltpu.VMEM((8, D), f32),
         ],
-        compiler_params=params_of(),
+        compiler_params=params_of(52),
         name="project",
     )(origin, tokens, first_near, first_far)
 
@@ -667,26 +628,27 @@
         out_specs=[pair_rows, sums_block],
         out_shape=[shaped((D, slots), bf16), shaped((PAIRS, blocks, 2 * LANES), f32)],
         scratch_shapes=[pltpu.VMEM((blocks, WINDOW, LANES), f32)],
-        compiler_params=params_of(),
+        compiler_params=params_of(56),
         name="attend",
     )(limits, segments, qt, key, vt)
 
     attended, *rest_pieces = together(attended, *rest_pieces)
-    rest = jnp.concatenate(rest_pieces, axis=0)
-    rest_near, rest_far = to_kernel(*gather_phase(rest, phases[0], count))
+    rest_far += [exchange(piece, 1, count) for piece in rest_pieces[1:]]
+    rest_pieces = to_kernel(rest_pieces + rest_far, 1)
     half_rest = whole((D // 2, REST_WIDTH))
     layer_output, grad_attended, grad_both, keep_rest, send_rest, feed_sums = pl.pallas_call(
-        functools.partial(feed_kernel, codes),
+        functools.partial(feed_kernel, codes, len(rest_pieces)),
         grid=(steps,),
         in_specs=[
             smem(), smem(), across, across, down,
-            whole((D, LANES)), half_rest, half_rest,
-        ],
+            whole((D, LANES)),
+        ]
+        + [whole(piece.shape) for piece in rest_pieces],
         out_specs=[down, across, across, half_rest, half_rest, whole((D, LANES))],
         out_shape=[
             shaped((slots, D), bf16),
             shaped((D, slots), bf16),
-            shaped((D, slots), f32),
+            shaped((D, slots), bf16),
             shaped((D // 2, REST_WIDTH), bf16),
             shaped((D // 2, REST_WIDTH), bf16),
             shaped((D, LANES), f32),
@@ -705,20 +667,19 @@
             pltpu.VMEM((6, D, LANES), f32),
         ]
         + [pltpu.VMEM((rows, TILE), bf16) for rows in (FF, FF, D + BLOCK, D, D, D)] * 2,
-        compiler_params=params_of(),
+        compiler_params=params_of(60),
         name="feed",
-    )(origin, limits, xt, attended, cotangent, vectors, rest_near, rest_far)
-
-    def scatter(parts, at, holds_vectors):
+    )(origin, limits, xt, attended, cotangent, vectors, *rest_pieces)
+
+    def scatter(parts, at):
         if at == len(phases) - 1:
-            return cut_sum(parts, 1, f32, holds_vectors)
-        return cut_sum(parts, len(phases[at + 1]), bf16, holds_vectors)
+            return cut_sum(parts, 1, f32)
+        return cut_sum(parts, len(phases[at + 1]), bf16)
 
     parts = scatter_phase(from_kernel(keep_rest, send_rest), phases[0], count)
-    grad_attended, *pieces = together(grad_attended, *scatter(parts, 0, False))
+    grad_attended, *pieces = together(grad_attended, *scatter(parts, 0))
     rest_parts = scatter_phase(pieces, phases[1], count)
 
-    half_all = whole((D // 2, 3 * D + 2 * LANES))
     grads, keep_first, send_first = pl.pallas_call(
         functools.partial(attend_back_kernel, codes),
         grid=(PAIRS,),
@@ -729,33 +690,39 @@
         ],
         out_specs=[
             pl.BlockSpec((1, 3 * PAIR, slots), lambda at: (at, 0, 0)),
-            half_all,
-            half_all,
+            resident(),
+            resident(),
         ],
         out_shape=[
             shaped((PAIRS, 3 * PAIR, slots), bf16),
-            shaped((D // 2, 3 * D + 2 * LANES), bf16),
-            shaped((D // 2, 3 * D + 2 * LANES), bf16),
+            shaped((D // 2, FIRST_WIDTH), bf16),
+            shaped((D // 2, FIRST_WIDTH), bf16),
         ],
         scratch_shapes=[
             pltpu.VMEM((blocks, WINDOW, LANES), f32),
             pltpu.VMEM((PAIR, slots), f32),
             pltpu.VMEM((PAIR, slots), f32),
             pltpu.VMEM((D, 3 * PAIR), f32),
-            pltpu.VMEM((D, 2 * LANES), f32),
+            pltpu.VMEM((D, LANES), f32),
         ],
-        compiler_params=params_of(),
+        compiler_params=params_of(54),
         name="attend_back",
     )(origin, limits, segments, xt, qt, kt, key, value, attended, grad_attended, logsum, feed_sums)
 
     keep_first, send_first, *rest_parts = together(keep_first, send_first, *rest_parts)
     parts = scatter_phase(from_kernel(keep_first, send_first), phases[0], count)
-    pieces = scatter(parts, 0, True)
+    pieces = scatter(parts, 0)
     grads, *held = together(grads, *pieces, *rest_parts)
     pieces, rest_parts = held[: len(pieces)], held[len(pieces) :]
     parts = scatter_phase(pieces, phases[1], count)
-    rest_pieces = scatter(rest_parts, 1, False)
-    grads, *rest_pieces = together(grads, *rest_pieces)
+    rest_pieces = scatter(rest_parts, 1)
+    for at in range(2, len(phases)):
+        pieces = scatter(parts, at - 1)
+        grads, *pieces = together(grads, *pieces)
+        parts = scatter_phase(pieces, phases[at], count)
+        rest_parts = scatter_phase(rest_pieces, phases[at], count)
+        if at < len(phases) - 1:
+            rest_pieces = scatter(rest_parts, at)
     input_grad = pl.pallas_call(
         input_kernel,
         grid=(steps,),
@@ -766,21 +733,16 @@
         ],
         out_specs=down,
         out_shape=shaped((slots, D), f32),
-        compiler_params=params_of(),
+        compiler_params=params_of(20),
         name="input_grad",
     )(grads, pair_weights, grad_both)
-
+    input_grad, *rest_parts = together(input_grad, *rest_parts)
     input_grad, *parts = together(input_grad, *parts)
-    for at in range(2, len(phases)):
-        pieces = scatter(parts, at - 1, True)
-        parts = scatter_phase(pieces, phases[at], count)
-        rest_parts = scatter_phase(rest_pieces, phases[at], count)
-        rest_pieces = scatter(rest_parts, at, False)
-    (own_rest,) = rest_pieces
+    (own_rest,) = scatter(rest_parts, len(phases) - 1)
     own_first, share = pl.pallas_call(
         own_kernel,
         out_shape=[shaped((own_count, 3 * D), f32), shaped((own_count, LANES), f32)],
-        compiler_params=params_of(),
+        compiler_params=params_of(8),
         name="own",
     )(*parts, own_rest)
     shares = share
@@ -788,13 +750,13 @@
         shares = jnp.concatenate(gather_phase(shares, masks, count), axis=0)
     vector_grads, norms = pl.pallas_call(
         functools.partial(settle_kernel, codes),
-        in_specs=[smem()] + [whole((D // 2, LANES))] * 2,
+        in_specs=[smem()] + [resident()] * 2,
         out_specs=[whole((VECTORS, D)), whole((8, LANES))],
         out_shape=[shaped((VECTORS, D), f32), shaped((8, LANES), f32)],
         scratch_shapes=[pltpu.VMEM((D, LANES), f32)],
-        compiler_params=params_of(),
+        compiler_params=params_of(8),
         name="settle",
-    )(origin, *to_kernel(*gather_phase(shares, phases[0], count)))
+    )(origin, *to_kernel(gather_phase(shares, phases[0], count), 2))
     grad_norm = norms[0, 0]
     vector_grads = vector_grads.T
 

time: 230 us -> 206 us (0.90)
  Pallas kernels: 132 us -> 112 us
  local copies, waits for them, and re-layouts: 9.16 us -> 2.59 us
  starting transfers between devices: 45.9 us -> 49.9 us
    pallas_call x3 -> x1, Pallas kernels: 62.5 us -> 52.7 us  [body(): pl.pallas_call(functools.partial(feed_kernel, codes, len(rest_pieces)), g...]
    unnamed x40 -> x35, local copies, waits for them, and re-layouts: 7.2 us -> 1.57 us
    ppermute x35 -> x38, starting transfers between devices: 45.9 us -> 49.9 us  [exchange(): return lax.ppermute(values, 'dp', [(at, at ^ bit) for at in range(count)])]
    pallas_call x1, Pallas kernels: 9.62 us -> 6.41 us  [body(): pl.pallas_call(input_kernel, grid=(steps,), in_specs=[pl.BlockSpec((PAIRS...]
    ppermute x35 -> x38, waiting for transfers between devices: 32.6 us -> 32.3 us  [exchange(): return lax.ppermute(values, 'dp', [(at, at ^ bit) for at in range(count)])]
  transfers between devices with their start and end apart: 35 -> 38, of which waited for: 17 -> 18; matrix products, arithmetic and copies ran while one was open for 1% -> 1% of each run, Pallas kernels for 30% -> 28%
where the time goes in v4:
time: 206 us
  Pallas kernels  112 us (54%)
  starting transfers between devices  49.9 us (24%)
  waiting for transfers between devices  32.3 us (16%)
  other arithmetic  7.08 us (3%)
  local copies, waits for them, and re-layouts  2.59 us (1%)
  between operations  2.34 us (1%)
    pallas_call x1, Pallas kernels, body(): pl.pallas_call(functools.partial(feed_kernel, codes, len(rest_pieces)), g...  52.7 us
    ppermute x38, starting transfers between devices, exchange(): return lax.ppermute(values, 'dp', [(at, at ^ bit) for at in range(count)])  49.9 us
    ppermute x38, waiting for transfers between devices, exchange(): return lax.ppermute(values, 'dp', [(at, at ^ bit) for at in range(count)])  32.3 us
    pallas_call x1, Pallas kernels, body(): pl.pallas_call(functools.partial(attend_back_kernel, codes), grid=(PAIRS,...  26.1 us
    pallas_call x1, Pallas kernels, body(): pl.pallas_call(attend_kernel, grid=(PAIRS,), in_specs=[smem(), whole((blo...  15.1 us
    pallas_call x1, Pallas kernels, body(): pl.pallas_call(functools.partial(project_kernel, codes), grid=(steps,), i...  10.3 us
    pallas_call x1, Pallas kernels, body(): pl.pallas_call(input_kernel, grid=(steps,), in_specs=[pl.BlockSpec((PAIRS...  6.41 us
    convert_element_type x4, other arithmetic, cut_sum(): sum((part[at * rows:(at + 1) * rows].astype(f32) for part in parts))  4.13 us
  transfers between devices with their start and end apart: 38, of which 18 were waited for; matrix products, arithmetic and copies ran while one was open for 1% of the time, Pallas kernels for 28%

profile of v4, /device:TPU:0, one launch (start us, length us, event | category | flops | bytes accessed | tf_op | source)
XLA Modules:
  0.0 205.7 jit_solution(10873440410486240639)
XLA Ops:
  0.6 1.0 convert_element_type.209
  2.0 5.1 %collective-permute-start.2 = (bf16[16,1664]{1,0:T(8,128)(2,1)S(1)}, bf16[16,1664]{1,0:T(8,128)(2,1)S(1)}, u32[]{:S(2)}, u32[]{:S(2)}) collective-permute-start(bf16[16,1664]{1,0:T(8,128)(2,1)S(1)} %pad_maximum_fusion.3), channel_id=1, source_target_pairs={{0,24},{1,25},{2,26},{3,27},{4,28},{5,29},{6,30},{7,31},{8,16},{9,... | collective-permute-start | bytes 159752 | tf_op jit(solution)/shard_map/ppermute | solution.py:484
  7.8 1.6 collective-permute-done.2
  9.4 2.7 %collective-permute-done.1 = bf16[16,1664]{1,0:T(8,128)(2,1)S(1)} collective-permute-done((bf16[16,1664]{1,0:T(8,128)(2,1)S(1)}, bf16[16,1664]{1,0:T(8,128)(2,1)S(1)}, u32[]{:S(2)}, u32[]{:S(2)}) %collective-permute-start.1) | collective-permute-done | bytes 53280 | tf_op jit(solution)/shard_map/ppermute | solution.py:484
  12.2 2.4 %collective-permute-start.8 = (bf16[16,4608]{1,0:T(8,128)(2,1)S(1)}, bf16[16,4608]{1,0:T(8,128)(2,1)S(1)}, u32[]{:S(2)}, u32[]{:S(2)}) collective-permute-start(bf16[16,4608]{1,0:T(8,128)(2,1)S(1)} %slice.214), channel_id=1, source_target_pairs={{0,24},{1,25},{2,26},{3,27},{4,28},{5,29},{6,30},{7,31},{8,16},{9,... | collective-permute-start | bytes 442376 | tf_op jit(solution)/shard_map/ppermute | solution.py:484
  14.6 2.0 collective-permute-start.6
  16.6 2.4 %collective-permute-start.5 = (bf16[64,1664]{1,0:T(8,128)(2,1)S(1)}, bf16[64,1664]{1,0:T(8,128)(2,1)S(1)}, u32[]{:S(2)}, u32[]{:S(2)}) collective-permute-start(bf16[64,1664]{1,0:T(8,128)(2,1)S(1)} %pad_maximum_fusion.2), channel_id=1, source_target_pairs={{0,6},{1,7},{2,4},{3,5},{4,2},{5,3},{6,0},{7,1},{8,14},{9,15},{10,... | collective-permute-start | bytes 638984 | tf_op jit(solution)/shard_map/ppermute | solution.py:484
  19.6 1.3 collective-permute-done.8
  20.9 1.5 collective-permute-start.3
  22.3 4.3 %collective-permute-done.7 = bf16[16,4608]{1,0:T(8,128)(2,1)S(1)} collective-permute-done((bf16[16,4608]{1,0:T(8,128)(2,1)S(1)}, bf16[16,4608]{1,0:T(8,128)(2,1)S(1)}, u32[]{:S(2)}, u32[]{:S(2)}) %collective-permute-start.7) | collective-permute-done | bytes 147488 | tf_op jit(solution)/shard_map/ppermute | solution.py:484
  26.7 0.7 collective-permute-done.4
  27.6 1.8 collective-permute-start.12
  29.4 1.2 collective-permute-start.11
  32.4 10.3 %project.1 = (bf16[512,2048]{1,0:T(8,128)(2,1)}, bf16[512,2048]{1,0:T(8,128)(2,1)}, bf16[512,2048]{1,0:T(8,128)(2,1)}, bf16[512,2048]{1,0:T(8,128)(2,1)}, bf16[2...) custom-call(s32[1]{0:T(128)} %bitcast.mine_ref.refs_0_, ...), custom_call_target="tpu_custom_call" | custom-call | tf_op jit(solution)/shard_map/project/pallas_call | solution.py:603
  42.8 0.7 copy-done.3
  43.5 15.1 %attend.1 = (bf16[512,2048]{1,0:T(8,128)(2,1)}, f32[4,16,256]{2,1,0:T(8,128)}) custom-call(s32[3]{0:T(128)} %pad_add_fusion.limits_ref.refs_1_, s32[16,128]{1,0:T(8,128)} %bitcast.6, bf16[512,2048]{1,0:T(8,128)(2,1)} %get-tuple-element.78.qt_ref, bf16[2048,512]{1,0:T(8,128)(2,1)} %get-tuple-element.79.k_ref, bf16[512,2048]{1,0:T(8,128)(2,1)} %get-tuple-element.80.vt_ref), custom_call_target="tpu_custom_call" | custom-call | tf_op jit(solution)/shard_map/attend/pallas_call | solution.py:624
  59.6 1.3 collective-permute-done.14.refs_11_
  61.6 0.8 collective-permute-done.16.refs_13_
  62.4 0.8 copy-done.11
  63.2 52.7 %feed.1 = (bf16[2048,512]{1,0:T(8,128)(2,1)}, bf16[512,2048]{1,0:T(8,128)(2,1)}, bf16[512,2048]{1,0:T(8,128)(2,1)}, bf16[256,4608]{1,0:T(8,128)(2,1)}, bf16[256,4608]{1,0:T(8,128)(2,1)}, /*index=5*/f32[512,128]{1,0:T(8,128)}) custom-call(s32[1]{0:T(128)} %bitcast.mine_ref.refs_0_, s32[3]{0:T(128)} %pad_add_fusion.limits_ref.refs_1_, ...), custom_call_target="tpu_custom_call" | custom-call | tf_op jit(solution)/shard_map/feed/pallas_call | solution.py:639
  116.3 4.4 %collective-permute-done.17 = bf16[256,4608]{1,0:T(8,128)(2,1)S(1)} collective-permute-done((bf16[256,4608]{1,0:T(8,128)(2,1)}, bf16[256,4608]{1,0:T(8,128)(2,1)S(1)}, u32[]{:S(2)}, u32[]{:S(2)}) %collective-permute-start.17) | collective-permute-done | bytes 2359328 | tf_op jit(solution)/shard_map/ppermute | solution.py:484
  120.7 2.1 %add_convert_fusion = (bf16[64,4608]{1,0:T(8,128)(2,1)S(1)}, bf16[64,4608]{1,0:T(8,128)(2,1)S(1)}, bf16[64,4608]{1,0:T(8,128)(2,1)S(1)}, bf16[64,4608]{1,0:T(8,128)(2,1)S(1)}) fusion(bf16[256,4608]{1,0:T(8,128)(2,1)S(1)} %collective-permute-done.17, bf16[256,4608]{1,0:T(8,128)(2,1)} %get-tuple-element.93), kind=kLoop, calls=%fused_computation | loop fusion | flops 4718592 | bytes 7077888 | tf_op jit(solution)/shard_map/convert_element_type | solution.py:516
  122.9 1.6 collective-permute-start.18
  124.4 0.8 collective-permute-start.19
  125.2 1.2 collective-permute-start.20
  126.4 26.1 %attend_back.1 = (bf16[4,384,2048]{2,1,0:T(8,128)(2,1)}, bf16[256,1664]{1,0:T(8,128)(2,1)}, bf16[256,1664]{1,0:T(8,128)(2,1)}) custom-call(s32[1]{0:T(128)} %bitcast.mine_ref.refs_0_, s32[3]{0:T(128)} %pad_add_fusion.limits_ref.refs_1_, s32[16,128]{1,0:T(8,128)} %bitcast.7, bf16[512,2048]{1,0:T(8,128)(2,1)} %get-tuple-element.77.refs_2_.xt_ref, ...), custom_call_target="tpu_custom_call" | custom-call | tf_op jit(solution)/shard_map/attend_back/pallas_call | solution.py:683
  152.6 2.6 %collective-permute-done.21 = bf16[256,1664]{1,0:T(8,128)(2,1)S(1)} collective-permute-done((bf16[256,1664]{1,0:T(8,128)(2,1)}, bf16[256,1664]{1,0:T(8,128)(2,1)S(1)}, u32[]{:S(2)}, u32[]{:S(2)}) %collective-permute-start.21) | collective-permute-done | bytes 852000 | tf_op jit(solution)/shard_map/ppermute | solution.py:484
  155.2 1.6 add_convert_fusion.4
  156.8 1.6 collective-permute-start.22
  158.3 0.8 collective-permute-start.23
  159.1 1.2 collective-permute-start.24
  160.6 2.2 %collective-permute-start.27 = (bf16[16,4608]{1,0:T(8,128)(2,1)S(1)}, bf16[16,4608]{1,0:T(8,128)(2,1)S(1)}, u32[]{:S(2)}, u32[]{:S(2)}) collective-permute-start(bf16[16,4608]{1,0:T(8,128)(2,1)S(1)} %get-tuple-element.148), channel_id=1, source_target_pairs={{0,24},{1,25},{2,26},{3,27},{4,28},{5,29},{6,30},{7,31},{8,16},{9,... | collective-permute-start | bytes 442376 | tf_op jit(solution)/shard_map/ppermute | solution.py:484
  162.8 3.4 %collective-permute-start.26 = (bf16[16,4608]{1,0:T(8,128)(2,1)S(1)}, bf16[16,4608]{1,0:T(8,128)(2,1)S(1)}, u32[]{:S(2)}, u32[]{:S(2)}) collective-permute-start(bf16[16,4608]{1,0:T(8,128)(2,1)S(1)} %get-tuple-element.149), channel_id=1, source_target_pairs={{0,16},{1,17},{2,18},{3,19},{4,20},{5,21},{6,22},{7,23},{8,24},{9,... | collective-permute-start | bytes 442376 | tf_op jit(solution)/shard_map/ppermute | solution.py:484
  166.2 2.8 %collective-permute-start.25 = (bf16[16,4608]{1,0:T(8,128)(2,1)S(1)}, bf16[16,4608]{1,0:T(8,128)(2,1)S(1)}, u32[]{:S(2)}, u32[]{:S(2)}) collective-permute-start(bf16[16,4608]{1,0:T(8,128)(2,1)S(1)} %get-tuple-element.150), channel_id=1, source_target_pairs={{0,8},{1,9},{2,10},{3,11},{4,12},{5,13},{6,14},{7,15},{8,0},{9,1},... | collective-permute-start | bytes 442376 | tf_op jit(solution)/shard_map/ppermute | solution.py:484
  169.0 1.0 collective-permute-done.23
  170.0 4.1 %collective-permute-start.28 = (bf16[16,1664]{1,0:T(8,128)(2,1)S(1)}, bf16[16,1664]{1,0:T(8,128)(2,1)S(1)}, u32[]{:S(2)}, u32[]{:S(2)}) collective-permute-start(bf16[16,1664]{1,0:T(8,128)(2,1)S(1)} %get-tuple-element.125), channel_id=1, source_target_pairs={{0,8},{1,9},{2,10},{3,11},{4,12},{5,13},{6,14},{7,15},{8,0},{9,1},... | collective-permute-start | bytes 159752 | tf_op jit(solution)/shard_map/ppermute | solution.py:484
  174.8 6.4 %input_grad.1 = f32[2048,512]{1,0:T(8,128)} custom-call(bf16[4,384,2048]{2,1,0:T(8,128)(2,1)S(1)} %copy-done, bf16[512,1536]{1,0:T(8,128)(2,1)S(1)} %copy-done.2, bf16[512,2048]{1,0:T(8,128)(2,1)S(1)} %copy-done.1), custom_call_target="tpu_custom_call" | custom-call | tf_op jit(solution)/shard_map/input_grad/pallas_call | solution.py:726
  181.2 1.8 collective-permute-start.30
  183.2 4.1 %collective-permute-done.30.refs_3_ = bf16[16,1664]{1,0:T(8,128)(2,1)S(1)} collective-permute-done((bf16[16,1664]{1,0:T(8,128)(2,1)S(1)}, bf16[16,1664]{1,0:T(8,128)(2,1)S(1)}, u32[]{:S(2)}, u32[]{:S(2)}) %collective-permute-start.30) | collective-permute-done | bytes 53280 | tf_op jit(solution)/shard_map/ppermute | solution.py:484
  187.4 1.9 collective-permute-start.33
  189.7 2.2 %collective-permute-start.31 = (f32[16,128]{1,0:T(8,128)S(1)}, f32[16,128]{1,0:T(8,128)S(1)}, u32[]{:S(2)}, u32[]{:S(2)}) collective-permute-start(f32[16,128]{1,0:T(8,128)S(1)} %get-tuple-element.137), channel_id=1, source_target_pairs={{0,8},{1,9},{2,10},{3,11},{4,12},{5,13},{6,14},{7,15},{8,0},{9,1},... | collective-permute-start | bytes 24584 | tf_op jit(solution)/shard_map/ppermute | solution.py:484
  191.9 1.6 collective-permute-done.31
  193.9 1.3 collective-permute-start.34
  195.2 1.8 collective-permute-start.36
  197.8 3.0 %collective-permute-done.35 = f32[64,128]{1,0:T(8,128)S(1)} collective-permute-done((f32[64,128]{1,0:T(8,128)S(1)}, f32[64,128]{1,0:T(8,128)S(1)}, u32[]{:S(2)}, u32[]{:S(2)}) %collective-permute-start.35) | collective-permute-done | bytes 32800 | tf_op jit(solution)/shard_map/ppermute | solution.py:484
  200.9 1.3 collective-permute-done.37.far_ref
  202.2 0.8 settle.1
  204.5 1.1 add_multiply_fusion
  (92 shorter events, 8.8 us)
Async XLA Ops:
  2.0 7.4 %collective-permute-start.2 = (bf16[16,1664]{1,0:T(8,128)(2,1)S(1)}, bf16[16,1664]{1,0:T(8,128)(2,1)S(1)}, u32[]{:S(2)}, u32[]{:S(2)}) collective-permute-start(bf16[16,1664]{1,0:T(8,128)(2,1)S(1)} %pad_maximum_fusion.3), channel_id=1, source_target_pairs={{0,24},{1,25},{2,26},{3,27},{4,28},{5,29},{6,30},{7,31},{8,16},{9,... | collective-permute-start | bytes 159752 | tf_op jit(solution)/shard_map/ppermute | solution.py:484
  7.1 5.0 %collective-permute-start.1 = (bf16[16,1664]{1,0:T(8,128)(2,1)S(1)}, bf16[16,1664]{1,0:T(8,128)(2,1)S(1)}, u32[]{:S(2)}, u32[]{:S(2)}) collective-permute-start(bf16[16,1664]{1,0:T(8,128)(2,1)S(1)} %pad_maximum_fusion.3), channel_id=1, source_target_pairs={{0,16},{1,17},{2,18},{3,19},{4,20},{5,21},{6,22},{7,23},{8,24},{9,... | collective-permute-start | bytes 159752 | tf_op jit(solution)/shard_map/ppermute | solution.py:484
  7.1 5.0 %collective-permute-start = (bf16[16,1664]{1,0:T(8,128)(2,1)S(1)}, bf16[16,1664]{1,0:T(8,128)(2,1)S(1)}, u32[]{:S(2)}, u32[]{:S(2)}) collective-permute-start(bf16[16,1664]{1,0:T(8,128)(2,1)S(1)} %pad_maximum_fusion.3), channel_id=1, source_target_pairs={{0,8},{1,9},{2,10},{3,11},{4,12},{5,13},{6,14},{7,15},{8,0},{9,1},... | collective-permute-start | bytes 159752 | tf_op jit(solution)/shard_map/ppermute | solution.py:484
  7.8 24.1 %copy-start.14 = (s32[2]{0:T(128)S(1)}, s32[2]{0:T(128)}, u32[]{:S(2)}) copy-start(s32[2]{0:T(128)} %param.11) | copy-start | bytes 28
  12.2 8.7 %collective-permute-start.8 = (bf16[16,4608]{1,0:T(8,128)(2,1)S(1)}, bf16[16,4608]{1,0:T(8,128)(2,1)S(1)}, u32[]{:S(2)}, u32[]{:S(2)}) collective-permute-start(bf16[16,4608]{1,0:T(8,128)(2,1)S(1)} %slice.214), channel_id=1, source_target_pairs={{0,24},{1,25},{2,26},{3,27},{4,28},{5,29},{6,30},{7,31},{8,16},{9,... | collective-permute-start | bytes 442376 | tf_op jit(solution)/shard_map/ppermute | solution.py:484
  14.6 12.1 %collective-permute-start.7 = (bf16[16,4608]{1,0:T(8,128)(2,1)S(1)}, bf16[16,4608]{1,0:T(8,128)(2,1)S(1)}, u32[]{:S(2)}, u32[]{:S(2)}) collective-permute-start(bf16[16,4608]{1,0:T(8,128)(2,1)S(1)} %slice.214), channel_id=1, source_target_pairs={{0,16},{1,17},{2,18},{3,19},{4,20},{5,21},{6,22},{7,23},{8,24},{9,... | collective-permute-start | bytes 442376 | tf_op jit(solution)/shard_map/ppermute | solution.py:484
  14.6 12.1 %collective-permute-start.6 = (bf16[16,4608]{1,0:T(8,128)(2,1)S(1)}, bf16[16,4608]{1,0:T(8,128)(2,1)S(1)}, u32[]{:S(2)}, u32[]{:S(2)}) collective-permute-start(bf16[16,4608]{1,0:T(8,128)(2,1)S(1)} %slice.214), channel_id=1, source_target_pairs={{0,8},{1,9},{2,10},{3,11},{4,12},{5,13},{6,14},{7,15},{8,0},{9,1},... | collective-permute-start | bytes 442376 | tf_op jit(solution)/shard_map/ppermute | solution.py:484
  16.6 10.1 %collective-permute-start.5 = (bf16[64,1664]{1,0:T(8,128)(2,1)S(1)}, bf16[64,1664]{1,0:T(8,128)(2,1)S(1)}, u32[]{:S(2)}, u32[]{:S(2)}) collective-permute-start(bf16[64,1664]{1,0:T(8,128)(2,1)S(1)} %pad_maximum_fusion.2), channel_id=1, source_target_pairs={{0,6},{1,7},{2,4},{3,5},{4,2},{5,3},{6,0},{7,1},{8,14},{9,15},{10,... | collective-permute-start | bytes 638984 | tf_op jit(solution)/shard_map/ppermute | solution.py:484
  19.1 8.3 %collective-permute-start.4 = (bf16[64,1664]{1,0:T(8,128)(2,1)S(1)}, bf16[64,1664]{1,0:T(8,128)(2,1)S(1)}, u32[]{:S(2)}, u32[]{:S(2)}) collective-permute-start(bf16[64,1664]{1,0:T(8,128)(2,1)S(1)} %pad_maximum_fusion.2), channel_id=1, source_target_pairs={{0,4},{1,5},{2,6},{3,7},{4,0},{5,1},{6,2},{7,3},{8,12},{9,13},{10,... | collective-permute-start | bytes 638984 | tf_op jit(solution)/shard_map/ppermute | solution.py:484
  20.9 6.6 %collective-permute-start.3 = (bf16[64,1664]{1,0:T(8,128)(2,1)S(1)}, bf16[64,1664]{1,0:T(8,128)(2,1)S(1)}, u32[]{:S(2)}, u32[]{:S(2)}) collective-permute-start(bf16[64,1664]{1,0:T(8,128)(2,1)S(1)} %pad_maximum_fusion.2), channel_id=1, source_target_pairs={{0,2},{1,3},{2,0},{3,1},{4,6},{5,7},{6,4},{7,5},{8,10},{9,11},{10,... | collective-permute-start | bytes 638984 | tf_op jit(solution)/shard_map/ppermute | solution.py:484
  26.7 16.1 %copy-start.4 = (bf16[64,4608]{1,0:T(8,128)(2,1)}, bf16[64,4608]{1,0:T(8,128)(2,1)S(1)}, u32[]{:S(2)}) copy-start(bf16[64,4608]{1,0:T(8,128)(2,1)S(1)} %pad_maximum_fusion.1.refs_6_) | copy-start | bytes 1769476
  27.6 4.9 %collective-permute-start.9 = (bf16[256,1664]{1,0:T(8,128)(2,1)S(1)}, bf16[256,1664]{1,0:T(8,128)(2,1)S(1)}, u32[]{:S(2)}, u32[]{:S(2)}) collective-permute-start(bf16[256,1664]{1,0:T(8,128)(2,1)S(1)} %pad_maximum_fusion.near_ref), channel_id=1, source_target_pairs={{0,1},{1,0},{2,3},{3,2},{4,5},{5,4},{6,7},{7,6},{8,9},{9,8},{10,11... | collective-permute-start | bytes 2555912 | tf_op jit(solution)/shard_map/ppermute | solution.py:484
  27.6 30.9 %collective-permute-start.12 = (bf16[64,4608]{1,0:T(8,128)(2,1)S(1)}, bf16[64,4608]{1,0:T(8,128)(2,1)S(1)}, u32[]{:S(2)}, u32[]{:S(2)}) collective-permute-start(bf16[64,4608]{1,0:T(8,128)(2,1)S(1)} %pad_maximum_fusion.1.refs_6_), channel_id=1, source_target_pairs={{0,6},{1,7},{2,4},{3,5},{4,2},{5,3},{6,0},{7,1},{8,14},{9,15},{10,... | collective-permute-start | bytes 1769480 | tf_op jit(solution)/shard_map/ppermute | solution.py:484
  29.4 29.2 %collective-permute-start.11 = (bf16[64,4608]{1,0:T(8,128)(2,1)S(1)}, bf16[64,4608]{1,0:T(8,128)(2,1)S(1)}, u32[]{:S(2)}, u32[]{:S(2)}) collective-permute-start(bf16[64,4608]{1,0:T(8,128)(2,1)S(1)} %pad_maximum_fusion.1.refs_6_), channel_id=1, source_target_pairs={{0,4},{1,5},{2,6},{3,7},{4,0},{5,1},{6,2},{7,3},{8,12},{9,13},{10,... | collective-permute-start | bytes 1769480 | tf_op jit(solution)/shard_map/ppermute | solution.py:484
  30.7 28.0 %collective-permute-start.10 = (bf16[64,4608]{1,0:T(8,128)(2,1)S(1)}, bf16[64,4608]{1,0:T(8,128)(2,1)}, u32[]{:S(2)}, u32[]{:S(2)}) collective-permute-start(bf16[64,4608]{1,0:T(8,128)(2,1)S(1)} %pad_maximum_fusion.1.refs_6_), channel_id=1, source_target_pairs={{0,2},{1,3},{2,0},{3,1},{4,6},{5,7},{6,4},{7,5},{8,10},{9,11},{10,... | collective-permute-start | bytes 1769480 | tf_op jit(solution)/shard_map/ppermute | solution.py:484
  32.4 27.2 %collective-permute-start.13 = (bf16[64,4608]{1,0:T(8,128)(2,1)S(1)}, bf16[64,4608]{1,0:T(8,128)(2,1)S(1)}, u32[]{:S(2)}, u32[]{:S(2)}) collective-permute-start(bf16[64,4608]{1,0:T(8,128)(2,1)S(1)} %pad_maximum_fusion.1.refs_6_), channel_id=1, source_target_pairs={{0,1},{1,0},{2,3},{3,2},{4,5},{5,4},{6,7},{7,6},{8,9},{9,8},{10,11... | collective-permute-start | bytes 1769480 | tf_op jit(solution)/shard_map/ppermute | solution.py:484
  58.6 3.8 %copy-start.6 = (bf16[64,4608]{1,0:T(8,128)(2,1)}, bf16[64,4608]{1,0:T(8,128)(2,1)S(1)}, u32[]{:S(2)}) copy-start(bf16[64,4608]{1,0:T(8,128)(2,1)S(1)} %collective-permute-done.12.refs_9_) | copy-start | bytes 1769476
  58.6 3.8 %copy-start.7 = (bf16[64,4608]{1,0:T(8,128)(2,1)}, bf16[64,4608]{1,0:T(8,128)(2,1)S(1)}, u32[]{:S(2)}) copy-start(bf16[64,4608]{1,0:T(8,128)(2,1)S(1)} %collective-permute-done.11.refs_8_) | copy-start | bytes 1769476
  58.6 2.3 %collective-permute-start.14 = (bf16[64,4608]{1,0:T(8,128)(2,1)}, bf16[64,4608]{1,0:T(8,128)(2,1)S(1)}, u32[]{:S(2)}, u32[]{:S(2)}) collective-permute-start(bf16[64,4608]{1,0:T(8,128)(2,1)} %collective-permute-done.10.refs_7_), channel_id=1, source_target_pairs={{0,1},{1,0},{2,3},{3,2},{4,5},{5,4},{6,7},{7,6},{8,9},{9,8},{10,11... | collective-permute-start | bytes 1769480 | tf_op jit(solution)/shard_map/ppermute | solution.py:484
  59.1 2.5 %collective-permute-start.15 = (bf16[64,4608]{1,0:T(8,128)(2,1)S(1)}, bf16[64,4608]{1,0:T(8,128)(2,1)S(1)}, u32[]{:S(2)}, u32[]{:S(2)}) collective-permute-start(bf16[64,4608]{1,0:T(8,128)(2,1)S(1)} %collective-permute-done.11.refs_8_), channel_id=1, source_target_pairs={{0,1},{1,0},{2,3},{3,2},{4,5},{5,4},{6,7},{7,6},{8,9},{9,8},{10,11... | collective-permute-start | bytes 1769480 | tf_op jit(solution)/shard_map/ppermute | solution.py:484
  59.2 3.2 %collective-permute-start.16 = (bf16[64,4608]{1,0:T(8,128)(2,1)S(1)}, bf16[64,4608]{1,0:T(8,128)(2,1)S(1)}, u32[]{:S(2)}, u32[]{:S(2)}) collective-permute-start(bf16[64,4608]{1,0:T(8,128)(2,1)S(1)} %collective-permute-done.12.refs_9_), channel_id=1, source_target_pairs={{0,1},{1,0},{2,3},{3,2},{4,5},{5,4},{6,7},{7,6},{8,9},{9,8},{10,11... | collective-permute-start | bytes 1769480 | tf_op jit(solution)/shard_map/ppermute | solution.py:484
  115.9 4.8 %collective-permute-start.17 = (bf16[256,4608]{1,0:T(8,128)(2,1)}, bf16[256,4608]{1,0:T(8,128)(2,1)S(1)}, u32[]{:S(2)}, u32[]{:S(2)}) collective-permute-start(bf16[256,4608]{1,0:T(8,128)(2,1)} %get-tuple-element.94), channel_id=1, source_target_pairs={{0,1},{1,0},{2,3},{3,2},{4,5},{5,4},{6,7},{7,6},{8,9},{9,8},{10,11... | collective-permute-start | bytes 7077896 | tf_op jit(solution)/shard_map/ppermute | solution.py:484
  122.9 29.6 %collective-permute-start.18 = (bf16[64,4608]{1,0:T(8,128)(2,1)S(1)}, bf16[64,4608]{1,0:T(8,128)(2,1)S(1)}, u32[]{:S(2)}, u32[]{:S(2)}) collective-permute-start(bf16[64,4608]{1,0:T(8,128)(2,1)S(1)} %get-tuple-element.102), channel_id=1, source_target_pairs={{0,2},{1,3},{2,0},{3,1},{4,6},{5,7},{6,4},{7,5},{8,10},{9,11},{10,... | collective-permute-start | bytes 1769480 | tf_op jit(solution)/shard_map/ppermute | solution.py:484
  124.4 28.1 %collective-permute-start.19 = (bf16[64,4608]{1,0:T(8,128)(2,1)S(1)}, bf16[64,4608]{1,0:T(8,128)(2,1)S(1)}, u32[]{:S(2)}, u32[]{:S(2)}) collective-permute-start(bf16[64,4608]{1,0:T(8,128)(2,1)S(1)} %get-tuple-element.103), channel_id=1, source_target_pairs={{0,4},{1,5},{2,6},{3,7},{4,0},{5,1},{6,2},{7,3},{8,12},{9,13},{10,... | collective-permute-start | bytes 1769480 | tf_op jit(solution)/shard_map/ppermute | solution.py:484
  125.2 27.3 %collective-permute-start.20 = (bf16[64,4608]{1,0:T(8,128)(2,1)S(1)}, bf16[64,4608]{1,0:T(8,128)(2,1)S(1)}, u32[]{:S(2)}, u32[]{:S(2)}) collective-permute-start(bf16[64,4608]{1,0:T(8,128)(2,1)S(1)} %get-tuple-element.104), channel_id=1, source_target_pairs={{0,6},{1,7},{2,4},{3,5},{4,2},{5,3},{6,0},{7,1},{8,14},{9,15},{10,... | collective-permute-start | bytes 1769480 | tf_op jit(solution)/shard_map/ppermute | solution.py:484
  126.4 48.4 %copy-start.1 = (bf16[512,2048]{1,0:T(8,128)(2,1)S(1)}, bf16[512,2048]{1,0:T(8,128)(2,1)}, u32[]{:S(2)}) copy-start(bf16[512,2048]{1,0:T(8,128)(2,1)} %get-tuple-element.118.both_ref) | copy-start | bytes 6291460
  126.4 48.4 %copy-start.2 = (bf16[512,1536]{1,0:T(8,128)(2,1)S(1)}, bf16[512,1536]{1,0:T(8,128)(2,1)}, u32[]{:S(2)}) copy-start(bf16[512,1536]{1,0:T(8,128)(2,1)} %get-tuple-element.117.weights_ref) | copy-start | bytes 4718596
  152.5 2.7 %collective-permute-start.21 = (bf16[256,1664]{1,0:T(8,128)(2,1)}, bf16[256,1664]{1,0:T(8,128)(2,1)S(1)}, u32[]{:S(2)}, u32[]{:S(2)}) collective-permute-start(bf16[256,1664]{1,0:T(8,128)(2,1)} %get-tuple-element.106), channel_id=1, source_target_pairs={{0,1},{1,0},{2,3},{3,2},{4,5},{5,4},{6,7},{7,6},{8,9},{9,8},{10,11... | collective-permute-start | bytes 2555912 | tf_op jit(solution)/shard_map/ppermute | solution.py:484
  155.2 19.6 %copy-start = (bf16[4,384,2048]{2,1,0:T(8,128)(2,1)S(1)}, bf16[4,384,2048]{2,1,0:T(8,128)(2,1)}, u32[]{:S(2)}) copy-start(bf16[4,384,2048]{2,1,0:T(8,128)(2,1)} %get-tuple-element.116.grads_ref) | copy-start | bytes 18874372
  156.8 9.4 %collective-permute-start.22 = (bf16[64,1664]{1,0:T(8,128)(2,1)S(1)}, bf16[64,1664]{1,0:T(8,128)(2,1)S(1)}, u32[]{:S(2)}, u32[]{:S(2)}) collective-permute-start(bf16[64,1664]{1,0:T(8,128)(2,1)S(1)} %get-tuple-element.113), channel_id=1, source_target_pairs={{0,2},{1,3},{2,0},{3,1},{4,6},{5,7},{6,4},{7,5},{8,10},{9,11},{10,... | collective-permute-start | bytes 638984 | tf_op jit(solution)/shard_map/ppermute | solution.py:484
  158.3 11.6 %collective-permute-start.23 = (bf16[64,1664]{1,0:T(8,128)(2,1)S(1)}, bf16[64,1664]{1,0:T(8,128)(2,1)S(1)}, u32[]{:S(2)}, u32[]{:S(2)}) collective-permute-start(bf16[64,1664]{1,0:T(8,128)(2,1)S(1)} %get-tuple-element.114), channel_id=1, source_target_pairs={{0,4},{1,5},{2,6},{3,7},{4,0},{5,1},{6,2},{7,3},{8,12},{9,13},{10,... | collective-permute-start | bytes 638984 | tf_op jit(solution)/shard_map/ppermute | solution.py:484
  159.1 10.8 %collective-permute-start.24 = (bf16[64,1664]{1,0:T(8,128)(2,1)S(1)}, bf16[64,1664]{1,0:T(8,128)(2,1)S(1)}, u32[]{:S(2)}, u32[]{:S(2)}) collective-permute-start(bf16[64,1664]{1,0:T(8,128)(2,1)S(1)} %get-tuple-element.115), channel_id=1, source_target_pairs={{0,6},{1,7},{2,4},{3,5},{4,2},{5,3},{6,0},{7,1},{8,14},{9,15},{10,... | collective-permute-start | bytes 638984 | tf_op jit(solution)/shard_map/ppermute | solution.py:484
  160.6 20.6 %collective-permute-start.27 = (bf16[16,4608]{1,0:T(8,128)(2,1)S(1)}, bf16[16,4608]{1,0:T(8,128)(2,1)S(1)}, u32[]{:S(2)}, u32[]{:S(2)}) collective-permute-start(bf16[16,4608]{1,0:T(8,128)(2,1)S(1)} %get-tuple-element.148), channel_id=1, source_target_pairs={{0,24},{1,25},{2,26},{3,27},{4,28},{5,29},{6,30},{7,31},{8,16},{9,... | collective-permute-start | bytes 442376 | tf_op jit(solution)/shard_map/ppermute | solution.py:484
  162.8 20.3 %collective-permute-start.26 = (bf16[16,4608]{1,0:T(8,128)(2,1)S(1)}, bf16[16,4608]{1,0:T(8,128)(2,1)S(1)}, u32[]{:S(2)}, u32[]{:S(2)}) collective-permute-start(bf16[16,4608]{1,0:T(8,128)(2,1)S(1)} %get-tuple-element.149), channel_id=1, source_target_pairs={{0,16},{1,17},{2,18},{3,19},{4,20},{5,21},{6,22},{7,23},{8,24},{9,... | collective-permute-start | bytes 442376 | tf_op jit(solution)/shard_map/ppermute | solution.py:484
  166.2 16.9 %collective-permute-start.25 = (bf16[16,4608]{1,0:T(8,128)(2,1)S(1)}, bf16[16,4608]{1,0:T(8,128)(2,1)S(1)}, u32[]{:S(2)}, u32[]{:S(2)}) collective-permute-start(bf16[16,4608]{1,0:T(8,128)(2,1)S(1)} %get-tuple-element.150), channel_id=1, source_target_pairs={{0,8},{1,9},{2,10},{3,11},{4,12},{5,13},{6,14},{7,15},{8,0},{9,1},... | collective-permute-start | bytes 442376 | tf_op jit(solution)/shard_map/ppermute | solution.py:484
  170.0 13.1 %collective-permute-start.28 = (bf16[16,1664]{1,0:T(8,128)(2,1)S(1)}, bf16[16,1664]{1,0:T(8,128)(2,1)S(1)}, u32[]{:S(2)}, u32[]{:S(2)}) collective-permute-start(bf16[16,1664]{1,0:T(8,128)(2,1)S(1)} %get-tuple-element.125), channel_id=1, source_target_pairs={{0,8},{1,9},{2,10},{3,11},{4,12},{5,13},{6,14},{7,15},{8,0},{9,1},... | collective-permute-start | bytes 159752 | tf_op jit(solution)/shard_map/ppermute | solution.py:484
  174.2 9.0 %collective-permute-start.29 = (bf16[16,1664]{1,0:T(8,128)(2,1)S(1)}, bf16[16,1664]{1,0:T(8,128)(2,1)S(1)}, u32[]{:S(2)}, u32[]{:S(2)}) collective-permute-start(bf16[16,1664]{1,0:T(8,128)(2,1)S(1)} %get-tuple-element.126), channel_id=1, source_target_pairs={{0,16},{1,17},{2,18},{3,19},{4,20},{5,21},{6,22},{7,23},{8,24},{9,... | collective-permute-start | bytes 159752 | tf_op jit(solution)/shard_map/ppermute | solution.py:484
  181.2 6.0 %collective-permute-start.30 = (bf16[16,1664]{1,0:T(8,128)(2,1)S(1)}, bf16[16,1664]{1,0:T(8,128)(2,1)S(1)}, u32[]{:S(2)}, u32[]{:S(2)}) collective-permute-start(bf16[16,1664]{1,0:T(8,128)(2,1)S(1)} %get-tuple-element.127), channel_id=1, source_target_pairs={{0,24},{1,25},{2,26},{3,27},{4,28},{5,29},{6,30},{7,31},{8,16},{9,... | collective-permute-start | bytes 159752 | tf_op jit(solution)/shard_map/ppermute | solution.py:484
  183.0 21.5 %copy-start.5 = (f32[98496]{0:T(1024)S(1)}, f32[98496]{0:T(1024)}, u32[]{:S(2)}) copy-start(f32[98496]{0:T(1024)} %param.13) | copy-start | bytes 1181956
  183.1 21.5 %copy-start.12 = (f32[98496]{0:T(1024)S(1)}, f32[98496]{0:T(1024)}, u32[]{:S(2)}) copy-start(f32[98496]{0:T(1024)} %param.15) | copy-start | bytes 1181956
  183.1 21.5 %copy-start.13 = (f32[98496]{0:T(1024)S(1)}, f32[98496]{0:T(1024)}, u32[]{:S(2)}) copy-start(f32[98496]{0:T(1024)} %param.14) | copy-start | bytes 1181956
  187.4 6.4 %collective-permute-start.33 = (f32[16,128]{1,0:T(8,128)S(1)}, f32[16,128]{1,0:T(8,128)S(1)}, u32[]{:S(2)}, u32[]{:S(2)}) collective-permute-start(f32[16,128]{1,0:T(8,128)S(1)} %get-tuple-element.137), channel_id=1, source_target_pairs={{0,24},{1,25},{2,26},{3,27},{4,28},{5,29},{6,30},{7,31},{8,16},{9,... | collective-permute-start | bytes 24584 | tf_op jit(solution)/shard_map/ppermute | solution.py:484
  189.3 4.5 %collective-permute-start.32 = (f32[16,128]{1,0:T(8,128)S(1)}, f32[16,128]{1,0:T(8,128)S(1)}, u32[]{:S(2)}, u32[]{:S(2)}) collective-permute-start(f32[16,128]{1,0:T(8,128)S(1)} %get-tuple-element.137), channel_id=1, source_target_pairs={{0,16},{1,17},{2,18},{3,19},{4,20},{5,21},{6,22},{7,23},{8,24},{9,... | collective-permute-start | bytes 24584 | tf_op jit(solution)/shard_map/ppermute | solution.py:484
  189.7 3.9 %collective-permute-start.31 = (f32[16,128]{1,0:T(8,128)S(1)}, f32[16,128]{1,0:T(8,128)S(1)}, u32[]{:S(2)}, u32[]{:S(2)}) collective-permute-start(f32[16,128]{1,0:T(8,128)S(1)} %get-tuple-element.137), channel_id=1, source_target_pairs={{0,8},{1,9},{2,10},{3,11},{4,12},{5,13},{6,14},{7,15},{8,0},{9,1},... | collective-permute-start | bytes 24584 | tf_op jit(solution)/shard_map/ppermute | solution.py:484
  193.9 4.0 %collective-permute-start.34 = (f32[64,128]{1,0:T(8,128)S(1)}, f32[64,128]{1,0:T(8,128)S(1)}, u32[]{:S(2)}, u32[]{:S(2)}) collective-permute-start(f32[64,128]{1,0:T(8,128)S(1)} %get-tuple-element.160), channel_id=1, source_target_pairs={{0,2},{1,3},{2,0},{3,1},{4,6},{5,7},{6,4},{7,5},{8,10},{9,11},{10,... | collective-permute-start | bytes 98312 | tf_op jit(solution)/shard_map/ppermute | solution.py:484
  195.2 5.7 %collective-permute-start.36 = (f32[64,128]{1,0:T(8,128)S(1)}, f32[64,128]{1,0:T(8,128)S(1)}, u32[]{:S(2)}, u32[]{:S(2)}) collective-permute-start(f32[64,128]{1,0:T(8,128)S(1)} %get-tuple-element.160), channel_id=1, source_target_pairs={{0,6},{1,7},{2,4},{3,5},{4,2},{5,3},{6,0},{7,1},{8,14},{9,15},{10,... | collective-permute-start | bytes 98312 | tf_op jit(solution)/shard_map/ppermute | solution.py:484
  196.9 3.9 %collective-permute-start.35 = (f32[64,128]{1,0:T(8,128)S(1)}, f32[64,128]{1,0:T(8,128)S(1)}, u32[]{:S(2)}, u32[]{:S(2)}) collective-permute-start(f32[64,128]{1,0:T(8,128)S(1)} %get-tuple-element.160), channel_id=1, source_target_pairs={{0,4},{1,5},{2,6},{3,7},{4,0},{5,1},{6,2},{7,3},{8,12},{9,13},{10,... | collective-permute-start | bytes 98312 | tf_op jit(solution)/shard_map/ppermute | solution.py:484
  200.8 1.4 collective-permute-start.37
  (5 other events, 6.7 us)

commit v5 on v4

--- a/solution.py
+++ b/solution.py
@@ -236,7 +236,7 @@
     table, out_turned, up_turned, down_turned, columns, up_bias, slopes = refs[
         12 + amount : 19 + amount
     ]
-    acc_down, acc_up, acc_out, acc_vec, *kept = refs[19 + amount :]
+    acc_down, acc_up, acc_out, acc_vec, done, *kept = refs[19 + amount :]
     step = pl.program_id(0)
     chunk = TILE
     chunks = FF // chunk
@@ -367,12 +367,25 @@
 
     @pl.when(step == pl.num_programs(0) - 1)
     def _():
-        for part in weight_parts(kept[each:], acc_down, acc_up, acc_out):
-            part()
-        halves = (keep_ref, send_ref)
-        spread_blocks(halves, acc_out, codes, mine_ref[0], 0, D)
-        spread_blocks(halves, acc_up, codes, mine_ref[0], D, FF)
-        spread_blocks(halves, acc_down, codes, mine_ref[0], D + FF, FF)
+        parts = weight_parts(kept[each:], acc_down, acc_up, acc_out)
+        copies = []
+        for source, begin, width, some in (
+            (acc_up, D, FF, parts[8:16]),
+            (acc_down, D + FF, FF, parts[:8]),
+            (acc_out, 0, D, parts[16:]),
+        ):
+            for part in some:
+                part()
+            halves = (table.at[: D // 2, :], table.at[D // 2 :, :])
+            spread_blocks(halves, source, codes, mine_ref[0], begin, width)
+            across = slice(begin, begin + width)
+            for half, target in zip(halves, (keep_ref, send_ref), strict=True):
+                copies.append(
+                    pltpu.make_async_copy(
+                        half.at[:, across], target.at[:, across], done.at[len(copies)]
+                    )
+                )
+                copies[-1].start()
         up_sums = jnp.broadcast_to(acc_up[D : D + 1, :], (LANES, FF))
         for at in range(0, FF, LANES):
             up_bias[at : at + LANES, :] = up_sums[:, at : at + LANES].T
@@ -384,6 +397,8 @@
         for at in range(4):
             vectors = jnp.where(lane == 8 + at, up_bias[pl.ds(at, D, stride=4), :], vectors)
         sums_ref[...] = vectors
+        for copy in copies:
+            copy.wait()
 
 
 def attend_back_kernel(
@@ -484,18 +499,26 @@
     return lax.ppermute(values, "dp", [(at, at ^ bit) for at in range(count)])
 
 
-def mask_phases(count):
+def mask_phases(count, size):
     bits = [1 << at for at in range(1, count.bit_length() - 1)]
-    phases = [bits[at : at + 2] for at in range(0, len(bits), 2)]
+    groups = [bits[:2]]
+    for bit in bits[2:]:
+        if len(groups[-1]) < size and len(groups) > 1:
+            groups[-1].append(bit)
+        else:
+            groups.append([bit])
     return [[0, 1]] + [
-        [sum(bit for at, bit in enumerate(phase) if choice >> at & 1) for choice in range(1 << len(phase))]
-        for phase in phases
+        [
+            sum(bit for at, bit in enumerate(group) if choice >> at & 1)
+            for choice in range(1 << len(group))
+        ]
+        for group in groups
     ]
 
 
-def block_codes(count):
+def block_codes(phases):
     codes = [0]
-    for masks in reversed(mask_phases(count)):
+    for masks in reversed(phases):
         codes = [mask ^ code for mask in masks for code in codes]
     return codes
 
@@ -550,27 +573,29 @@
     table_width = params.shape[0] // own_count
     blocks = slots // LANES
     direct = own_count == BLOCK
+    phases = mask_phases(count, 2)
+    slow_phases = mask_phases(count, 1)
+    order = block_codes(phases)
+    slow_order = block_codes(slow_phases)
     if direct:
-        codes = block_codes(count)
+        codes, slow_codes = order, slow_order
         origin = mine.reshape(1)
     else:
-        codes = list(range(BLOCKS))
+        codes = slow_codes = list(range(BLOCKS))
         origin = jnp.zeros((1,), jnp.int32)
-        spread = jnp.array(block_codes(count), jnp.int32)
-        places_of = jnp.argsort(spread)
-
-    def to_kernel(pieces, amount):
+
+    def to_kernel(pieces, order, amount):
         if direct:
             return pieces
+        places = jnp.argsort(jnp.array(order, jnp.int32))[jnp.arange(count) ^ mine]
         table = jnp.concatenate(pieces, axis=0).reshape(count, own_count, -1)
-        table = jnp.take(table, places_of[jnp.arange(count) ^ mine], axis=0)
-        return list(table.reshape(amount, D // amount, -1))
-
-    def from_kernel(keep, send):
+        return list(jnp.take(table, places, axis=0).reshape(amount, D // amount, -1))
+
+    def from_kernel(keep, send, order):
         if direct:
             return keep, send
         table = jnp.concatenate([keep, send], axis=0).reshape(count, own_count, -1)
-        table = jnp.take(table, spread ^ mine, axis=0).reshape(D, -1)
+        table = jnp.take(table, jnp.array(order, jnp.int32) ^ mine, axis=0).reshape(D, -1)
         return table[: D // 2], table[D // 2 :]
 
     own_table = params.astype(bf16).reshape(own_count, table_width)
@@ -582,17 +607,19 @@
         axis=1,
     )
     own_rest = own_table[:, 3 * D : 12 * D]
-    phases = mask_phases(count)
     outer = phases[:0:-1]
     first, rest = own_first, own_rest
-    for masks in outer:
+    for at, masks in enumerate(slow_phases[:1:-1]):
+        if at == 1:
+            first = jnp.concatenate(gather_phase(first, outer[0], count), axis=0)
+            _, rest = together(first, rest)
+        rest = jnp.concatenate(gather_phase(rest, masks, count), axis=0)
+    for masks in outer[1:]:
         first = jnp.concatenate(gather_phase(first, masks, count), axis=0)
-        first, rest = together(first, rest)
-        rest_pieces = gather_phase(rest, masks, count)
-        if masks is not outer[-1]:
-            rest = jnp.concatenate(rest_pieces, axis=0)
+    first, rest = together(first, rest)
+    rest_pieces = gather_phase(rest, slow_phases[1], count)
     rest_far = [exchange(rest, 1, count)]
-    first_near, first_far = to_kernel(gather_phase(first, phases[0], count), 2)
+    first_near, first_far = to_kernel(gather_phase(first, phases[0], count), order, 2)
     limits = jnp.concatenate([row_lengths, row_widths])
     segments = segment_ids.reshape(blocks, LANES)
 
@@ -634,17 +661,18 @@
 
     attended, *rest_pieces = together(attended, *rest_pieces)
     rest_far += [exchange(piece, 1, count) for piece in rest_pieces[1:]]
-    rest_pieces = to_kernel(rest_pieces + rest_far, 1)
-    half_rest = whole((D // 2, REST_WIDTH))
+    rest_pieces = to_kernel(rest_pieces + rest_far, slow_order, 1)
     layer_output, grad_attended, grad_both, keep_rest, send_rest, feed_sums = pl.pallas_call(
-        functools.partial(feed_kernel, codes, len(rest_pieces)),
+        functools.partial(feed_kernel, slow_codes, len(rest_pieces)),
         grid=(steps,),
         in_specs=[
             smem(), smem(), across, across, down,
             whole((D, LANES)),
         ]
         + [whole(piece.shape) for piece in rest_pieces],
-        out_specs=[down, across, across, half_rest, half_rest, whole((D, LANES))],
+        out_specs=[down, across, across]
+        + [pl.BlockSpec(memory_space=pl.ANY)] * 2
+        + [whole((D, LANES))],
         out_shape=[
             shaped((slots, D), bf16),
             shaped((D, slots), bf16),
@@ -665,20 +693,21 @@
             pltpu.VMEM((D + BLOCK, FF), f32),
             pltpu.VMEM((D, D), f32),
             pltpu.VMEM((6, D, LANES), f32),
+            pltpu.SemaphoreType.DMA((6,)),
         ]
         + [pltpu.VMEM((rows, TILE), bf16) for rows in (FF, FF, D + BLOCK, D, D, D)] * 2,
-        compiler_params=params_of(60),
+        compiler_params=params_of(46 if direct else 60),
         name="feed",
     )(origin, limits, xt, attended, cotangent, vectors, *rest_pieces)
 
-    def scatter(parts, at):
-        if at == len(phases) - 1:
+    def scatter(parts, way, at):
+        if at == len(way) - 1:
             return cut_sum(parts, 1, f32)
-        return cut_sum(parts, len(phases[at + 1]), bf16)
-
-    parts = scatter_phase(from_kernel(keep_rest, send_rest), phases[0], count)
-    grad_attended, *pieces = together(grad_attended, *scatter(parts, 0))
-    rest_parts = scatter_phase(pieces, phases[1], count)
+        return cut_sum(parts, len(way[at + 1]), bf16)
+
+    parts = scatter_phase(from_kernel(keep_rest, send_rest, slow_order), slow_phases[0], count)
+    grad_attended, *pieces = together(grad_attended, *scatter(parts, slow_phases, 0))
+    rest_parts = scatter_phase(pieces, slow_phases[1], count)
 
     grads, keep_first, send_first = pl.pallas_call(
         functools.partial(attend_back_kernel, codes),
@@ -705,24 +734,18 @@
             pltpu.VMEM((D, 3 * PAIR), f32),
             pltpu.VMEM((D, LANES), f32),
         ],
-        compiler_params=params_of(54),
+        compiler_params=params_of(31),
         name="attend_back",
     )(origin, limits, segments, xt, qt, kt, key, value, attended, grad_attended, logsum, feed_sums)
 
     keep_first, send_first, *rest_parts = together(keep_first, send_first, *rest_parts)
-    parts = scatter_phase(from_kernel(keep_first, send_first), phases[0], count)
-    pieces = scatter(parts, 0)
+    parts = scatter_phase(from_kernel(keep_first, send_first, order), phases[0], count)
+    pieces = scatter(parts, phases, 0)
     grads, *held = together(grads, *pieces, *rest_parts)
     pieces, rest_parts = held[: len(pieces)], held[len(pieces) :]
     parts = scatter_phase(pieces, phases[1], count)
-    rest_pieces = scatter(rest_parts, 1)
-    for at in range(2, len(phases)):
-        pieces = scatter(parts, at - 1)
-        grads, *pieces = together(grads, *pieces)
-        parts = scatter_phase(pieces, phases[at], count)
-        rest_parts = scatter_phase(rest_pieces, phases[at], count)
-        if at < len(phases) - 1:
-            rest_pieces = scatter(rest_parts, at)
+    grads, *rest_pieces = together(grads, *scatter(rest_parts, slow_phases, 1))
+    rest_parts = scatter_phase(rest_pieces, slow_phases[2], count)
     input_grad = pl.pallas_call(
         input_kernel,
         grid=(steps,),
@@ -736,9 +759,15 @@
         compiler_params=params_of(20),
         name="input_grad",
     )(grads, pair_weights, grad_both)
-    input_grad, *rest_parts = together(input_grad, *rest_parts)
     input_grad, *parts = together(input_grad, *parts)
-    (own_rest,) = scatter(rest_parts, len(phases) - 1)
+    for at in range(2, len(phases)):
+        pieces = scatter(parts, phases, at - 1)
+        pieces[0], *rest_parts = together(pieces[0], *rest_parts)
+        parts = scatter_phase(pieces, phases[at], count)
+    for at in range(3, len(slow_phases)):
+        rest_pieces = scatter(rest_parts, slow_phases, at - 1)
+        rest_parts = scatter_phase(rest_pieces, slow_phases[at], count)
+    (own_rest,) = scatter(rest_parts, slow_phases, len(slow_phases) - 1)
     own_first, share = pl.pallas_call(
         own_kernel,
         out_shape=[shaped((own_count, 3 * D), f32), shaped((own_count, LANES), f32)],
@@ -756,7 +785,7 @@
         scratch_shapes=[pltpu.VMEM((D, LANES), f32)],
         compiler_params=params_of(8),
         name="settle",
-    )(origin, *to_kernel(gather_phase(shares, phases[0], count), 2))
+    )(origin, *to_kernel(gather_phase(shares, phases[0], count), order, 2))
     grad_norm = norms[0, 0]
     vector_grads = vector_grads.T
 

time: 206 us -> 197 us (0.956)
  starting transfers between devices: 49.9 us -> 41.2 us
  waiting for transfers between devices: 32.3 us -> 39.9 us
  Pallas kernels: 112 us -> 107 us
    ppermute x38 -> x36, starting transfers between devices: 49.9 us -> 41.2 us  [exchange(): return lax.ppermute(values, 'dp', [(at, at ^ bit) for at in range(count)])]
    ppermute x38 -> x36, waiting for transfers between devices: 32.3 us -> 39.9 us  [exchange(): return lax.ppermute(values, 'dp', [(at, at ^ bit) for at in range(count)])]
    pallas_call x1, Pallas kernels: 26.1 us -> 22.4 us  [body(): pl.pallas_call(functools.partial(attend_back_kernel, codes), grid=(PAIRS,...]
    convert_element_type x4 -> x5, other arithmetic: 4.13 us -> 2.97 us  [cut_sum(): sum((part[at * rows:(at + 1) * rows].astype(f32) for part in parts))]
  transfers between devices with their start and end apart: 38 -> 36, of which waited for: 18 -> 18; matrix products, arithmetic and copies ran while one was open for 1% -> 1% of each run, Pallas kernels for 28% -> 27%
where the time goes in v5:
time: 197 us
  Pallas kernels  107 us (54%)
  starting transfers between devices  41.2 us (21%)
  waiting for transfers between devices  39.9 us (20%)
  other arithmetic  5.88 us (3%)
  between operations  2.35 us (1%)
    pallas_call x1, Pallas kernels, body(): pl.pallas_call(functools.partial(feed_kernel, slow_codes, len(rest_pieces...  51.4 us
    ppermute x36, starting transfers between devices, exchange(): return lax.ppermute(values, 'dp', [(at, at ^ bit) for at in range(count)])  41.2 us
    ppermute x36, waiting for transfers between devices, exchange(): return lax.ppermute(values, 'dp', [(at, at ^ bit) for at in range(count)])  39.9 us
    pallas_call x1, Pallas kernels, body(): pl.pallas_call(functools.partial(attend_back_kernel, codes), grid=(PAIRS,...  22.4 us
    pallas_call x1, Pallas kernels, body(): pl.pallas_call(attend_kernel, grid=(PAIRS,), in_specs=[smem(), whole((blo...  15.1 us
    pallas_call x1, Pallas kernels, body(): pl.pallas_call(functools.partial(project_kernel, codes), grid=(steps,), i...  10.2 us
    pallas_call x1, Pallas kernels, body(): pl.pallas_call(input_kernel, grid=(steps,), in_specs=[pl.BlockSpec((PAIRS...  6.41 us
  transfers between devices with their start and end apart: 36, of which 18 were waited for; matrix products, arithmetic and copies ran while one was open for 1% of the time, Pallas kernels for 27%

profile of v5, /device:TPU:0, one launch (start us, length us, event | category | flops | bytes accessed | tf_op | source)
XLA Modules:
  0.0 197.0 jit_solution(18044415768399077713)
XLA Ops:
  0.6 1.0 convert_element_type.191
  2.0 4.1 %collective-permute-start.1 = (bf16[16,1664]{1,0:T(8,128)(2,1)S(1)}, bf16[16,1664]{1,0:T(8,128)(2,1)S(1)}, u32[]{:S(2)}, u32[]{:S(2)}) collective-permute-start(bf16[16,1664]{1,0:T(8,128)(2,1)S(1)} %get-tuple-element.148), channel_id=1, source_target_pairs={{0,16},{1,17},{2,18},{3,19},{4,20},{5,21},{6,22},{7,23},{8,24},{9,... | collective-permute-start | bytes 159752 | tf_op jit(solution)/shard_map/ppermute | solution.py:499
  6.1 1.6 collective-permute-start
  7.7 2.0 %collective-permute-start.6 = (bf16[16,4608]{1,0:T(8,128)(2,1)S(1)}, bf16[16,4608]{1,0:T(8,128)(2,1)S(1)}, u32[]{:S(2)}, u32[]{:S(2)}) collective-permute-start(bf16[16,4608]{1,0:T(8,128)(2,1)S(1)} %slice.198), channel_id=1, source_target_pairs={{0,16},{1,17},{2,18},{3,19},{4,20},{5,21},{6,22},{7,23},{8,24},{9,... | collective-permute-start | bytes 442376 | tf_op jit(solution)/shard_map/ppermute | solution.py:499
  9.7 0.6 collective-permute-done
  10.2 3.9 %collective-permute-done.2 = bf16[16,1664]{1,0:T(8,128)(2,1)S(1)} collective-permute-done((bf16[16,1664]{1,0:T(8,128)(2,1)S(1)}, bf16[16,1664]{1,0:T(8,128)(2,1)S(1)}, u32[]{:S(2)}, u32[]{:S(2)}) %collective-permute-start.2) | collective-permute-done | bytes 53280 | tf_op jit(solution)/shard_map/ppermute | solution.py:499
  14.2 2.5 %collective-permute-start.5 = (bf16[64,1664]{1,0:T(8,128)(2,1)S(1)}, bf16[64,1664]{1,0:T(8,128)(2,1)S(1)}, u32[]{:S(2)}, u32[]{:S(2)}) collective-permute-start(bf16[64,1664]{1,0:T(8,128)(2,1)S(1)} %pad_maximum_fusion.2), channel_id=1, source_target_pairs={{0,6},{1,7},{2,4},{3,5},{4,2},{5,3},{6,0},{7,1},{8,14},{9,15},{10,... | collective-permute-start | bytes 638984 | tf_op jit(solution)/shard_map/ppermute | solution.py:499
  17.8 0.8 collective-permute-done.6
  18.6 2.2 %collective-permute-start.7 = (bf16[32,4608]{1,0:T(8,128)(2,1)S(1)}, bf16[32,4608]{1,0:T(8,128)(2,1)S(1)}, u32[]{:S(2)}, u32[]{:S(2)}) collective-permute-start(bf16[32,4608]{1,0:T(8,128)(2,1)S(1)} %pad_maximum_fusion.1), channel_id=1, source_target_pairs={{0,8},{1,9},{2,10},{3,11},{4,12},{5,13},{6,14},{7,15},{8,0},{9,1},... | collective-permute-start | bytes 884744 | tf_op jit(solution)/shard_map/ppermute | solution.py:499
  20.8 3.9 %collective-permute-done.3 = bf16[64,1664]{1,0:T(8,128)(2,1)S(1)} collective-permute-done((bf16[64,1664]{1,0:T(8,128)(2,1)S(1)}, bf16[64,1664]{1,0:T(8,128)(2,1)S(1)}, u32[]{:S(2)}, u32[]{:S(2)}) %collective-permute-start.3) | collective-permute-done | bytes 213024 | tf_op jit(solution)/shard_map/ppermute | solution.py:499
  24.8 1.8 collective-permute-done.7
  26.7 2.5 %collective-permute-start.11 = (bf16[64,4608]{1,0:T(8,128)(2,1)S(1)}, bf16[64,4608]{1,0:T(8,128)(2,1)S(1)}, u32[]{:S(2)}, u32[]{:S(2)}) collective-permute-start(bf16[64,4608]{1,0:T(8,128)(2,1)S(1)} %pad_maximum_fusion.refs_6_), channel_id=1, source_target_pairs={{0,6},{1,7},{2,4},{3,5},{4,2},{5,3},{6,0},{7,1},{8,14},{9,15},{10,... | collective-permute-start | bytes 1769480 | tf_op jit(solution)/shard_map/ppermute | solution.py:499
  30.9 0.6 pad_add_fusion.limits_ref.refs_1_
  31.5 10.2 %project.1 = (bf16[512,2048]{1,0:T(8,128)(2,1)}, bf16[512,2048]{1,0:T(8,128)(2,1)}, bf16[512,2048]{1,0:T(8,128)(2,1)}, bf16[512,2048]{1,0:T(8,128)(2,1)}, bf16[2...) custom-call(s32[1]{0:T(128)} %bitcast.mine_ref.refs_0_, ...), custom_call_target="tpu_custom_call" | custom-call | tf_op jit(solution)/shard_map/project/pallas_call | solution.py:630
  41.7 15.1 %attend.1 = (bf16[512,2048]{1,0:T(8,128)(2,1)}, f32[4,16,256]{2,1,0:T(8,128)}) custom-call(s32[3]{0:T(128)} %pad_add_fusion.limits_ref.refs_1_, s32[16,128]{1,0:T(8,128)} %bitcast.5, bf16[512,2048]{1,0:T(8,128)(2,1)} %get-tuple-element.72.qt_ref, bf16[2048,512]{1,0:T(8,128)(2,1)} %get-tuple-element.73.k_ref, bf16[512,2048]{1,0:T(8,128)(2,1)} %get-tuple-element.74.vt_ref), custom_call_target="tpu_custom_call" | custom-call | tf_op jit(solution)/shard_map/attend/pallas_call | solution.py:651
  57.9 1.3 collective-permute-done.13.refs_11_
  59.2 1.7 collective-permute-done.14.refs_12_
  60.9 51.4 %feed.1 = (bf16[2048,512]{1,0:T(8,128)(2,1)}, bf16[512,2048]{1,0:T(8,128)(2,1)S(1)}, bf16[512,2048]{1,0:T(8,128)(2,1)}, bf16[256,4608]{1,0:T(8,128)(2,1)}, bf16[...) custom-call(s32[1]{0:T(128)} %bitcast.mine_ref.refs_0_, s32[3]{0:T(128)S(1)} %copy-done.10, ...), custom_call_target="tpu_custom_call" | custom-call | tf_op jit(solution)/shard_map/feed/pallas_call | solution.py:665
  112.8 4.4 %collective-permute-done.16 = bf16[256,4608]{1,0:T(8,128)(2,1)S(1)} collective-permute-done((bf16[256,4608]{1,0:T(8,128)(2,1)}, bf16[256,4608]{1,0:T(8,128)(2,1)S(1)}, u32[]{:S(2)}, u32[]{:S(2)}) %collective-permute-start.16) | collective-permute-done | bytes 2359328 | tf_op jit(solution)/shard_map/ppermute | solution.py:499
  117.2 2.3 %add_convert_fusion = (bf16[64,4608]{1,0:T(8,128)(2,1)S(1)}, bf16[64,4608]{1,0:T(8,128)(2,1)S(1)}, bf16[64,4608]{1,0:T(8,128)(2,1)S(1)}, bf16[64,4608]{1,0:T(8,128)(2,1)S(1)}) fusion(bf16[256,4608]{1,0:T(8,128)(2,1)S(1)} %collective-permute-done.16, bf16[256,4608]{1,0:T(8,128)(2,1)} %get-tuple-element.87), kind=kLoop, calls=%fused_computation | loop fusion | flops 4718592 | bytes 7077888 | tf_op jit(solution)/shard_map/convert_element_type | solution.py:539
  119.5 1.6 collective-permute-start.17
  121.1 1.5 collective-permute-start.18
  123.1 22.4 %attend_back.1 = (bf16[4,384,2048]{2,1,0:T(8,128)(2,1)S(1)}, bf16[256,1664]{1,0:T(8,128)(2,1)S(1)}, bf16[256,1664]{1,0:T(8,128)(2,1)S(1)}) custom-call(s32[1]{0:T(128)} %bitcast.mine_ref.refs_0_, s32[3]{0:T(128)S(1)} %copy-done.10, s32[16,128]{1,0:T(8,128)S(1)} %bitcast.6, bf16[512,2048]{1,0:T(8,128)(2,1)S(1)} %copy-done.2, bf16[512,2048]{1,0:T(8,128)(2,1)S(1)} %copy-done, ...), custom_call_target="tpu_custom_call" | custom-call | tf_op jit(solution)/shard_map/attend_back/pallas_call | solution.py:712
  145.6 3.4 %collective-permute-done.18 = bf16[64,4608]{1,0:T(8,128)(2,1)S(1)} collective-permute-done((bf16[64,4608]{1,0:T(8,128)(2,1)S(1)}, bf16[64,4608]{1,0:T(8,128)(2,1)S(1)}, u32[]{:S(2)}, u32[]{:S(2)}) %collective-permute-start.18) | collective-permute-done | bytes 589856 | tf_op jit(solution)/shard_map/ppermute | solution.py:499
  149.1 2.4 %collective-permute-done.20 = bf16[256,1664]{1,0:T(8,128)(2,1)S(1)} collective-permute-done((bf16[256,1664]{1,0:T(8,128)(2,1)S(1)}, bf16[256,1664]{1,0:T(8,128)(2,1)S(1)}, u32[]{:S(2)}, u32[]{:S(2)}) %collective-permute-start.20) | collective-permute-done | bytes 852000 | tf_op jit(solution)/shard_map/ppermute | solution.py:499
  151.7 1.3 collective-permute-start.21
  153.0 0.8 collective-permute-start.22
  153.8 1.4 collective-permute-start.23
  155.5 1.0 collective-permute-start.24
  156.6 6.4 %input_grad.1 = f32[2048,512]{1,0:T(8,128)} custom-call(bf16[4,384,2048]{2,1,0:T(8,128)(2,1)S(1)} %get-tuple-element.110.grads_ref, bf16[512,1536]{1,0:T(8,128)(2,1)S(1)} %copy-done.7, bf16[512,2048]{1,0:T(8,128)(2,1)S(1)} %copy-done.4), custom_call_target="tpu_custom_call" | custom-call | tf_op jit(solution)/shard_map/input_grad/pallas_call | solution.py:749
  163.0 1.6 collective-permute-done.23
  164.8 2.1 %collective-permute-start.28 = (bf16[16,4608]{1,0:T(8,128)(2,1)S(1)}, bf16[16,4608]{1,0:T(8,128)(2,1)S(1)}, u32[]{:S(2)}, u32[]{:S(2)}) collective-permute-start(bf16[16,4608]{1,0:T(8,128)(2,1)S(1)} %add_convert_fusion.10), channel_id=1, source_target_pairs={{0,16},{1,17},{2,18},{3,19},{4,20},{5,21},{6,22},{7,23},{8,24},{9,... | collective-permute-start | bytes 442376 | tf_op jit(solution)/shard_map/ppermute | solution.py:499
  166.8 1.3 collective-permute-start.27
  168.1 1.9 collective-permute-start.26
  170.0 1.2 collective-permute-start.25
  171.2 5.7 %collective-permute-done.28 = bf16[16,4608]{1,0:T(8,128)(2,1)S(1)} collective-permute-done((bf16[16,4608]{1,0:T(8,128)(2,1)S(1)}, bf16[16,4608]{1,0:T(8,128)(2,1)S(1)}, u32[]{:S(2)}, u32[]{:S(2)}) %collective-permute-start.28) | collective-permute-done | bytes 147488 | tf_op jit(solution)/shard_map/ppermute | solution.py:499
  177.0 1.5 collective-permute-done.26.refs_2_
  178.7 3.0 %collective-permute-start.31 = (f32[16,128]{1,0:T(8,128)S(1)}, f32[16,128]{1,0:T(8,128)S(1)}, u32[]{:S(2)}, u32[]{:S(2)}) collective-permute-start(f32[16,128]{1,0:T(8,128)S(1)} %get-tuple-element.127), channel_id=1, source_target_pairs={{0,24},{1,25},{2,26},{3,27},{4,28},{5,29},{6,30},{7,31},{8,16},{9,... | collective-permute-start | bytes 24584 | tf_op jit(solution)/shard_map/ppermute | solution.py:499
  181.6 1.5 collective-permute-start.29
  183.1 2.2 %collective-permute-done.29 = f32[16,128]{1,0:T(8,128)S(1)} collective-permute-done((f32[16,128]{1,0:T(8,128)S(1)}, f32[16,128]{1,0:T(8,128)S(1)}, u32[]{:S(2)}, u32[]{:S(2)}) %collective-permute-start.29) | collective-permute-done | bytes 8224 | tf_op jit(solution)/shard_map/ppermute | solution.py:499
  185.3 0.9 collective-permute-done.30
  186.2 0.7 collective-permute-start.32
  186.9 1.4 collective-permute-start.34
  188.3 1.5 collective-permute-start.33
  190.2 2.0 %collective-permute-done.33 = f32[64,128]{1,0:T(8,128)S(1)} collective-permute-done((f32[64,128]{1,0:T(8,128)S(1)}, f32[64,128]{1,0:T(8,128)S(1)}, u32[]{:S(2)}, u32[]{:S(2)}) %collective-permute-start.33) | collective-permute-done | bytes 32800 | tf_op jit(solution)/shard_map/ppermute | solution.py:499
  192.3 1.3 collective-permute-done.35.far_ref
  193.6 0.8 settle.1
  195.9 1.1 add_multiply_fusion
  (95 shorter events, 6.9 us)
Async XLA Ops:
  2.0 28.9 %copy-start.14 = (s32[2]{0:T(128)S(1)}, s32[2]{0:T(128)}, u32[]{:S(2)}) copy-start(s32[2]{0:T(128)} %param.11) | copy-start | bytes 28
  2.0 7.7 %collective-permute-start.1 = (bf16[16,1664]{1,0:T(8,128)(2,1)S(1)}, bf16[16,1664]{1,0:T(8,128)(2,1)S(1)}, u32[]{:S(2)}, u32[]{:S(2)}) collective-permute-start(bf16[16,1664]{1,0:T(8,128)(2,1)S(1)} %get-tuple-element.148), channel_id=1, source_target_pairs={{0,16},{1,17},{2,18},{3,19},{4,20},{5,21},{6,22},{7,23},{8,24},{9,... | collective-permute-start | bytes 159752 | tf_op jit(solution)/shard_map/ppermute | solution.py:499
  6.1 4.1 %collective-permute-start = (bf16[16,1664]{1,0:T(8,128)(2,1)S(1)}, bf16[16,1664]{1,0:T(8,128)(2,1)S(1)}, u32[]{:S(2)}, u32[]{:S(2)}) collective-permute-start(bf16[16,1664]{1,0:T(8,128)(2,1)S(1)} %get-tuple-element.148), channel_id=1, source_target_pairs={{0,8},{1,9},{2,10},{3,11},{4,12},{5,13},{6,14},{7,15},{8,0},{9,1},... | collective-permute-start | bytes 159752 | tf_op jit(solution)/shard_map/ppermute | solution.py:499
  7.7 6.5 %collective-permute-start.2 = (bf16[16,1664]{1,0:T(8,128)(2,1)S(1)}, bf16[16,1664]{1,0:T(8,128)(2,1)S(1)}, u32[]{:S(2)}, u32[]{:S(2)}) collective-permute-start(bf16[16,1664]{1,0:T(8,128)(2,1)S(1)} %get-tuple-element.148), channel_id=1, source_target_pairs={{0,24},{1,25},{2,26},{3,27},{4,28},{5,29},{6,30},{7,31},{8,16},{9,... | collective-permute-start | bytes 159752 | tf_op jit(solution)/shard_map/ppermute | solution.py:499
  7.7 10.9 %collective-permute-start.6 = (bf16[16,4608]{1,0:T(8,128)(2,1)S(1)}, bf16[16,4608]{1,0:T(8,128)(2,1)S(1)}, u32[]{:S(2)}, u32[]{:S(2)}) collective-permute-start(bf16[16,4608]{1,0:T(8,128)(2,1)S(1)} %slice.198), channel_id=1, source_target_pairs={{0,16},{1,17},{2,18},{3,19},{4,20},{5,21},{6,22},{7,23},{8,24},{9,... | collective-permute-start | bytes 442376 | tf_op jit(solution)/shard_map/ppermute | solution.py:499
  14.2 10.6 %collective-permute-start.5 = (bf16[64,1664]{1,0:T(8,128)(2,1)S(1)}, bf16[64,1664]{1,0:T(8,128)(2,1)S(1)}, u32[]{:S(2)}, u32[]{:S(2)}) collective-permute-start(bf16[64,1664]{1,0:T(8,128)(2,1)S(1)} %pad_maximum_fusion.2), channel_id=1, source_target_pairs={{0,6},{1,7},{2,4},{3,5},{4,2},{5,3},{6,0},{7,1},{8,14},{9,15},{10,... | collective-permute-start | bytes 638984 | tf_op jit(solution)/shard_map/ppermute | solution.py:499
  16.7 8.0 %collective-permute-start.4 = (bf16[64,1664]{1,0:T(8,128)(2,1)S(1)}, bf16[64,1664]{1,0:T(8,128)(2,1)S(1)}, u32[]{:S(2)}, u32[]{:S(2)}) collective-permute-start(bf16[64,1664]{1,0:T(8,128)(2,1)S(1)} %pad_maximum_fusion.2), channel_id=1, source_target_pairs={{0,4},{1,5},{2,6},{3,7},{4,0},{5,1},{6,2},{7,3},{8,12},{9,13},{10,... | collective-permute-start | bytes 638984 | tf_op jit(solution)/shard_map/ppermute | solution.py:499
  17.2 7.5 %collective-permute-start.3 = (bf16[64,1664]{1,0:T(8,128)(2,1)S(1)}, bf16[64,1664]{1,0:T(8,128)(2,1)S(1)}, u32[]{:S(2)}, u32[]{:S(2)}) collective-permute-start(bf16[64,1664]{1,0:T(8,128)(2,1)S(1)} %pad_maximum_fusion.2), channel_id=1, source_target_pairs={{0,2},{1,3},{2,0},{3,1},{4,6},{5,7},{6,4},{7,5},{8,10},{9,11},{10,... | collective-permute-start | bytes 638984 | tf_op jit(solution)/shard_map/ppermute | solution.py:499
  18.6 8.0 %collective-permute-start.7 = (bf16[32,4608]{1,0:T(8,128)(2,1)S(1)}, bf16[32,4608]{1,0:T(8,128)(2,1)S(1)}, u32[]{:S(2)}, u32[]{:S(2)}) collective-permute-start(bf16[32,4608]{1,0:T(8,128)(2,1)S(1)} %pad_maximum_fusion.1), channel_id=1, source_target_pairs={{0,8},{1,9},{2,10},{3,11},{4,12},{5,13},{6,14},{7,15},{8,0},{9,1},... | collective-permute-start | bytes 884744 | tf_op jit(solution)/shard_map/ppermute | solution.py:499
  26.6 4.9 %collective-permute-start.8 = (bf16[256,1664]{1,0:T(8,128)(2,1)S(1)}, bf16[256,1664]{1,0:T(8,128)(2,1)S(1)}, u32[]{:S(2)}, u32[]{:S(2)}) collective-permute-start(bf16[256,1664]{1,0:T(8,128)(2,1)S(1)} %constant_dynamic-update-slice_fusion.near_ref), channel_id=1, source_target_pairs={{0,1},{1,0},{2,3},{3,2},{4,5},{5,4},{6,7},{7,6},{8,9},{9,8},{10,11... | collective-permute-start | bytes 2555912 | tf_op jit(solution)/shard_map/ppermute | solution.py:499
  26.7 30.1 %collective-permute-start.11 = (bf16[64,4608]{1,0:T(8,128)(2,1)S(1)}, bf16[64,4608]{1,0:T(8,128)(2,1)S(1)}, u32[]{:S(2)}, u32[]{:S(2)}) collective-permute-start(bf16[64,4608]{1,0:T(8,128)(2,1)S(1)} %pad_maximum_fusion.refs_6_), channel_id=1, source_target_pairs={{0,6},{1,7},{2,4},{3,5},{4,2},{5,3},{6,0},{7,1},{8,14},{9,15},{10,... | collective-permute-start | bytes 1769480 | tf_op jit(solution)/shard_map/ppermute | solution.py:499
  29.2 27.6 %collective-permute-start.10 = (bf16[64,4608]{1,0:T(8,128)(2,1)S(1)}, bf16[64,4608]{1,0:T(8,128)(2,1)}, u32[]{:S(2)}, u32[]{:S(2)}) collective-permute-start(bf16[64,4608]{1,0:T(8,128)(2,1)S(1)} %pad_maximum_fusion.refs_6_), channel_id=1, source_target_pairs={{0,4},{1,5},{2,6},{3,7},{4,0},{5,1},{6,2},{7,3},{8,12},{9,13},{10,... | collective-permute-start | bytes 1769480 | tf_op jit(solution)/shard_map/ppermute | solution.py:499
  29.7 27.1 %collective-permute-start.9 = (bf16[64,4608]{1,0:T(8,128)(2,1)S(1)}, bf16[64,4608]{1,0:T(8,128)(2,1)}, u32[]{:S(2)}, u32[]{:S(2)}) collective-permute-start(bf16[64,4608]{1,0:T(8,128)(2,1)S(1)} %pad_maximum_fusion.refs_6_), channel_id=1, source_target_pairs={{0,2},{1,3},{2,0},{3,1},{4,6},{5,7},{6,4},{7,5},{8,10},{9,11},{10,... | collective-permute-start | bytes 1769480 | tf_op jit(solution)/shard_map/ppermute | solution.py:499
  31.5 26.4 %collective-permute-start.12 = (bf16[64,4608]{1,0:T(8,128)(2,1)S(1)}, bf16[64,4608]{1,0:T(8,128)(2,1)S(1)}, u32[]{:S(2)}, u32[]{:S(2)}) collective-permute-start(bf16[64,4608]{1,0:T(8,128)(2,1)S(1)} %pad_maximum_fusion.refs_6_), channel_id=1, source_target_pairs={{0,1},{1,0},{2,3},{3,2},{4,5},{5,4},{6,7},{7,6},{8,9},{9,8},{10,11... | collective-permute-start | bytes 1769480 | tf_op jit(solution)/shard_map/ppermute | solution.py:499
  41.7 19.2 %copy-start.10 = (s32[3]{0:T(128)S(1)}, s32[3]{0:T(128)}, u32[]{:S(2)}) copy-start(s32[3]{0:T(128)} %pad_add_fusion.limits_ref.refs_1_) | copy-start | bytes 40
  56.8 2.4 %collective-permute-start.13 = (bf16[64,4608]{1,0:T(8,128)(2,1)}, bf16[64,4608]{1,0:T(8,128)(2,1)S(1)}, u32[]{:S(2)}, u32[]{:S(2)}) collective-permute-start(bf16[64,4608]{1,0:T(8,128)(2,1)} %collective-permute-done.9.refs_7_), channel_id=1, source_target_pairs={{0,1},{1,0},{2,3},{3,2},{4,5},{5,4},{6,7},{7,6},{8,9},{9,8},{10,11... | collective-permute-start | bytes 1769480 | tf_op jit(solution)/shard_map/ppermute | solution.py:499
  57.4 3.5 %collective-permute-start.14 = (bf16[64,4608]{1,0:T(8,128)(2,1)}, bf16[64,4608]{1,0:T(8,128)(2,1)S(1)}, u32[]{:S(2)}, u32[]{:S(2)}) collective-permute-start(bf16[64,4608]{1,0:T(8,128)(2,1)} %collective-permute-done.10.refs_8_), channel_id=1, source_target_pairs={{0,1},{1,0},{2,3},{3,2},{4,5},{5,4},{6,7},{7,6},{8,9},{9,8},{10,11... | collective-permute-start | bytes 1769480 | tf_op jit(solution)/shard_map/ppermute | solution.py:499
  57.5 3.5 %collective-permute-start.15 = (bf16[64,4608]{1,0:T(8,128)(2,1)S(1)}, bf16[64,4608]{1,0:T(8,128)(2,1)S(1)}, u32[]{:S(2)}, u32[]{:S(2)}) collective-permute-start(bf16[64,4608]{1,0:T(8,128)(2,1)S(1)} %collective-permute-done.11.refs_9_), channel_id=1, source_target_pairs={{0,1},{1,0},{2,3},{3,2},{4,5},{5,4},{6,7},{7,6},{8,9},{9,8},{10,11... | collective-permute-start | bytes 1769480 | tf_op jit(solution)/shard_map/ppermute | solution.py:499
  60.9 62.2 %copy-start.3 = (bf16[512,2048]{1,0:T(8,128)(2,1)S(1)}, bf16[512,2048]{1,0:T(8,128)(2,1)}, u32[]{:S(2)}) copy-start(bf16[512,2048]{1,0:T(8,128)(2,1)} %get-tuple-element.77.refs_3_.att_ref) | copy-start | bytes 6291460
  60.9 62.2 %copy-start.5 = (bf16[512,2048]{1,0:T(8,128)(2,1)S(1)}, bf16[512,2048]{1,0:T(8,128)(2,1)}, u32[]{:S(2)}) copy-start(bf16[512,2048]{1,0:T(8,128)(2,1)} %get-tuple-element.84.kt_ref) | copy-start | bytes 6291460
  60.9 62.2 %copy-start.6 = (bf16[2048,512]{1,0:T(8,128)(2,1)S(1)}, bf16[2048,512]{1,0:T(8,128)(2,1)}, u32[]{:S(2)}) copy-start(bf16[2048,512]{1,0:T(8,128)(2,1)} %get-tuple-element.85.v_ref) | copy-start | bytes 6291460
  112.4 4.8 %collective-permute-start.16 = (bf16[256,4608]{1,0:T(8,128)(2,1)}, bf16[256,4608]{1,0:T(8,128)(2,1)S(1)}, u32[]{:S(2)}, u32[]{:S(2)}) collective-permute-start(bf16[256,4608]{1,0:T(8,128)(2,1)} %get-tuple-element.88), channel_id=1, source_target_pairs={{0,1},{1,0},{2,3},{3,2},{4,5},{5,4},{6,7},{7,6},{8,9},{9,8},{10,11... | collective-permute-start | bytes 7077896 | tf_op jit(solution)/shard_map/ppermute | solution.py:499
  117.2 5.9 %copy-start.1 = (bf16[2048,512]{1,0:T(8,128)(2,1)S(1)}, bf16[2048,512]{1,0:T(8,128)(2,1)}, u32[]{:S(2)}) copy-start(bf16[2048,512]{1,0:T(8,128)(2,1)} %get-tuple-element.73.k_ref) | copy-start | bytes 6291460
  117.2 5.9 %copy-start.2 = (bf16[512,2048]{1,0:T(8,128)(2,1)S(1)}, bf16[512,2048]{1,0:T(8,128)(2,1)}, u32[]{:S(2)}) copy-start(bf16[512,2048]{1,0:T(8,128)(2,1)} %get-tuple-element.71.refs_2_.xt_ref) | copy-start | bytes 6291460
  117.2 5.9 %copy-start.8 = (f32[4,16,256]{2,1,0:T(8,128)S(1)}, f32[4,16,256]{2,1,0:T(8,128)}, u32[]{:S(2)}) copy-start(f32[4,16,256]{2,1,0:T(8,128)} %get-tuple-element.90.logsum_ref) | copy-start | bytes 196612
  117.2 5.9 %copy-start.9 = (s32[2048]{0:T(1024)S(1)}, s32[2048]{0:T(1024)}, u32[]{:S(2)}) copy-start(s32[2048]{0:T(1024)} %param.10) | copy-start | bytes 24580
  119.5 26.1 %collective-permute-start.17 = (bf16[64,4608]{1,0:T(8,128)(2,1)S(1)}, bf16[64,4608]{1,0:T(8,128)(2,1)S(1)}, u32[]{:S(2)}, u32[]{:S(2)}) collective-permute-start(bf16[64,4608]{1,0:T(8,128)(2,1)S(1)} %get-tuple-element.96), channel_id=1, source_target_pairs={{0,2},{1,3},{2,0},{3,1},{4,6},{5,7},{6,4},{7,5},{8,10},{9,11},{10,... | collective-permute-start | bytes 1769480 | tf_op jit(solution)/shard_map/ppermute | solution.py:499
  121.1 28.0 %collective-permute-start.18 = (bf16[64,4608]{1,0:T(8,128)(2,1)S(1)}, bf16[64,4608]{1,0:T(8,128)(2,1)S(1)}, u32[]{:S(2)}, u32[]{:S(2)}) collective-permute-start(bf16[64,4608]{1,0:T(8,128)(2,1)S(1)} %get-tuple-element.97), channel_id=1, source_target_pairs={{0,4},{1,5},{2,6},{3,7},{4,0},{5,1},{6,2},{7,3},{8,12},{9,13},{10,... | collective-permute-start | bytes 1769480 | tf_op jit(solution)/shard_map/ppermute | solution.py:499
  122.6 26.4 %collective-permute-start.19 = (bf16[64,4608]{1,0:T(8,128)(2,1)S(1)}, bf16[64,4608]{1,0:T(8,128)(2,1)S(1)}, u32[]{:S(2)}, u32[]{:S(2)}) collective-permute-start(bf16[64,4608]{1,0:T(8,128)(2,1)S(1)} %get-tuple-element.98), channel_id=1, source_target_pairs={{0,6},{1,7},{2,4},{3,5},{4,2},{5,3},{6,0},{7,1},{8,14},{9,15},{10,... | collective-permute-start | bytes 1769480 | tf_op jit(solution)/shard_map/ppermute | solution.py:499
  149.1 2.4 %collective-permute-start.20 = (bf16[256,1664]{1,0:T(8,128)(2,1)S(1)}, bf16[256,1664]{1,0:T(8,128)(2,1)S(1)}, u32[]{:S(2)}, u32[]{:S(2)}) collective-permute-start(bf16[256,1664]{1,0:T(8,128)(2,1)S(1)} %get-tuple-element.100), channel_id=1, source_target_pairs={{0,1},{1,0},{2,3},{3,2},{4,5},{5,4},{6,7},{7,6},{8,9},{9,8},{10,11... | collective-permute-start | bytes 2555912 | tf_op jit(solution)/shard_map/ppermute | solution.py:499
  151.7 11.3 %collective-permute-start.21 = (bf16[64,1664]{1,0:T(8,128)(2,1)S(1)}, bf16[64,1664]{1,0:T(8,128)(2,1)S(1)}, u32[]{:S(2)}, u32[]{:S(2)}) collective-permute-start(bf16[64,1664]{1,0:T(8,128)(2,1)S(1)} %get-tuple-element.114), channel_id=1, source_target_pairs={{0,2},{1,3},{2,0},{3,1},{4,6},{5,7},{6,4},{7,5},{8,10},{9,11},{10,... | collective-permute-start | bytes 638984 | tf_op jit(solution)/shard_map/ppermute | solution.py:499
  153.0 10.0 %collective-permute-start.22 = (bf16[64,1664]{1,0:T(8,128)(2,1)S(1)}, bf16[64,1664]{1,0:T(8,128)(2,1)S(1)}, u32[]{:S(2)}, u32[]{:S(2)}) collective-permute-start(bf16[64,1664]{1,0:T(8,128)(2,1)S(1)} %get-tuple-element.115), channel_id=1, source_target_pairs={{0,4},{1,5},{2,6},{3,7},{4,0},{5,1},{6,2},{7,3},{8,12},{9,13},{10,... | collective-permute-start | bytes 638984 | tf_op jit(solution)/shard_map/ppermute | solution.py:499
  153.8 10.8 %collective-permute-start.23 = (bf16[64,1664]{1,0:T(8,128)(2,1)S(1)}, bf16[64,1664]{1,0:T(8,128)(2,1)S(1)}, u32[]{:S(2)}, u32[]{:S(2)}) collective-permute-start(bf16[64,1664]{1,0:T(8,128)(2,1)S(1)} %get-tuple-element.116), channel_id=1, source_target_pairs={{0,6},{1,7},{2,4},{3,5},{4,2},{5,3},{6,0},{7,1},{8,14},{9,15},{10,... | collective-permute-start | bytes 638984 | tf_op jit(solution)/shard_map/ppermute | solution.py:499
  155.5 9.2 %collective-permute-start.24 = (bf16[32,4608]{1,0:T(8,128)(2,1)S(1)}, bf16[32,4608]{1,0:T(8,128)(2,1)S(1)}, u32[]{:S(2)}, u32[]{:S(2)}) collective-permute-start(bf16[32,4608]{1,0:T(8,128)(2,1)S(1)} %get-tuple-element.123), channel_id=1, source_target_pairs={{0,8},{1,9},{2,10},{3,11},{4,12},{5,13},{6,14},{7,15},{8,0},{9,1},... | collective-permute-start | bytes 884744 | tf_op jit(solution)/shard_map/ppermute | solution.py:499
  164.7 31.2 %copy-start.11 = (f32[98496]{0:T(1024)S(1)}, f32[98496]{0:T(1024)}, u32[]{:S(2)}) copy-start(f32[98496]{0:T(1024)} %param.13) | copy-start | bytes 1181956
  164.7 31.2 %copy-start.12 = (f32[98496]{0:T(1024)S(1)}, f32[98496]{0:T(1024)}, u32[]{:S(2)}) copy-start(f32[98496]{0:T(1024)} %param.15) | copy-start | bytes 1181956
  164.7 31.2 %copy-start.13 = (f32[98496]{0:T(1024)S(1)}, f32[98496]{0:T(1024)}, u32[]{:S(2)}) copy-start(f32[98496]{0:T(1024)} %param.14) | copy-start | bytes 1181956
  164.8 12.1 %collective-permute-start.28 = (bf16[16,4608]{1,0:T(8,128)(2,1)S(1)}, bf16[16,4608]{1,0:T(8,128)(2,1)S(1)}, u32[]{:S(2)}, u32[]{:S(2)}) collective-permute-start(bf16[16,4608]{1,0:T(8,128)(2,1)S(1)} %add_convert_fusion.10), channel_id=1, source_target_pairs={{0,16},{1,17},{2,18},{3,19},{4,20},{5,21},{6,22},{7,23},{8,24},{9,... | collective-permute-start | bytes 442376 | tf_op jit(solution)/shard_map/ppermute | solution.py:499
  166.8 10.1 %collective-permute-start.27 = (bf16[16,1664]{1,0:T(8,128)(2,1)S(1)}, bf16[16,1664]{1,0:T(8,128)(2,1)S(1)}, u32[]{:S(2)}, u32[]{:S(2)}) collective-permute-start(bf16[16,1664]{1,0:T(8,128)(2,1)S(1)} %get-tuple-element.144), channel_id=1, source_target_pairs={{0,24},{1,25},{2,26},{3,27},{4,28},{5,29},{6,30},{7,31},{8,16},{9,... | collective-permute-start | bytes 159752 | tf_op jit(solution)/shard_map/ppermute | solution.py:499
  168.1 10.4 %collective-permute-start.26 = (bf16[16,1664]{1,0:T(8,128)(2,1)S(1)}, bf16[16,1664]{1,0:T(8,128)(2,1)S(1)}, u32[]{:S(2)}, u32[]{:S(2)}) collective-permute-start(bf16[16,1664]{1,0:T(8,128)(2,1)S(1)} %get-tuple-element.145), channel_id=1, source_target_pairs={{0,16},{1,17},{2,18},{3,19},{4,20},{5,21},{6,22},{7,23},{8,24},{9,... | collective-permute-start | bytes 159752 | tf_op jit(solution)/shard_map/ppermute | solution.py:499
  170.0 8.5 %collective-permute-start.25 = (bf16[16,1664]{1,0:T(8,128)(2,1)S(1)}, bf16[16,1664]{1,0:T(8,128)(2,1)S(1)}, u32[]{:S(2)}, u32[]{:S(2)}) collective-permute-start(bf16[16,1664]{1,0:T(8,128)(2,1)S(1)} %get-tuple-element.146), channel_id=1, source_target_pairs={{0,8},{1,9},{2,10},{3,11},{4,12},{5,13},{6,14},{7,15},{8,0},{9,1},... | collective-permute-start | bytes 159752 | tf_op jit(solution)/shard_map/ppermute | solution.py:499
  178.7 7.5 %collective-permute-start.31 = (f32[16,128]{1,0:T(8,128)S(1)}, f32[16,128]{1,0:T(8,128)S(1)}, u32[]{:S(2)}, u32[]{:S(2)}) collective-permute-start(f32[16,128]{1,0:T(8,128)S(1)} %get-tuple-element.127), channel_id=1, source_target_pairs={{0,24},{1,25},{2,26},{3,27},{4,28},{5,29},{6,30},{7,31},{8,16},{9,... | collective-permute-start | bytes 24584 | tf_op jit(solution)/shard_map/ppermute | solution.py:499
  181.6 4.5 %collective-permute-start.30 = (f32[16,128]{1,0:T(8,128)S(1)}, f32[16,128]{1,0:T(8,128)S(1)}, u32[]{:S(2)}, u32[]{:S(2)}) collective-permute-start(f32[16,128]{1,0:T(8,128)S(1)} %get-tuple-element.127), channel_id=1, source_target_pairs={{0,16},{1,17},{2,18},{3,19},{4,20},{5,21},{6,22},{7,23},{8,24},{9,... | collective-permute-start | bytes 24584 | tf_op jit(solution)/shard_map/ppermute | solution.py:499
  181.6 3.7 %collective-permute-start.29 = (f32[16,128]{1,0:T(8,128)S(1)}, f32[16,128]{1,0:T(8,128)S(1)}, u32[]{:S(2)}, u32[]{:S(2)}) collective-permute-start(f32[16,128]{1,0:T(8,128)S(1)} %get-tuple-element.127), channel_id=1, source_target_pairs={{0,8},{1,9},{2,10},{3,11},{4,12},{5,13},{6,14},{7,15},{8,0},{9,1},... | collective-permute-start | bytes 24584 | tf_op jit(solution)/shard_map/ppermute | solution.py:499
  186.2 4.0 %collective-permute-start.32 = (f32[64,128]{1,0:T(8,128)S(1)}, f32[64,128]{1,0:T(8,128)S(1)}, u32[]{:S(2)}, u32[]{:S(2)}) collective-permute-start(f32[64,128]{1,0:T(8,128)S(1)} %get-tuple-element.150), channel_id=1, source_target_pairs={{0,2},{1,3},{2,0},{3,1},{4,6},{5,7},{6,4},{7,5},{8,10},{9,11},{10,... | collective-permute-start | bytes 98312 | tf_op jit(solution)/shard_map/ppermute | solution.py:499
  186.9 5.4 %collective-permute-start.34 = (f32[64,128]{1,0:T(8,128)S(1)}, f32[64,128]{1,0:T(8,128)S(1)}, u32[]{:S(2)}, u32[]{:S(2)}) collective-permute-start(f32[64,128]{1,0:T(8,128)S(1)} %get-tuple-element.150), channel_id=1, source_target_pairs={{0,6},{1,7},{2,4},{3,5},{4,2},{5,3},{6,0},{7,1},{8,14},{9,15},{10,... | collective-permute-start | bytes 98312 | tf_op jit(solution)/shard_map/ppermute | solution.py:499
  188.3 3.9 %collective-permute-start.33 = (f32[64,128]{1,0:T(8,128)S(1)}, f32[64,128]{1,0:T(8,128)S(1)}, u32[]{:S(2)}, u32[]{:S(2)}) collective-permute-start(f32[64,128]{1,0:T(8,128)S(1)} %get-tuple-element.150), channel_id=1, source_target_pairs={{0,4},{1,5},{2,6},{3,7},{4,0},{5,1},{6,2},{7,3},{8,12},{9,13},{10,... | collective-permute-start | bytes 98312 | tf_op jit(solution)/shard_map/ppermute | solution.py:499
  192.2 1.4 collective-permute-start.35
  (3 other events, 15.9 us)

commit v6 on v5

--- a/solution.py
+++ b/solution.py
@@ -236,7 +236,7 @@
     table, out_turned, up_turned, down_turned, columns, up_bias, slopes = refs[
         12 + amount : 19 + amount
     ]
-    acc_down, acc_up, acc_out, acc_vec, done, *kept = refs[19 + amount :]
+    acc_down, acc_up, acc_out, acc_vec, *kept = refs[19 + amount :]
     step = pl.program_id(0)
     chunk = TILE
     chunks = FF // chunk
@@ -368,7 +368,6 @@
     @pl.when(step == pl.num_programs(0) - 1)
     def _():
         parts = weight_parts(kept[each:], acc_down, acc_up, acc_out)
-        copies = []
         for source, begin, width, some in (
             (acc_up, D, FF, parts[8:16]),
             (acc_down, D + FF, FF, parts[:8]),
@@ -376,16 +375,7 @@
         ):
             for part in some:
                 part()
-            halves = (table.at[: D // 2, :], table.at[D // 2 :, :])
-            spread_blocks(halves, source, codes, mine_ref[0], begin, width)
-            across = slice(begin, begin + width)
-            for half, target in zip(halves, (keep_ref, send_ref), strict=True):
-                copies.append(
-                    pltpu.make_async_copy(
-                        half.at[:, across], target.at[:, across], done.at[len(copies)]
-                    )
-                )
-                copies[-1].start()
+            spread_blocks((keep_ref, send_ref), source, codes, mine_ref[0], begin, width)
         up_sums = jnp.broadcast_to(acc_up[D : D + 1, :], (LANES, FF))
         for at in range(0, FF, LANES):
             up_bias[at : at + LANES, :] = up_sums[:, at : at + LANES].T
@@ -397,8 +387,6 @@
         for at in range(4):
             vectors = jnp.where(lane == 8 + at, up_bias[pl.ds(at, D, stride=4), :], vectors)
         sums_ref[...] = vectors
-        for copy in copies:
-            copy.wait()
 
 
 def attend_back_kernel(
@@ -488,11 +476,22 @@
     share_ref[...] = jnp.where(lane == VECTORS, squares, vectors)
 
 
-def settle_kernel(codes, mine_ref, near_ref, far_ref, vectors_ref, norm_ref, table):
+def settle_kernel(
+    codes, mine_ref, near_ref, far_ref, grad_ref, params_ref, momenta_ref, averages_ref,
+    vectors_ref, norm_ref, new_params_ref, new_momenta_ref, new_averages_ref, table,
+):
     place_blocks(table, (near_ref, far_ref), codes, mine_ref[0])
     vectors_ref[...] = table[...].T[:VECTORS, :]
     squares = jnp.sum(table[...], axis=0, keepdims=True)[:, VECTORS : VECTORS + 1]
-    norm_ref[...] = jnp.broadcast_to(jnp.sqrt(squares), (8, LANES))
+    norm = jnp.sqrt(squares)
+    norm_ref[0] = norm[0, 0]
+    factor = jnp.minimum(1.0, CLIP_NORM / (norm + 1e-06))[0, 0]
+    clipped = grad_ref[...] * factor
+    momenta = MOMENTUM * momenta_ref[...] + clipped
+    params = params_ref[...] - LEARN_RATE * (clipped + MOMENTUM * momenta)
+    new_momenta_ref[...] = momenta
+    new_params_ref[...] = params
+    new_averages_ref[...] = AVERAGE_DECAY * averages_ref[...] + (1.0 - AVERAGE_DECAY) * params
 
 
 def exchange(values, bit, count):
@@ -671,14 +670,14 @@
         ]
         + [whole(piece.shape) for piece in rest_pieces],
         out_specs=[down, across, across]
-        + [pl.BlockSpec(memory_space=pl.ANY)] * 2
+        + [resident()] * 2
         + [whole((D, LANES))],
         out_shape=[
             shaped((slots, D), bf16),
             shaped((D, slots), bf16),
             shaped((D, slots), bf16),
-            shaped((D // 2, REST_WIDTH), bf16),
-            shaped((D // 2, REST_WIDTH), bf16),
+            pltpu.VMEM((D // 2, REST_WIDTH), bf16),
+            pltpu.VMEM((D // 2, REST_WIDTH), bf16),
             shaped((D, LANES), f32),
         ],
         scratch_shapes=[
@@ -693,10 +692,9 @@
             pltpu.VMEM((D + BLOCK, FF), f32),
             pltpu.VMEM((D, D), f32),
             pltpu.VMEM((6, D, LANES), f32),
-            pltpu.SemaphoreType.DMA((6,)),
         ]
         + [pltpu.VMEM((rows, TILE), bf16) for rows in (FF, FF, D + BLOCK, D, D, D)] * 2,
-        compiler_params=params_of(46 if direct else 60),
+        compiler_params=params_of(50 if direct else 54),
         name="feed",
     )(origin, limits, xt, attended, cotangent, vectors, *rest_pieces)
 
@@ -777,23 +775,26 @@
     shares = share
     for masks in outer:
         shares = jnp.concatenate(gather_phase(shares, masks, count), axis=0)
-    vector_grads, norms = pl.pallas_call(
+    own_grad = jnp.concatenate([own_first, own_rest, share[:, :VECTORS]], axis=1).reshape(-1)
+    flat = shaped(params.shape, f32)
+    vector_grads, norms, new_params, new_momenta, new_averages = pl.pallas_call(
         functools.partial(settle_kernel, codes),
-        in_specs=[smem()] + [resident()] * 2,
-        out_specs=[whole((VECTORS, D)), whole((8, LANES))],
-        out_shape=[shaped((VECTORS, D), f32), shaped((8, LANES), f32)],
+        in_specs=[smem()] + [resident()] * 6,
+        out_specs=[whole((VECTORS, D)), smem()] + [resident()] * 3,
+        out_shape=[shaped((VECTORS, D), f32), shaped((1,), f32)] + [flat] * 3,
         scratch_shapes=[pltpu.VMEM((D, LANES), f32)],
-        compiler_params=params_of(8),
+        compiler_params=params_of(16),
         name="settle",
-    )(origin, *to_kernel(gather_phase(shares, phases[0], count), order, 2))
-    grad_norm = norms[0, 0]
+    )(
+        origin,
+        *to_kernel(gather_phase(shares, phases[0], count), order, 2),
+        own_grad,
+        params,
+        momenta,
+        averages,
+    )
+    grad_norm = norms.reshape(())
     vector_grads = vector_grads.T
-
-    own_grad = jnp.concatenate([own_first, own_rest, share[:, :VECTORS]], axis=1).reshape(-1)
-    clipped = own_grad * jnp.minimum(1.0, CLIP_NORM / (grad_norm + 1e-06))
-    new_momenta = MOMENTUM * momenta + clipped
-    new_params = params - LEARN_RATE * (clipped + MOMENTUM * new_momenta)
-    new_averages = AVERAGE_DECAY * averages + (1.0 - AVERAGE_DECAY) * new_params
     return (
         layer_output, input_grad, grad_norm, vector_grads, new_params, new_momenta, new_averages,
     )

time: 197 us -> 195 us (0.990)
  other arithmetic: 5.88 us -> 3.01 us
  local copies, waits for them, and re-layouts: 1.2 us -> 3.83 us
  waiting for transfers between devices: 39.9 us -> 37.6 us
    unnamed x40 -> x60, local copies, waits for them, and re-layouts: 0.16 us -> 3.3 us
    ppermute x36, waiting for transfers between devices: 39.9 us -> 37.6 us  [exchange(): return lax.ppermute(values, 'dp', [(at, at ^ bit) for at in range(count)])]
  transfers between devices with their start and end apart: 36 -> 36, of which waited for: 18 -> 19; matrix products, arithmetic and copies ran while one was open for 1% -> 1% of each run, Pallas kernels for 27% -> 28%
where the time goes in v6:
time: 195 us; the launch traced here: 194 us
  Pallas kernels  107 us (55%)
  starting transfers between devices  41.3 us (21%)
  waiting for transfers between devices  37.6 us (19%)
  local copies, waits for them, and re-layouts  3.83 us (2%)
  other arithmetic  3.01 us (2%)
    pallas_call x1, Pallas kernels, body(): pl.pallas_call(functools.partial(feed_kernel, slow_codes, len(rest_pieces...  51.2 us
    ppermute x36, starting transfers between devices, exchange(): return lax.ppermute(values, 'dp', [(at, at ^ bit) for at in range(count)])  41.3 us
    ppermute x36, waiting for transfers between devices, exchange(): return lax.ppermute(values, 'dp', [(at, at ^ bit) for at in range(count)])  37.6 us
    pallas_call x1, Pallas kernels, body(): pl.pallas_call(functools.partial(attend_back_kernel, codes), grid=(PAIRS,...  22.2 us
    pallas_call x1, Pallas kernels, body(): pl.pallas_call(attend_kernel, grid=(PAIRS,), in_specs=[smem(), whole((blo...  15 us
    pallas_call x1, Pallas kernels, body(): pl.pallas_call(functools.partial(project_kernel, codes), grid=(steps,), i...  10.2 us
    pallas_call x1, Pallas kernels, body(): pl.pallas_call(input_kernel, grid=(steps,), in_specs=[pl.BlockSpec((PAIRS...  6.41 us
  transfers between devices with their start and end apart: 36, of which 19 were waited for; matrix products, arithmetic and copies ran while one was open for 1% of the time, Pallas kernels for 28%

profile of v6, /device:TPU:0, one launch (start us, length us, event | category | flops | bytes accessed | tf_op | source)
XLA Modules:
  0.0 194.4 jit_solution(5999902514010323486)
XLA Ops:
  0.6 1.0 convert_element_type.191
  2.0 4.1 %collective-permute-start.1 = (bf16[16,1664]{1,0:T(8,128)(2,1)S(1)}, bf16[16,1664]{1,0:T(8,128)(2,1)S(1)}, u32[]{:S(2)}, u32[]{:S(2)}) collective-permute-start(bf16[16,1664]{1,0:T(8,128)(2,1)S(1)} %get-tuple-element.151), channel_id=1, source_target_pairs={{0,16},{1,17},{2,18},{3,19},{4,20},{5,21},{6,22},{7,23},{8,24},{9,... | collective-permute-start | bytes 159752 | tf_op jit(solution)/shard_map/ppermute | solution.py:498
  6.1 1.6 collective-permute-start
  7.7 2.0 %collective-permute-start.6 = (bf16[16,4608]{1,0:T(8,128)(2,1)S(1)}, bf16[16,4608]{1,0:T(8,128)(2,1)S(1)}, u32[]{:S(2)}, u32[]{:S(2)}) collective-permute-start(bf16[16,4608]{1,0:T(8,128)(2,1)S(1)} %slice.194), channel_id=1, source_target_pairs={{0,16},{1,17},{2,18},{3,19},{4,20},{5,21},{6,22},{7,23},{8,24},{9,... | collective-permute-start | bytes 442376 | tf_op jit(solution)/shard_map/ppermute | solution.py:498
  10.2 3.9 %collective-permute-done.2 = bf16[16,1664]{1,0:T(8,128)(2,1)S(1)} collective-permute-done((bf16[16,1664]{1,0:T(8,128)(2,1)S(1)}, bf16[16,1664]{1,0:T(8,128)(2,1)S(1)}, u32[]{:S(2)}, u32[]{:S(2)}) %collective-permute-start.2) | collective-permute-done | bytes 53280 | tf_op jit(solution)/shard_map/ppermute | solution.py:498
  14.2 2.5 %collective-permute-start.5 = (bf16[64,1664]{1,0:T(8,128)(2,1)S(1)}, bf16[64,1664]{1,0:T(8,128)(2,1)S(1)}, u32[]{:S(2)}, u32[]{:S(2)}) collective-permute-start(bf16[64,1664]{1,0:T(8,128)(2,1)S(1)} %pad_maximum_fusion.3), channel_id=1, source_target_pairs={{0,6},{1,7},{2,4},{3,5},{4,2},{5,3},{6,0},{7,1},{8,14},{9,15},{10,... | collective-permute-start | bytes 638984 | tf_op jit(solution)/shard_map/ppermute | solution.py:498
  17.8 0.8 collective-permute-done.6
  18.6 2.2 %collective-permute-start.7 = (bf16[32,4608]{1,0:T(8,128)(2,1)S(1)}, bf16[32,4608]{1,0:T(8,128)(2,1)S(1)}, u32[]{:S(2)}, u32[]{:S(2)}) collective-permute-start(bf16[32,4608]{1,0:T(8,128)(2,1)S(1)} %pad_maximum_fusion.2), channel_id=1, source_target_pairs={{0,8},{1,9},{2,10},{3,11},{4,12},{5,13},{6,14},{7,15},{8,0},{9,1},... | collective-permute-start | bytes 884744 | tf_op jit(solution)/shard_map/ppermute | solution.py:498
  20.8 3.9 %collective-permute-done.3 = bf16[64,1664]{1,0:T(8,128)(2,1)S(1)} collective-permute-done((bf16[64,1664]{1,0:T(8,128)(2,1)S(1)}, bf16[64,1664]{1,0:T(8,128)(2,1)S(1)}, u32[]{:S(2)}, u32[]{:S(2)}) %collective-permute-start.3) | collective-permute-done | bytes 213024 | tf_op jit(solution)/shard_map/ppermute | solution.py:498
  24.8 1.8 collective-permute-done.7
  26.7 2.5 %collective-permute-start.11 = (bf16[64,4608]{1,0:T(8,128)(2,1)S(1)}, bf16[64,4608]{1,0:T(8,128)(2,1)S(1)}, u32[]{:S(2)}, u32[]{:S(2)}) collective-permute-start(bf16[64,4608]{1,0:T(8,128)(2,1)S(1)} %pad_maximum_fusion.refs_6_), channel_id=1, source_target_pairs={{0,6},{1,7},{2,4},{3,5},{4,2},{5,3},{6,0},{7,1},{8,14},{9,15},{10,... | collective-permute-start | bytes 1769480 | tf_op jit(solution)/shard_map/ppermute | solution.py:498
  31.5 10.2 %project.1 = (bf16[512,2048]{1,0:T(8,128)(2,1)}, bf16[512,2048]{1,0:T(8,128)(2,1)}, bf16[512,2048]{1,0:T(8,128)(2,1)}, bf16[512,2048]{1,0:T(8,128)(2,1)}, bf16[2...) custom-call(s32[1]{0:T(128)} %bitcast.mine_ref.refs_0_, ...), custom_call_target="tpu_custom_call" | custom-call | tf_op jit(solution)/shard_map/project/pallas_call | solution.py:629
  41.8 0.7 copy-done.13
  42.5 15.0 %attend.1 = (bf16[512,2048]{1,0:T(8,128)(2,1)}, f32[4,16,256]{2,1,0:T(8,128)}) custom-call(s32[3]{0:T(128)} %pad_add_fusion.limits_ref.refs_1_, s32[16,128]{1,0:T(8,128)} %bitcast.5, bf16[512,2048]{1,0:T(8,128)(2,1)} %get-tuple-element.75.qt_ref, bf16[2048,512]{1,0:T(8,128)(2,1)} %get-tuple-element.76.k_ref, bf16[512,2048]{1,0:T(8,128)(2,1)} %get-tuple-element.77.vt_ref), custom_call_target="tpu_custom_call" | custom-call | tf_op jit(solution)/shard_map/attend/pallas_call | solution.py:650
  57.6 0.7 collective-permute-start.13
  58.8 1.4 collective-permute-done.13.refs_11_
  60.7 0.8 collective-permute-done.15.refs_13_
  61.6 0.8 copy-done.23
  62.5 51.2 %feed.1 = (bf16[2048,512]{1,0:T(8,128)(2,1)}, bf16[512,2048]{1,0:T(8,128)(2,1)}, bf16[512,2048]{1,0:T(8,128)(2,1)}, bf16[256,4608]{1,0:T(8,128)(2,1)S(1)}, bf16[...) custom-call(s32[1]{0:T(128)} %bitcast.mine_ref.refs_0_, s32[3]{0:T(128)} %pad_add_fusion.limits_ref.refs_1_, ...), custom_call_target="tpu_custom_call" | custom-call | tf_op jit(solution)/shard_map/feed/pallas_call | solution.py:664
  114.1 4.2 %collective-permute-done.16 = bf16[256,4608]{1,0:T(8,128)(2,1)S(1)} collective-permute-done((bf16[256,4608]{1,0:T(8,128)(2,1)S(1)}, bf16[256,4608]{1,0:T(8,128)(2,1)S(1)}, u32[]{:S(2)}, u32[]{:S(2)}) %collective-permute-start.16) | collective-permute-done | bytes 2359328 | tf_op jit(solution)/shard_map/ppermute | solution.py:498
  118.9 1.4 collective-permute-start.17
  120.3 1.5 collective-permute-start.18
  122.5 1.6 copy-done.7
  124.1 22.2 %attend_back.1 = (bf16[4,384,2048]{2,1,0:T(8,128)(2,1)S(1)}, bf16[256,1664]{1,0:T(8,128)(2,1)S(1)}, bf16[256,1664]{1,0:T(8,128)(2,1)S(1)}) custom-call(s32[1]{0:T(128)} %bitcast.mine_ref.refs_0_, s32[3]{0:T(128)S(1)} %copy-done.16, s32[16,128]{1,0:T(8,128)S(1)} %bitcast.6, bf16[512,2048]{1,0:T(8,128)(2,1)S(1)} %copy-done.2, bf16[512,2048]{1,0:T(8,128)(2,1)S(1)} %copy-done, ...), custom_call_target="tpu_custom_call" | custom-call | tf_op jit(solution)/shard_map/attend_back/pallas_call | solution.py:710
  146.4 1.9 collective-permute-done.18
  148.3 2.4 %collective-permute-done.20 = bf16[256,1664]{1,0:T(8,128)(2,1)S(1)} collective-permute-done((bf16[256,1664]{1,0:T(8,128)(2,1)S(1)}, bf16[256,1664]{1,0:T(8,128)(2,1)S(1)}, u32[]{:S(2)}, u32[]{:S(2)}) %collective-permute-start.20) | collective-permute-done | bytes 852000 | tf_op jit(solution)/shard_map/ppermute | solution.py:498
  150.9 1.3 collective-permute-start.21
  152.2 0.8 collective-permute-start.22
  153.0 1.4 collective-permute-start.23
  154.8 1.0 collective-permute-start.24
  155.8 6.4 %input_grad.1 = f32[2048,512]{1,0:T(8,128)} custom-call(bf16[4,384,2048]{2,1,0:T(8,128)(2,1)S(1)} %get-tuple-element.113.grads_ref, bf16[512,1536]{1,0:T(8,128)(2,1)S(1)} %copy-done.9, bf16[512,2048]{1,0:T(8,128)(2,1)S(1)} %copy-done.4), custom_call_target="tpu_custom_call" | custom-call | tf_op jit(solution)/shard_map/input_grad/pallas_call | solution.py:747
  162.2 1.6 collective-permute-done.23
  163.9 2.1 %collective-permute-start.28 = (bf16[16,4608]{1,0:T(8,128)(2,1)S(1)}, bf16[16,4608]{1,0:T(8,128)(2,1)S(1)}, u32[]{:S(2)}, u32[]{:S(2)}) collective-permute-start(bf16[16,4608]{1,0:T(8,128)(2,1)S(1)} %add_convert_fusion.10), channel_id=1, source_target_pairs={{0,16},{1,17},{2,18},{3,19},{4,20},{5,21},{6,22},{7,23},{8,24},{9,... | collective-permute-start | bytes 442376 | tf_op jit(solution)/shard_map/ppermute | solution.py:498
  166.0 1.3 collective-permute-start.27
  167.3 1.9 collective-permute-start.26
  169.2 1.2 collective-permute-start.25
  170.4 5.7 %collective-permute-done.28 = bf16[16,4608]{1,0:T(8,128)(2,1)S(1)} collective-permute-done((bf16[16,4608]{1,0:T(8,128)(2,1)S(1)}, bf16[16,4608]{1,0:T(8,128)(2,1)S(1)}, u32[]{:S(2)}, u32[]{:S(2)}) %collective-permute-start.28) | collective-permute-done | bytes 147488 | tf_op jit(solution)/shard_map/ppermute | solution.py:498
  176.1 1.5 collective-permute-done.26.refs_2_
  177.8 3.0 %collective-permute-start.31 = (f32[16,128]{1,0:T(8,128)S(1)}, f32[16,128]{1,0:T(8,128)S(1)}, u32[]{:S(2)}, u32[]{:S(2)}) collective-permute-start(f32[16,128]{1,0:T(8,128)S(1)} %get-tuple-element.130), channel_id=1, source_target_pairs={{0,24},{1,25},{2,26},{3,27},{4,28},{5,29},{6,30},{7,31},{8,16},{9,... | collective-permute-start | bytes 24584 | tf_op jit(solution)/shard_map/ppermute | solution.py:498
  180.8 1.5 collective-permute-start.29
  182.3 2.2 %collective-permute-done.29 = f32[16,128]{1,0:T(8,128)S(1)} collective-permute-done((f32[16,128]{1,0:T(8,128)S(1)}, f32[16,128]{1,0:T(8,128)S(1)}, u32[]{:S(2)}, u32[]{:S(2)}) %collective-permute-start.29) | collective-permute-done | bytes 8224 | tf_op jit(solution)/shard_map/ppermute | solution.py:498
  184.4 0.9 collective-permute-done.30
  185.3 0.8 collective-permute-start.32
  186.1 1.3 collective-permute-start.34
  187.4 1.5 collective-permute-start.33
  189.3 2.0 %collective-permute-done.33 = f32[64,128]{1,0:T(8,128)S(1)} collective-permute-done((f32[64,128]{1,0:T(8,128)S(1)}, f32[64,128]{1,0:T(8,128)S(1)}, u32[]{:S(2)}, u32[]{:S(2)}) %collective-permute-start.33) | collective-permute-done | bytes 32800 | tf_op jit(solution)/shard_map/ppermute | solution.py:498
  191.7 1.1 collective-permute-done.35.far_ref
  192.8 1.4 settle.1
  (113 shorter events, 8.3 us)
Async XLA Ops:
  2.0 28.9 %copy-start.24 = (s32[2]{0:T(128)S(1)}, s32[2]{0:T(128)}, u32[]{:S(2)}) copy-start(s32[2]{0:T(128)} %param.11) | copy-start | bytes 28
  2.0 7.7 %collective-permute-start.1 = (bf16[16,1664]{1,0:T(8,128)(2,1)S(1)}, bf16[16,1664]{1,0:T(8,128)(2,1)S(1)}, u32[]{:S(2)}, u32[]{:S(2)}) collective-permute-start(bf16[16,1664]{1,0:T(8,128)(2,1)S(1)} %get-tuple-element.151), channel_id=1, source_target_pairs={{0,16},{1,17},{2,18},{3,19},{4,20},{5,21},{6,22},{7,23},{8,24},{9,... | collective-permute-start | bytes 159752 | tf_op jit(solution)/shard_map/ppermute | solution.py:498
  6.1 4.1 %collective-permute-start = (bf16[16,1664]{1,0:T(8,128)(2,1)S(1)}, bf16[16,1664]{1,0:T(8,128)(2,1)S(1)}, u32[]{:S(2)}, u32[]{:S(2)}) collective-permute-start(bf16[16,1664]{1,0:T(8,128)(2,1)S(1)} %get-tuple-element.151), channel_id=1, source_target_pairs={{0,8},{1,9},{2,10},{3,11},{4,12},{5,13},{6,14},{7,15},{8,0},{9,1},... | collective-permute-start | bytes 159752 | tf_op jit(solution)/shard_map/ppermute | solution.py:498
  7.7 6.5 %collective-permute-start.2 = (bf16[16,1664]{1,0:T(8,128)(2,1)S(1)}, bf16[16,1664]{1,0:T(8,128)(2,1)S(1)}, u32[]{:S(2)}, u32[]{:S(2)}) collective-permute-start(bf16[16,1664]{1,0:T(8,128)(2,1)S(1)} %get-tuple-element.151), channel_id=1, source_target_pairs={{0,24},{1,25},{2,26},{3,27},{4,28},{5,29},{6,30},{7,31},{8,16},{9,... | collective-permute-start | bytes 159752 | tf_op jit(solution)/shard_map/ppermute | solution.py:498
  7.7 10.9 %collective-permute-start.6 = (bf16[16,4608]{1,0:T(8,128)(2,1)S(1)}, bf16[16,4608]{1,0:T(8,128)(2,1)S(1)}, u32[]{:S(2)}, u32[]{:S(2)}) collective-permute-start(bf16[16,4608]{1,0:T(8,128)(2,1)S(1)} %slice.194), channel_id=1, source_target_pairs={{0,16},{1,17},{2,18},{3,19},{4,20},{5,21},{6,22},{7,23},{8,24},{9,... | collective-permute-start | bytes 442376 | tf_op jit(solution)/shard_map/ppermute | solution.py:498
  14.2 10.6 %collective-permute-start.5 = (bf16[64,1664]{1,0:T(8,128)(2,1)S(1)}, bf16[64,1664]{1,0:T(8,128)(2,1)S(1)}, u32[]{:S(2)}, u32[]{:S(2)}) collective-permute-start(bf16[64,1664]{1,0:T(8,128)(2,1)S(1)} %pad_maximum_fusion.3), channel_id=1, source_target_pairs={{0,6},{1,7},{2,4},{3,5},{4,2},{5,3},{6,0},{7,1},{8,14},{9,15},{10,... | collective-permute-start | bytes 638984 | tf_op jit(solution)/shard_map/ppermute | solution.py:498
  16.7 8.0 %collective-permute-start.4 = (bf16[64,1664]{1,0:T(8,128)(2,1)S(1)}, bf16[64,1664]{1,0:T(8,128)(2,1)S(1)}, u32[]{:S(2)}, u32[]{:S(2)}) collective-permute-start(bf16[64,1664]{1,0:T(8,128)(2,1)S(1)} %pad_maximum_fusion.3), channel_id=1, source_target_pairs={{0,4},{1,5},{2,6},{3,7},{4,0},{5,1},{6,2},{7,3},{8,12},{9,13},{10,... | collective-permute-start | bytes 638984 | tf_op jit(solution)/shard_map/ppermute | solution.py:498
  17.2 7.5 %collective-permute-start.3 = (bf16[64,1664]{1,0:T(8,128)(2,1)S(1)}, bf16[64,1664]{1,0:T(8,128)(2,1)S(1)}, u32[]{:S(2)}, u32[]{:S(2)}) collective-permute-start(bf16[64,1664]{1,0:T(8,128)(2,1)S(1)} %pad_maximum_fusion.3), channel_id=1, source_target_pairs={{0,2},{1,3},{2,0},{3,1},{4,6},{5,7},{6,4},{7,5},{8,10},{9,11},{10,... | collective-permute-start | bytes 638984 | tf_op jit(solution)/shard_map/ppermute | solution.py:498
  18.6 8.0 %collective-permute-start.7 = (bf16[32,4608]{1,0:T(8,128)(2,1)S(1)}, bf16[32,4608]{1,0:T(8,128)(2,1)S(1)}, u32[]{:S(2)}, u32[]{:S(2)}) collective-permute-start(bf16[32,4608]{1,0:T(8,128)(2,1)S(1)} %pad_maximum_fusion.2), channel_id=1, source_target_pairs={{0,8},{1,9},{2,10},{3,11},{4,12},{5,13},{6,14},{7,15},{8,0},{9,1},... | collective-permute-start | bytes 884744 | tf_op jit(solution)/shard_map/ppermute | solution.py:498
  26.6 30.9 %copy-start.17 = (bf16[64,4608]{1,0:T(8,128)(2,1)}, bf16[64,4608]{1,0:T(8,128)(2,1)S(1)}, u32[]{:S(2)}) copy-start(bf16[64,4608]{1,0:T(8,128)(2,1)S(1)} %pad_maximum_fusion.refs_6_) | copy-start | bytes 1769476
  26.6 4.9 %collective-permute-start.8 = (bf16[256,1664]{1,0:T(8,128)(2,1)S(1)}, bf16[256,1664]{1,0:T(8,128)(2,1)S(1)}, u32[]{:S(2)}, u32[]{:S(2)}) collective-permute-start(bf16[256,1664]{1,0:T(8,128)(2,1)S(1)} %constant_dynamic-update-slice_fusion.near_ref), channel_id=1, source_target_pairs={{0,1},{1,0},{2,3},{3,2},{4,5},{5,4},{6,7},{7,6},{8,9},{9,8},{10,11... | collective-permute-start | bytes 2555912 | tf_op jit(solution)/shard_map/ppermute | solution.py:498
  26.7 30.8 %collective-permute-start.11 = (bf16[64,4608]{1,0:T(8,128)(2,1)S(1)}, bf16[64,4608]{1,0:T(8,128)(2,1)S(1)}, u32[]{:S(2)}, u32[]{:S(2)}) collective-permute-start(bf16[64,4608]{1,0:T(8,128)(2,1)S(1)} %pad_maximum_fusion.refs_6_), channel_id=1, source_target_pairs={{0,6},{1,7},{2,4},{3,5},{4,2},{5,3},{6,0},{7,1},{8,14},{9,15},{10,... | collective-permute-start | bytes 1769480 | tf_op jit(solution)/shard_map/ppermute | solution.py:498
  29.2 28.3 %collective-permute-start.10 = (bf16[64,4608]{1,0:T(8,128)(2,1)S(1)}, bf16[64,4608]{1,0:T(8,128)(2,1)S(1)}, u32[]{:S(2)}, u32[]{:S(2)}) collective-permute-start(bf16[64,4608]{1,0:T(8,128)(2,1)S(1)} %pad_maximum_fusion.refs_6_), channel_id=1, source_target_pairs={{0,4},{1,5},{2,6},{3,7},{4,0},{5,1},{6,2},{7,3},{8,12},{9,13},{10,... | collective-permute-start | bytes 1769480 | tf_op jit(solution)/shard_map/ppermute | solution.py:498
  29.7 27.8 %collective-permute-start.9 = (bf16[64,4608]{1,0:T(8,128)(2,1)S(1)}, bf16[64,4608]{1,0:T(8,128)(2,1)}, u32[]{:S(2)}, u32[]{:S(2)}) collective-permute-start(bf16[64,4608]{1,0:T(8,128)(2,1)S(1)} %pad_maximum_fusion.refs_6_), channel_id=1, source_target_pairs={{0,2},{1,3},{2,0},{3,1},{4,6},{5,7},{6,4},{7,5},{8,10},{9,11},{10,... | collective-permute-start | bytes 1769480 | tf_op jit(solution)/shard_map/ppermute | solution.py:498
  31.5 27.3 %collective-permute-start.12 = (bf16[64,4608]{1,0:T(8,128)(2,1)S(1)}, bf16[64,4608]{1,0:T(8,128)(2,1)S(1)}, u32[]{:S(2)}, u32[]{:S(2)}) collective-permute-start(bf16[64,4608]{1,0:T(8,128)(2,1)S(1)} %pad_maximum_fusion.refs_6_), channel_id=1, source_target_pairs={{0,1},{1,0},{2,3},{3,2},{4,5},{5,4},{6,7},{7,6},{8,9},{9,8},{10,11... | collective-permute-start | bytes 1769480 | tf_op jit(solution)/shard_map/ppermute | solution.py:498
  57.5 4.9 %copy-start.18 = (bf16[64,4608]{1,0:T(8,128)(2,1)}, bf16[64,4608]{1,0:T(8,128)(2,1)S(1)}, u32[]{:S(2)}) copy-start(bf16[64,4608]{1,0:T(8,128)(2,1)S(1)} %collective-permute-done.11.refs_9_) | copy-start | bytes 1769476
  57.5 4.9 %copy-start.19 = (bf16[64,4608]{1,0:T(8,128)(2,1)}, bf16[64,4608]{1,0:T(8,128)(2,1)S(1)}, u32[]{:S(2)}) copy-start(bf16[64,4608]{1,0:T(8,128)(2,1)S(1)} %collective-permute-done.10.refs_8_) | copy-start | bytes 1769476
  57.6 2.6 %collective-permute-start.13 = (bf16[64,4608]{1,0:T(8,128)(2,1)}, bf16[64,4608]{1,0:T(8,128)(2,1)S(1)}, u32[]{:S(2)}, u32[]{:S(2)}) collective-permute-start(bf16[64,4608]{1,0:T(8,128)(2,1)} %collective-permute-done.9.refs_7_), channel_id=1, source_target_pairs={{0,1},{1,0},{2,3},{3,2},{4,5},{5,4},{6,7},{7,6},{8,9},{9,8},{10,11... | collective-permute-start | bytes 1769480 | tf_op jit(solution)/shard_map/ppermute | solution.py:498
  58.3 2.5 %collective-permute-start.14 = (bf16[64,4608]{1,0:T(8,128)(2,1)S(1)}, bf16[64,4608]{1,0:T(8,128)(2,1)S(1)}, u32[]{:S(2)}, u32[]{:S(2)}) collective-permute-start(bf16[64,4608]{1,0:T(8,128)(2,1)S(1)} %collective-permute-done.10.refs_8_), channel_id=1, source_target_pairs={{0,1},{1,0},{2,3},{3,2},{4,5},{5,4},{6,7},{7,6},{8,9},{9,8},{10,11... | collective-permute-start | bytes 1769480 | tf_op jit(solution)/shard_map/ppermute | solution.py:498
  58.4 3.2 %collective-permute-start.15 = (bf16[64,4608]{1,0:T(8,128)(2,1)S(1)}, bf16[64,4608]{1,0:T(8,128)(2,1)S(1)}, u32[]{:S(2)}, u32[]{:S(2)}) collective-permute-start(bf16[64,4608]{1,0:T(8,128)(2,1)S(1)} %collective-permute-done.11.refs_9_), channel_id=1, source_target_pairs={{0,1},{1,0},{2,3},{3,2},{4,5},{5,4},{6,7},{7,6},{8,9},{9,8},{10,11... | collective-permute-start | bytes 1769480 | tf_op jit(solution)/shard_map/ppermute | solution.py:498
  62.4 60.0 %copy-start.3 = (bf16[512,2048]{1,0:T(8,128)(2,1)S(1)}, bf16[512,2048]{1,0:T(8,128)(2,1)}, u32[]{:S(2)}) copy-start(bf16[512,2048]{1,0:T(8,128)(2,1)} %get-tuple-element.80.refs_3_.att_ref) | copy-start | bytes 6291460
  62.4 60.0 %copy-start.5 = (bf16[512,2048]{1,0:T(8,128)(2,1)S(1)}, bf16[512,2048]{1,0:T(8,128)(2,1)}, u32[]{:S(2)}) copy-start(bf16[512,2048]{1,0:T(8,128)(2,1)} %get-tuple-element.87.kt_ref) | copy-start | bytes 6291460
  62.5 60.0 %copy-start.6 = (bf16[2048,512]{1,0:T(8,128)(2,1)S(1)}, bf16[2048,512]{1,0:T(8,128)(2,1)}, u32[]{:S(2)}) copy-start(bf16[2048,512]{1,0:T(8,128)(2,1)} %get-tuple-element.88.v_ref) | copy-start | bytes 6291460
  113.7 4.6 %collective-permute-start.16 = (bf16[256,4608]{1,0:T(8,128)(2,1)S(1)}, bf16[256,4608]{1,0:T(8,128)(2,1)S(1)}, u32[]{:S(2)}, u32[]{:S(2)}) collective-permute-start(bf16[256,4608]{1,0:T(8,128)(2,1)S(1)} %get-tuple-element.91), channel_id=1, source_target_pairs={{0,1},{1,0},{2,3},{3,2},{4,5},{5,4},{6,7},{7,6},{8,9},{9,8},{10,11... | collective-permute-start | bytes 7077896 | tf_op jit(solution)/shard_map/ppermute | solution.py:498
  118.9 27.5 %collective-permute-start.17 = (bf16[64,4608]{1,0:T(8,128)(2,1)S(1)}, bf16[64,4608]{1,0:T(8,128)(2,1)S(1)}, u32[]{:S(2)}, u32[]{:S(2)}) collective-permute-start(bf16[64,4608]{1,0:T(8,128)(2,1)S(1)} %get-tuple-element.99), channel_id=1, source_target_pairs={{0,2},{1,3},{2,0},{3,1},{4,6},{5,7},{6,4},{7,5},{8,10},{9,11},{10,... | collective-permute-start | bytes 1769480 | tf_op jit(solution)/shard_map/ppermute | solution.py:498
  120.3 28.0 %collective-permute-start.18 = (bf16[64,4608]{1,0:T(8,128)(2,1)S(1)}, bf16[64,4608]{1,0:T(8,128)(2,1)S(1)}, u32[]{:S(2)}, u32[]{:S(2)}) collective-permute-start(bf16[64,4608]{1,0:T(8,128)(2,1)S(1)} %get-tuple-element.100), channel_id=1, source_target_pairs={{0,4},{1,5},{2,6},{3,7},{4,0},{5,1},{6,2},{7,3},{8,12},{9,13},{10,... | collective-permute-start | bytes 1769480 | tf_op jit(solution)/shard_map/ppermute | solution.py:498
  121.8 26.4 %collective-permute-start.19 = (bf16[64,4608]{1,0:T(8,128)(2,1)S(1)}, bf16[64,4608]{1,0:T(8,128)(2,1)S(1)}, u32[]{:S(2)}, u32[]{:S(2)}) collective-permute-start(bf16[64,4608]{1,0:T(8,128)(2,1)S(1)} %get-tuple-element.101), channel_id=1, source_target_pairs={{0,6},{1,7},{2,4},{3,5},{4,2},{5,3},{6,0},{7,1},{8,14},{9,15},{10,... | collective-permute-start | bytes 1769480 | tf_op jit(solution)/shard_map/ppermute | solution.py:498
  148.3 2.4 %collective-permute-start.20 = (bf16[256,1664]{1,0:T(8,128)(2,1)S(1)}, bf16[256,1664]{1,0:T(8,128)(2,1)S(1)}, u32[]{:S(2)}, u32[]{:S(2)}) collective-permute-start(bf16[256,1664]{1,0:T(8,128)(2,1)S(1)} %get-tuple-element.103), channel_id=1, source_target_pairs={{0,1},{1,0},{2,3},{3,2},{4,5},{5,4},{6,7},{7,6},{8,9},{9,8},{10,11... | collective-permute-start | bytes 2555912 | tf_op jit(solution)/shard_map/ppermute | solution.py:498
  150.7 5.1 %copy-start.9 = (bf16[512,1536]{1,0:T(8,128)(2,1)S(1)}, bf16[512,1536]{1,0:T(8,128)(2,1)}, u32[]{:S(2)}) copy-start(bf16[512,1536]{1,0:T(8,128)(2,1)} %get-tuple-element.114.weights_ref) | copy-start | bytes 4718596
  150.9 4.9 %copy-start.4 = (bf16[512,2048]{1,0:T(8,128)(2,1)S(1)}, bf16[512,2048]{1,0:T(8,128)(2,1)}, u32[]{:S(2)}) copy-start(bf16[512,2048]{1,0:T(8,128)(2,1)} %get-tuple-element.115.both_ref) | copy-start | bytes 6291460
  150.9 11.3 %collective-permute-start.21 = (bf16[64,1664]{1,0:T(8,128)(2,1)S(1)}, bf16[64,1664]{1,0:T(8,128)(2,1)S(1)}, u32[]{:S(2)}, u32[]{:S(2)}) collective-permute-start(bf16[64,1664]{1,0:T(8,128)(2,1)S(1)} %get-tuple-element.117), channel_id=1, source_target_pairs={{0,2},{1,3},{2,0},{3,1},{4,6},{5,7},{6,4},{7,5},{8,10},{9,11},{10,... | collective-permute-start | bytes 638984 | tf_op jit(solution)/shard_map/ppermute | solution.py:498
  152.2 10.0 %collective-permute-start.22 = (bf16[64,1664]{1,0:T(8,128)(2,1)S(1)}, bf16[64,1664]{1,0:T(8,128)(2,1)S(1)}, u32[]{:S(2)}, u32[]{:S(2)}) collective-permute-start(bf16[64,1664]{1,0:T(8,128)(2,1)S(1)} %get-tuple-element.118), channel_id=1, source_target_pairs={{0,4},{1,5},{2,6},{3,7},{4,0},{5,1},{6,2},{7,3},{8,12},{9,13},{10,... | collective-permute-start | bytes 638984 | tf_op jit(solution)/shard_map/ppermute | solution.py:498
  153.0 10.7 %collective-permute-start.23 = (bf16[64,1664]{1,0:T(8,128)(2,1)S(1)}, bf16[64,1664]{1,0:T(8,128)(2,1)S(1)}, u32[]{:S(2)}, u32[]{:S(2)}) collective-permute-start(bf16[64,1664]{1,0:T(8,128)(2,1)S(1)} %get-tuple-element.119), channel_id=1, source_target_pairs={{0,6},{1,7},{2,4},{3,5},{4,2},{5,3},{6,0},{7,1},{8,14},{9,15},{10,... | collective-permute-start | bytes 638984 | tf_op jit(solution)/shard_map/ppermute | solution.py:498
  154.8 9.1 %collective-permute-start.24 = (bf16[32,4608]{1,0:T(8,128)(2,1)S(1)}, bf16[32,4608]{1,0:T(8,128)(2,1)S(1)}, u32[]{:S(2)}, u32[]{:S(2)}) collective-permute-start(bf16[32,4608]{1,0:T(8,128)(2,1)S(1)} %get-tuple-element.126), channel_id=1, source_target_pairs={{0,8},{1,9},{2,10},{3,11},{4,12},{5,13},{6,14},{7,15},{8,0},{9,1},... | collective-permute-start | bytes 884744 | tf_op jit(solution)/shard_map/ppermute | solution.py:498
  162.2 30.6 %copy-start.8 = (f32[98496]{0:T(1024)S(1)}, f32[98496]{0:T(1024)}, u32[]{:S(2)}) copy-start(f32[98496]{0:T(1024)} %params_ref.1) | copy-start | bytes 1181956
  162.2 30.6 %copy-start.10 = (f32[98496]{0:T(1024)S(1)}, f32[98496]{0:T(1024)}, u32[]{:S(2)}) copy-start(f32[98496]{0:T(1024)} %momenta_ref.1) | copy-start | bytes 1181956
  162.2 30.6 %copy-start.11 = (f32[98496]{0:T(1024)S(1)}, f32[98496]{0:T(1024)}, u32[]{:S(2)}) copy-start(f32[98496]{0:T(1024)} %averages_ref.1) | copy-start | bytes 1181956
  163.9 12.2 %collective-permute-start.28 = (bf16[16,4608]{1,0:T(8,128)(2,1)S(1)}, bf16[16,4608]{1,0:T(8,128)(2,1)S(1)}, u32[]{:S(2)}, u32[]{:S(2)}) collective-permute-start(bf16[16,4608]{1,0:T(8,128)(2,1)S(1)} %add_convert_fusion.10), channel_id=1, source_target_pairs={{0,16},{1,17},{2,18},{3,19},{4,20},{5,21},{6,22},{7,23},{8,24},{9,... | collective-permute-start | bytes 442376 | tf_op jit(solution)/shard_map/ppermute | solution.py:498
  166.0 10.2 %collective-permute-start.27 = (bf16[16,1664]{1,0:T(8,128)(2,1)S(1)}, bf16[16,1664]{1,0:T(8,128)(2,1)S(1)}, u32[]{:S(2)}, u32[]{:S(2)}) collective-permute-start(bf16[16,1664]{1,0:T(8,128)(2,1)S(1)} %get-tuple-element.147), channel_id=1, source_target_pairs={{0,24},{1,25},{2,26},{3,27},{4,28},{5,29},{6,30},{7,31},{8,16},{9,... | collective-permute-start | bytes 159752 | tf_op jit(solution)/shard_map/ppermute | solution.py:498
  167.3 10.4 %collective-permute-start.26 = (bf16[16,1664]{1,0:T(8,128)(2,1)S(1)}, bf16[16,1664]{1,0:T(8,128)(2,1)S(1)}, u32[]{:S(2)}, u32[]{:S(2)}) collective-permute-start(bf16[16,1664]{1,0:T(8,128)(2,1)S(1)} %get-tuple-element.148), channel_id=1, source_target_pairs={{0,16},{1,17},{2,18},{3,19},{4,20},{5,21},{6,22},{7,23},{8,24},{9,... | collective-permute-start | bytes 159752 | tf_op jit(solution)/shard_map/ppermute | solution.py:498
  169.2 8.5 %collective-permute-start.25 = (bf16[16,1664]{1,0:T(8,128)(2,1)S(1)}, bf16[16,1664]{1,0:T(8,128)(2,1)S(1)}, u32[]{:S(2)}, u32[]{:S(2)}) collective-permute-start(bf16[16,1664]{1,0:T(8,128)(2,1)S(1)} %get-tuple-element.149), channel_id=1, source_target_pairs={{0,8},{1,9},{2,10},{3,11},{4,12},{5,13},{6,14},{7,15},{8,0},{9,1},... | collective-permute-start | bytes 159752 | tf_op jit(solution)/shard_map/ppermute | solution.py:498
  177.8 7.5 %collective-permute-start.31 = (f32[16,128]{1,0:T(8,128)S(1)}, f32[16,128]{1,0:T(8,128)S(1)}, u32[]{:S(2)}, u32[]{:S(2)}) collective-permute-start(f32[16,128]{1,0:T(8,128)S(1)} %get-tuple-element.130), channel_id=1, source_target_pairs={{0,24},{1,25},{2,26},{3,27},{4,28},{5,29},{6,30},{7,31},{8,16},{9,... | collective-permute-start | bytes 24584 | tf_op jit(solution)/shard_map/ppermute | solution.py:498
  180.8 4.5 %collective-permute-start.30 = (f32[16,128]{1,0:T(8,128)S(1)}, f32[16,128]{1,0:T(8,128)S(1)}, u32[]{:S(2)}, u32[]{:S(2)}) collective-permute-start(f32[16,128]{1,0:T(8,128)S(1)} %get-tuple-element.130), channel_id=1, source_target_pairs={{0,16},{1,17},{2,18},{3,19},{4,20},{5,21},{6,22},{7,23},{8,24},{9,... | collective-permute-start | bytes 24584 | tf_op jit(solution)/shard_map/ppermute | solution.py:498
  180.8 3.7 %collective-permute-start.29 = (f32[16,128]{1,0:T(8,128)S(1)}, f32[16,128]{1,0:T(8,128)S(1)}, u32[]{:S(2)}, u32[]{:S(2)}) collective-permute-start(f32[16,128]{1,0:T(8,128)S(1)} %get-tuple-element.130), channel_id=1, source_target_pairs={{0,8},{1,9},{2,10},{3,11},{4,12},{5,13},{6,14},{7,15},{8,0},{9,1},... | collective-permute-start | bytes 24584 | tf_op jit(solution)/shard_map/ppermute | solution.py:498
  185.3 4.0 %collective-permute-start.32 = (f32[64,128]{1,0:T(8,128)S(1)}, f32[64,128]{1,0:T(8,128)S(1)}, u32[]{:S(2)}, u32[]{:S(2)}) collective-permute-start(f32[64,128]{1,0:T(8,128)S(1)} %get-tuple-element.153), channel_id=1, source_target_pairs={{0,2},{1,3},{2,0},{3,1},{4,6},{5,7},{6,4},{7,5},{8,10},{9,11},{10,... | collective-permute-start | bytes 98312 | tf_op jit(solution)/shard_map/ppermute | solution.py:498
  186.1 5.2 %collective-permute-start.34 = (f32[64,128]{1,0:T(8,128)S(1)}, f32[64,128]{1,0:T(8,128)S(1)}, u32[]{:S(2)}, u32[]{:S(2)}) collective-permute-start(f32[64,128]{1,0:T(8,128)S(1)} %get-tuple-element.153), channel_id=1, source_target_pairs={{0,6},{1,7},{2,4},{3,5},{4,2},{5,3},{6,0},{7,1},{8,14},{9,15},{10,... | collective-permute-start | bytes 98312 | tf_op jit(solution)/shard_map/ppermute | solution.py:498
  187.4 3.9 %collective-permute-start.33 = (f32[64,128]{1,0:T(8,128)S(1)}, f32[64,128]{1,0:T(8,128)S(1)}, u32[]{:S(2)}, u32[]{:S(2)}) collective-permute-start(f32[64,128]{1,0:T(8,128)S(1)} %get-tuple-element.153), channel_id=1, source_target_pairs={{0,4},{1,5},{2,6},{3,7},{4,0},{5,1},{6,2},{7,3},{8,12},{9,13},{10,... | collective-permute-start | bytes 98312 | tf_op jit(solution)/shard_map/ppermute | solution.py:498
  191.4 1.4 collective-permute-start.35
  (13 other events, 39.2 us)

commit v7 on v6

--- a/solution.py
+++ b/solution.py
@@ -106,14 +106,14 @@
     v_ref[...] = (nn(x, table[:, 2 * D : 3 * D]) + rows[1:2, :]).astype(bf16)
 
 
-def fill_bias(bias, seg_ref, limits_ref):
+def fill_bias(bias, seg_ref, limits_ref, widths_ref):
     blocks = bias.shape[0]
     lane = lax.broadcasted_iota(jnp.int32, (1, LANES), 1)
     across = lax.broadcasted_iota(jnp.int32, (LANES, LANES), 1)
     down = lax.broadcasted_iota(jnp.int32, (LANES, LANES), 0)
 
     def codes_of(block):
-        row = jnp.where(limits_ref[2] == 1, 0, block // (ROW // LANES))
+        row = jnp.where(widths_ref[0] == 1, 0, block // (ROW // LANES))
         limit = jnp.where(row == 0, limits_ref[0], limits_ref[1])
         code = seg_ref[block : block + 1, :] * 2 + row
         live = lane + block * LANES - row * ROW < limit
@@ -181,10 +181,12 @@
                     del held[item]
 
 
-def attend_kernel(limits_ref, seg_ref, qt_ref, k_ref, vt_ref, att_ref, logsum_ref, bias):
+def attend_kernel(
+    limits_ref, widths_ref, seg_ref, qt_ref, k_ref, vt_ref, att_ref, logsum_ref, bias
+):
     @pl.when(pl.program_id(0) == 0)
     def _():
-        fill_bias(bias, seg_ref, limits_ref)
+        fill_bias(bias, seg_ref, limits_ref, widths_ref)
 
     blocks = bias.shape[0]
 
@@ -230,13 +232,13 @@
 
 
 def feed_kernel(codes, amount, *refs):
-    mine_ref, limits_ref, xt_ref, att_ref, cot_ref, vec_ref = refs[:6]
-    piece_refs = refs[6 : 6 + amount]
-    layer_ref, ga_ref, both_ref, keep_ref, send_ref, sums_ref = refs[6 + amount : 12 + amount]
+    mine_ref, limits_ref, widths_ref, xt_ref, att_ref, cot_ref, vec_ref = refs[:7]
+    piece_refs = refs[7 : 7 + amount]
+    layer_ref, ga_ref, both_ref, keep_ref, send_ref, sums_ref = refs[7 + amount : 13 + amount]
     table, out_turned, up_turned, down_turned, columns, up_bias, slopes = refs[
-        12 + amount : 19 + amount
+        13 + amount : 20 + amount
     ]
-    acc_down, acc_up, acc_out, acc_vec, *kept = refs[19 + amount :]
+    acc_down, acc_up, acc_out, acc_vec, *kept = refs[20 + amount :]
     step = pl.program_id(0)
     chunk = TILE
     chunks = FF // chunk
@@ -274,7 +276,7 @@
 
         here = slice(tile * TILE, (tile + 1) * TILE)
         place = lax.broadcasted_iota(jnp.int32, (1, TILE), 1) + (step * 2 + tile) * TILE
-        row = jnp.where(limits_ref[2] == 1, 0, place // ROW)
+        row = jnp.where(widths_ref[0] == 1, 0, place // ROW)
         limit = jnp.where(row == 0, limits_ref[0], limits_ref[1])
         live = place - row * ROW < limit
 
@@ -390,7 +392,7 @@
 
 
 def attend_back_kernel(
-    codes, mine_ref, limits_ref, seg_ref, xt_ref, qt_ref, kt_ref, k_ref, v_ref, att_ref, ga_ref,
+    codes, mine_ref, limits_ref, widths_ref, seg_ref, xt_ref, qt_ref, kt_ref, k_ref, v_ref, att_ref, ga_ref,
     logsum_ref, sums_ref, grads_ref, keep_ref, send_ref, bias, acc_key, acc_value, weight_grad,
     vectors,
 ):
@@ -398,7 +400,7 @@
 
     @pl.when(pair == 0)
     def _():
-        fill_bias(bias, seg_ref, limits_ref)
+        fill_bias(bias, seg_ref, limits_ref, widths_ref)
 
     blocks = bias.shape[0]
     acc_key[...] = jnp.zeros_like(acc_key)
@@ -619,7 +621,6 @@
     rest_pieces = gather_phase(rest, slow_phases[1], count)
     rest_far = [exchange(rest, 1, count)]
     first_near, first_far = to_kernel(gather_phase(first, phases[0], count), order, 2)
-    limits = jnp.concatenate([row_lengths, row_widths])
     segments = segment_ids.reshape(blocks, LANES)
 
     tile = 2 * TILE
@@ -650,13 +651,13 @@
     attended, logsum = pl.pallas_call(
         attend_kernel,
         grid=(PAIRS,),
-        in_specs=[smem(), whole((blocks, LANES)), pair_rows, pair_columns, pair_rows],
+        in_specs=[smem(), smem(), whole((blocks, LANES)), pair_rows, pair_columns, pair_rows],
         out_specs=[pair_rows, sums_block],
         out_shape=[shaped((D, slots), bf16), shaped((PAIRS, blocks, 2 * LANES), f32)],
         scratch_shapes=[pltpu.VMEM((blocks, WINDOW, LANES), f32)],
         compiler_params=params_of(56),
         name="attend",
-    )(limits, segments, qt, key, vt)
+    )(row_lengths, row_widths, segments, qt, key, vt)
 
     attended, *rest_pieces = together(attended, *rest_pieces)
     rest_far += [exchange(piece, 1, count) for piece in rest_pieces[1:]]
@@ -665,7 +666,7 @@
         functools.partial(feed_kernel, slow_codes, len(rest_pieces)),
         grid=(steps,),
         in_specs=[
-            smem(), smem(), across, across, down,
+            smem(), smem(), smem(), across, across, down,
             whole((D, LANES)),
         ]
         + [whole(piece.shape) for piece in rest_pieces],
@@ -696,7 +697,7 @@
         + [pltpu.VMEM((rows, TILE), bf16) for rows in (FF, FF, D + BLOCK, D, D, D)] * 2,
         compiler_params=params_of(50 if direct else 54),
         name="feed",
-    )(origin, limits, xt, attended, cotangent, vectors, *rest_pieces)
+    )(origin, row_lengths, row_widths, xt, attended, cotangent, vectors, *rest_pieces)
 
     def scatter(parts, way, at):
         if at == len(way) - 1:
@@ -711,7 +712,7 @@
         functools.partial(attend_back_kernel, codes),
         grid=(PAIRS,),
         in_specs=[
-            smem(), smem(), whole((blocks, LANES)), whole((D, slots)),
+            smem(), smem(), smem(), whole((blocks, LANES)), whole((D, slots)),
             pair_rows, pair_rows, pair_columns, pair_columns, pair_rows, pair_rows, sums_block,
             whole((D, LANES)),
         ],
@@ -721,9 +722,9 @@
             resident(),
         ],
         out_shape=[
-            shaped((PAIRS, 3 * PAIR, slots), bf16),
-            shaped((D // 2, FIRST_WIDTH), bf16),
-            shaped((D // 2, FIRST_WIDTH), bf16),
+            pltpu.VMEM((PAIRS, 3 * PAIR, slots), bf16),
+            pltpu.VMEM((D // 2, FIRST_WIDTH), bf16),
+            pltpu.VMEM((D // 2, FIRST_WIDTH), bf16),
         ],
         scratch_shapes=[
             pltpu.VMEM((blocks, WINDOW, LANES), f32),
@@ -732,9 +733,9 @@
             pltpu.VMEM((D, 3 * PAIR), f32),
             pltpu.VMEM((D, LANES), f32),
         ],
-        compiler_params=params_of(31),
+        compiler_params=params_of(46),
         name="attend_back",
-    )(origin, limits, segments, xt, qt, kt, key, value, attended, grad_attended, logsum, feed_sums)
+    )(origin, row_lengths, row_widths, segments, xt, qt, kt, key, value, attended, grad_attended, logsum, feed_sums)
 
     keep_first, send_first, *rest_parts = together(keep_first, send_first, *rest_parts)
     parts = scatter_phase(from_kernel(keep_first, send_first, order), phases[0], count)

time: 195 us -> 194 us (level)
  transfers between devices with their start and end apart: 36 -> 36, of which waited for: 19 -> 19; matrix products, arithmetic and copies ran while one was open for 1% -> 0% of each run, Pallas kernels for 28% -> 29%
where the time goes in v7:
time: 194 us
  Pallas kernels  108 us (56%)
  starting transfers between devices  41.2 us (21%)
  waiting for transfers between devices  37.5 us (19%)
  other arithmetic  2.38 us (1%)
  local copies, waits for them, and re-layouts  2.19 us (1%)
    pallas_call x1, Pallas kernels, body(): pl.pallas_call(functools.partial(feed_kernel, slow_codes, len(rest_pieces...  51.1 us
    ppermute x36, starting transfers between devices, exchange(): return lax.ppermute(values, 'dp', [(at, at ^ bit) for at in range(count)])  41.2 us
    ppermute x36, waiting for transfers between devices, exchange(): return lax.ppermute(values, 'dp', [(at, at ^ bit) for at in range(count)])  37.5 us
    pallas_call x1, Pallas kernels, body(): pl.pallas_call(functools.partial(attend_back_kernel, codes), grid=(PAIRS,...  24.1 us
    pallas_call x1, Pallas kernels, body(): pl.pallas_call(attend_kernel, grid=(PAIRS,), in_specs=[smem(), smem(), wh...  15.1 us
    pallas_call x1, Pallas kernels, body(): pl.pallas_call(functools.partial(project_kernel, codes), grid=(steps,), i...  10.3 us
    pallas_call x1, Pallas kernels, body(): pl.pallas_call(input_kernel, grid=(steps,), in_specs=[pl.BlockSpec((PAIRS...  6.41 us
  transfers between devices with their start and end apart: 36, of which 19 were waited for; matrix products, arithmetic and copies ran while one was open for 0% of the time, Pallas kernels for 29%

profile of v7, /device:TPU:0, one launch (start us, length us, event | category | flops | bytes accessed | tf_op | source)
XLA Modules:
  0.0 193.6 jit_solution(17379768763096481922)
XLA Ops:
  0.6 1.0 convert_element_type.191
  2.0 4.1 %collective-permute-start.1 = (bf16[16,1664]{1,0:T(8,128)(2,1)S(1)}, bf16[16,1664]{1,0:T(8,128)(2,1)S(1)}, u32[]{:S(2)}, u32[]{:S(2)}) collective-permute-start(bf16[16,1664]{1,0:T(8,128)(2,1)S(1)} %get-tuple-element.151), channel_id=1, source_target_pairs={{0,16},{1,17},{2,18},{3,19},{4,20},{5,21},{6,22},{7,23},{8,24},{9,... | collective-permute-start | bytes 159752 | tf_op jit(solution)/shard_map/ppermute | solution.py:500
  6.1 1.6 collective-permute-start
  7.7 2.0 %collective-permute-start.6 = (bf16[16,4608]{1,0:T(8,128)(2,1)S(1)}, bf16[16,4608]{1,0:T(8,128)(2,1)S(1)}, u32[]{:S(2)}, u32[]{:S(2)}) collective-permute-start(bf16[16,4608]{1,0:T(8,128)(2,1)S(1)} %slice.194), channel_id=1, source_target_pairs={{0,16},{1,17},{2,18},{3,19},{4,20},{5,21},{6,22},{7,23},{8,24},{9,... | collective-permute-start | bytes 442376 | tf_op jit(solution)/shard_map/ppermute | solution.py:500
  9.7 0.6 collective-permute-done
  10.2 3.9 %collective-permute-done.2 = bf16[16,1664]{1,0:T(8,128)(2,1)S(1)} collective-permute-done((bf16[16,1664]{1,0:T(8,128)(2,1)S(1)}, bf16[16,1664]{1,0:T(8,128)(2,1)S(1)}, u32[]{:S(2)}, u32[]{:S(2)}) %collective-permute-start.2) | collective-permute-done | bytes 53280 | tf_op jit(solution)/shard_map/ppermute | solution.py:500
  14.2 2.5 %collective-permute-start.5 = (bf16[64,1664]{1,0:T(8,128)(2,1)S(1)}, bf16[64,1664]{1,0:T(8,128)(2,1)S(1)}, u32[]{:S(2)}, u32[]{:S(2)}) collective-permute-start(bf16[64,1664]{1,0:T(8,128)(2,1)S(1)} %pad_maximum_fusion.3), channel_id=1, source_target_pairs={{0,6},{1,7},{2,4},{3,5},{4,2},{5,3},{6,0},{7,1},{8,14},{9,15},{10,... | collective-permute-start | bytes 638984 | tf_op jit(solution)/shard_map/ppermute | solution.py:500
  17.8 0.8 collective-permute-done.6
  18.6 2.2 %collective-permute-start.7 = (bf16[32,4608]{1,0:T(8,128)(2,1)S(1)}, bf16[32,4608]{1,0:T(8,128)(2,1)S(1)}, u32[]{:S(2)}, u32[]{:S(2)}) collective-permute-start(bf16[32,4608]{1,0:T(8,128)(2,1)S(1)} %pad_maximum_fusion.2), channel_id=1, source_target_pairs={{0,8},{1,9},{2,10},{3,11},{4,12},{5,13},{6,14},{7,15},{8,0},{9,1},... | collective-permute-start | bytes 884744 | tf_op jit(solution)/shard_map/ppermute | solution.py:500
  20.8 3.9 %collective-permute-done.3 = bf16[64,1664]{1,0:T(8,128)(2,1)S(1)} collective-permute-done((bf16[64,1664]{1,0:T(8,128)(2,1)S(1)}, bf16[64,1664]{1,0:T(8,128)(2,1)S(1)}, u32[]{:S(2)}, u32[]{:S(2)}) %collective-permute-start.3) | collective-permute-done | bytes 213024 | tf_op jit(solution)/shard_map/ppermute | solution.py:500
  24.8 1.8 collective-permute-done.7
  26.7 2.5 %collective-permute-start.11 = (bf16[64,4608]{1,0:T(8,128)(2,1)S(1)}, bf16[64,4608]{1,0:T(8,128)(2,1)S(1)}, u32[]{:S(2)}, u32[]{:S(2)}) collective-permute-start(bf16[64,4608]{1,0:T(8,128)(2,1)S(1)} %pad_maximum_fusion.refs_7_), channel_id=1, source_target_pairs={{0,6},{1,7},{2,4},{3,5},{4,2},{5,3},{6,0},{7,1},{8,14},{9,15},{10,... | collective-permute-start | bytes 1769480 | tf_op jit(solution)/shard_map/ppermute | solution.py:500
  31.0 10.3 %project.1 = (bf16[512,2048]{1,0:T(8,128)(2,1)}, bf16[512,2048]{1,0:T(8,128)(2,1)}, bf16[512,2048]{1,0:T(8,128)(2,1)}, bf16[512,2048]{1,0:T(8,128)(2,1)}, bf16[2...) custom-call(s32[1]{0:T(128)} %bitcast.mine_ref.refs_0_, ...), custom_call_target="tpu_custom_call" | custom-call | tf_op jit(solution)/shard_map/project/pallas_call | solution.py:630
  41.3 0.7 copy-done.5
  42.0 15.1 %attend.1 = (bf16[512,2048]{1,0:T(8,128)(2,1)}, f32[4,16,256]{2,1,0:T(8,128)}) custom-call(s32[2]{0:T(128)} %limits_ref.3, s32[1]{0:T(128)S(6)} %copy.30.widths_ref.refs_2_, s32[16,128]{1,0:T(8,128)} %bitcast.5, bf16[512,2048]{1,0:T(8,128)(2,1)} %get-tuple-element.75.qt_ref, bf16[2048,512]{1,0:T(8,128)(2,1)} %get-tuple-element.76.k_ref, ...), custom_call_target="tpu_custom_call" | custom-call | tf_op jit(solution)/shard_map/attend/pallas_call | solution.py:651
  58.1 1.4 collective-permute-done.13.refs_12_
  59.5 0.6 collective-permute-done.14.refs_13_
  60.1 0.8 collective-permute-done.15.refs_14_
  61.0 0.8 copy-done.15
  61.8 51.1 %feed.1 = (bf16[2048,512]{1,0:T(8,128)(2,1)}, bf16[512,2048]{1,0:T(8,128)(2,1)}, bf16[512,2048]{1,0:T(8,128)(2,1)}, bf16[256,4608]{1,0:T(8,128)(2,1)S(1)}, bf16[...) custom-call(s32[1]{0:T(128)} %bitcast.mine_ref.refs_0_, s32[2]{0:T(128)} %limits_ref.3, s32[1]{0:T(128)S(6)} %copy.30.widths_ref.refs_2_, ...), custom_call_target="tpu_custom_call" | custom-call | tf_op jit(solution)/shard_map/feed/pallas_call | solution.py:665
  113.3 4.2 %collective-permute-done.16 = bf16[256,4608]{1,0:T(8,128)(2,1)S(1)} collective-permute-done((bf16[256,4608]{1,0:T(8,128)(2,1)S(1)}, bf16[256,4608]{1,0:T(8,128)(2,1)S(1)}, u32[]{:S(2)}, u32[]{:S(2)}) %collective-permute-start.16) | collective-permute-done | bytes 2359328 | tf_op jit(solution)/shard_map/ppermute | solution.py:500
  118.0 1.6 collective-permute-start.17
  119.6 1.6 collective-permute-start.18
  121.6 24.1 %attend_back.1 = (bf16[4,384,2048]{2,1,0:T(8,128)(2,1)S(1)}, bf16[256,1664]{1,0:T(8,128)(2,1)S(1)}, bf16[256,1664]{1,0:T(8,128)(2,1)S(1)}) custom-call(s32[1]{0:T(128)} %bitcast.mine_ref.refs_0_, s32[2]{0:T(128)S(1)} %copy-done.8, s32[1]{0:T(128)S(6)} %copy.30.widths_ref.refs_2_, s32[16,128]{1,0:T(8,128)S(1)} %bitcast.6, ...), custom_call_target="tpu_custom_call" | custom-call | tf_op jit(solution)/shard_map/attend_back/pallas_call | solution.py:711
  145.7 1.8 collective-permute-done.18
  147.5 2.4 %collective-permute-done.20 = bf16[256,1664]{1,0:T(8,128)(2,1)S(1)} collective-permute-done((bf16[256,1664]{1,0:T(8,128)(2,1)S(1)}, bf16[256,1664]{1,0:T(8,128)(2,1)S(1)}, u32[]{:S(2)}, u32[]{:S(2)}) %collective-permute-start.20) | collective-permute-done | bytes 852000 | tf_op jit(solution)/shard_map/ppermute | solution.py:500
  150.1 1.3 collective-permute-start.21
  151.5 0.8 collective-permute-start.22
  152.2 1.4 collective-permute-start.23
  154.0 1.0 collective-permute-start.24
  155.0 6.4 %input_grad.1 = f32[2048,512]{1,0:T(8,128)} custom-call(bf16[4,384,2048]{2,1,0:T(8,128)(2,1)S(1)} %get-tuple-element.113.grads_ref, bf16[512,1536]{1,0:T(8,128)(2,1)S(1)} %copy-done.2, bf16[512,2048]{1,0:T(8,128)(2,1)S(1)} %copy-done), custom_call_target="tpu_custom_call" | custom-call | tf_op jit(solution)/shard_map/input_grad/pallas_call | solution.py:748
  161.4 1.6 collective-permute-done.23
  163.2 2.1 %collective-permute-start.28 = (bf16[16,4608]{1,0:T(8,128)(2,1)S(1)}, bf16[16,4608]{1,0:T(8,128)(2,1)S(1)}, u32[]{:S(2)}, u32[]{:S(2)}) collective-permute-start(bf16[16,4608]{1,0:T(8,128)(2,1)S(1)} %add_convert_fusion.10), channel_id=1, source_target_pairs={{0,16},{1,17},{2,18},{3,19},{4,20},{5,21},{6,22},{7,23},{8,24},{9,... | collective-permute-start | bytes 442376 | tf_op jit(solution)/shard_map/ppermute | solution.py:500
  165.3 1.3 collective-permute-start.27
  166.5 1.9 collective-permute-start.26
  168.5 1.2 collective-permute-start.25
  169.7 5.7 %collective-permute-done.28 = bf16[16,4608]{1,0:T(8,128)(2,1)S(1)} collective-permute-done((bf16[16,4608]{1,0:T(8,128)(2,1)S(1)}, bf16[16,4608]{1,0:T(8,128)(2,1)S(1)}, u32[]{:S(2)}, u32[]{:S(2)}) %collective-permute-start.28) | collective-permute-done | bytes 147488 | tf_op jit(solution)/shard_map/ppermute | solution.py:500
  175.4 1.5 collective-permute-done.26.refs_2_
  177.1 3.0 %collective-permute-start.31 = (f32[16,128]{1,0:T(8,128)S(1)}, f32[16,128]{1,0:T(8,128)S(1)}, u32[]{:S(2)}, u32[]{:S(2)}) collective-permute-start(f32[16,128]{1,0:T(8,128)S(1)} %get-tuple-element.130), channel_id=1, source_target_pairs={{0,24},{1,25},{2,26},{3,27},{4,28},{5,29},{6,30},{7,31},{8,16},{9,... | collective-permute-start | bytes 24584 | tf_op jit(solution)/shard_map/ppermute | solution.py:500
  180.1 1.5 collective-permute-start.29
  181.6 2.2 %collective-permute-done.29 = f32[16,128]{1,0:T(8,128)S(1)} collective-permute-done((f32[16,128]{1,0:T(8,128)S(1)}, f32[16,128]{1,0:T(8,128)S(1)}, u32[]{:S(2)}, u32[]{:S(2)}) %collective-permute-start.29) | collective-permute-done | bytes 8224 | tf_op jit(solution)/shard_map/ppermute | solution.py:500
  183.7 0.9 collective-permute-done.30
  184.6 0.6 collective-permute-start.32
  185.2 1.4 collective-permute-start.34
  186.7 1.5 collective-permute-start.33
  188.6 2.0 %collective-permute-done.33 = f32[64,128]{1,0:T(8,128)S(1)} collective-permute-done((f32[64,128]{1,0:T(8,128)S(1)}, f32[64,128]{1,0:T(8,128)S(1)}, u32[]{:S(2)}, u32[]{:S(2)}) %collective-permute-start.33) | collective-permute-done | bytes 32800 | tf_op jit(solution)/shard_map/ppermute | solution.py:500
  190.9 1.1 collective-permute-done.35.far_ref
  192.0 1.4 settle.1
  (94 shorter events, 6.9 us)
Async XLA Ops:
  2.0 7.7 %collective-permute-start.1 = (bf16[16,1664]{1,0:T(8,128)(2,1)S(1)}, bf16[16,1664]{1,0:T(8,128)(2,1)S(1)}, u32[]{:S(2)}, u32[]{:S(2)}) collective-permute-start(bf16[16,1664]{1,0:T(8,128)(2,1)S(1)} %get-tuple-element.151), channel_id=1, source_target_pairs={{0,16},{1,17},{2,18},{3,19},{4,20},{5,21},{6,22},{7,23},{8,24},{9,... | collective-permute-start | bytes 159752 | tf_op jit(solution)/shard_map/ppermute | solution.py:500
  6.1 4.1 %collective-permute-start = (bf16[16,1664]{1,0:T(8,128)(2,1)S(1)}, bf16[16,1664]{1,0:T(8,128)(2,1)S(1)}, u32[]{:S(2)}, u32[]{:S(2)}) collective-permute-start(bf16[16,1664]{1,0:T(8,128)(2,1)S(1)} %get-tuple-element.151), channel_id=1, source_target_pairs={{0,8},{1,9},{2,10},{3,11},{4,12},{5,13},{6,14},{7,15},{8,0},{9,1},... | collective-permute-start | bytes 159752 | tf_op jit(solution)/shard_map/ppermute | solution.py:500
  7.7 6.5 %collective-permute-start.2 = (bf16[16,1664]{1,0:T(8,128)(2,1)S(1)}, bf16[16,1664]{1,0:T(8,128)(2,1)S(1)}, u32[]{:S(2)}, u32[]{:S(2)}) collective-permute-start(bf16[16,1664]{1,0:T(8,128)(2,1)S(1)} %get-tuple-element.151), channel_id=1, source_target_pairs={{0,24},{1,25},{2,26},{3,27},{4,28},{5,29},{6,30},{7,31},{8,16},{9,... | collective-permute-start | bytes 159752 | tf_op jit(solution)/shard_map/ppermute | solution.py:500
  7.7 10.9 %collective-permute-start.6 = (bf16[16,4608]{1,0:T(8,128)(2,1)S(1)}, bf16[16,4608]{1,0:T(8,128)(2,1)S(1)}, u32[]{:S(2)}, u32[]{:S(2)}) collective-permute-start(bf16[16,4608]{1,0:T(8,128)(2,1)S(1)} %slice.194), channel_id=1, source_target_pairs={{0,16},{1,17},{2,18},{3,19},{4,20},{5,21},{6,22},{7,23},{8,24},{9,... | collective-permute-start | bytes 442376 | tf_op jit(solution)/shard_map/ppermute | solution.py:500
  14.2 10.6 %collective-permute-start.5 = (bf16[64,1664]{1,0:T(8,128)(2,1)S(1)}, bf16[64,1664]{1,0:T(8,128)(2,1)S(1)}, u32[]{:S(2)}, u32[]{:S(2)}) collective-permute-start(bf16[64,1664]{1,0:T(8,128)(2,1)S(1)} %pad_maximum_fusion.3), channel_id=1, source_target_pairs={{0,6},{1,7},{2,4},{3,5},{4,2},{5,3},{6,0},{7,1},{8,14},{9,15},{10,... | collective-permute-start | bytes 638984 | tf_op jit(solution)/shard_map/ppermute | solution.py:500
  16.7 8.0 %collective-permute-start.4 = (bf16[64,1664]{1,0:T(8,128)(2,1)S(1)}, bf16[64,1664]{1,0:T(8,128)(2,1)S(1)}, u32[]{:S(2)}, u32[]{:S(2)}) collective-permute-start(bf16[64,1664]{1,0:T(8,128)(2,1)S(1)} %pad_maximum_fusion.3), channel_id=1, source_target_pairs={{0,4},{1,5},{2,6},{3,7},{4,0},{5,1},{6,2},{7,3},{8,12},{9,13},{10,... | collective-permute-start | bytes 638984 | tf_op jit(solution)/shard_map/ppermute | solution.py:500
  17.2 7.5 %collective-permute-start.3 = (bf16[64,1664]{1,0:T(8,128)(2,1)S(1)}, bf16[64,1664]{1,0:T(8,128)(2,1)S(1)}, u32[]{:S(2)}, u32[]{:S(2)}) collective-permute-start(bf16[64,1664]{1,0:T(8,128)(2,1)S(1)} %pad_maximum_fusion.3), channel_id=1, source_target_pairs={{0,2},{1,3},{2,0},{3,1},{4,6},{5,7},{6,4},{7,5},{8,10},{9,11},{10,... | collective-permute-start | bytes 638984 | tf_op jit(solution)/shard_map/ppermute | solution.py:500
  18.6 8.0 %collective-permute-start.7 = (bf16[32,4608]{1,0:T(8,128)(2,1)S(1)}, bf16[32,4608]{1,0:T(8,128)(2,1)S(1)}, u32[]{:S(2)}, u32[]{:S(2)}) collective-permute-start(bf16[32,4608]{1,0:T(8,128)(2,1)S(1)} %pad_maximum_fusion.2), channel_id=1, source_target_pairs={{0,8},{1,9},{2,10},{3,11},{4,12},{5,13},{6,14},{7,15},{8,0},{9,1},... | collective-permute-start | bytes 884744 | tf_op jit(solution)/shard_map/ppermute | solution.py:500
  26.6 30.4 %copy-start.9 = (bf16[64,4608]{1,0:T(8,128)(2,1)}, bf16[64,4608]{1,0:T(8,128)(2,1)S(1)}, u32[]{:S(2)}) copy-start(bf16[64,4608]{1,0:T(8,128)(2,1)S(1)} %pad_maximum_fusion.refs_7_) | copy-start | bytes 1769476
  26.6 4.4 %collective-permute-start.8 = (bf16[256,1664]{1,0:T(8,128)(2,1)S(1)}, bf16[256,1664]{1,0:T(8,128)(2,1)S(1)}, u32[]{:S(2)}, u32[]{:S(2)}) collective-permute-start(bf16[256,1664]{1,0:T(8,128)(2,1)S(1)} %constant_dynamic-update-slice_fusion.near_ref), channel_id=1, source_target_pairs={{0,1},{1,0},{2,3},{3,2},{4,5},{5,4},{6,7},{7,6},{8,9},{9,8},{10,11... | collective-permute-start | bytes 2555912 | tf_op jit(solution)/shard_map/ppermute | solution.py:500
  26.7 30.3 %collective-permute-start.11 = (bf16[64,4608]{1,0:T(8,128)(2,1)S(1)}, bf16[64,4608]{1,0:T(8,128)(2,1)S(1)}, u32[]{:S(2)}, u32[]{:S(2)}) collective-permute-start(bf16[64,4608]{1,0:T(8,128)(2,1)S(1)} %pad_maximum_fusion.refs_7_), channel_id=1, source_target_pairs={{0,6},{1,7},{2,4},{3,5},{4,2},{5,3},{6,0},{7,1},{8,14},{9,15},{10,... | collective-permute-start | bytes 1769480 | tf_op jit(solution)/shard_map/ppermute | solution.py:500
  29.2 27.8 %collective-permute-start.10 = (bf16[64,4608]{1,0:T(8,128)(2,1)S(1)}, bf16[64,4608]{1,0:T(8,128)(2,1)S(1)}, u32[]{:S(2)}, u32[]{:S(2)}) collective-permute-start(bf16[64,4608]{1,0:T(8,128)(2,1)S(1)} %pad_maximum_fusion.refs_7_), channel_id=1, source_target_pairs={{0,4},{1,5},{2,6},{3,7},{4,0},{5,1},{6,2},{7,3},{8,12},{9,13},{10,... | collective-permute-start | bytes 1769480 | tf_op jit(solution)/shard_map/ppermute | solution.py:500
  29.7 27.4 %collective-permute-start.9 = (bf16[64,4608]{1,0:T(8,128)(2,1)S(1)}, bf16[64,4608]{1,0:T(8,128)(2,1)}, u32[]{:S(2)}, u32[]{:S(2)}) collective-permute-start(bf16[64,4608]{1,0:T(8,128)(2,1)S(1)} %pad_maximum_fusion.refs_7_), channel_id=1, source_target_pairs={{0,2},{1,3},{2,0},{3,1},{4,6},{5,7},{6,4},{7,5},{8,10},{9,11},{10,... | collective-permute-start | bytes 1769480 | tf_op jit(solution)/shard_map/ppermute | solution.py:500
  30.9 27.2 %collective-permute-start.12 = (bf16[64,4608]{1,0:T(8,128)(2,1)S(1)}, bf16[64,4608]{1,0:T(8,128)(2,1)S(1)}, u32[]{:S(2)}, u32[]{:S(2)}) collective-permute-start(bf16[64,4608]{1,0:T(8,128)(2,1)S(1)} %pad_maximum_fusion.refs_7_), channel_id=1, source_target_pairs={{0,1},{1,0},{2,3},{3,2},{4,5},{5,4},{6,7},{7,6},{8,9},{9,8},{10,11... | collective-permute-start | bytes 1769480 | tf_op jit(solution)/shard_map/ppermute | solution.py:500
  57.0 3.9 %copy-start.10 = (bf16[64,4608]{1,0:T(8,128)(2,1)}, bf16[64,4608]{1,0:T(8,128)(2,1)S(1)}, u32[]{:S(2)}) copy-start(bf16[64,4608]{1,0:T(8,128)(2,1)S(1)} %collective-permute-done.11.refs_10_) | copy-start | bytes 1769476
  57.1 3.9 %copy-start.11 = (bf16[64,4608]{1,0:T(8,128)(2,1)}, bf16[64,4608]{1,0:T(8,128)(2,1)S(1)}, u32[]{:S(2)}) copy-start(bf16[64,4608]{1,0:T(8,128)(2,1)S(1)} %collective-permute-done.10.refs_9_) | copy-start | bytes 1769476
  57.1 2.4 %collective-permute-start.13 = (bf16[64,4608]{1,0:T(8,128)(2,1)}, bf16[64,4608]{1,0:T(8,128)(2,1)S(1)}, u32[]{:S(2)}, u32[]{:S(2)}) collective-permute-start(bf16[64,4608]{1,0:T(8,128)(2,1)} %collective-permute-done.9.refs_8_), channel_id=1, source_target_pairs={{0,1},{1,0},{2,3},{3,2},{4,5},{5,4},{6,7},{7,6},{8,9},{9,8},{10,11... | collective-permute-start | bytes 1769480 | tf_op jit(solution)/shard_map/ppermute | solution.py:500
  57.6 2.5 %collective-permute-start.14 = (bf16[64,4608]{1,0:T(8,128)(2,1)S(1)}, bf16[64,4608]{1,0:T(8,128)(2,1)S(1)}, u32[]{:S(2)}, u32[]{:S(2)}) collective-permute-start(bf16[64,4608]{1,0:T(8,128)(2,1)S(1)} %collective-permute-done.10.refs_9_), channel_id=1, source_target_pairs={{0,1},{1,0},{2,3},{3,2},{4,5},{5,4},{6,7},{7,6},{8,9},{9,8},{10,11... | collective-permute-start | bytes 1769480 | tf_op jit(solution)/shard_map/ppermute | solution.py:500
  57.7 3.2 %collective-permute-start.15 = (bf16[64,4608]{1,0:T(8,128)(2,1)S(1)}, bf16[64,4608]{1,0:T(8,128)(2,1)S(1)}, u32[]{:S(2)}, u32[]{:S(2)}) collective-permute-start(bf16[64,4608]{1,0:T(8,128)(2,1)S(1)} %collective-permute-done.11.refs_10_), channel_id=1, source_target_pairs={{0,1},{1,0},{2,3},{3,2},{4,5},{5,4},{6,7},{7,6},{8,9},{9,8},{10,11... | collective-permute-start | bytes 1769480 | tf_op jit(solution)/shard_map/ppermute | solution.py:500
  58.1 2.8 %copy-start.12 = (bf16[64,4608]{1,0:T(8,128)(2,1)}, bf16[64,4608]{1,0:T(8,128)(2,1)S(1)}, u32[]{:S(2)}) copy-start(bf16[64,4608]{1,0:T(8,128)(2,1)S(1)} %collective-permute-done.12.refs_11_) | copy-start | bytes 1769476
  112.9 4.6 %collective-permute-start.16 = (bf16[256,4608]{1,0:T(8,128)(2,1)S(1)}, bf16[256,4608]{1,0:T(8,128)(2,1)S(1)}, u32[]{:S(2)}, u32[]{:S(2)}) collective-permute-start(bf16[256,4608]{1,0:T(8,128)(2,1)S(1)} %get-tuple-element.91), channel_id=1, source_target_pairs={{0,1},{1,0},{2,3},{3,2},{4,5},{5,4},{6,7},{7,6},{8,9},{9,8},{10,11... | collective-permute-start | bytes 7077896 | tf_op jit(solution)/shard_map/ppermute | solution.py:500
  117.5 4.1 %copy-start.6 = (f32[4,16,256]{2,1,0:T(8,128)S(1)}, f32[4,16,256]{2,1,0:T(8,128)}, u32[]{:S(2)}) copy-start(f32[4,16,256]{2,1,0:T(8,128)} %get-tuple-element.93.logsum_ref) | copy-start | bytes 196612
  117.5 4.1 %copy-start.7 = (s32[2048]{0:T(1024)S(1)}, s32[2048]{0:T(1024)}, u32[]{:S(2)}) copy-start(s32[2048]{0:T(1024)} %param.10) | copy-start | bytes 24580
  117.5 4.1 %copy-start.8 = (s32[2]{0:T(128)S(1)}, s32[2]{0:T(128)}, u32[]{:S(2)}) copy-start(s32[2]{0:T(128)} %limits_ref.3) | copy-start | bytes 28
  118.0 27.7 %collective-permute-start.17 = (bf16[64,4608]{1,0:T(8,128)(2,1)S(1)}, bf16[64,4608]{1,0:T(8,128)(2,1)S(1)}, u32[]{:S(2)}, u32[]{:S(2)}) collective-permute-start(bf16[64,4608]{1,0:T(8,128)(2,1)S(1)} %get-tuple-element.99), channel_id=1, source_target_pairs={{0,2},{1,3},{2,0},{3,1},{4,6},{5,7},{6,4},{7,5},{8,10},{9,11},{10,... | collective-permute-start | bytes 1769480 | tf_op jit(solution)/shard_map/ppermute | solution.py:500
  119.6 27.9 %collective-permute-start.18 = (bf16[64,4608]{1,0:T(8,128)(2,1)S(1)}, bf16[64,4608]{1,0:T(8,128)(2,1)S(1)}, u32[]{:S(2)}, u32[]{:S(2)}) collective-permute-start(bf16[64,4608]{1,0:T(8,128)(2,1)S(1)} %get-tuple-element.100), channel_id=1, source_target_pairs={{0,4},{1,5},{2,6},{3,7},{4,0},{5,1},{6,2},{7,3},{8,12},{9,13},{10,... | collective-permute-start | bytes 1769480 | tf_op jit(solution)/shard_map/ppermute | solution.py:500
  121.1 26.4 %collective-permute-start.19 = (bf16[64,4608]{1,0:T(8,128)(2,1)S(1)}, bf16[64,4608]{1,0:T(8,128)(2,1)S(1)}, u32[]{:S(2)}, u32[]{:S(2)}) collective-permute-start(bf16[64,4608]{1,0:T(8,128)(2,1)S(1)} %get-tuple-element.101), channel_id=1, source_target_pairs={{0,6},{1,7},{2,4},{3,5},{4,2},{5,3},{6,0},{7,1},{8,14},{9,15},{10,... | collective-permute-start | bytes 1769480 | tf_op jit(solution)/shard_map/ppermute | solution.py:500
  147.5 2.4 %collective-permute-start.20 = (bf16[256,1664]{1,0:T(8,128)(2,1)S(1)}, bf16[256,1664]{1,0:T(8,128)(2,1)S(1)}, u32[]{:S(2)}, u32[]{:S(2)}) collective-permute-start(bf16[256,1664]{1,0:T(8,128)(2,1)S(1)} %get-tuple-element.103), channel_id=1, source_target_pairs={{0,1},{1,0},{2,3},{3,2},{4,5},{5,4},{6,7},{7,6},{8,9},{9,8},{10,11... | collective-permute-start | bytes 2555912 | tf_op jit(solution)/shard_map/ppermute | solution.py:500
  149.9 5.1 %copy-start.2 = (bf16[512,1536]{1,0:T(8,128)(2,1)S(1)}, bf16[512,1536]{1,0:T(8,128)(2,1)}, u32[]{:S(2)}) copy-start(bf16[512,1536]{1,0:T(8,128)(2,1)} %get-tuple-element.114.weights_ref) | copy-start | bytes 4718596
  150.1 4.9 %copy-start = (bf16[512,2048]{1,0:T(8,128)(2,1)S(1)}, bf16[512,2048]{1,0:T(8,128)(2,1)}, u32[]{:S(2)}) copy-start(bf16[512,2048]{1,0:T(8,128)(2,1)} %get-tuple-element.115.both_ref) | copy-start | bytes 6291460
  150.1 11.3 %collective-permute-start.21 = (bf16[64,1664]{1,0:T(8,128)(2,1)S(1)}, bf16[64,1664]{1,0:T(8,128)(2,1)S(1)}, u32[]{:S(2)}, u32[]{:S(2)}) collective-permute-start(bf16[64,1664]{1,0:T(8,128)(2,1)S(1)} %get-tuple-element.117), channel_id=1, source_target_pairs={{0,2},{1,3},{2,0},{3,1},{4,6},{5,7},{6,4},{7,5},{8,10},{9,11},{10,... | collective-permute-start | bytes 638984 | tf_op jit(solution)/shard_map/ppermute | solution.py:500
  151.5 10.0 %collective-permute-start.22 = (bf16[64,1664]{1,0:T(8,128)(2,1)S(1)}, bf16[64,1664]{1,0:T(8,128)(2,1)S(1)}, u32[]{:S(2)}, u32[]{:S(2)}) collective-permute-start(bf16[64,1664]{1,0:T(8,128)(2,1)S(1)} %get-tuple-element.118), channel_id=1, source_target_pairs={{0,4},{1,5},{2,6},{3,7},{4,0},{5,1},{6,2},{7,3},{8,12},{9,13},{10,... | collective-permute-start | bytes 638984 | tf_op jit(solution)/shard_map/ppermute | solution.py:500
  152.2 10.8 %collective-permute-start.23 = (bf16[64,1664]{1,0:T(8,128)(2,1)S(1)}, bf16[64,1664]{1,0:T(8,128)(2,1)S(1)}, u32[]{:S(2)}, u32[]{:S(2)}) collective-permute-start(bf16[64,1664]{1,0:T(8,128)(2,1)S(1)} %get-tuple-element.119), channel_id=1, source_target_pairs={{0,6},{1,7},{2,4},{3,5},{4,2},{5,3},{6,0},{7,1},{8,14},{9,15},{10,... | collective-permute-start | bytes 638984 | tf_op jit(solution)/shard_map/ppermute | solution.py:500
  154.0 9.2 %collective-permute-start.24 = (bf16[32,4608]{1,0:T(8,128)(2,1)S(1)}, bf16[32,4608]{1,0:T(8,128)(2,1)S(1)}, u32[]{:S(2)}, u32[]{:S(2)}) collective-permute-start(bf16[32,4608]{1,0:T(8,128)(2,1)S(1)} %get-tuple-element.126), channel_id=1, source_target_pairs={{0,8},{1,9},{2,10},{3,11},{4,12},{5,13},{6,14},{7,15},{8,0},{9,1},... | collective-permute-start | bytes 884744 | tf_op jit(solution)/shard_map/ppermute | solution.py:500
  161.4 30.6 %copy-start.1 = (f32[98496]{0:T(1024)S(1)}, f32[98496]{0:T(1024)}, u32[]{:S(2)}) copy-start(f32[98496]{0:T(1024)} %params_ref.1) | copy-start | bytes 1181956
  161.4 30.6 %copy-start.3 = (f32[98496]{0:T(1024)S(1)}, f32[98496]{0:T(1024)}, u32[]{:S(2)}) copy-start(f32[98496]{0:T(1024)} %momenta_ref.1) | copy-start | bytes 1181956
  161.4 30.6 %copy-start.4 = (f32[98496]{0:T(1024)S(1)}, f32[98496]{0:T(1024)}, u32[]{:S(2)}) copy-start(f32[98496]{0:T(1024)} %averages_ref.1) | copy-start | bytes 1181956
  163.2 12.1 %collective-permute-start.28 = (bf16[16,4608]{1,0:T(8,128)(2,1)S(1)}, bf16[16,4608]{1,0:T(8,128)(2,1)S(1)}, u32[]{:S(2)}, u32[]{:S(2)}) collective-permute-start(bf16[16,4608]{1,0:T(8,128)(2,1)S(1)} %add_convert_fusion.10), channel_id=1, source_target_pairs={{0,16},{1,17},{2,18},{3,19},{4,20},{5,21},{6,22},{7,23},{8,24},{9,... | collective-permute-start | bytes 442376 | tf_op jit(solution)/shard_map/ppermute | solution.py:500
  165.3 10.1 %collective-permute-start.27 = (bf16[16,1664]{1,0:T(8,128)(2,1)S(1)}, bf16[16,1664]{1,0:T(8,128)(2,1)S(1)}, u32[]{:S(2)}, u32[]{:S(2)}) collective-permute-start(bf16[16,1664]{1,0:T(8,128)(2,1)S(1)} %get-tuple-element.147), channel_id=1, source_target_pairs={{0,24},{1,25},{2,26},{3,27},{4,28},{5,29},{6,30},{7,31},{8,16},{9,... | collective-permute-start | bytes 159752 | tf_op jit(solution)/shard_map/ppermute | solution.py:500
  166.5 10.4 %collective-permute-start.26 = (bf16[16,1664]{1,0:T(8,128)(2,1)S(1)}, bf16[16,1664]{1,0:T(8,128)(2,1)S(1)}, u32[]{:S(2)}, u32[]{:S(2)}) collective-permute-start(bf16[16,1664]{1,0:T(8,128)(2,1)S(1)} %get-tuple-element.148), channel_id=1, source_target_pairs={{0,16},{1,17},{2,18},{3,19},{4,20},{5,21},{6,22},{7,23},{8,24},{9,... | collective-permute-start | bytes 159752 | tf_op jit(solution)/shard_map/ppermute | solution.py:500
  168.5 8.5 %collective-permute-start.25 = (bf16[16,1664]{1,0:T(8,128)(2,1)S(1)}, bf16[16,1664]{1,0:T(8,128)(2,1)S(1)}, u32[]{:S(2)}, u32[]{:S(2)}) collective-permute-start(bf16[16,1664]{1,0:T(8,128)(2,1)S(1)} %get-tuple-element.149), channel_id=1, source_target_pairs={{0,8},{1,9},{2,10},{3,11},{4,12},{5,13},{6,14},{7,15},{8,0},{9,1},... | collective-permute-start | bytes 159752 | tf_op jit(solution)/shard_map/ppermute | solution.py:500
  177.1 7.5 %collective-permute-start.31 = (f32[16,128]{1,0:T(8,128)S(1)}, f32[16,128]{1,0:T(8,128)S(1)}, u32[]{:S(2)}, u32[]{:S(2)}) collective-permute-start(f32[16,128]{1,0:T(8,128)S(1)} %get-tuple-element.130), channel_id=1, source_target_pairs={{0,24},{1,25},{2,26},{3,27},{4,28},{5,29},{6,30},{7,31},{8,16},{9,... | collective-permute-start | bytes 24584 | tf_op jit(solution)/shard_map/ppermute | solution.py:500
  180.1 4.5 %collective-permute-start.30 = (f32[16,128]{1,0:T(8,128)S(1)}, f32[16,128]{1,0:T(8,128)S(1)}, u32[]{:S(2)}, u32[]{:S(2)}) collective-permute-start(f32[16,128]{1,0:T(8,128)S(1)} %get-tuple-element.130), channel_id=1, source_target_pairs={{0,16},{1,17},{2,18},{3,19},{4,20},{5,21},{6,22},{7,23},{8,24},{9,... | collective-permute-start | bytes 24584 | tf_op jit(solution)/shard_map/ppermute | solution.py:500
  180.1 3.7 %collective-permute-start.29 = (f32[16,128]{1,0:T(8,128)S(1)}, f32[16,128]{1,0:T(8,128)S(1)}, u32[]{:S(2)}, u32[]{:S(2)}) collective-permute-start(f32[16,128]{1,0:T(8,128)S(1)} %get-tuple-element.130), channel_id=1, source_target_pairs={{0,8},{1,9},{2,10},{3,11},{4,12},{5,13},{6,14},{7,15},{8,0},{9,1},... | collective-permute-start | bytes 24584 | tf_op jit(solution)/shard_map/ppermute | solution.py:500
  184.6 4.0 %collective-permute-start.32 = (f32[64,128]{1,0:T(8,128)S(1)}, f32[64,128]{1,0:T(8,128)S(1)}, u32[]{:S(2)}, u32[]{:S(2)}) collective-permute-start(f32[64,128]{1,0:T(8,128)S(1)} %get-tuple-element.153), channel_id=1, source_target_pairs={{0,2},{1,3},{2,0},{3,1},{4,6},{5,7},{6,4},{7,5},{8,10},{9,11},{10,... | collective-permute-start | bytes 98312 | tf_op jit(solution)/shard_map/ppermute | solution.py:500
  185.2 5.4 %collective-permute-start.34 = (f32[64,128]{1,0:T(8,128)S(1)}, f32[64,128]{1,0:T(8,128)S(1)}, u32[]{:S(2)}, u32[]{:S(2)}) collective-permute-start(f32[64,128]{1,0:T(8,128)S(1)} %get-tuple-element.153), channel_id=1, source_target_pairs={{0,6},{1,7},{2,4},{3,5},{4,2},{5,3},{6,0},{7,1},{8,14},{9,15},{10,... | collective-permute-start | bytes 98312 | tf_op jit(solution)/shard_map/ppermute | solution.py:500
  186.7 3.9 %collective-permute-start.33 = (f32[64,128]{1,0:T(8,128)S(1)}, f32[64,128]{1,0:T(8,128)S(1)}, u32[]{:S(2)}, u32[]{:S(2)}) collective-permute-start(f32[64,128]{1,0:T(8,128)S(1)} %get-tuple-element.153), channel_id=1, source_target_pairs={{0,4},{1,5},{2,6},{3,7},{4,0},{5,1},{6,2},{7,3},{8,12},{9,13},{10,... | collective-permute-start | bytes 98312 | tf_op jit(solution)/shard_map/ppermute | solution.py:500
  190.6 1.4 collective-permute-start.35
  (4 other events, 3.8 us)

commit v8 on v7

--- a/solution.py
+++ b/solution.py
@@ -655,7 +655,7 @@
         out_specs=[pair_rows, sums_block],
         out_shape=[shaped((D, slots), bf16), shaped((PAIRS, blocks, 2 * LANES), f32)],
         scratch_shapes=[pltpu.VMEM((blocks, WINDOW, LANES), f32)],
-        compiler_params=params_of(56),
+        compiler_params=params_of(52),
         name="attend",
     )(row_lengths, row_widths, segments, qt, key, vt)
 

time: 194 us -> 194 us (level)
  no operation moved by 1% of the time
where the time goes in v8:
time: 194 us
  Pallas kernels  108 us (56%)
  starting transfers between devices  41.3 us (21%)
  waiting for transfers between devices  37.5 us (19%)
  other arithmetic  2.61 us (1%)
  local copies, waits for them, and re-layouts  2.19 us (1%)
    pallas_call x1, Pallas kernels, body(): pl.pallas_call(functools.partial(feed_kernel, slow_codes, len(rest_pieces...  51.1 us
    ppermute x36, starting transfers between devices, exchange(): return lax.ppermute(values, 'dp', [(at, at ^ bit) for at in range(count)])  41.3 us
    ppermute x36, waiting for transfers between devices, exchange(): return lax.ppermute(values, 'dp', [(at, at ^ bit) for at in range(count)])  37.5 us
    pallas_call x1, Pallas kernels, body(): pl.pallas_call(functools.partial(attend_back_kernel, codes), grid=(PAIRS,...  24.1 us
    pallas_call x1, Pallas kernels, body(): pl.pallas_call(attend_kernel, grid=(PAIRS,), in_specs=[smem(), smem(), wh...  15.1 us
    pallas_call x1, Pallas kernels, body(): pl.pallas_call(functools.partial(project_kernel, codes), grid=(steps,), i...  10.3 us
    pallas_call x1, Pallas kernels, body(): pl.pallas_call(input_kernel, grid=(steps,), in_specs=[pl.BlockSpec((PAIRS...  6.41 us
  transfers between devices with their start and end apart: 36, of which 19 were waited for; matrix products, arithmetic and copies ran while one was open for 0% of the time, Pallas kernels for 29%

profile of v8, /device:TPU:0, one launch (start us, length us, event | category | flops | bytes accessed | tf_op | source)
XLA Modules:
  0.0 193.8 jit_solution(16532745478082718294)
XLA Ops:
  0.6 1.0 convert_element_type.191
  2.0 4.1 %collective-permute-start.1 = (bf16[16,1664]{1,0:T(8,128)(2,1)S(1)}, bf16[16,1664]{1,0:T(8,128)(2,1)S(1)}, u32[]{:S(2)}, u32[]{:S(2)}) collective-permute-start(bf16[16,1664]{1,0:T(8,128)(2,1)S(1)} %get-tuple-element.151), channel_id=1, source_target_pairs={{0,16},{1,17},{2,18},{3,19},{4,20},{5,21},{6,22},{7,23},{8,24},{9,... | collective-permute-start | bytes 159752 | tf_op jit(solution)/shard_map/ppermute | solution.py:500
  6.1 1.6 collective-permute-start
  7.7 2.0 %collective-permute-start.6 = (bf16[16,4608]{1,0:T(8,128)(2,1)S(1)}, bf16[16,4608]{1,0:T(8,128)(2,1)S(1)}, u32[]{:S(2)}, u32[]{:S(2)}) collective-permute-start(bf16[16,4608]{1,0:T(8,128)(2,1)S(1)} %slice.194), channel_id=1, source_target_pairs={{0,16},{1,17},{2,18},{3,19},{4,20},{5,21},{6,22},{7,23},{8,24},{9,... | collective-permute-start | bytes 442376 | tf_op jit(solution)/shard_map/ppermute | solution.py:500
  10.2 3.9 %collective-permute-done.2 = bf16[16,1664]{1,0:T(8,128)(2,1)S(1)} collective-permute-done((bf16[16,1664]{1,0:T(8,128)(2,1)S(1)}, bf16[16,1664]{1,0:T(8,128)(2,1)S(1)}, u32[]{:S(2)}, u32[]{:S(2)}) %collective-permute-start.2) | collective-permute-done | bytes 53280 | tf_op jit(solution)/shard_map/ppermute | solution.py:500
  14.2 2.5 %collective-permute-start.5 = (bf16[64,1664]{1,0:T(8,128)(2,1)S(1)}, bf16[64,1664]{1,0:T(8,128)(2,1)S(1)}, u32[]{:S(2)}, u32[]{:S(2)}) collective-permute-start(bf16[64,1664]{1,0:T(8,128)(2,1)S(1)} %pad_maximum_fusion.3), channel_id=1, source_target_pairs={{0,6},{1,7},{2,4},{3,5},{4,2},{5,3},{6,0},{7,1},{8,14},{9,15},{10,... | collective-permute-start | bytes 638984 | tf_op jit(solution)/shard_map/ppermute | solution.py:500
  17.8 0.8 collective-permute-done.6
  18.6 2.2 %collective-permute-start.7 = (bf16[32,4608]{1,0:T(8,128)(2,1)S(1)}, bf16[32,4608]{1,0:T(8,128)(2,1)S(1)}, u32[]{:S(2)}, u32[]{:S(2)}) collective-permute-start(bf16[32,4608]{1,0:T(8,128)(2,1)S(1)} %pad_maximum_fusion.2), channel_id=1, source_target_pairs={{0,8},{1,9},{2,10},{3,11},{4,12},{5,13},{6,14},{7,15},{8,0},{9,1},... | collective-permute-start | bytes 884744 | tf_op jit(solution)/shard_map/ppermute | solution.py:500
  20.8 3.9 %collective-permute-done.3 = bf16[64,1664]{1,0:T(8,128)(2,1)S(1)} collective-permute-done((bf16[64,1664]{1,0:T(8,128)(2,1)S(1)}, bf16[64,1664]{1,0:T(8,128)(2,1)S(1)}, u32[]{:S(2)}, u32[]{:S(2)}) %collective-permute-start.3) | collective-permute-done | bytes 213024 | tf_op jit(solution)/shard_map/ppermute | solution.py:500
  24.8 1.8 collective-permute-done.7
  26.7 2.5 %collective-permute-start.11 = (bf16[64,4608]{1,0:T(8,128)(2,1)S(1)}, bf16[64,4608]{1,0:T(8,128)(2,1)S(1)}, u32[]{:S(2)}, u32[]{:S(2)}) collective-permute-start(bf16[64,4608]{1,0:T(8,128)(2,1)S(1)} %pad_maximum_fusion.refs_7_), channel_id=1, source_target_pairs={{0,6},{1,7},{2,4},{3,5},{4,2},{5,3},{6,0},{7,1},{8,14},{9,15},{10,... | collective-permute-start | bytes 1769480 | tf_op jit(solution)/shard_map/ppermute | solution.py:500
  31.0 10.3 %project.1 = (bf16[512,2048]{1,0:T(8,128)(2,1)}, bf16[512,2048]{1,0:T(8,128)(2,1)}, bf16[512,2048]{1,0:T(8,128)(2,1)}, bf16[512,2048]{1,0:T(8,128)(2,1)}, bf16[2...) custom-call(s32[1]{0:T(128)} %bitcast.mine_ref.refs_0_, ...), custom_call_target="tpu_custom_call" | custom-call | tf_op jit(solution)/shard_map/project/pallas_call | solution.py:630
  41.3 0.7 copy-done.5
  42.0 15.1 %attend.1 = (bf16[512,2048]{1,0:T(8,128)(2,1)}, f32[4,16,256]{2,1,0:T(8,128)S(1)}) custom-call(s32[2]{0:T(128)S(1)} %copy-done.7, s32[1]{0:T(128)S(6)} %copy.30.widths_ref.refs_2_, s32[16,128]{1,0:T(8,128)S(1)} %bitcast.5, bf16[512,2048]{1,0:T(8,128)(2,1)} %get-tuple-element.75.qt_ref, bf16[2048,512]{1,0:T(8,128)(2,1)} %get-tuple-element.76.k_ref, ...), custom_call_target="tpu_custom_call" | custom-call | tf_op jit(solution)/shard_map/attend/pallas_call | solution.py:651
  58.2 1.4 collective-permute-done.13.refs_12_
  59.5 0.6 collective-permute-done.14.refs_13_
  60.1 0.8 collective-permute-done.15.refs_14_
  61.0 0.8 copy-done.15
  61.8 51.1 %feed.1 = (bf16[2048,512]{1,0:T(8,128)(2,1)}, bf16[512,2048]{1,0:T(8,128)(2,1)}, bf16[512,2048]{1,0:T(8,128)(2,1)}, bf16[256,4608]{1,0:T(8,128)(2,1)S(1)}, bf16[...) custom-call(s32[1]{0:T(128)} %bitcast.mine_ref.refs_0_, s32[2]{0:T(128)} %limits_ref.3, s32[1]{0:T(128)S(6)} %copy.30.widths_ref.refs_2_, ...), custom_call_target="tpu_custom_call" | custom-call | tf_op jit(solution)/shard_map/feed/pallas_call | solution.py:665
  113.3 4.2 %collective-permute-done.16 = bf16[256,4608]{1,0:T(8,128)(2,1)S(1)} collective-permute-done((bf16[256,4608]{1,0:T(8,128)(2,1)S(1)}, bf16[256,4608]{1,0:T(8,128)(2,1)S(1)}, u32[]{:S(2)}, u32[]{:S(2)}) %collective-permute-start.16) | collective-permute-done | bytes 2359328 | tf_op jit(solution)/shard_map/ppermute | solution.py:500
  117.5 0.7 add_convert_fusion
  118.2 1.6 collective-permute-start.17
  119.8 1.5 collective-permute-start.18
  121.8 24.1 %attend_back.1 = (bf16[4,384,2048]{2,1,0:T(8,128)(2,1)S(1)}, bf16[256,1664]{1,0:T(8,128)(2,1)S(1)}, bf16[256,1664]{1,0:T(8,128)(2,1)S(1)}) custom-call(s32[1]{0:T(128)} %bitcast.mine_ref.refs_0_, s32[2]{0:T(128)S(1)} %copy-done.8, s32[1]{0:T(128)S(6)} %copy.30.widths_ref.refs_2_, s32[16,128]{1,0:T(8,128)S(1)} %bitcast.6, ...), custom_call_target="tpu_custom_call" | custom-call | tf_op jit(solution)/shard_map/attend_back/pallas_call | solution.py:711
  145.9 1.8 collective-permute-done.18
  147.7 2.4 %collective-permute-done.20 = bf16[256,1664]{1,0:T(8,128)(2,1)S(1)} collective-permute-done((bf16[256,1664]{1,0:T(8,128)(2,1)S(1)}, bf16[256,1664]{1,0:T(8,128)(2,1)S(1)}, u32[]{:S(2)}, u32[]{:S(2)}) %collective-permute-start.20) | collective-permute-done | bytes 852000 | tf_op jit(solution)/shard_map/ppermute | solution.py:500
  150.3 1.3 collective-permute-start.21
  151.6 0.8 collective-permute-start.22
  152.5 1.4 collective-permute-start.23
  154.2 1.0 collective-permute-start.24
  155.2 6.4 %input_grad.1 = f32[2048,512]{1,0:T(8,128)} custom-call(bf16[4,384,2048]{2,1,0:T(8,128)(2,1)S(1)} %get-tuple-element.113.grads_ref, bf16[512,1536]{1,0:T(8,128)(2,1)S(1)} %copy-done.2, bf16[512,2048]{1,0:T(8,128)(2,1)S(1)} %copy-done), custom_call_target="tpu_custom_call" | custom-call | tf_op jit(solution)/shard_map/input_grad/pallas_call | solution.py:748
  161.7 1.5 collective-permute-done.23
  163.4 2.1 %collective-permute-start.28 = (bf16[16,4608]{1,0:T(8,128)(2,1)S(1)}, bf16[16,4608]{1,0:T(8,128)(2,1)S(1)}, u32[]{:S(2)}, u32[]{:S(2)}) collective-permute-start(bf16[16,4608]{1,0:T(8,128)(2,1)S(1)} %add_convert_fusion.10), channel_id=1, source_target_pairs={{0,16},{1,17},{2,18},{3,19},{4,20},{5,21},{6,22},{7,23},{8,24},{9,... | collective-permute-start | bytes 442376 | tf_op jit(solution)/shard_map/ppermute | solution.py:500
  165.4 1.3 collective-permute-start.27
  166.8 1.9 collective-permute-start.26
  168.7 1.2 collective-permute-start.25
  169.8 5.7 %collective-permute-done.28 = bf16[16,4608]{1,0:T(8,128)(2,1)S(1)} collective-permute-done((bf16[16,4608]{1,0:T(8,128)(2,1)S(1)}, bf16[16,4608]{1,0:T(8,128)(2,1)S(1)}, u32[]{:S(2)}, u32[]{:S(2)}) %collective-permute-start.28) | collective-permute-done | bytes 147488 | tf_op jit(solution)/shard_map/ppermute | solution.py:500
  175.6 1.5 collective-permute-done.26.refs_2_
  177.3 3.0 %collective-permute-start.31 = (f32[16,128]{1,0:T(8,128)S(1)}, f32[16,128]{1,0:T(8,128)S(1)}, u32[]{:S(2)}, u32[]{:S(2)}) collective-permute-start(f32[16,128]{1,0:T(8,128)S(1)} %get-tuple-element.130), channel_id=1, source_target_pairs={{0,24},{1,25},{2,26},{3,27},{4,28},{5,29},{6,30},{7,31},{8,16},{9,... | collective-permute-start | bytes 24584 | tf_op jit(solution)/shard_map/ppermute | solution.py:500
  180.3 1.5 collective-permute-start.29
  181.7 2.2 %collective-permute-done.29 = f32[16,128]{1,0:T(8,128)S(1)} collective-permute-done((f32[16,128]{1,0:T(8,128)S(1)}, f32[16,128]{1,0:T(8,128)S(1)}, u32[]{:S(2)}, u32[]{:S(2)}) %collective-permute-start.29) | collective-permute-done | bytes 8224 | tf_op jit(solution)/shard_map/ppermute | solution.py:500
  183.9 0.9 collective-permute-done.30
  184.8 0.6 collective-permute-start.32
  185.5 1.4 collective-permute-start.34
  186.9 1.5 collective-permute-start.33
  188.8 2.0 %collective-permute-done.33 = f32[64,128]{1,0:T(8,128)S(1)} collective-permute-done((f32[64,128]{1,0:T(8,128)S(1)}, f32[64,128]{1,0:T(8,128)S(1)}, u32[]{:S(2)}, u32[]{:S(2)}) %collective-permute-start.33) | collective-permute-done | bytes 32800 | tf_op jit(solution)/shard_map/ppermute | solution.py:500
  191.2 1.1 collective-permute-done.35.far_ref
  192.2 1.4 settle.1
  (94 shorter events, 7.0 us)
Async XLA Ops:
  2.0 7.7 %collective-permute-start.1 = (bf16[16,1664]{1,0:T(8,128)(2,1)S(1)}, bf16[16,1664]{1,0:T(8,128)(2,1)S(1)}, u32[]{:S(2)}, u32[]{:S(2)}) collective-permute-start(bf16[16,1664]{1,0:T(8,128)(2,1)S(1)} %get-tuple-element.151), channel_id=1, source_target_pairs={{0,16},{1,17},{2,18},{3,19},{4,20},{5,21},{6,22},{7,23},{8,24},{9,... | collective-permute-start | bytes 159752 | tf_op jit(solution)/shard_map/ppermute | solution.py:500
  6.1 4.1 %collective-permute-start = (bf16[16,1664]{1,0:T(8,128)(2,1)S(1)}, bf16[16,1664]{1,0:T(8,128)(2,1)S(1)}, u32[]{:S(2)}, u32[]{:S(2)}) collective-permute-start(bf16[16,1664]{1,0:T(8,128)(2,1)S(1)} %get-tuple-element.151), channel_id=1, source_target_pairs={{0,8},{1,9},{2,10},{3,11},{4,12},{5,13},{6,14},{7,15},{8,0},{9,1},... | collective-permute-start | bytes 159752 | tf_op jit(solution)/shard_map/ppermute | solution.py:500
  7.7 6.5 %collective-permute-start.2 = (bf16[16,1664]{1,0:T(8,128)(2,1)S(1)}, bf16[16,1664]{1,0:T(8,128)(2,1)S(1)}, u32[]{:S(2)}, u32[]{:S(2)}) collective-permute-start(bf16[16,1664]{1,0:T(8,128)(2,1)S(1)} %get-tuple-element.151), channel_id=1, source_target_pairs={{0,24},{1,25},{2,26},{3,27},{4,28},{5,29},{6,30},{7,31},{8,16},{9,... | collective-permute-start | bytes 159752 | tf_op jit(solution)/shard_map/ppermute | solution.py:500
  7.7 10.9 %collective-permute-start.6 = (bf16[16,4608]{1,0:T(8,128)(2,1)S(1)}, bf16[16,4608]{1,0:T(8,128)(2,1)S(1)}, u32[]{:S(2)}, u32[]{:S(2)}) collective-permute-start(bf16[16,4608]{1,0:T(8,128)(2,1)S(1)} %slice.194), channel_id=1, source_target_pairs={{0,16},{1,17},{2,18},{3,19},{4,20},{5,21},{6,22},{7,23},{8,24},{9,... | collective-permute-start | bytes 442376 | tf_op jit(solution)/shard_map/ppermute | solution.py:500
  14.2 10.6 %collective-permute-start.5 = (bf16[64,1664]{1,0:T(8,128)(2,1)S(1)}, bf16[64,1664]{1,0:T(8,128)(2,1)S(1)}, u32[]{:S(2)}, u32[]{:S(2)}) collective-permute-start(bf16[64,1664]{1,0:T(8,128)(2,1)S(1)} %pad_maximum_fusion.3), channel_id=1, source_target_pairs={{0,6},{1,7},{2,4},{3,5},{4,2},{5,3},{6,0},{7,1},{8,14},{9,15},{10,... | collective-permute-start | bytes 638984 | tf_op jit(solution)/shard_map/ppermute | solution.py:500
  16.7 8.0 %collective-permute-start.4 = (bf16[64,1664]{1,0:T(8,128)(2,1)S(1)}, bf16[64,1664]{1,0:T(8,128)(2,1)S(1)}, u32[]{:S(2)}, u32[]{:S(2)}) collective-permute-start(bf16[64,1664]{1,0:T(8,128)(2,1)S(1)} %pad_maximum_fusion.3), channel_id=1, source_target_pairs={{0,4},{1,5},{2,6},{3,7},{4,0},{5,1},{6,2},{7,3},{8,12},{9,13},{10,... | collective-permute-start | bytes 638984 | tf_op jit(solution)/shard_map/ppermute | solution.py:500
  17.2 7.5 %collective-permute-start.3 = (bf16[64,1664]{1,0:T(8,128)(2,1)S(1)}, bf16[64,1664]{1,0:T(8,128)(2,1)S(1)}, u32[]{:S(2)}, u32[]{:S(2)}) collective-permute-start(bf16[64,1664]{1,0:T(8,128)(2,1)S(1)} %pad_maximum_fusion.3), channel_id=1, source_target_pairs={{0,2},{1,3},{2,0},{3,1},{4,6},{5,7},{6,4},{7,5},{8,10},{9,11},{10,... | collective-permute-start | bytes 638984 | tf_op jit(solution)/shard_map/ppermute | solution.py:500
  18.6 8.0 %collective-permute-start.7 = (bf16[32,4608]{1,0:T(8,128)(2,1)S(1)}, bf16[32,4608]{1,0:T(8,128)(2,1)S(1)}, u32[]{:S(2)}, u32[]{:S(2)}) collective-permute-start(bf16[32,4608]{1,0:T(8,128)(2,1)S(1)} %pad_maximum_fusion.2), channel_id=1, source_target_pairs={{0,8},{1,9},{2,10},{3,11},{4,12},{5,13},{6,14},{7,15},{8,0},{9,1},... | collective-permute-start | bytes 884744 | tf_op jit(solution)/shard_map/ppermute | solution.py:500
  26.6 30.5 %copy-start.9 = (bf16[64,4608]{1,0:T(8,128)(2,1)}, bf16[64,4608]{1,0:T(8,128)(2,1)S(1)}, u32[]{:S(2)}) copy-start(bf16[64,4608]{1,0:T(8,128)(2,1)S(1)} %pad_maximum_fusion.refs_7_) | copy-start | bytes 1769476
  26.6 15.4 %copy-start.6 = (s32[2048]{0:T(1024)S(1)}, s32[2048]{0:T(1024)}, u32[]{:S(2)}) copy-start(s32[2048]{0:T(1024)} %param.10) | copy-start | bytes 24580
  26.6 15.4 %copy-start.7 = (s32[2]{0:T(128)S(1)}, s32[2]{0:T(128)}, u32[]{:S(2)}) copy-start(s32[2]{0:T(128)} %limits_ref.3) | copy-start | bytes 28
  26.6 4.4 %collective-permute-start.8 = (bf16[256,1664]{1,0:T(8,128)(2,1)S(1)}, bf16[256,1664]{1,0:T(8,128)(2,1)S(1)}, u32[]{:S(2)}, u32[]{:S(2)}) collective-permute-start(bf16[256,1664]{1,0:T(8,128)(2,1)S(1)} %constant_dynamic-update-slice_fusion.near_ref), channel_id=1, source_target_pairs={{0,1},{1,0},{2,3},{3,2},{4,5},{5,4},{6,7},{7,6},{8,9},{9,8},{10,11... | collective-permute-start | bytes 2555912 | tf_op jit(solution)/shard_map/ppermute | solution.py:500
  26.7 30.3 %collective-permute-start.11 = (bf16[64,4608]{1,0:T(8,128)(2,1)S(1)}, bf16[64,4608]{1,0:T(8,128)(2,1)S(1)}, u32[]{:S(2)}, u32[]{:S(2)}) collective-permute-start(bf16[64,4608]{1,0:T(8,128)(2,1)S(1)} %pad_maximum_fusion.refs_7_), channel_id=1, source_target_pairs={{0,6},{1,7},{2,4},{3,5},{4,2},{5,3},{6,0},{7,1},{8,14},{9,15},{10,... | collective-permute-start | bytes 1769480 | tf_op jit(solution)/shard_map/ppermute | solution.py:500
  29.2 27.8 %collective-permute-start.10 = (bf16[64,4608]{1,0:T(8,128)(2,1)S(1)}, bf16[64,4608]{1,0:T(8,128)(2,1)S(1)}, u32[]{:S(2)}, u32[]{:S(2)}) collective-permute-start(bf16[64,4608]{1,0:T(8,128)(2,1)S(1)} %pad_maximum_fusion.refs_7_), channel_id=1, source_target_pairs={{0,4},{1,5},{2,6},{3,7},{4,0},{5,1},{6,2},{7,3},{8,12},{9,13},{10,... | collective-permute-start | bytes 1769480 | tf_op jit(solution)/shard_map/ppermute | solution.py:500
  29.7 27.4 %collective-permute-start.9 = (bf16[64,4608]{1,0:T(8,128)(2,1)S(1)}, bf16[64,4608]{1,0:T(8,128)(2,1)}, u32[]{:S(2)}, u32[]{:S(2)}) collective-permute-start(bf16[64,4608]{1,0:T(8,128)(2,1)S(1)} %pad_maximum_fusion.refs_7_), channel_id=1, source_target_pairs={{0,2},{1,3},{2,0},{3,1},{4,6},{5,7},{6,4},{7,5},{8,10},{9,11},{10,... | collective-permute-start | bytes 1769480 | tf_op jit(solution)/shard_map/ppermute | solution.py:500
  30.9 27.2 %collective-permute-start.12 = (bf16[64,4608]{1,0:T(8,128)(2,1)S(1)}, bf16[64,4608]{1,0:T(8,128)(2,1)S(1)}, u32[]{:S(2)}, u32[]{:S(2)}) collective-permute-start(bf16[64,4608]{1,0:T(8,128)(2,1)S(1)} %pad_maximum_fusion.refs_7_), channel_id=1, source_target_pairs={{0,1},{1,0},{2,3},{3,2},{4,5},{5,4},{6,7},{7,6},{8,9},{9,8},{10,11... | collective-permute-start | bytes 1769480 | tf_op jit(solution)/shard_map/ppermute | solution.py:500
  57.1 3.9 %copy-start.10 = (bf16[64,4608]{1,0:T(8,128)(2,1)}, bf16[64,4608]{1,0:T(8,128)(2,1)S(1)}, u32[]{:S(2)}) copy-start(bf16[64,4608]{1,0:T(8,128)(2,1)S(1)} %collective-permute-done.11.refs_10_) | copy-start | bytes 1769476
  57.1 3.9 %copy-start.11 = (bf16[64,4608]{1,0:T(8,128)(2,1)}, bf16[64,4608]{1,0:T(8,128)(2,1)S(1)}, u32[]{:S(2)}) copy-start(bf16[64,4608]{1,0:T(8,128)(2,1)S(1)} %collective-permute-done.10.refs_9_) | copy-start | bytes 1769476
  57.1 2.4 %collective-permute-start.13 = (bf16[64,4608]{1,0:T(8,128)(2,1)}, bf16[64,4608]{1,0:T(8,128)(2,1)S(1)}, u32[]{:S(2)}, u32[]{:S(2)}) collective-permute-start(bf16[64,4608]{1,0:T(8,128)(2,1)} %collective-permute-done.9.refs_8_), channel_id=1, source_target_pairs={{0,1},{1,0},{2,3},{3,2},{4,5},{5,4},{6,7},{7,6},{8,9},{9,8},{10,11... | collective-permute-start | bytes 1769480 | tf_op jit(solution)/shard_map/ppermute | solution.py:500
  57.6 2.5 %collective-permute-start.14 = (bf16[64,4608]{1,0:T(8,128)(2,1)S(1)}, bf16[64,4608]{1,0:T(8,128)(2,1)S(1)}, u32[]{:S(2)}, u32[]{:S(2)}) collective-permute-start(bf16[64,4608]{1,0:T(8,128)(2,1)S(1)} %collective-permute-done.10.refs_9_), channel_id=1, source_target_pairs={{0,1},{1,0},{2,3},{3,2},{4,5},{5,4},{6,7},{7,6},{8,9},{9,8},{10,11... | collective-permute-start | bytes 1769480 | tf_op jit(solution)/shard_map/ppermute | solution.py:500
  57.7 3.2 %collective-permute-start.15 = (bf16[64,4608]{1,0:T(8,128)(2,1)S(1)}, bf16[64,4608]{1,0:T(8,128)(2,1)S(1)}, u32[]{:S(2)}, u32[]{:S(2)}) collective-permute-start(bf16[64,4608]{1,0:T(8,128)(2,1)S(1)} %collective-permute-done.11.refs_10_), channel_id=1, source_target_pairs={{0,1},{1,0},{2,3},{3,2},{4,5},{5,4},{6,7},{7,6},{8,9},{9,8},{10,11... | collective-permute-start | bytes 1769480 | tf_op jit(solution)/shard_map/ppermute | solution.py:500
  58.2 2.8 %copy-start.12 = (bf16[64,4608]{1,0:T(8,128)(2,1)}, bf16[64,4608]{1,0:T(8,128)(2,1)S(1)}, u32[]{:S(2)}) copy-start(bf16[64,4608]{1,0:T(8,128)(2,1)S(1)} %collective-permute-done.12.refs_11_) | copy-start | bytes 1769476
  112.9 4.6 %collective-permute-start.16 = (bf16[256,4608]{1,0:T(8,128)(2,1)S(1)}, bf16[256,4608]{1,0:T(8,128)(2,1)S(1)}, u32[]{:S(2)}, u32[]{:S(2)}) collective-permute-start(bf16[256,4608]{1,0:T(8,128)(2,1)S(1)} %get-tuple-element.91), channel_id=1, source_target_pairs={{0,1},{1,0},{2,3},{3,2},{4,5},{5,4},{6,7},{7,6},{8,9},{9,8},{10,11... | collective-permute-start | bytes 7077896 | tf_op jit(solution)/shard_map/ppermute | solution.py:500
  117.5 4.3 %copy-start.8 = (s32[2]{0:T(128)S(1)}, s32[2]{0:T(128)}, u32[]{:S(2)}) copy-start(s32[2]{0:T(128)} %limits_ref.3) | copy-start | bytes 28
  118.2 27.7 %collective-permute-start.17 = (bf16[64,4608]{1,0:T(8,128)(2,1)S(1)}, bf16[64,4608]{1,0:T(8,128)(2,1)S(1)}, u32[]{:S(2)}, u32[]{:S(2)}) collective-permute-start(bf16[64,4608]{1,0:T(8,128)(2,1)S(1)} %get-tuple-element.99), channel_id=1, source_target_pairs={{0,2},{1,3},{2,0},{3,1},{4,6},{5,7},{6,4},{7,5},{8,10},{9,11},{10,... | collective-permute-start | bytes 1769480 | tf_op jit(solution)/shard_map/ppermute | solution.py:500
  119.8 28.0 %collective-permute-start.18 = (bf16[64,4608]{1,0:T(8,128)(2,1)S(1)}, bf16[64,4608]{1,0:T(8,128)(2,1)S(1)}, u32[]{:S(2)}, u32[]{:S(2)}) collective-permute-start(bf16[64,4608]{1,0:T(8,128)(2,1)S(1)} %get-tuple-element.100), channel_id=1, source_target_pairs={{0,4},{1,5},{2,6},{3,7},{4,0},{5,1},{6,2},{7,3},{8,12},{9,13},{10,... | collective-permute-start | bytes 1769480 | tf_op jit(solution)/shard_map/ppermute | solution.py:500
  121.3 26.4 %collective-permute-start.19 = (bf16[64,4608]{1,0:T(8,128)(2,1)S(1)}, bf16[64,4608]{1,0:T(8,128)(2,1)S(1)}, u32[]{:S(2)}, u32[]{:S(2)}) collective-permute-start(bf16[64,4608]{1,0:T(8,128)(2,1)S(1)} %get-tuple-element.101), channel_id=1, source_target_pairs={{0,6},{1,7},{2,4},{3,5},{4,2},{5,3},{6,0},{7,1},{8,14},{9,15},{10,... | collective-permute-start | bytes 1769480 | tf_op jit(solution)/shard_map/ppermute | solution.py:500
  147.7 2.4 %collective-permute-start.20 = (bf16[256,1664]{1,0:T(8,128)(2,1)S(1)}, bf16[256,1664]{1,0:T(8,128)(2,1)S(1)}, u32[]{:S(2)}, u32[]{:S(2)}) collective-permute-start(bf16[256,1664]{1,0:T(8,128)(2,1)S(1)} %get-tuple-element.103), channel_id=1, source_target_pairs={{0,1},{1,0},{2,3},{3,2},{4,5},{5,4},{6,7},{7,6},{8,9},{9,8},{10,11... | collective-permute-start | bytes 2555912 | tf_op jit(solution)/shard_map/ppermute | solution.py:500
  150.1 5.1 %copy-start.2 = (bf16[512,1536]{1,0:T(8,128)(2,1)S(1)}, bf16[512,1536]{1,0:T(8,128)(2,1)}, u32[]{:S(2)}) copy-start(bf16[512,1536]{1,0:T(8,128)(2,1)} %get-tuple-element.114.weights_ref) | copy-start | bytes 4718596
  150.3 4.9 %copy-start = (bf16[512,2048]{1,0:T(8,128)(2,1)S(1)}, bf16[512,2048]{1,0:T(8,128)(2,1)}, u32[]{:S(2)}) copy-start(bf16[512,2048]{1,0:T(8,128)(2,1)} %get-tuple-element.115.both_ref) | copy-start | bytes 6291460
  150.3 11.3 %collective-permute-start.21 = (bf16[64,1664]{1,0:T(8,128)(2,1)S(1)}, bf16[64,1664]{1,0:T(8,128)(2,1)S(1)}, u32[]{:S(2)}, u32[]{:S(2)}) collective-permute-start(bf16[64,1664]{1,0:T(8,128)(2,1)S(1)} %get-tuple-element.117), channel_id=1, source_target_pairs={{0,2},{1,3},{2,0},{3,1},{4,6},{5,7},{6,4},{7,5},{8,10},{9,11},{10,... | collective-permute-start | bytes 638984 | tf_op jit(solution)/shard_map/ppermute | solution.py:500
  151.6 10.0 %collective-permute-start.22 = (bf16[64,1664]{1,0:T(8,128)(2,1)S(1)}, bf16[64,1664]{1,0:T(8,128)(2,1)S(1)}, u32[]{:S(2)}, u32[]{:S(2)}) collective-permute-start(bf16[64,1664]{1,0:T(8,128)(2,1)S(1)} %get-tuple-element.118), channel_id=1, source_target_pairs={{0,4},{1,5},{2,6},{3,7},{4,0},{5,1},{6,2},{7,3},{8,12},{9,13},{10,... | collective-permute-start | bytes 638984 | tf_op jit(solution)/shard_map/ppermute | solution.py:500
  152.5 10.8 %collective-permute-start.23 = (bf16[64,1664]{1,0:T(8,128)(2,1)S(1)}, bf16[64,1664]{1,0:T(8,128)(2,1)S(1)}, u32[]{:S(2)}, u32[]{:S(2)}) collective-permute-start(bf16[64,1664]{1,0:T(8,128)(2,1)S(1)} %get-tuple-element.119), channel_id=1, source_target_pairs={{0,6},{1,7},{2,4},{3,5},{4,2},{5,3},{6,0},{7,1},{8,14},{9,15},{10,... | collective-permute-start | bytes 638984 | tf_op jit(solution)/shard_map/ppermute | solution.py:500
  154.2 9.1 %collective-permute-start.24 = (bf16[32,4608]{1,0:T(8,128)(2,1)S(1)}, bf16[32,4608]{1,0:T(8,128)(2,1)S(1)}, u32[]{:S(2)}, u32[]{:S(2)}) collective-permute-start(bf16[32,4608]{1,0:T(8,128)(2,1)S(1)} %get-tuple-element.126), channel_id=1, source_target_pairs={{0,8},{1,9},{2,10},{3,11},{4,12},{5,13},{6,14},{7,15},{8,0},{9,1},... | collective-permute-start | bytes 884744 | tf_op jit(solution)/shard_map/ppermute | solution.py:500
  161.7 30.6 %copy-start.1 = (f32[98496]{0:T(1024)S(1)}, f32[98496]{0:T(1024)}, u32[]{:S(2)}) copy-start(f32[98496]{0:T(1024)} %params_ref.1) | copy-start | bytes 1181956
  161.7 30.6 %copy-start.3 = (f32[98496]{0:T(1024)S(1)}, f32[98496]{0:T(1024)}, u32[]{:S(2)}) copy-start(f32[98496]{0:T(1024)} %momenta_ref.1) | copy-start | bytes 1181956
  161.7 30.6 %copy-start.4 = (f32[98496]{0:T(1024)S(1)}, f32[98496]{0:T(1024)}, u32[]{:S(2)}) copy-start(f32[98496]{0:T(1024)} %averages_ref.1) | copy-start | bytes 1181956
  163.4 12.2 %collective-permute-start.28 = (bf16[16,4608]{1,0:T(8,128)(2,1)S(1)}, bf16[16,4608]{1,0:T(8,128)(2,1)S(1)}, u32[]{:S(2)}, u32[]{:S(2)}) collective-permute-start(bf16[16,4608]{1,0:T(8,128)(2,1)S(1)} %add_convert_fusion.10), channel_id=1, source_target_pairs={{0,16},{1,17},{2,18},{3,19},{4,20},{5,21},{6,22},{7,23},{8,24},{9,... | collective-permute-start | bytes 442376 | tf_op jit(solution)/shard_map/ppermute | solution.py:500
  165.4 10.2 %collective-permute-start.27 = (bf16[16,1664]{1,0:T(8,128)(2,1)S(1)}, bf16[16,1664]{1,0:T(8,128)(2,1)S(1)}, u32[]{:S(2)}, u32[]{:S(2)}) collective-permute-start(bf16[16,1664]{1,0:T(8,128)(2,1)S(1)} %get-tuple-element.147), channel_id=1, source_target_pairs={{0,24},{1,25},{2,26},{3,27},{4,28},{5,29},{6,30},{7,31},{8,16},{9,... | collective-permute-start | bytes 159752 | tf_op jit(solution)/shard_map/ppermute | solution.py:500
  166.8 10.4 %collective-permute-start.26 = (bf16[16,1664]{1,0:T(8,128)(2,1)S(1)}, bf16[16,1664]{1,0:T(8,128)(2,1)S(1)}, u32[]{:S(2)}, u32[]{:S(2)}) collective-permute-start(bf16[16,1664]{1,0:T(8,128)(2,1)S(1)} %get-tuple-element.148), channel_id=1, source_target_pairs={{0,16},{1,17},{2,18},{3,19},{4,20},{5,21},{6,22},{7,23},{8,24},{9,... | collective-permute-start | bytes 159752 | tf_op jit(solution)/shard_map/ppermute | solution.py:500
  168.7 8.5 %collective-permute-start.25 = (bf16[16,1664]{1,0:T(8,128)(2,1)S(1)}, bf16[16,1664]{1,0:T(8,128)(2,1)S(1)}, u32[]{:S(2)}, u32[]{:S(2)}) collective-permute-start(bf16[16,1664]{1,0:T(8,128)(2,1)S(1)} %get-tuple-element.149), channel_id=1, source_target_pairs={{0,8},{1,9},{2,10},{3,11},{4,12},{5,13},{6,14},{7,15},{8,0},{9,1},... | collective-permute-start | bytes 159752 | tf_op jit(solution)/shard_map/ppermute | solution.py:500
  177.3 7.5 %collective-permute-start.31 = (f32[16,128]{1,0:T(8,128)S(1)}, f32[16,128]{1,0:T(8,128)S(1)}, u32[]{:S(2)}, u32[]{:S(2)}) collective-permute-start(f32[16,128]{1,0:T(8,128)S(1)} %get-tuple-element.130), channel_id=1, source_target_pairs={{0,24},{1,25},{2,26},{3,27},{4,28},{5,29},{6,30},{7,31},{8,16},{9,... | collective-permute-start | bytes 24584 | tf_op jit(solution)/shard_map/ppermute | solution.py:500
  180.2 4.5 %collective-permute-start.30 = (f32[16,128]{1,0:T(8,128)S(1)}, f32[16,128]{1,0:T(8,128)S(1)}, u32[]{:S(2)}, u32[]{:S(2)}) collective-permute-start(f32[16,128]{1,0:T(8,128)S(1)} %get-tuple-element.130), channel_id=1, source_target_pairs={{0,16},{1,17},{2,18},{3,19},{4,20},{5,21},{6,22},{7,23},{8,24},{9,... | collective-permute-start | bytes 24584 | tf_op jit(solution)/shard_map/ppermute | solution.py:500
  180.3 3.7 %collective-permute-start.29 = (f32[16,128]{1,0:T(8,128)S(1)}, f32[16,128]{1,0:T(8,128)S(1)}, u32[]{:S(2)}, u32[]{:S(2)}) collective-permute-start(f32[16,128]{1,0:T(8,128)S(1)} %get-tuple-element.130), channel_id=1, source_target_pairs={{0,8},{1,9},{2,10},{3,11},{4,12},{5,13},{6,14},{7,15},{8,0},{9,1},... | collective-permute-start | bytes 24584 | tf_op jit(solution)/shard_map/ppermute | solution.py:500
  184.8 4.0 %collective-permute-start.32 = (f32[64,128]{1,0:T(8,128)S(1)}, f32[64,128]{1,0:T(8,128)S(1)}, u32[]{:S(2)}, u32[]{:S(2)}) collective-permute-start(f32[64,128]{1,0:T(8,128)S(1)} %get-tuple-element.153), channel_id=1, source_target_pairs={{0,2},{1,3},{2,0},{3,1},{4,6},{5,7},{6,4},{7,5},{8,10},{9,11},{10,... | collective-permute-start | bytes 98312 | tf_op jit(solution)/shard_map/ppermute | solution.py:500
  185.5 5.4 %collective-permute-start.34 = (f32[64,128]{1,0:T(8,128)S(1)}, f32[64,128]{1,0:T(8,128)S(1)}, u32[]{:S(2)}, u32[]{:S(2)}) collective-permute-start(f32[64,128]{1,0:T(8,128)S(1)} %get-tuple-element.153), channel_id=1, source_target_pairs={{0,6},{1,7},{2,4},{3,5},{4,2},{5,3},{6,0},{7,1},{8,14},{9,15},{10,... | collective-permute-start | bytes 98312 | tf_op jit(solution)/shard_map/ppermute | solution.py:500
  186.9 3.9 %collective-permute-start.33 = (f32[64,128]{1,0:T(8,128)S(1)}, f32[64,128]{1,0:T(8,128)S(1)}, u32[]{:S(2)}, u32[]{:S(2)}) collective-permute-start(f32[64,128]{1,0:T(8,128)S(1)} %get-tuple-element.153), channel_id=1, source_target_pairs={{0,4},{1,5},{2,6},{3,7},{4,0},{5,1},{6,2},{7,3},{8,12},{9,13},{10,... | collective-permute-start | bytes 98312 | tf_op jit(solution)/shard_map/ppermute | solution.py:500
  190.8 1.4 collective-permute-start.35
  (4 other events, 3.8 us)
